TPU v7x, 32 devices: a whole 2x2x4 slice. The times are simulated.
32 devices in a mesh: ctx: 4 (over x, core), vocab: 8 (over z, y).
Axes of the slice: x: 2, y: 2, z: 4, core: 2. Of those that a mesh axis runs over, the one named last changes fastest.
Arguments:
- hidden_state: bfloat16 [512, 7168], P('ctx'), may hold values from -50 to 50
- embedded_next: bfloat16 [512, 7168], P('ctx'), may hold values from -50 to 50
- gain_hidden: float32 [7168], replicated, may hold values from 0.1 to 1.9
- gain_embed: float32 [7168], replicated, may hold values from 0.1 to 1.9
- proj_hidden: bfloat16 [7168, 7168], P('ctx', 'vocab'), may hold values from -0.0625 to 0.0625
- proj_embed: bfloat16 [7168, 7168], P('ctx', 'vocab'), may hold values from -0.0625 to 0.0625
- final_gain: float32 [7168], P('vocab'), may hold values from 0.1 to 1.9
- head: bfloat16 [65536, 7168], P(('ctx', 'vocab')), may hold values from -0.4375 to 0.4375
- targets: int32 [512], replicated, may hold values from 0 to 65535
- loss_mask: int32 [512], replicated, may hold values 0 or 1
Outputs:
- mean_loss: float32 [], replicated
- grad_hidden: bfloat16 [512, 7168], P('ctx', 'vocab')
- grad_embed: bfloat16 [512, 7168], P('ctx', 'vocab')
- grad_gain_hidden: float32 [7168], P('vocab')
- grad_gain_embed: float32 [7168], P('vocab')
- grad_proj_hidden: bfloat16 [7168, 7168], P('ctx', 'vocab')
- grad_proj_embed: bfloat16 [7168, 7168], P('ctx', 'vocab')
- grad_final_gain: float32 [7168], P('vocab')
- grad_head: bfloat16 [65536, 7168], P(('ctx', 'vocab'))
All inputs are finite; a program needn't handle non-finite values.
Results may differ from a plain program's by a relative error of at most 0.023.
Values may be sent and summed in bfloat16 or wider, within the bound.
No kernel may reach another device: no remote copies, remote signals or barrier semaphores. Data moves between devices by JAX's collectives and lax.ppermute only.
A program may use at most 256 MiB of HBM per device.

v0:
```python
import jax
import jax.numpy as jnp
from jax import lax
from jax.sharding import PartitionSpec as P

EPSILON = 1e-06


def scale_of(values):
    return lax.rsqrt(jnp.mean(values * values, axis=-1, keepdims=True) + EPSILON)


def contract_first(left, right):
    return lax.dot_general(
        left, right, (((0,), (0,)), ((), ())), preferred_element_type=jnp.float32
    )


def contract_last(left, right):
    return lax.dot_general(
        left, right, (((1,), (1,)), ((), ())), preferred_element_type=jnp.float32
    )


def local(
    hidden_state,
    embedded_next,
    gain_hidden,
    gain_embed,
    proj_hidden,
    proj_embed,
    final_gain,
    head,
    targets,
    loss_mask,
):
    model_width = hidden_state.shape[1]
    token_total = targets.shape[0]
    hidden_wide = hidden_state.astype(jnp.float32)
    embed_wide = embedded_next.astype(jnp.float32)
    hidden_scale = scale_of(hidden_wide)
    embed_scale = scale_of(embed_wide)
    normed_hidden = (hidden_wide * hidden_scale * gain_hidden).astype(jnp.bfloat16)
    normed_embed = (embed_wide * embed_scale * gain_embed).astype(jnp.bfloat16)
    hidden_cols, embed_cols = (
        lax.all_to_all(normed_hidden, "ctx", split_axis=1, concat_axis=0, tiled=True),
        lax.all_to_all(normed_embed, "ctx", split_axis=1, concat_axis=0, tiled=True),
    )
    partial_proj = jnp.dot(hidden_cols, proj_hidden, preferred_element_type=jnp.float32) + jnp.dot(
        embed_cols, proj_embed, preferred_element_type=jnp.float32
    )
    projected = lax.psum(partial_proj, "ctx")
    row_squares = lax.psum(jnp.sum(projected * projected, axis=-1), "vocab")
    row_scale = lax.rsqrt(row_squares / model_width + EPSILON)[:, None]
    normed_piece = (projected * row_scale * final_gain).astype(jnp.bfloat16)
    normed_rows = lax.all_gather(normed_piece, "vocab", axis=1, tiled=True)
    logits = contract_last(normed_rows, head)
    vocab_local = head.shape[0]
    vocab_start = (
        lax.axis_index("ctx") * lax.axis_size("vocab") + lax.axis_index("vocab")
    ) * vocab_local
    vocab_ids = vocab_start + lax.iota(jnp.int32, vocab_local)
    is_target = targets[:, None] == vocab_ids[None, :]
    exp_part = jnp.sum(jnp.exp(logits), axis=-1)
    target_part = jnp.sum(jnp.where(is_target, logits, jnp.float32(0.0)), axis=-1)
    exp_total, target_logit = lax.psum((exp_part, target_part), ("ctx", "vocab"))
    log_total = jnp.log(exp_total)
    mask_weight = loss_mask.astype(jnp.float32)
    mean_loss = jnp.sum(mask_weight * (log_total - target_logit)) / token_total
    probs = jnp.exp(logits - log_total[:, None])
    logit_grad = (mask_weight[:, None] * (probs - is_target.astype(jnp.float32))).astype(
        jnp.bfloat16
    )
    grad_head = contract_first(logit_grad, normed_rows).astype(jnp.bfloat16)
    normed_part = jnp.dot(logit_grad, head, preferred_element_type=jnp.float32)
    vocab_summed = lax.psum_scatter(
        normed_part.astype(jnp.bfloat16), "vocab", scatter_dimension=1, tiled=True
    )
    normed_grad = lax.psum(vocab_summed, "ctx").astype(jnp.float32)
    grad_final_gain = jnp.sum(normed_grad * projected * row_scale, axis=0)
    scaled_grad = normed_grad * final_gain
    row_dot = lax.psum(jnp.sum(scaled_grad * projected, axis=-1), "vocab")
    proj_grad = (
        row_scale * scaled_grad
        - projected * (row_scale * row_scale * row_scale) * (row_dot[:, None] / model_width)
    ).astype(jnp.bfloat16)
    grad_proj_hidden = contract_first(hidden_cols, proj_grad).astype(jnp.bfloat16)
    grad_proj_embed = contract_first(embed_cols, proj_grad).astype(jnp.bfloat16)
    hidden_part = contract_last(proj_grad, proj_hidden)
    embed_part = contract_last(proj_grad, proj_embed)
    hidden_tokens, embed_tokens = (
        lax.all_to_all(
            hidden_part.astype(jnp.bfloat16), "ctx", split_axis=0, concat_axis=1, tiled=True
        ).astype(hidden_part.dtype),
        lax.all_to_all(
            embed_part.astype(jnp.bfloat16), "ctx", split_axis=0, concat_axis=1, tiled=True
        ).astype(embed_part.dtype),
    )
    hidden_back, embed_back = (
        lax.psum_scatter(
            hidden_tokens.astype(jnp.bfloat16), "vocab", scatter_dimension=1, tiled=True
        ).astype(jnp.float32),
        lax.psum_scatter(
            embed_tokens.astype(jnp.bfloat16), "vocab", scatter_dimension=1, tiled=True
        ).astype(jnp.float32),
    )
    slice_width = hidden_back.shape[1]
    feature_start = lax.axis_index("vocab") * slice_width
    hidden_slice = lax.dynamic_slice_in_dim(hidden_wide, feature_start, slice_width, 1)
    embed_slice = lax.dynamic_slice_in_dim(embed_wide, feature_start, slice_width, 1)
    hidden_gain_slice = lax.dynamic_slice_in_dim(gain_hidden, feature_start, slice_width, 0)
    embed_gain_slice = lax.dynamic_slice_in_dim(gain_embed, feature_start, slice_width, 0)
    hidden_dot, embed_dot = lax.psum(
        (
            jnp.sum(hidden_back * hidden_gain_slice * hidden_slice, axis=-1),
            jnp.sum(embed_back * embed_gain_slice * embed_slice, axis=-1),
        ),
        "vocab",
    )
    grad_hidden = (
        hidden_scale * (hidden_back * hidden_gain_slice)
        - hidden_slice
        * (hidden_scale * hidden_scale * hidden_scale)
        * (hidden_dot[:, None] / model_width)
    ).astype(jnp.bfloat16)
    grad_embed = (
        embed_scale * (embed_back * embed_gain_slice)
        - embed_slice
        * (embed_scale * embed_scale * embed_scale)
        * (embed_dot[:, None] / model_width)
    ).astype(jnp.bfloat16)
    grad_gain_hidden, grad_gain_embed = lax.psum(
        (
            jnp.sum(hidden_back * hidden_slice * hidden_scale, axis=0),
            jnp.sum(embed_back * embed_slice * embed_scale, axis=0),
        ),
        "ctx",
    )
    return (
        mean_loss,
        grad_hidden,
        grad_embed,
        grad_gain_hidden,
        grad_gain_embed,
        grad_proj_hidden,
        grad_proj_embed,
        grad_final_gain,
        grad_head,
    )


def solution(mesh):
    in_specs = (
        P("ctx", None),
        P("ctx", None),
        P(),
        P(),
        P("ctx", "vocab"),
        P("ctx", "vocab"),
        P("vocab"),
        P(("ctx", "vocab"), None),
        P(),
        P(),
    )
    out_specs = (
        P(),
        P("ctx", "vocab"),
        P("ctx", "vocab"),
        P("vocab"),
        P("vocab"),
        P("ctx", "vocab"),
        P("ctx", "vocab"),
        P("vocab"),
        P(("ctx", "vocab"), None),
    )
    return jax.shard_map(local, mesh=mesh, in_specs=in_specs, out_specs=out_specs, check_vma=False)
```

profile of v0, /device:TPU:2, one launch (start us, length us, event | category | flops | bytes accessed | tf_op | source)
XLA Modules:
  0.0 765.1 jit_solution(9192266195982598947)
XLA Ops:
  7.2 4.0 copy.33
  11.2 2.5 multiply_reduce_fusion
  13.7 5.1 multiply_convert_fusion
  18.8 4.4 all-to-all-start.1
  23.2 3.9 copy.31
  27.1 2.5 multiply_reduce_fusion.1
  29.6 5.1 multiply_convert_fusion.1
  34.6 8.9 %all-to-all-done.1 = bf16[128,4,1792]{0,2,1:T(8,128)(2,1)} async-done(((bf16[128,4,1792]{0,2,1:T(8,128)(2,1)}), bf16[128,4,1792]{0,2,1:T(8,128)(2,1)}, u32[]{:S(2)}, u32[]{:S(2)}) %all-to-all-start.1) | async-done | bytes 1835040 | tf_op jit(solution)/shard_map/all_to_all | solution.py:47
  43.6 6.6 all-to-all-start
  50.2 3.9 copy.34
  54.1 17.5 %all-to-all-done = bf16[128,4,1792]{0,2,1:T(8,128)(2,1)} async-done(((bf16[128,4,1792]{0,2,1:T(8,128)(2,1)}), bf16[128,4,1792]{0,2,1:T(8,128)(2,1)}, u32[]{:S(2)}, u32[]{:S(2)}) %all-to-all-start) | async-done | bytes 1835040 | tf_op jit(solution)/shard_map/all_to_all | solution.py:46
  71.5 3.8 copy.32
  75.4 4.6 fusion.28
  80.0 3.3 convolution_add_fusion
  83.5 48.4 %all-reduce.6.cloned.1.call-done = f32[512,896]{1,0:T(8,128)} async-done(((f32[512,896]{1,0:T(8,128)}), f32[512,896]{1,0:T(8,128)}) %all-reduce.6.cloned.1.call-update) | async-done | bytes 1835024 | tf_op jit(solution)/shard_map/psum | solution.py:52
  131.9 1.7 multiply_reduce_fusion.2
  133.6 21.6 %psum.71 = f32[512]{0:T(512)S(1)} all-reduce(f32[512]{0:T(512)S(1)} %multiply_reduce_fusion.2), channel_id=1, replica_groups=mesh['ctx'=4,'vocab'=8] {'vocab'}, use_global_device_ids=true, to_apply=%region_4.0 | all-reduce | flops 512 | bytes 4096 | tf_op jit(solution)/shard_map/psum | solution.py:53
  155.2 2.7 multiply_convert_fusion.2
  158.1 109.1 %all-gather.2.cloned.1.call-done = bf16[512,7168]{1,0:T(8,128)(2,1)} async-done(((bf16[512,896]{1,0:T(8,128)(2,1)}), bf16[512,7168]{1,0:T(8,128)(2,1)}) %all-gather.2.cloned.1.call-update) | async-done | bytes 7340048 | tf_op jit(solution)/shard_map/all_gather | solution.py:56
  267.2 22.7 %exponential_reduce_fusion = (f32[512]{0:T(512)S(1)}, f32[512]{0:T(512)S(1)}, f32[512,2048]{1,0:T(8,128)}) fusion(s32[2048]{0:T(1024)S(1)} %iota_add_fusion, s32[512]{0:T(512)S(1)} %copy-done.10, bf16[512,7168]{1,0:T(8,128)(2,1)} %all-gather.2.cloned.1.call-done, bf16[2048,7168]{1,0:T(8,128)(2,1)} %param.17), kind=kOutput, calls=%fused_computation.8 | convolution fusion | flops 15036579840 | bytes 40908800 | tf_op jit(solution)/shard_map/dot_general | solution.py:20
  289.9 39.3 %all-reduce = (f32[512]{0:T(512)S(1)}, f32[512]{0:T(512)S(1)}) all-reduce(f32[512]{0:T(512)S(1)} %get-tuple-element.28, f32[512]{0:T(512)S(1)} %get-tuple-element.27), channel_id=1, replica_groups=mesh['ctx'=4,'vocab'=8] {'ctx','vocab'}, use_global_device_ids=true, to_apply=%region_8.9 | all-reduce | flops 1024 | bytes 8192 | tf_op jit(solution)/shard_map/psum | solution.py:66
  329.8 24.8 %convolution_convert_fusion.1 = bf16[512,7168]{1,0:T(8,128)(2,1)} fusion(bf16[2048,7168]{1,0:T(8,128)(2,1)} %param.17, f32[512,2048]{1,0:T(8,128)} %get-tuple-element.49, f32[512]{0:T(512)S(1)} %get-tuple-element.43, f32[512]{0:T(512)S(1)} %convert_element_type.64, s32[2048]{0:T(1024)S(1)} %iota_add_fusion, s32[512]{0:T(512)S(1)} %copy-done.10), kind=kOutput, calls=%fused_computation.1 | convolution fusion | flops 15042347008 | bytes 40908800 | tf_op jit(solution)/shard_map/dot_general | solution.py:75
  354.7 10.4 %copy.39 = bf16[512,7168]{0,1:T(8,128)(2,1)} copy(bf16[512,7168]{1,0:T(8,128)(2,1)} %convolution_convert_fusion.1) | data formatting | bytes 14680064
  365.1 132.6 %reduce-scatter.10.cloned.1.call-done = bf16[896,512]{1,0:T(8,128)(2,1)} async-done(((bf16[7168,512]{1,0:T(8,128)(2,1)}), bf16[896,512]{1,0:T(8,128)(2,1)}) %reduce-scatter.10.cloned.1.call-update) | async-done | bytes 917520
  497.7 2.2 copy.40
  500.0 34.2 %all-reduce.8.cloned.1.call-done = bf16[512,896]{1,0:T(8,128)(2,1)} async-done(((bf16[512,896]{1,0:T(8,128)(2,1)}), bf16[512,896]{1,0:T(8,128)(2,1)}) %all-reduce.8.cloned.1.call-update) | async-done | bytes 917520 | tf_op jit(solution)/shard_map/psum | solution.py:79
  534.2 2.9 fusion.10
  537.2 21.5 %psum.75 = f32[512]{0:T(512)S(1)} all-reduce(f32[512]{0:T(512)S(1)} %get-tuple-element.34), channel_id=1, replica_groups=mesh['ctx'=4,'vocab'=8] {'vocab'}, use_global_device_ids=true, to_apply=%region_13.14 | all-reduce | flops 512 | bytes 4096 | tf_op jit(solution)/shard_map/psum | solution.py:82
  558.6 2.2 fusion.7
  560.9 2.1 convolution_convert_fusion.4
  563.0 25.7 %all_to_all.76 = bf16[4,128,1792]{2,1,0:T(8,128)(2,1)} all-to-all(bf16[4,128,1792]{2,1,0:T(8,128)(2,1)S(1)} %bitcast.41), channel_id=1, replica_groups=mesh['ctx'=4,'vocab'=8] {'ctx'}, dimensions={0} | all-to-all | bytes 3670016 | tf_op jit(solution)/shard_map/all_to_all | solution.py:95
  588.6 3.8 copy.36
  592.5 5.5 convolution_convert_fusion.5
  598.0 6.0 all-to-all-start.2
  604.2 3.7 convert_element_type.67
  607.9 2.2 convert_element_type.65
  610.8 14.6 %all-to-all-done.2 = bf16[4,128,1792]{2,1,0:T(8,128)(2,1)} async-done(((bf16[4,128,1792]{2,1,0:T(8,128)(2,1)}), bf16[4,128,1792]{2,1,0:T(8,128)(2,1)}, u32[]{:S(2)}, u32[]{:S(2)}) %all-to-all-start.2) | async-done | bytes 1835040 | tf_op jit(solution)/shard_map/all_to_all | solution.py:92
  625.4 3.8 copy.35
  629.2 24.8 %convolution_convert_fusion = bf16[2048,7168]{1,0:T(8,128)(2,1)} fusion(bf16[512,7168]{1,0:T(8,128)(2,1)} %all-gather.2.cloned.1.call-done, f32[512,2048]{1,0:T(8,128)} %get-tuple-element.49, f32[512]{0:T(512)S(1)} %get-tuple-element.43, f32[512]{0:T(512)S(1)} %convert_element_type.64, s32[2048]{0:T(1024)S(1)} %iota_add_fusion, s32[512]{0:T(512)S(1)} %copy-done.10), kind=kOutput, calls=%fused_computation | convolution fusion | flops 15053357056 | bytes 40908800 | tf_op jit(solution)/shard_map/dot_general | solution.py:14
  654.1 5.7 convolution_convert_fusion.2
  659.8 3.8 convolution_convert_fusion.3
  663.6 1.5 fusion.24
  665.1 59.9 %reduce-scatter.6.cloned.1.call-done = bf16[128,896]{0,1:T(8,128)(2,1)} async-done(((bf16[128,7168]{0,1:T(8,128)(2,1)}), bf16[128,896]{0,1:T(8,128)(2,1)}) %reduce-scatter.6.cloned.1.call-update) | async-done | bytes 229392 | tf_op jit(solution)/shard_map/reduce_scatter | solution.py:100
  725.0 1.5 fusion.22
  726.5 19.1 %all-reduce.1 = (f32[128]{0:T(128)S(1)}, f32[128]{0:T(128)S(1)}) all-reduce(f32[128]{0:T(128)S(1)} %get-tuple-element.32, f32[128]{0:T(128)S(1)} %get-tuple-element.30), channel_id=1, replica_groups=mesh['ctx'=4,'vocab'=8] {'vocab'}, use_global_device_ids=true, to_apply=%region_16.17 | all-reduce | flops 256 | bytes 2048 | tf_op jit(solution)/shard_map/psum | solution.py:113
  745.6 2.3 fusion.16
  747.9 1.8 copy.38
  750.5 6.7 all-reduce.2
  (47 shorter events, 2.2 us)
Async XLA Ops:
  7.2 72.8 %copy-start = (bf16[1792,896]{1,0:T(8,128)(2,1)S(1)}, bf16[1792,896]{1,0:T(8,128)(2,1)}, u32[]{:S(2)}) copy-start(bf16[1792,896]{1,0:T(8,128)(2,1)} %param.15) | copy-start | bytes 9633796
  7.2 6.5 copy-start.7
  18.8 24.8 %all-to-all-start.1 = ((bf16[128,4,1792]{0,2,1:T(8,128)(2,1)}), bf16[128,4,1792]{0,2,1:T(8,128)(2,1)}, u32[]{:S(2)}, u32[]{:S(2)}) async-start(bf16[128,4,1792]{0,2,1:T(8,128)(2,1)} %bitcast.34), calls=%async_computation.1 | async-start | bytes 3670016 | tf_op jit(solution)/shard_map/all_to_all | solution.py:47
  23.2 6.4 copy-start.6
  43.6 28.0 %all-to-all-start = ((bf16[128,4,1792]{0,2,1:T(8,128)(2,1)}), bf16[128,4,1792]{0,2,1:T(8,128)(2,1)}, u32[]{:S(2)}, u32[]{:S(2)}) async-start(bf16[128,4,1792]{0,2,1:T(8,128)(2,1)} %bitcast.33), calls=%async_computation | async-start | bytes 3670016 | tf_op jit(solution)/shard_map/all_to_all | solution.py:46
  50.2 81.7 %all-reduce.6.cloned.1.call-start = ((), (), s32[]{:S(2)}) async-start(), calls=%async_computation.7 | async-start | bytes 3670016 | tf_op jit(solution)/shard_map/psum | solution.py:52
  75.4 4.7 copy-start.2
  83.4 71.8 %copy-start.8 = (f32[896]{0:T(1024)S(1)}, f32[896]{0:T(1024)}, u32[]{:S(2)}) copy-start(f32[896]{0:T(1024)} %param.16) | copy-start | bytes 10756
  83.4 74.7 %copy-start.9 = (s32[512]{0:T(512)S(1)}, s32[512]{0:T(512)}, u32[]{:S(2)}) copy-start(s32[512]{0:T(512)} %param.19) | copy-start | bytes 6148
  83.4 183.8 %copy-start.10 = (s32[512]{0:T(512)S(1)}, s32[512]{0:T(512)}, u32[]{:S(2)}) copy-start(s32[512]{0:T(512)} %param.18) | copy-start | bytes 6148
  83.4 183.8 %all-gather.2.cloned.1.call-start = ((), (), s32[]{:S(2)}) async-start(), calls=%async_computation.8 | async-start | bytes 8257536 | tf_op jit(solution)/shard_map/all_gather | solution.py:56
  157.8 339.9 %reduce-scatter.10.cloned.1.call-start = ((), (), s32[]{:S(2)}) async-start(), calls=%async_computation.12 | async-start | bytes 8257536
  365.1 169.1 %all-reduce.8.cloned.1.call-start = ((), (), s32[]{:S(2)}) async-start(), calls=%async_computation.9 | async-start | bytes 1835008 | tf_op jit(solution)/shard_map/psum | solution.py:79
  500.0 163.6 %reduce-scatter.8.cloned.1.call-start = ((), (), s32[]{:S(2)}) async-start(), calls=%async_computation.11 | async-start | bytes 2064384 | tf_op jit(solution)/shard_map/reduce_scatter | solution.py:103
  560.9 2.1 copy-start.4
  598.0 27.4 %all-to-all-start.2 = ((bf16[4,128,1792]{2,1,0:T(8,128)(2,1)}), bf16[4,128,1792]{2,1,0:T(8,128)(2,1)}, u32[]{:S(2)}, u32[]{:S(2)}) async-start(bf16[4,128,1792]{2,1,0:T(8,128)(2,1)} %bitcast.40), calls=%async_computation.2 | async-start | bytes 3670016 | tf_op jit(solution)/shard_map/all_to_all | solution.py:92
  604.0 120.9 %reduce-scatter.6.cloned.1.call-start = ((), (), s32[]{:S(2)}) async-start(), calls=%async_computation.10 | async-start | bytes 2064384 | tf_op jit(solution)/shard_map/reduce_scatter | solution.py:100
  604.0 3.9 copy-start.1
  654.1 5.7 copy-start.3
  654.1 5.7 copy-start.5
Sparse Core Ops, SparseCore 0:
  83.5 48.3 all-reduce.5
  158.0 109.1 all-gather.1
  365.2 132.4 reduce-scatter.9
  500.5 33.6 all-reduce.7
  592.6 63.5 reduce-scatter.7
  659.9 65.0 reduce-scatter.5
where the time goes:
time: 768 us; the launch traced here: 765 us
  waiting for transfers between devices  425 us (55%)
  blocking collectives  134 us (17%)
  matrix products  97.4 us (13%)
  local copies, waits for them, and re-layouts  38.7 us (5%)
  other arithmetic  36.4 us (5%)
  starting transfers between devices  17.4 us (2%)
  between operations  16.1 us (2%)
    unnamed x7, waiting for transfers between devices  133 us
    all_gather x1, waiting for transfers between devices, local(): normed_rows = lax.all_gather(normed_piece, 'vocab', axis=1, tiled=True)  109 us
    reduce_scatter x1, waiting for transfers between devices, local(): lax.psum_scatter(hidden_tokens.astype(jnp.bfloat16), 'vocab', scatter_dim...  59.9 us
    psum x1, waiting for transfers between devices, local(): projected = lax.psum(partial_proj, 'ctx')  48.4 us
    psum x1, blocking collectives, local(): lax.psum((exp_part, target_part), ('ctx', 'vocab'))  39.3 us
    dot_general x3, matrix products, contract_first(): lax.dot_general(left, right, (((0,), (0,)), ((), ())), preferred_element_...  34.3 us
    psum x1, waiting for transfers between devices, local(): normed_grad = lax.psum(vocab_summed, 'ctx').astype(jnp.float32)  34.2 us
    dot_general x3, matrix products, contract_last(): lax.dot_general(left, right, (((1,), (1,)), ((), ())), preferred_element_...  30.3 us
  transfers between devices with their start and end apart: 9, of which 8 were waited for; matrix products, arithmetic and copies ran while one was open for 9% of the time, Pallas kernels for 0%

commit v1 on v0

v1 whole, which is shorter than its diff:
```python
import jax
import jax.numpy as jnp
from jax import lax
from jax.sharding import PartitionSpec as P

EPSILON = 1e-06
PARTS = 2
F32 = jnp.float32
BF16 = jnp.bfloat16


class Dim:
    def __init__(self, axis, size, n, stride):
        self.axis, self.size, self.n, self.stride = axis, size, n, stride

    def place(self):
        return (lax.axis_index(self.axis) // self.stride) % self.n

    def move(self, value, target):
        pairs = []
        for index in range(self.size):
            here = (index // self.stride) % self.n
            there = target(here)
            if there is not None and 0 <= there < self.n:
                pairs.append((index, index + (there - here) * self.stride))
        return lax.ppermute(value, self.axis, pairs)

    def swap(self, value, bit):
        return self.move(value, lambda here: here ^ bit)

    def turn(self, value, by):
        return self.move(value, lambda here: (here + by) % self.n)


def butterfly(value, dims):
    for dim in dims:
        bit = 1
        while bit < dim.n:
            value = value + dim.swap(value, bit)
            bit *= 2
    return value


def line_gather(value, dim):
    n, here = dim.n, dim.place()
    if n == 2:
        other = dim.swap(value, 1)
        return [jnp.where(here == 0, value, other), jnp.where(here == 0, other, value)]
    up, down = [value], [value]
    for step in range(1, n):
        up.append(dim.move(up[-1], lambda k: k + 1 if k >= step - 1 else None))
        down.append(dim.move(down[-1], lambda k: k - 1 if k <= n - step else None))
    out = []
    for spot in range(n):
        piece = value
        for step in range(1, n):
            if spot + step < n:
                piece = jnp.where(here == spot + step, up[step], piece)
            if spot - step >= 0:
                piece = jnp.where(here == spot - step, down[step], piece)
        out.append(piece)
    return out


def line_scatter(chunks, dim):
    n, here = dim.n, dim.place()

    def pick(at):
        return lax.dynamic_index_in_dim(chunks, jnp.clip(at, 0, n - 1), 0, keepdims=False)

    if n == 2:
        return pick(here).astype(F32) + dim.swap(pick(1 - here), 1).astype(F32)
    up = down = None
    for step in range(1, n):
        up_send, down_send = pick(here + n - step), pick(here - n + step)
        if up is not None:
            up_send = (up_send.astype(F32) + up.astype(F32)).astype(BF16)
            down_send = (down_send.astype(F32) + down.astype(F32)).astype(BF16)
        up = dim.move(up_send, lambda k: k + 1 if k <= step - 1 else None)
        down = dim.move(down_send, lambda k: k - 1 if k >= n - step else None)
    return pick(here).astype(F32) + up.astype(F32) + down.astype(F32)


def contract_first(left, right):
    return lax.dot_general(left, right, (((0,), (0,)), ((), ())), preferred_element_type=F32)


def contract_last(left, right):
    return lax.dot_general(left, right, (((1,), (1,)), ((), ())), preferred_element_type=F32)


def dot(left, right):
    return jnp.dot(left, right, preferred_element_type=F32)


def cut(array, start, width, axis):
    return lax.dynamic_slice_in_dim(array, start, width, axis)


def local(
    hidden_state,
    embedded_next,
    gain_hidden,
    gain_embed,
    proj_hidden,
    proj_embed,
    final_gain,
    head,
    targets,
    loss_mask,
):
    nc, nv = lax.axis_size("ctx"), lax.axis_size("vocab")
    nx, va = nc // 2, 4
    vb = nv // va
    core = Dim("ctx", nc, 2, 1)
    dim_x = Dim("ctx", nc, nx, 2)
    dim_b = Dim("vocab", nv, vb, 1)
    dim_a = Dim("vocab", nv, va, vb)
    every = (core, dim_x, dim_b, dim_a)
    own, slot = lax.axis_index("ctx"), lax.axis_index("vocab")
    x, c, a, b = own // 2, own % 2, slot // vb, slot % vb
    even = b % 2 == 0

    width = hidden_state.shape[1]
    block = hidden_state.shape[0]
    token_total = targets.shape[0]
    feat, cols = proj_hidden.shape
    rows = block // PARTS
    half = rows // 2
    vocab_local = head.shape[0]

    def relative_place(block_index):
        return (c ^ (block_index % 2)) * nx + (x - block_index // 2) % nx

    order = jnp.stack([relative_place(jnp.int32(i)) for i in range(nc)])
    to_absolute = order[:, None] == jnp.arange(nc, dtype=jnp.int32)[None, :]

    def absolute(value):
        value = value.reshape(value.shape[:-1] + (nc, rows))
        return jnp.sum(jnp.where(to_absolute[:, :, None], value[..., None, :, :], 0), axis=-2)

    def relative(value):
        value = jnp.sum(jnp.where(to_absolute[:, :, None], value[..., :, None, :], 0), axis=-3)
        return value.reshape(value.shape[:-2] + (nc * rows,))

    def gather_x(value):
        return jnp.stack([value] + [dim_x.turn(value, r) for r in range(1, nx)])

    hidden_wide, embed_wide = hidden_state.astype(F32), embedded_next.astype(F32)
    scales = lax.rsqrt(
        jnp.stack(
            [jnp.mean(hidden_wide * hidden_wide, axis=-1), jnp.mean(embed_wide * embed_wide, axis=-1)]
        )
        + EPSILON
    )
    scales_x = gather_x(scales)
    scales_all = jnp.concatenate([scales_x, core.swap(scales_x, 1)])
    gain_h_own = cut(gain_hidden, own * feat, feat, 0)
    gain_e_own = cut(gain_embed, own * feat, feat, 0)

    def inputs(part):
        hid = hidden_state[part * rows : (part + 1) * rows]
        emb = embedded_next[part * rows : (part + 1) * rows]
        hid_list = [cut(hid, x * 2 * feat, 2 * feat, 1)]
        emb_list = [cut(emb, x * 2 * feat, 2 * feat, 1)]
        for r in range(1, nx):
            start = ((x + r) % nx) * 2 * feat
            send = jnp.where(even, cut(hid, start, 2 * feat, 1), cut(emb, start, 2 * feat, 1))
            got = dim_x.turn(send, r)
            twin = dim_b.swap(got, 1)
            hid_list.append(jnp.where(even, got, twin))
            emb_list.append(jnp.where(even, twin, got))
        out = []
        for kind, (pieces, gain) in enumerate(((hid_list, gain_h_own), (emb_list, gain_e_own))):
            mine = [cut(piece, c * feat, feat, 1) for piece in pieces]
            theirs = [core.swap(cut(piece, (1 - c) * feat, feat, 1), 1) for piece in pieces]
            raw = jnp.concatenate(mine + theirs).astype(F32)
            scale = scales_all[:, kind, part * rows : (part + 1) * rows].reshape(nc * rows, 1)
            out.append((raw * scale * gain).astype(BF16))
        return out

    def project(normed_h, normed_e):
        part_h, part_e = dot(normed_h, proj_hidden), dot(normed_e, proj_embed)
        total = part_h + part_e
        mine, theirs = total[: nx * rows], total[nx * rows :].astype(BF16)
        mine = mine + core.swap(theirs, 1).astype(F32)
        projected = mine[:rows]
        for r in range(1, nx):
            piece = mine[r * rows : (r + 1) * rows].astype(BF16)
            projected = projected + dim_x.turn(piece, -r).astype(F32)
        return projected, part_h, part_e

    def spread(projected):
        squares = jnp.sum(projected * projected, axis=-1)
        mine = jnp.arange(nc, dtype=jnp.int32)[:, None] == own
        squares = butterfly(jnp.where(mine, squares[None, :], 0.0), every)
        row_scale = relative(lax.rsqrt(squares / width + EPSILON))
        piece = (projected * final_gain).astype(BF16)
        along = jnp.stack(line_gather(piece, dim_a))
        first = jnp.stack(line_gather(along[:, :half], dim_b))
        first = gather_x(first)
        second = gather_x(along[:, half:])
        second = jnp.stack(line_gather(second, dim_b), axis=1)
        lines = []
        for r in range(nx):
            for source in (first, second):
                lines.append(
                    jnp.concatenate(
                        [source[r, q, p] for p in range(va) for q in range(vb)], axis=1
                    )
                )
        mine = jnp.concatenate(lines)
        return jnp.concatenate([mine, core.swap(mine, 1)]), row_scale

    vocab_ids = (own * nv + slot) * vocab_local + lax.iota(jnp.int32, vocab_local)
    mask_weight = loss_mask.astype(F32).reshape(nc, block)
    target_blocks = targets.reshape(nc, block)

    def cross_entropy(part, gathered, row_scale):
        logits = contract_last(gathered, head) * row_scale[:, None]
        target = relative(target_blocks[:, part * rows : (part + 1) * rows])
        mask = relative(mask_weight[:, part * rows : (part + 1) * rows])
        is_target = target[:, None] == vocab_ids[None, :]
        power = jnp.exp(logits)
        sums = jnp.stack(
            [
                jnp.sum(power, axis=-1),
                jnp.sum(power * (logits * F32(1.0 / 256.0)), axis=-1),
                jnp.sum(jnp.where(is_target, logits, F32(0.0)), axis=-1),
            ]
        )
        sums = butterfly(absolute(sums), every)
        total, weighted, target_logit = sums[0], sums[1], sums[2]
        log_total = jnp.log(total)
        loss = jnp.sum(
            mask_weight[:, part * rows : (part + 1) * rows] * (log_total - target_logit)
        )
        scaled_dot = mask * relative(weighted / total * F32(256.0) - target_logit)
        probs = jnp.exp(logits - relative(log_total)[:, None])
        scaled_grad = ((mask * row_scale)[:, None] * (probs - is_target.astype(F32))).astype(BF16)
        return scaled_grad, scaled_dot, loss

    def column_chunk(value, place):
        return jnp.stack([cut(value, (p * vb + place) * cols, cols, value.ndim - 1) for p in range(va)])

    def collect(scaled_grad):
        partial = dot(scaled_grad, head)
        mine, theirs = partial[: nx * rows], partial[nx * rows :].astype(BF16)
        mine = (mine + core.swap(theirs, 1).astype(F32)).astype(BF16)
        mine = mine.reshape(nx, rows, width)
        first = mine[0, :half].astype(F32)
        for r in range(1, nx):
            first = first + dim_x.turn(mine[r, :half], -r).astype(F32)
        first = first.astype(BF16)
        kept = column_chunk(first, b).astype(F32)
        for r in range(1, vb):
            kept = kept + dim_b.turn(column_chunk(first, (b + r) % vb), r).astype(F32)
        first = kept.astype(BF16)
        second = mine[:, half:]
        kept = column_chunk(second, b).astype(F32)
        for r in range(1, vb):
            kept = kept + dim_b.turn(column_chunk(second, (b + r) % vb), r).astype(F32)
        second = kept.astype(BF16)
        kept = second[:, 0].astype(F32)
        for r in range(1, nx):
            kept = kept + dim_x.turn(second[:, r], -r).astype(F32)
        second = kept.astype(BF16)
        summed = line_scatter(jnp.concatenate([first, second], axis=1), dim_a).astype(BF16)
        along = gather_x(summed)
        along = jnp.concatenate([along, core.swap(along, 1)])
        return along.reshape(nc * rows, cols)

    def final_move(value):
        pairs = []
        ratio = nv // nc
        for i in range(nc):
            for j in range(nv):
                pairs.append((i * nv + j, (j // ratio) * nv + i * ratio + j % ratio))
        return lax.ppermute(value, ("ctx", "vocab"), pairs)

    def back(proj_grad, weight):
        def product(place):
            picked = [
                cut(proj_grad, relative_place((p * vb + place) // 2) * rows, rows, 0)
                for p in range(va)
            ]
            weight_half = cut(weight, (place % 2) * cols, cols, 0)
            return contract_last(jnp.concatenate(picked), weight_half)

        sends = [dim_b.swap(product(b ^ r).astype(BF16), r) for r in range(1, vb)]
        kept = product(b)
        for got in sends:
            kept = kept + got.astype(F32)
        kept = kept.astype(BF16).reshape(va, rows, cols)
        return final_move(line_scatter(kept, dim_a).astype(BF16)).astype(F32)

    normed_h, normed_e, halves, gathered, row_scales = [], [], [], [], []
    for part in range(PARTS):
        nh, ne = inputs(part)
        projected, part_h, part_e = project(nh, ne)
        rows_all, row_scale = spread(projected)
        normed_h.append(nh)
        normed_e.append(ne)
        halves.append((part_h, part_e))
        gathered.append(rows_all)
        row_scales.append(row_scale)

    logit_grads, scaled_dots = [], []
    mean_loss = F32(0.0)
    for part in range(PARTS):
        scaled_grad, scaled_dot, loss = cross_entropy(part, gathered[part], row_scales[part])
        logit_grads.append(scaled_grad)
        scaled_dots.append(scaled_dot)
        mean_loss = mean_loss + loss
    mean_loss = mean_loss / token_total

    proj_grads, hidden_backs, embed_backs, dots = [], [], [], []
    grad_final_gain = jnp.zeros((cols,), F32)
    for part in range(PARTS):
        scaled = collect(logit_grads[part]).astype(F32)
        projected = cut(gathered[part], slot * cols, cols, 1).astype(F32) / final_gain
        grad_final_gain = grad_final_gain + jnp.sum(scaled * projected, axis=0)
        coefficient = row_scales[part] * row_scales[part] * scaled_dots[part] / width
        proj_grad = (scaled * final_gain - projected * coefficient[:, None]).astype(BF16)
        proj_grads.append(proj_grad)
        wide = proj_grad.astype(F32)
        part_h, part_e = halves[part]
        sums = jnp.stack([jnp.sum(wide * part_h, axis=-1), jnp.sum(wide * part_e, axis=-1)])
        sums = butterfly(absolute(sums), every)
        dots.append(lax.dynamic_index_in_dim(sums, own, 1, keepdims=False))
        hidden_backs.append(back(proj_grad, proj_hidden))
        embed_backs.append(back(proj_grad, proj_embed))

    rows_all = jnp.concatenate(gathered)
    grad_head = contract_first(jnp.concatenate(logit_grads), rows_all).astype(BF16)
    proj_grad = jnp.concatenate(proj_grads)
    wide_h = contract_first(jnp.concatenate(normed_h), proj_grad)
    wide_e = contract_first(jnp.concatenate(normed_e), proj_grad)
    grad_proj_hidden, grad_proj_embed = wide_h.astype(BF16), wide_e.astype(BF16)
    gains = jnp.stack(
        [
            jnp.sum(wide_h * proj_hidden.astype(F32), axis=1) / gain_h_own,
            jnp.sum(wide_e * proj_embed.astype(F32), axis=1) / gain_e_own,
        ]
    )
    gains = butterfly(gains, (dim_b, dim_a))
    gains = final_move(cut(gains, (b % 2) * cols, cols, 1))

    def finish(backs, wide, gain, kind):
        back_all = jnp.concatenate(backs)
        scale = scales[kind][:, None]
        dot_all = jnp.concatenate([pair[kind] for pair in dots])[:, None]
        source = cut(wide, slot * cols, cols, 1).astype(F32)
        gain_piece = cut(gain, slot * cols, cols, 0)
        return (
            scale * (back_all * gain_piece) - source * (scale * scale) * (dot_all / width)
        ).astype(BF16)

    return (
        mean_loss,
        finish(hidden_backs, hidden_state, gain_hidden, 0),
        finish(embed_backs, embedded_next, gain_embed, 1),
        gains[0],
        gains[1],
        grad_proj_hidden,
        grad_proj_embed,
        grad_final_gain,
        grad_head,
    )


def solution(mesh):
    in_specs = (
        P("ctx", None),
        P("ctx", None),
        P(),
        P(),
        P("ctx", "vocab"),
        P("ctx", "vocab"),
        P("vocab"),
        P(("ctx", "vocab"), None),
        P(),
        P(),
    )
    out_specs = (
        P(),
        P("ctx", "vocab"),
        P("ctx", "vocab"),
        P("vocab"),
        P("vocab"),
        P("ctx", "vocab"),
        P("ctx", "vocab"),
        P("vocab"),
        P(("ctx", "vocab"), None),
    )
    return jax.shard_map(local, mesh=mesh, in_specs=in_specs, out_specs=out_specs, check_vma=False)
```

time: 768 us -> 665 us (0.87)
  waiting for transfers between devices: 425 us -> 133 us
  starting transfers between devices: 17.4 us -> 246 us
  blocking collectives: 134 us -> 0 us
  local copies, waits for them, and re-layouts: 38.7 us -> 103 us
  other arithmetic: 36.4 us -> 57.4 us
  matrix products: 97.4 us -> 110 us
  between operations: 16.1 us -> 5.65 us
    ppermute x0 -> x132, starting transfers between devices: none -> 246 us  [the longest x127 218 us: move(): return lax.ppermute(value, self.axis, pairs)]
    unnamed x7 -> x0, waiting for transfers between devices: 133 us -> none
    ppermute x0 -> x132, waiting for transfers between devices: none -> 133 us  [the longest x127 123 us: move(): return lax.ppermute(value, self.axis, pairs)]
    all_gather x1 -> x0, waiting for transfers between devices: 109 us -> none  [local(): normed_rows = lax.all_gather(normed_piece, 'vocab', axis=1, tiled=True)]
    psum x5 -> x0, blocking collectives: 108 us -> none  [the longest x1 39.3 us: local(): lax.psum((exp_part, target_part), ('ctx', 'vocab'))]
    psum x2 -> x0, waiting for transfers between devices: 82.6 us -> none  [the longest x1 48.4 us: local(): projected = lax.psum(partial_proj, 'ctx')]
    reduce_scatter x2 -> x0, waiting for transfers between devices: 59.9 us -> none  [the longest x1 59.9 us: local(): lax.psum_scatter(hidden_tokens.astype(jnp.bfloat16), 'vocab', scatter_dim...]
    unnamed x28 -> x203, local copies, waits for them, and re-layouts: 23.2 us -> 72.8 us
  transfers between devices with their start and end apart: 9 -> 132, of which waited for: 8 -> 48; matrix products, arithmetic and copies ran while one was open for 9% -> 30% of each run, Pallas kernels for 0% -> 0%
where the time goes in v1:
time: 665 us; the launch traced here: 655 us
  starting transfers between devices  246 us (37%)
  waiting for transfers between devices  133 us (20%)
  matrix products  110 us (17%)
  local copies, waits for them, and re-layouts  103 us (15%)
  other arithmetic  57.4 us (9%)
    ppermute x127, starting transfers between devices, move(): return lax.ppermute(value, self.axis, pairs)  218 us
    ppermute x127, waiting for transfers between devices, move(): return lax.ppermute(value, self.axis, pairs)  123 us
    unnamed x203, local copies, waits for them, and re-layouts  72.8 us
    dot_general x10, matrix products, contract_last(): lax.dot_general(left, right, (((1,), (1,)), ((), ())), preferred_element_...  43 us
    dot_general x6, matrix products, dot(): return jnp.dot(left, right, preferred_element_type=F32)  36.8 us
    dot_general x3, matrix products, contract_first(): lax.dot_general(left, right, (((0,), (0,)), ((), ())), preferred_element_...  30.2 us
    ppermute x5, starting transfers between devices, final_move(): return lax.ppermute(value, ('ctx', 'vocab'), pairs)  28.2 us
    dynamic_slice x14, local copies, waits for them, and re-layouts, cut(): return lax.dynamic_slice_in_dim(array, start, width, axis)  14.2 us
  transfers between devices with their start and end apart: 132, of which 48 were waited for; matrix products, arithmetic and copies ran while one was open for 30% of the time, Pallas kernels for 0%

profile of v1, /device:TPU:2, one launch (start us, length us, event | category | flops | bytes accessed | tf_op | source)
XLA Modules:
  0.0 654.6 jit_solution(16077784038888772769)
XLA Ops:
  13.4 6.6 %collective-permute-start.31 = (bf16[64,3584]{1,0:T(8,128)(2,1)S(1)}, bf16[64,3584]{1,0:T(8,128)(2,1)}, u32[]{:S(2)}, u32[]{:S(2)}) collective-permute-start(bf16[64,3584]{1,0:T(8,128)(2,1)S(1)} %dynamic-slice_select_fusion), channel_id=1, source_target_pairs={{0,16},{8,24},{16,0},{24,8},{1,17},{9,25},{17,1},{25,9},{2,18},{10... | collective-permute-start | bytes 1376264 | tf_op jit(solution)/shard_map/ppermute | solution.py:26
  25.9 5.8 collective-permute-done.31
  36.8 4.4 collective-permute-done
  44.9 5.8 collective-permute-start.36
  54.8 5.8 collective-permute-start.7
  60.9 5.7 collective-permute-start.34
  79.7 3.8 collective-permute-done.9
  85.5 4.6 collective-permute-start.10
  92.0 5.2 collective-permute-start.39
  113.1 4.8 collective-permute-done.15
  134.9 5.7 collective-permute-done.18
  162.3 6.1 collective-permute-done.45
  172.5 5.5 collective-permute-done.22
  193.3 5.4 collective-permute-done.47
  227.3 15.9 %exponential_reduce_fusion.1 = (f32[256]{0:T(256)S(1)}, f32[256]{0:T(256)S(1)}, f32[256]{0:T(256)S(1)}, f32[256,2048]{1,0:T(8,128)}) fusion(s32[2048]{0:T(1024)S(1)} %iota_add_fusion, s32[256]{0:T(256)S(1)} %eq.217, f32[256]{0:T(256)S(1)} %mul.603, bf16[256,7168]{1,0:T(8,128)(2,1)} %copy-done.37, bf16[2048,7168]{1,0:T(8,128)(2,1)} %param.17), kind=kOutput, calls=%fused_computation.31 | convolution fusion | flops 7520387072 | bytes 35140608 | tf_op jit(solution)/shard_map/dot_general | solution.py:89
  260.8 4.9 collective-permute-start.54
  271.4 3.9 constant_dynamic-update-slice_fusion.88
  275.3 16.8 %exponential_reduce_fusion = (f32[256]{0:T(256)S(1)}, f32[256]{0:T(256)S(1)}, f32[256]{0:T(256)S(1)}, bf16[256,2048]{1,0:T(8,128)(2,1)}, f32[256,2048]{1,0:T(8,128)}) fusion(s32[2048]{0:T(1024)S(1)} %iota_add_fusion, s32[256]{0:T(256)S(1)} %eq.221, s32[256]{0:T(256)S(1)} %eq.217, f32[256,2048]{1,0:T(8,128)} %get-tuple-element.420, f32[256]{0:T(256)S(1)} %sub.288, ...), kind=kOutput, calls=%fused_computation.30 | convolution fusion | flops 7523532800 | bytes 38289408 | tf_op jit(solution)/shard_map/dot_general | solution.py:89
  305.1 3.6 copy.29
  308.7 5.6 copy.30
  316.9 13.6 %fusion.182 = f32[256,7168]{1,0:T(8,128)S(1)} fusion(bf16[256,2048]{1,0:T(8,128)(2,1)} %get-tuple-element.386, bf16[2048,7168]{1,0:T(8,128)(2,1)} %param.17), kind=kOutput, calls=%fused_computation.734 | convolution fusion | flops 7516192768 | bytes 37748736 | tf_op jit(solution)/shard_map/dot_general | solution.py:93
  339.0 16.8 %fusion.183 = f32[256,7168]{1,0:T(8,128)} fusion(bf16[256,2048]{1,0:T(8,128)(2,1)S(1)} %fusion.9, bf16[2048,7168]{1,0:T(8,128)(2,1)} %param.17), kind=kOutput, calls=%fused_computation.735 | convolution fusion | flops 7516192768 | bytes 37748736 | tf_op jit(solution)/shard_map/dot_general | solution.py:93
  366.1 8.3 %collective-permute-done.61 = bf16[32,7168]{1,0:T(8,128)(2,1)S(1)} collective-permute-done((bf16[32,7168]{1,0:T(8,128)(2,1)S(1)}, bf16[32,7168]{1,0:T(8,128)(2,1)S(1)}, u32[]{:S(2)}, u32[]{:S(2)}) %collective-permute-start.61) | collective-permute-done | bytes 458784 | tf_op jit(solution)/shard_map/ppermute | solution.py:26
  377.0 7.3 %collective-permute-done.82 = bf16[32,7168]{1,0:T(8,128)(2,1)S(1)} collective-permute-done((bf16[32,7168]{1,0:T(8,128)(2,1)S(1)}, bf16[32,7168]{1,0:T(8,128)(2,1)S(1)}, u32[]{:S(2)}, u32[]{:S(2)}) %collective-permute-start.82) | collective-permute-done | bytes 458784 | tf_op jit(solution)/shard_map/ppermute | solution.py:26
  400.1 4.0 collective-permute-start.87
  404.9 4.9 collective-permute-start.67
  411.2 5.2 collective-permute-start.88
  428.7 22.6 %convolution_convert_fusion = bf16[2048,7168]{1,0:T(8,128)(2,1)} fusion(bf16[512,7168]{1,0:T(8,128)(2,1)} %get-tuple-element.70, bf16[256,2048]{1,0:T(8,128)(2,1)S(1)} %fusion.9, bf16[256,2048]{1,0:T(8,128)(2,1)S(1)} %copy-done.58), kind=kOutput, calls=%fused_computation | convolution fusion | flops 15051259904 | bytes 38797312 | tf_op jit(solution)/shard_map/dot_general | solution.py:85
  454.9 4.3 fusion.58
  459.3 3.8 fusion.170
  463.1 3.8 fusion.171
  490.6 5.6 copy.31
  496.2 5.6 copy.32
  501.8 4.5 collective-permute-start.128
  516.3 4.8 collective-permute-start.120
  531.1 4.3 collective-permute-start.131
  557.5 4.3 collective-permute-start.75
  564.7 4.4 collective-permute-start.96
  574.1 6.1 collective-permute-start.115
  580.9 4.0 collective-permute-start.97
  585.7 9.9 %collective-permute-start.123 = (bf16[64,896]{1,0:T(8,128)(2,1)S(1)}, bf16[64,896]{1,0:T(8,128)(2,1)S(1)}, u32[]{:S(2)}, u32[]{:S(2)}) collective-permute-start(bf16[64,896]{1,0:T(8,128)(2,1)S(1)} %get-tuple-element.306), channel_id=1, source_target_pairs={{0,2},{1,3},{2,4},{3,5},{4,6},{5,7},{8,10},{9,11},{10,12},{11,13},... | collective-permute-start | bytes 344072 | tf_op jit(solution)/shard_map/ppermute | solution.py:26
  599.1 10.5 %collective-permute-done.79 = bf16[64,896]{1,0:T(8,128)(2,1)S(1)} collective-permute-done((bf16[64,896]{1,0:T(8,128)(2,1)S(1)}, bf16[64,896]{1,0:T(8,128)(2,1)S(1)}, u32[]{:S(2)}, u32[]{:S(2)}) %collective-permute-start.79) | collective-permute-done | bytes 114720 | tf_op jit(solution)/shard_map/ppermute | solution.py:26
  611.0 8.1 %collective-permute-start.126 = (bf16[64,896]{1,0:T(8,128)(2,1)S(1)}, bf16[64,896]{1,0:T(8,128)(2,1)S(1)}, u32[]{:S(2)}, u32[]{:S(2)}) collective-permute-start(bf16[64,896]{1,0:T(8,128)(2,1)S(1)} %fusion.64), channel_id=1, source_target_pairs={{2,0},{3,1},{4,2},{5,3},{6,4},{7,5},{10,8},{11,9},{12,10},{13,11},... | collective-permute-start | bytes 344072 | tf_op jit(solution)/shard_map/ppermute | solution.py:26
  619.1 4.9 collective-permute-start.80
  624.1 4.9 collective-permute-start.119
  629.1 7.0 %collective-permute-start.101 = (bf16[64,896]{1,0:T(8,128)(2,1)S(1)}, bf16[64,896]{1,0:T(8,128)(2,1)S(1)}, u32[]{:S(2)}, u32[]{:S(2)}) collective-permute-start(bf16[64,896]{1,0:T(8,128)(2,1)S(1)} %fusion.80), channel_id=1, source_target_pairs={{0,0},{1,1},{2,8},{3,9},{4,16},{5,17},{6,24},{7,25},{8,2},{9,3},{1... | collective-permute-start | bytes 344072 | tf_op jit(solution)/shard_map/ppermute | solution.py:279
  636.2 7.0 %collective-permute-start.127 = (bf16[64,896]{1,0:T(8,128)(2,1)S(1)}, bf16[64,896]{1,0:T(8,128)(2,1)S(1)}, u32[]{:S(2)}, u32[]{:S(2)}) collective-permute-start(bf16[64,896]{1,0:T(8,128)(2,1)S(1)} %fusion.68), channel_id=1, source_target_pairs={{0,0},{1,1},{2,8},{3,9},{4,16},{5,17},{6,24},{7,25},{8,2},{9,3},{1... | collective-permute-start | bytes 344072 | tf_op jit(solution)/shard_map/ppermute | solution.py:279
  646.2 5.3 collective-permute-done.127
  (651 shorter events, 327.3 us)
Async XLA Ops:
  4.7 28.9 %collective-permute-start.4 = (f32[2,128]{1,0:T(2,128)S(1)}, f32[2,128]{1,0:T(2,128)S(1)}, u32[]{:S(2)}, u32[]{:S(2)}) collective-permute-start(f32[2,128]{1,0:T(2,128)S(1)} %fusion.149), channel_id=1, source_target_pairs={{0,16},{8,24},{16,0},{24,8},{1,17},{9,25},{17,1},{25,9},{2,18},{10... | collective-permute-start | bytes 3080 | tf_op jit(solution)/shard_map/ppermute | solution.py:26
  9.9 60.6 %collective-permute-start.2 = (bf16[64,1792]{1,0:T(8,128)(2,1)}, bf16[64,1792]{1,0:T(8,128)(2,1)}, u32[]{:S(2)}, u32[]{:S(2)}) collective-permute-start(bf16[64,1792]{1,0:T(8,128)(2,1)} %get-tuple-element.101), channel_id=1, source_target_pairs={{0,8},{8,0},{16,24},{24,16},{1,9},{9,1},{17,25},{25,17},{2,10},{10... | collective-permute-start | bytes 688136 | tf_op jit(solution)/shard_map/ppermute | solution.py:26
  11.8 48.8 %collective-permute-start.6 = (bf16[64,1792]{1,0:T(8,128)(2,1)}, bf16[64,1792]{1,0:T(8,128)(2,1)}, u32[]{:S(2)}, u32[]{:S(2)}) collective-permute-start(bf16[64,1792]{1,0:T(8,128)(2,1)} %get-tuple-element.97), channel_id=1, source_target_pairs={{0,8},{8,0},{16,24},{24,16},{1,9},{9,1},{17,25},{25,17},{2,10},{10... | collective-permute-start | bytes 688136 | tf_op jit(solution)/shard_map/ppermute | solution.py:26
  13.4 18.2 %collective-permute-start.31 = (bf16[64,3584]{1,0:T(8,128)(2,1)S(1)}, bf16[64,3584]{1,0:T(8,128)(2,1)}, u32[]{:S(2)}, u32[]{:S(2)}) collective-permute-start(bf16[64,3584]{1,0:T(8,128)(2,1)S(1)} %dynamic-slice_select_fusion), channel_id=1, source_target_pairs={{0,16},{8,24},{16,0},{24,8},{1,17},{9,25},{17,1},{25,9},{2,18},{10... | collective-permute-start | bytes 1376264 | tf_op jit(solution)/shard_map/ppermute | solution.py:26
  21.3 19.9 %collective-permute-start = (bf16[64,3584]{1,0:T(8,128)(2,1)S(1)}, bf16[64,3584]{1,0:T(8,128)(2,1)}, u32[]{:S(2)}, u32[]{:S(2)}) collective-permute-start(bf16[64,3584]{1,0:T(8,128)(2,1)S(1)} %dynamic-slice_select_fusion.1), channel_id=1, source_target_pairs={{0,16},{8,24},{16,0},{24,8},{1,17},{9,25},{17,1},{25,9},{2,18},{10... | collective-permute-start | bytes 1376264 | tf_op jit(solution)/shard_map/ppermute | solution.py:26
  35.9 25.0 %collective-permute-start.35 = (bf16[64,1792]{1,0:T(8,128)(2,1)}, bf16[64,1792]{1,0:T(8,128)(2,1)S(1)}, u32[]{:S(2)}, u32[]{:S(2)}) collective-permute-start(bf16[64,1792]{1,0:T(8,128)(2,1)} %get-tuple-element.106), channel_id=1, source_target_pairs={{0,8},{8,0},{16,24},{24,16},{1,9},{9,1},{17,25},{25,17},{2,10},{10... | collective-permute-start | bytes 688136 | tf_op jit(solution)/shard_map/ppermute | solution.py:26
  44.9 21.7 %collective-permute-start.36 = (bf16[64,1792]{1,0:T(8,128)(2,1)S(1)}, bf16[64,1792]{1,0:T(8,128)(2,1)S(1)}, u32[]{:S(2)}, u32[]{:S(2)}) collective-permute-start(bf16[64,1792]{1,0:T(8,128)(2,1)S(1)} %get-tuple-element.375), channel_id=1, source_target_pairs={{0,8},{8,0},{16,24},{24,16},{1,9},{9,1},{17,25},{25,17},{2,10},{10... | collective-permute-start | bytes 688136 | tf_op jit(solution)/shard_map/ppermute | solution.py:26
  84.2 13.0 %collective-permute-start.13 = (bf16[64,896]{1,0:T(8,128)(2,1)S(1)}, bf16[64,896]{1,0:T(8,128)(2,1)S(1)}, u32[]{:S(2)}, u32[]{:S(2)}) collective-permute-start(bf16[64,896]{1,0:T(8,128)(2,1)S(1)} %get-tuple-element.118), channel_id=1, source_target_pairs={{2,0},{3,1},{4,2},{5,3},{6,4},{7,5},{10,8},{11,9},{12,10},{13,11},... | collective-permute-start | bytes 344072 | tf_op jit(solution)/shard_map/ppermute | solution.py:26
  85.5 13.0 %collective-permute-start.10 = (bf16[64,896]{1,0:T(8,128)(2,1)S(1)}, bf16[64,896]{1,0:T(8,128)(2,1)S(1)}, u32[]{:S(2)}, u32[]{:S(2)}) collective-permute-start(bf16[64,896]{1,0:T(8,128)(2,1)S(1)} %get-tuple-element.118), channel_id=1, source_target_pairs={{0,2},{1,3},{2,4},{3,5},{4,6},{5,7},{8,10},{9,11},{10,12},{11,13},... | collective-permute-start | bytes 344072 | tf_op jit(solution)/shard_map/ppermute | solution.py:26
  104.0 13.9 %collective-permute-start.15 = (bf16[64,896]{1,0:T(8,128)(2,1)}, bf16[64,896]{1,0:T(8,128)(2,1)}, u32[]{:S(2)}, u32[]{:S(2)}) collective-permute-start(bf16[64,896]{1,0:T(8,128)(2,1)} %collective-permute-done.14), channel_id=1, source_target_pairs={{2,0},{3,1},{10,8},{11,9},{18,16},{19,17},{26,24},{27,25}} | collective-permute-start | bytes 344072 | tf_op jit(solution)/shard_map/ppermute | solution.py:26
  126.1 19.7 %collective-permute-start.19 = (bf16[2,4,32,896]{3,2,1,0:T(8,128)(2,1)S(1)}, bf16[2,4,32,896]{3,2,1,0:T(8,128)(2,1)S(1)}, u32[]{:S(2)}, u32[]{:S(2)}) collective-permute-start(bf16[2,4,32,896]{3,2,1,0:T(8,128)(2,1)S(1)} %get-tuple-element.362), channel_id=1, source_target_pairs={{0,16},{8,24},{16,0},{24,8},{1,17},{9,25},{17,1},{25,9},{2,18},{10... | collective-permute-start | bytes 1376264 | tf_op jit(solution)/shard_map/ppermute | solution.py:26
  159.3 40.5 %collective-permute-start.20 = (bf16[128,7168]{1,0:T(8,128)(2,1)}, bf16[128,7168]{1,0:T(8,128)(2,1)}, u32[]{:S(2)}, u32[]{:S(2)}) collective-permute-start(bf16[128,7168]{1,0:T(8,128)(2,1)} %pad_maximum_fusion), channel_id=1, source_target_pairs={{0,8},{8,0},{16,24},{24,16},{1,9},{9,1},{17,25},{25,17},{2,10},{10... | collective-permute-start | bytes 5505032 | tf_op jit(solution)/shard_map/ppermute | solution.py:26
  170.4 17.5 %collective-permute-start.46 = (bf16[4,32,896]{2,1,0:T(8,128)(2,1)}, bf16[4,32,896]{2,1,0:T(8,128)(2,1)}, u32[]{:S(2)}, u32[]{:S(2)}) collective-permute-start(bf16[4,32,896]{2,1,0:T(8,128)(2,1)} %get-tuple-element.373), channel_id=1, source_target_pairs={{0,16},{8,24},{16,0},{24,8},{1,17},{9,25},{17,1},{25,9},{2,18},{10... | collective-permute-start | bytes 688136 | tf_op jit(solution)/shard_map/ppermute | solution.py:26
  192.7 21.1 %collective-permute-start.48 = (bf16[2,4,32,896]{3,2,1,0:T(8,128)(2,1)S(1)}, bf16[2,4,32,896]{3,2,1,0:T(8,128)(2,1)S(1)}, u32[]{:S(2)}, u32[]{:S(2)}) collective-permute-start(bf16[2,4,32,896]{3,2,1,0:T(8,128)(2,1)S(1)} %get-tuple-element.370), channel_id=1, source_target_pairs={{0,16},{8,24},{16,0},{24,8},{1,17},{9,25},{17,1},{25,9},{2,18},{10... | collective-permute-start | bytes 1376264 | tf_op jit(solution)/shard_map/ppermute | solution.py:26
  227.2 44.2 %collective-permute-start.49 = (bf16[128,7168]{1,0:T(8,128)(2,1)}, bf16[128,7168]{1,0:T(8,128)(2,1)}, u32[]{:S(2)}, u32[]{:S(2)}) collective-permute-start(bf16[128,7168]{1,0:T(8,128)(2,1)} %pad_maximum_fusion.1), channel_id=1, source_target_pairs={{0,8},{8,0},{16,24},{24,16},{1,9},{9,1},{17,25},{25,17},{2,10},{10... | collective-permute-start | bytes 5505032 | tf_op jit(solution)/shard_map/ppermute | solution.py:26
  300.9 13.5 %collective-permute-start.58 = (f32[3,4,64]{2,1,0:T(4,128)S(1)}, f32[3,4,64]{2,1,0:T(4,128)S(1)}, u32[]{:S(2)}, u32[]{:S(2)}) collective-permute-start(f32[3,4,64]{2,1,0:T(4,128)S(1)} %add.946), channel_id=1, source_target_pairs={{0,2},{1,3},{2,0},{3,1},{4,6},{5,7},{6,4},{7,5},{8,10},{9,11},{10,... | collective-permute-start | bytes 9224 | tf_op jit(solution)/shard_map/ppermute | solution.py:26
  314.4 20.6 %collective-permute-start.59 = (f32[3,4,64]{2,1,0:T(4,128)S(1)}, f32[3,4,64]{2,1,0:T(4,128)S(1)}, u32[]{:S(2)}, u32[]{:S(2)}) collective-permute-start(f32[3,4,64]{2,1,0:T(4,128)S(1)} %add.947), channel_id=1, source_target_pairs={{0,4},{1,5},{2,6},{3,7},{4,0},{5,1},{6,2},{7,3},{8,12},{9,13},{10,... | collective-permute-start | bytes 9224 | tf_op jit(solution)/shard_map/ppermute | solution.py:26
  335.0 23.8 %collective-permute-start.60 = (bf16[128,7168]{1,0:T(8,128)(2,1)}, bf16[128,7168]{1,0:T(8,128)(2,1)}, u32[]{:S(2)}, u32[]{:S(2)}) collective-permute-start(bf16[128,7168]{1,0:T(8,128)(2,1)} %slice.1119), channel_id=1, source_target_pairs={{0,8},{8,0},{16,24},{24,16},{1,9},{9,1},{17,25},{25,17},{2,10},{10... | collective-permute-start | bytes 5505032 | tf_op jit(solution)/shard_map/ppermute | solution.py:26
  361.0 13.5 %collective-permute-start.61 = (bf16[32,7168]{1,0:T(8,128)(2,1)S(1)}, bf16[32,7168]{1,0:T(8,128)(2,1)S(1)}, u32[]{:S(2)}, u32[]{:S(2)}) collective-permute-start(bf16[32,7168]{1,0:T(8,128)(2,1)S(1)} %slice_bitcast_fusion.2), channel_id=1, source_target_pairs={{0,16},{8,24},{16,0},{24,8},{1,17},{9,25},{17,1},{25,9},{2,18},{10... | collective-permute-start | bytes 1376264 | tf_op jit(solution)/shard_map/ppermute | solution.py:26
  361.8 14.4 %collective-permute-start.63 = (bf16[4,2,32,896]{3,2,0,1:T(8,128)(2,1)S(1)}, bf16[4,2,32,896]{3,2,0,1:T(8,128)(2,1)S(1)}, u32[]{:S(2)}, u32[]{:S(2)}) collective-permute-start(bf16[4,2,32,896]{3,2,0,1:T(8,128)(2,1)S(1)} %pad_maximum_fusion.11), channel_id=1, source_target_pairs={{0,1},{1,0},{2,3},{3,2},{4,5},{5,4},{6,7},{7,6},{8,9},{9,8},{10,11... | collective-permute-start | bytes 1376264 | tf_op jit(solution)/shard_map/ppermute | solution.py:26
  363.8 20.5 %collective-permute-start.82 = (bf16[32,7168]{1,0:T(8,128)(2,1)S(1)}, bf16[32,7168]{1,0:T(8,128)(2,1)S(1)}, u32[]{:S(2)}, u32[]{:S(2)}) collective-permute-start(bf16[32,7168]{1,0:T(8,128)(2,1)S(1)} %slice_bitcast_fusion), channel_id=1, source_target_pairs={{0,16},{8,24},{16,0},{24,8},{1,17},{9,25},{17,1},{25,9},{2,18},{10... | collective-permute-start | bytes 1376264 | tf_op jit(solution)/shard_map/ppermute | solution.py:26
  365.5 20.5 %collective-permute-start.84 = (bf16[4,2,32,896]{3,2,0,1:T(8,128)(2,1)S(1)}, bf16[4,2,32,896]{3,2,0,1:T(8,128)(2,1)S(1)}, u32[]{:S(2)}, u32[]{:S(2)}) collective-permute-start(bf16[4,2,32,896]{3,2,0,1:T(8,128)(2,1)S(1)} %pad_maximum_fusion.15), channel_id=1, source_target_pairs={{0,1},{1,0},{2,3},{3,2},{4,5},{5,4},{6,7},{7,6},{8,9},{9,8},{10,11... | collective-permute-start | bytes 1376264 | tf_op jit(solution)/shard_map/ppermute | solution.py:26
  374.7 15.4 %collective-permute-start.62 = (bf16[4,32,896]{2,1,0:T(8,128)(2,1)S(1)}, bf16[4,32,896]{2,1,0:T(8,128)(2,1)S(1)}, u32[]{:S(2)}, u32[]{:S(2)}) collective-permute-start(bf16[4,32,896]{2,1,0:T(8,128)(2,1)S(1)} %pad_maximum_fusion.19), channel_id=1, source_target_pairs={{0,1},{1,0},{2,3},{3,2},{4,5},{5,4},{6,7},{7,6},{8,9},{9,8},{10,11... | collective-permute-start | bytes 688136 | tf_op jit(solution)/shard_map/ppermute | solution.py:26
  425.3 27.3 %collective-permute-start.72 = (bf16[2,64,896]{2,1,0:T(8,128)(2,1)}, bf16[2,64,896]{2,1,0:T(8,128)(2,1)}, u32[]{:S(2)}, u32[]{:S(2)}) collective-permute-start(bf16[2,64,896]{2,1,0:T(8,128)(2,1)} %pad_maximum_fusion.20), channel_id=1, source_target_pairs={{0,8},{8,0},{16,24},{24,16},{1,9},{9,1},{17,25},{25,17},{2,10},{10... | collective-permute-start | bytes 688136 | tf_op jit(solution)/shard_map/ppermute | solution.py:26
  428.7 25.0 %collective-permute-start.93 = (bf16[2,64,896]{2,1,0:T(8,128)(2,1)}, bf16[2,64,896]{2,1,0:T(8,128)(2,1)}, u32[]{:S(2)}, u32[]{:S(2)}) collective-permute-start(bf16[2,64,896]{2,1,0:T(8,128)(2,1)} %pad_maximum_fusion.22), channel_id=1, source_target_pairs={{0,8},{8,0},{16,24},{24,16},{1,9},{9,1},{17,25},{25,17},{2,10},{10... | collective-permute-start | bytes 688136 | tf_op jit(solution)/shard_map/ppermute | solution.py:26
  487.0 22.7 %collective-permute-start.110 = (f32[2,4,64]{2,1,0:T(4,128)}, f32[2,4,64]{2,1,0:T(4,128)}, u32[]{:S(2)}, u32[]{:S(2)}) collective-permute-start(f32[2,4,64]{2,1,0:T(4,128)} %add.1052), channel_id=1, source_target_pairs={{0,2},{1,3},{2,0},{3,1},{4,6},{5,7},{6,4},{7,5},{8,10},{9,11},{10,... | collective-permute-start | bytes 6152 | tf_op jit(solution)/shard_map/ppermute | solution.py:26
  488.2 23.7 %collective-permute-start.106 = (f32[2,4,64]{2,1,0:T(4,128)}, f32[2,4,64]{2,1,0:T(4,128)}, u32[]{:S(2)}, u32[]{:S(2)}) collective-permute-start(f32[2,4,64]{2,1,0:T(4,128)} %add.1047), channel_id=1, source_target_pairs={{0,4},{1,5},{2,6},{3,7},{4,0},{5,1},{6,2},{7,3},{8,12},{9,13},{10,... | collective-permute-start | bytes 6152 | tf_op jit(solution)/shard_map/ppermute | solution.py:26
  501.8 19.4 %collective-permute-start.128 = (f32[2,1792]{1,0:T(2,128)}, f32[2,1792]{1,0:T(2,128)S(1)}, u32[]{:S(2)}, u32[]{:S(2)}) collective-permute-start(f32[2,1792]{1,0:T(2,128)} %pad_maximum_fusion.39), channel_id=1, source_target_pairs={{0,1},{1,0},{2,3},{3,2},{4,5},{5,4},{6,7},{7,6},{8,9},{9,8},{10,11... | collective-permute-start | bytes 43016 | tf_op jit(solution)/shard_map/ppermute | solution.py:26
  506.3 32.7 %collective-permute-start.73 = (bf16[256,896]{1,0:T(8,128)(2,1)}, bf16[256,896]{1,0:T(8,128)(2,1)S(1)}, u32[]{:S(2)}, u32[]{:S(2)}) collective-permute-start(bf16[256,896]{1,0:T(8,128)(2,1)} %fusion.37), channel_id=1, source_target_pairs={{0,1},{1,0},{2,3},{3,2},{4,5},{5,4},{6,7},{7,6},{8,9},{9,8},{10,11... | collective-permute-start | bytes 1376264 | tf_op jit(solution)/shard_map/ppermute | solution.py:26
  507.8 35.8 %collective-permute-start.112 = (bf16[256,896]{1,0:T(8,128)(2,1)}, bf16[256,896]{1,0:T(8,128)(2,1)S(1)}, u32[]{:S(2)}, u32[]{:S(2)}) collective-permute-start(bf16[256,896]{1,0:T(8,128)(2,1)} %fusion.43), channel_id=1, source_target_pairs={{0,1},{1,0},{2,3},{3,2},{4,5},{5,4},{6,7},{7,6},{8,9},{9,8},{10,11... | collective-permute-start | bytes 1376264 | tf_op jit(solution)/shard_map/ppermute | solution.py:26
  509.7 36.1 %collective-permute-start.94 = (bf16[256,896]{1,0:T(8,128)(2,1)}, bf16[256,896]{1,0:T(8,128)(2,1)S(1)}, u32[]{:S(2)}, u32[]{:S(2)}) collective-permute-start(bf16[256,896]{1,0:T(8,128)(2,1)} %fusion.40), channel_id=1, source_target_pairs={{0,1},{1,0},{2,3},{3,2},{4,5},{5,4},{6,7},{7,6},{8,9},{9,8},{10,11... | collective-permute-start | bytes 1376264 | tf_op jit(solution)/shard_map/ppermute | solution.py:26
  516.3 32.4 %collective-permute-start.120 = (bf16[256,896]{1,0:T(8,128)(2,1)}, bf16[256,896]{1,0:T(8,128)(2,1)S(1)}, u32[]{:S(2)}, u32[]{:S(2)}) collective-permute-start(bf16[256,896]{1,0:T(8,128)(2,1)} %fusion.46), channel_id=1, source_target_pairs={{0,1},{1,0},{2,3},{3,2},{4,5},{5,4},{6,7},{7,6},{8,9},{9,8},{10,11... | collective-permute-start | bytes 1376264 | tf_op jit(solution)/shard_map/ppermute | solution.py:26
  542.9 19.0 %collective-permute-start.77 = (bf16[64,896]{1,0:T(8,128)(2,1)S(1)}, bf16[64,896]{1,0:T(8,128)(2,1)S(1)}, u32[]{:S(2)}, u32[]{:S(2)}) collective-permute-start(bf16[64,896]{1,0:T(8,128)(2,1)S(1)} %get-tuple-element.313), channel_id=1, source_target_pairs={{6,4},{7,5},{14,12},{15,13},{22,20},{23,21},{30,28},{31,29}} | collective-permute-start | bytes 344072 | tf_op jit(solution)/shard_map/ppermute | solution.py:26
  545.7 23.5 %collective-permute-start.116 = (bf16[64,896]{1,0:T(8,128)(2,1)S(1)}, bf16[64,896]{1,0:T(8,128)(2,1)S(1)}, u32[]{:S(2)}, u32[]{:S(2)}) collective-permute-start(bf16[64,896]{1,0:T(8,128)(2,1)S(1)} %get-tuple-element.305), channel_id=1, source_target_pairs={{6,4},{7,5},{14,12},{15,13},{22,20},{23,21},{30,28},{31,29}} | collective-permute-start | bytes 344072 | tf_op jit(solution)/shard_map/ppermute | solution.py:26
  553.1 20.3 %collective-permute-start.98 = (bf16[64,896]{1,0:T(8,128)(2,1)S(1)}, bf16[64,896]{1,0:T(8,128)(2,1)S(1)}, u32[]{:S(2)}, u32[]{:S(2)}) collective-permute-start(bf16[64,896]{1,0:T(8,128)(2,1)S(1)} %get-tuple-element.339), channel_id=1, source_target_pairs={{6,4},{7,5},{14,12},{15,13},{22,20},{23,21},{30,28},{31,29}} | collective-permute-start | bytes 344072 | tf_op jit(solution)/shard_map/ppermute | solution.py:26
  555.3 25.0 %collective-permute-start.124 = (bf16[64,896]{1,0:T(8,128)(2,1)S(1)}, bf16[64,896]{1,0:T(8,128)(2,1)S(1)}, u32[]{:S(2)}, u32[]{:S(2)}) collective-permute-start(bf16[64,896]{1,0:T(8,128)(2,1)S(1)} %get-tuple-element.309), channel_id=1, source_target_pairs={{6,4},{7,5},{14,12},{15,13},{22,20},{23,21},{30,28},{31,29}} | collective-permute-start | bytes 344072 | tf_op jit(solution)/shard_map/ppermute | solution.py:26
  571.4 26.4 %collective-permute-start.76 = (bf16[64,896]{1,0:T(8,128)(2,1)S(1)}, bf16[64,896]{1,0:T(8,128)(2,1)S(1)}, u32[]{:S(2)}, u32[]{:S(2)}) collective-permute-start(bf16[64,896]{1,0:T(8,128)(2,1)S(1)} %get-tuple-element.310), channel_id=1, source_target_pairs={{0,2},{1,3},{2,4},{3,5},{4,6},{5,7},{8,10},{9,11},{10,12},{11,13},... | collective-permute-start | bytes 344072 | tf_op jit(solution)/shard_map/ppermute | solution.py:26
  574.1 36.9 %collective-permute-start.115 = (bf16[64,896]{1,0:T(8,128)(2,1)S(1)}, bf16[64,896]{1,0:T(8,128)(2,1)S(1)}, u32[]{:S(2)}, u32[]{:S(2)}) collective-permute-start(bf16[64,896]{1,0:T(8,128)(2,1)S(1)} %get-tuple-element.302), channel_id=1, source_target_pairs={{0,2},{1,3},{2,4},{3,5},{4,6},{5,7},{8,10},{9,11},{10,12},{11,13},... | collective-permute-start | bytes 344072 | tf_op jit(solution)/shard_map/ppermute | solution.py:26
  580.9 43.1 %collective-permute-start.97 = (bf16[64,896]{1,0:T(8,128)(2,1)S(1)}, bf16[64,896]{1,0:T(8,128)(2,1)S(1)}, u32[]{:S(2)}, u32[]{:S(2)}) collective-permute-start(bf16[64,896]{1,0:T(8,128)(2,1)S(1)} %get-tuple-element.336), channel_id=1, source_target_pairs={{0,2},{1,3},{2,4},{3,5},{4,6},{5,7},{8,10},{9,11},{10,12},{11,13},... | collective-permute-start | bytes 344072 | tf_op jit(solution)/shard_map/ppermute | solution.py:26
  585.7 50.3 %collective-permute-start.123 = (bf16[64,896]{1,0:T(8,128)(2,1)S(1)}, bf16[64,896]{1,0:T(8,128)(2,1)S(1)}, u32[]{:S(2)}, u32[]{:S(2)}) collective-permute-start(bf16[64,896]{1,0:T(8,128)(2,1)S(1)} %get-tuple-element.306), channel_id=1, source_target_pairs={{0,2},{1,3},{2,4},{3,5},{4,6},{5,7},{8,10},{9,11},{10,12},{11,13},... | collective-permute-start | bytes 344072 | tf_op jit(solution)/shard_map/ppermute | solution.py:26
  596.5 13.2 %collective-permute-start.79 = (bf16[64,896]{1,0:T(8,128)(2,1)S(1)}, bf16[64,896]{1,0:T(8,128)(2,1)S(1)}, u32[]{:S(2)}, u32[]{:S(2)}) collective-permute-start(bf16[64,896]{1,0:T(8,128)(2,1)S(1)} %fusion.88), channel_id=1, source_target_pairs={{2,0},{3,1},{4,2},{5,3},{6,4},{7,5},{10,8},{11,9},{12,10},{13,11},... | collective-permute-start | bytes 344072 | tf_op jit(solution)/shard_map/ppermute | solution.py:26
  597.8 21.2 %collective-permute-start.118 = (bf16[64,896]{1,0:T(8,128)(2,1)S(1)}, bf16[64,896]{1,0:T(8,128)(2,1)S(1)}, u32[]{:S(2)}, u32[]{:S(2)}) collective-permute-start(bf16[64,896]{1,0:T(8,128)(2,1)S(1)} %fusion.70), channel_id=1, source_target_pairs={{2,0},{3,1},{4,2},{5,3},{6,4},{7,5},{10,8},{11,9},{12,10},{13,11},... | collective-permute-start | bytes 344072 | tf_op jit(solution)/shard_map/ppermute | solution.py:26
  609.6 19.4 %collective-permute-start.100 = (bf16[64,896]{1,0:T(8,128)(2,1)S(1)}, bf16[64,896]{1,0:T(8,128)(2,1)S(1)}, u32[]{:S(2)}, u32[]{:S(2)}) collective-permute-start(bf16[64,896]{1,0:T(8,128)(2,1)S(1)} %fusion.76), channel_id=1, source_target_pairs={{2,0},{3,1},{4,2},{5,3},{6,4},{7,5},{10,8},{11,9},{12,10},{13,11},... | collective-permute-start | bytes 344072 | tf_op jit(solution)/shard_map/ppermute | solution.py:26
  611.0 25.1 %collective-permute-start.126 = (bf16[64,896]{1,0:T(8,128)(2,1)S(1)}, bf16[64,896]{1,0:T(8,128)(2,1)S(1)}, u32[]{:S(2)}, u32[]{:S(2)}) collective-permute-start(bf16[64,896]{1,0:T(8,128)(2,1)S(1)} %fusion.64), channel_id=1, source_target_pairs={{2,0},{3,1},{4,2},{5,3},{6,4},{7,5},{10,8},{11,9},{12,10},{13,11},... | collective-permute-start | bytes 344072 | tf_op jit(solution)/shard_map/ppermute | solution.py:26
  619.1 24.1 %collective-permute-start.80 = (bf16[64,896]{1,0:T(8,128)(2,1)S(1)}, bf16[64,896]{1,0:T(8,128)(2,1)S(1)}, u32[]{:S(2)}, u32[]{:S(2)}) collective-permute-start(bf16[64,896]{1,0:T(8,128)(2,1)S(1)} %fusion.92), channel_id=1, source_target_pairs={{0,0},{1,1},{2,8},{3,9},{4,16},{5,17},{6,24},{7,25},{8,2},{9,3},{1... | collective-permute-start | bytes 344072 | tf_op jit(solution)/shard_map/ppermute | solution.py:279
  624.1 22.1 %collective-permute-start.119 = (bf16[64,896]{1,0:T(8,128)(2,1)S(1)}, bf16[64,896]{1,0:T(8,128)(2,1)S(1)}, u32[]{:S(2)}, u32[]{:S(2)}) collective-permute-start(bf16[64,896]{1,0:T(8,128)(2,1)S(1)} %fusion.74), channel_id=1, source_target_pairs={{0,0},{1,1},{2,8},{3,9},{4,16},{5,17},{6,24},{7,25},{8,2},{9,3},{1... | collective-permute-start | bytes 344072 | tf_op jit(solution)/shard_map/ppermute | solution.py:279
  629.1 15.3 %collective-permute-start.101 = (bf16[64,896]{1,0:T(8,128)(2,1)S(1)}, bf16[64,896]{1,0:T(8,128)(2,1)S(1)}, u32[]{:S(2)}, u32[]{:S(2)}) collective-permute-start(bf16[64,896]{1,0:T(8,128)(2,1)S(1)} %fusion.80), channel_id=1, source_target_pairs={{0,0},{1,1},{2,8},{3,9},{4,16},{5,17},{6,24},{7,25},{8,2},{9,3},{1... | collective-permute-start | bytes 344072 | tf_op jit(solution)/shard_map/ppermute | solution.py:279
  636.2 15.3 %collective-permute-start.127 = (bf16[64,896]{1,0:T(8,128)(2,1)S(1)}, bf16[64,896]{1,0:T(8,128)(2,1)S(1)}, u32[]{:S(2)}, u32[]{:S(2)}) collective-permute-start(bf16[64,896]{1,0:T(8,128)(2,1)S(1)} %fusion.68), channel_id=1, source_target_pairs={{0,0},{1,1},{2,8},{3,9},{4,16},{5,17},{6,24},{7,25},{8,2},{9,3},{1... | collective-permute-start | bytes 344072 | tf_op jit(solution)/shard_map/ppermute | solution.py:279
  (147 other events, 1933.1 us)

commit v2 on v1

--- a/solution.py
+++ b/solution.py
@@ -4,7 +4,7 @@
 from jax.sharding import PartitionSpec as P
 
 EPSILON = 1e-06
-PARTS = 2
+PARTS = 1
 F32 = jnp.float32
 BF16 = jnp.bfloat16
 
@@ -32,53 +32,32 @@
         return self.move(value, lambda here: (here + by) % self.n)
 
 
-def butterfly(value, dims):
-    for dim in dims:
-        bit = 1
-        while bit < dim.n:
-            value = value + dim.swap(value, bit)
-            bit *= 2
-    return value
-
-
-def line_gather(value, dim):
-    n, here = dim.n, dim.place()
-    if n == 2:
-        other = dim.swap(value, 1)
-        return [jnp.where(here == 0, value, other), jnp.where(here == 0, other, value)]
-    up, down = [value], [value]
-    for step in range(1, n):
-        up.append(dim.move(up[-1], lambda k: k + 1 if k >= step - 1 else None))
-        down.append(dim.move(down[-1], lambda k: k - 1 if k <= n - step else None))
-    out = []
-    for spot in range(n):
-        piece = value
-        for step in range(1, n):
-            if spot + step < n:
-                piece = jnp.where(here == spot + step, up[step], piece)
-            if spot - step >= 0:
-                piece = jnp.where(here == spot - step, down[step], piece)
-        out.append(piece)
-    return out
-
-
-def line_scatter(chunks, dim):
-    n, here = dim.n, dim.place()
-
-    def pick(at):
-        return lax.dynamic_index_in_dim(chunks, jnp.clip(at, 0, n - 1), 0, keepdims=False)
-
-    if n == 2:
-        return pick(here).astype(F32) + dim.swap(pick(1 - here), 1).astype(F32)
-    up = down = None
-    for step in range(1, n):
-        up_send, down_send = pick(here + n - step), pick(here - n + step)
-        if up is not None:
-            up_send = (up_send.astype(F32) + up.astype(F32)).astype(BF16)
-            down_send = (down_send.astype(F32) + down.astype(F32)).astype(BF16)
-        up = dim.move(up_send, lambda k: k + 1 if k <= step - 1 else None)
-        down = dim.move(down_send, lambda k: k - 1 if k >= n - step else None)
-    return pick(here).astype(F32) + up.astype(F32) + down.astype(F32)
+def halving_scatter(chunks, dim):
+    here = dim.place()
+    held = {
+        offset: lax.dynamic_index_in_dim(chunks, here ^ offset, 0, keepdims=False)
+        for offset in range(dim.n)
+    }
+    bit = 1
+    while bit < dim.n:
+        send = jnp.stack([held[offset] for offset in range(dim.n) if offset in held and offset & bit])
+        got = dim.swap(send, bit)
+        keep = [offset for offset in sorted(held) if not offset & bit]
+        held = {
+            offset: (held[offset].astype(F32) + got[index].astype(F32))
+            for index, offset in enumerate(keep)
+        }
+        bit *= 2
+        if bit < dim.n:
+            held = {offset: piece.astype(BF16) for offset, piece in held.items()}
+    return held[0]
+
+
+def sum_everywhere(value):
+    axes = ("ctx", "vocab")
+    count = lax.axis_size("ctx") * lax.axis_size("vocab")
+    copies = jnp.broadcast_to(value[None], (count,) + value.shape)
+    return jnp.sum(lax.all_to_all(copies, axes, 0, 0, tiled=True), axis=0)
 
 
 def contract_first(left, right):
@@ -116,17 +95,14 @@
     dim_x = Dim("ctx", nc, nx, 2)
     dim_b = Dim("vocab", nv, vb, 1)
     dim_a = Dim("vocab", nv, va, vb)
-    every = (core, dim_x, dim_b, dim_a)
     own, slot = lax.axis_index("ctx"), lax.axis_index("vocab")
     x, c, a, b = own // 2, own % 2, slot // vb, slot % vb
-    even = b % 2 == 0
 
     width = hidden_state.shape[1]
     block = hidden_state.shape[0]
     token_total = targets.shape[0]
     feat, cols = proj_hidden.shape
     rows = block // PARTS
-    half = rows // 2
     vocab_local = head.shape[0]
 
     def relative_place(block_index):
@@ -155,6 +131,7 @@
     )
     scales_x = gather_x(scales)
     scales_all = jnp.concatenate([scales_x, core.swap(scales_x, 1)])
+    gain_all = lax.all_gather(final_gain, "vocab", tiled=True)
     gain_h_own = cut(gain_hidden, own * feat, feat, 0)
     gain_e_own = cut(gain_embed, own * feat, feat, 0)
 
@@ -165,11 +142,8 @@
         emb_list = [cut(emb, x * 2 * feat, 2 * feat, 1)]
         for r in range(1, nx):
             start = ((x + r) % nx) * 2 * feat
-            send = jnp.where(even, cut(hid, start, 2 * feat, 1), cut(emb, start, 2 * feat, 1))
-            got = dim_x.turn(send, r)
-            twin = dim_b.swap(got, 1)
-            hid_list.append(jnp.where(even, got, twin))
-            emb_list.append(jnp.where(even, twin, got))
+            hid_list.append(dim_x.turn(cut(hid, start, 2 * feat, 1), r))
+            emb_list.append(dim_x.turn(cut(emb, start, 2 * feat, 1), r))
         out = []
         for kind, (pieces, gain) in enumerate(((hid_list, gain_h_own), (emb_list, gain_e_own))):
             mine = [cut(piece, c * feat, feat, 1) for piece in pieces]
@@ -191,26 +165,19 @@
         return projected, part_h, part_e
 
     def spread(projected):
-        squares = jnp.sum(projected * projected, axis=-1)
-        mine = jnp.arange(nc, dtype=jnp.int32)[:, None] == own
-        squares = butterfly(jnp.where(mine, squares[None, :], 0.0), every)
-        row_scale = relative(lax.rsqrt(squares / width + EPSILON))
         piece = (projected * final_gain).astype(BF16)
-        along = jnp.stack(line_gather(piece, dim_a))
-        first = jnp.stack(line_gather(along[:, :half], dim_b))
-        first = gather_x(first)
-        second = gather_x(along[:, half:])
-        second = jnp.stack(line_gather(second, dim_b), axis=1)
+        pieces = lax.all_gather(piece, ("ctx", "vocab"))
+        pieces = pieces.reshape(nc, nv, rows, cols)
         lines = []
-        for r in range(nx):
-            for source in (first, second):
-                lines.append(
-                    jnp.concatenate(
-                        [source[r, q, p] for p in range(va) for q in range(vb)], axis=1
-                    )
-                )
-        mine = jnp.concatenate(lines)
-        return jnp.concatenate([mine, core.swap(mine, 1)]), row_scale
+        for rc in range(2):
+            for rx in range(nx):
+                at = ((x - rx) % nx) * 2 + (c ^ rc)
+                line = lax.dynamic_index_in_dim(pieces, at, 0, keepdims=False)
+                lines.append(line.transpose(1, 0, 2).reshape(rows, width))
+        gathered = jnp.concatenate(lines)
+        plain = gathered.astype(F32) / gain_all
+        squares = jnp.sum(plain * plain, axis=-1)
+        return gathered, lax.rsqrt(squares / width + EPSILON)
 
     vocab_ids = (own * nv + slot) * vocab_local + lax.iota(jnp.int32, vocab_local)
     mask_weight = loss_mask.astype(F32).reshape(nc, block)
@@ -229,7 +196,7 @@
                 jnp.sum(jnp.where(is_target, logits, F32(0.0)), axis=-1),
             ]
         )
-        sums = butterfly(absolute(sums), every)
+        sums = sum_everywhere(absolute(sums))
         total, weighted, target_logit = sums[0], sums[1], sums[2]
         log_total = jnp.log(total)
         loss = jnp.sum(
@@ -240,32 +207,14 @@
         scaled_grad = ((mask * row_scale)[:, None] * (probs - is_target.astype(F32))).astype(BF16)
         return scaled_grad, scaled_dot, loss
 
-    def column_chunk(value, place):
-        return jnp.stack([cut(value, (p * vb + place) * cols, cols, value.ndim - 1) for p in range(va)])
-
     def collect(scaled_grad):
-        partial = dot(scaled_grad, head)
-        mine, theirs = partial[: nx * rows], partial[nx * rows :].astype(BF16)
-        mine = (mine + core.swap(theirs, 1).astype(F32)).astype(BF16)
-        mine = mine.reshape(nx, rows, width)
-        first = mine[0, :half].astype(F32)
-        for r in range(1, nx):
-            first = first + dim_x.turn(mine[r, :half], -r).astype(F32)
-        first = first.astype(BF16)
-        kept = column_chunk(first, b).astype(F32)
-        for r in range(1, vb):
-            kept = kept + dim_b.turn(column_chunk(first, (b + r) % vb), r).astype(F32)
-        first = kept.astype(BF16)
-        second = mine[:, half:]
-        kept = column_chunk(second, b).astype(F32)
-        for r in range(1, vb):
-            kept = kept + dim_b.turn(column_chunk(second, (b + r) % vb), r).astype(F32)
-        second = kept.astype(BF16)
-        kept = second[:, 0].astype(F32)
-        for r in range(1, nx):
-            kept = kept + dim_x.turn(second[:, r], -r).astype(F32)
-        second = kept.astype(BF16)
-        summed = line_scatter(jnp.concatenate([first, second], axis=1), dim_a).astype(BF16)
+        partial = dot(scaled_grad, head).astype(BF16).reshape(nc, rows, width)
+        lines = []
+        for index in range(nc):
+            line = lax.dynamic_index_in_dim(partial, relative_place(index), 0, keepdims=False)
+            lines.append(line.reshape(rows, nv, cols).transpose(1, 0, 2))
+        pieces = jnp.concatenate(lines)
+        summed = lax.psum_scatter(pieces, ("ctx", "vocab"), scatter_dimension=0, tiled=False)
         along = gather_x(summed)
         along = jnp.concatenate([along, core.swap(along, 1)])
         return along.reshape(nc * rows, cols)
@@ -292,7 +241,7 @@
         for got in sends:
             kept = kept + got.astype(F32)
         kept = kept.astype(BF16).reshape(va, rows, cols)
-        return final_move(line_scatter(kept, dim_a).astype(BF16)).astype(F32)
+        return final_move(halving_scatter(kept, dim_a).astype(BF16)).astype(F32)
 
     normed_h, normed_e, halves, gathered, row_scales = [], [], [], [], []
     for part in range(PARTS):
@@ -326,25 +275,20 @@
         wide = proj_grad.astype(F32)
         part_h, part_e = halves[part]
         sums = jnp.stack([jnp.sum(wide * part_h, axis=-1), jnp.sum(wide * part_e, axis=-1)])
-        sums = butterfly(absolute(sums), every)
-        dots.append(lax.dynamic_index_in_dim(sums, own, 1, keepdims=False))
+        sums = absolute(sums)
+        sums = jnp.broadcast_to(sums.transpose(1, 0, 2)[:, None], (nc, nv, 2, rows))
+        sums = lax.all_to_all(
+            sums.reshape(nc * nv, 2, rows), ("ctx", "vocab"), 0, 0, tiled=True
+        )
+        dots.append(jnp.sum(sums, axis=0))
         hidden_backs.append(back(proj_grad, proj_hidden))
         embed_backs.append(back(proj_grad, proj_embed))
 
     rows_all = jnp.concatenate(gathered)
     grad_head = contract_first(jnp.concatenate(logit_grads), rows_all).astype(BF16)
     proj_grad = jnp.concatenate(proj_grads)
-    wide_h = contract_first(jnp.concatenate(normed_h), proj_grad)
-    wide_e = contract_first(jnp.concatenate(normed_e), proj_grad)
-    grad_proj_hidden, grad_proj_embed = wide_h.astype(BF16), wide_e.astype(BF16)
-    gains = jnp.stack(
-        [
-            jnp.sum(wide_h * proj_hidden.astype(F32), axis=1) / gain_h_own,
-            jnp.sum(wide_e * proj_embed.astype(F32), axis=1) / gain_e_own,
-        ]
-    )
-    gains = butterfly(gains, (dim_b, dim_a))
-    gains = final_move(cut(gains, (b % 2) * cols, cols, 1))
+    grad_proj_hidden = contract_first(jnp.concatenate(normed_h), proj_grad).astype(BF16)
+    grad_proj_embed = contract_first(jnp.concatenate(normed_e), proj_grad).astype(BF16)
 
     def finish(backs, wide, gain, kind):
         back_all = jnp.concatenate(backs)
@@ -352,16 +296,18 @@
         dot_all = jnp.concatenate([pair[kind] for pair in dots])[:, None]
         source = cut(wide, slot * cols, cols, 1).astype(F32)
         gain_piece = cut(gain, slot * cols, cols, 0)
-        return (
-            scale * (back_all * gain_piece) - source * (scale * scale) * (dot_all / width)
-        ).astype(BF16)
-
+        grad = scale * (back_all * gain_piece) - source * (scale * scale) * (dot_all / width)
+        return grad.astype(BF16), jnp.sum(back_all * source * scale, axis=0)
+
+    grad_hidden, gain_h = finish(hidden_backs, hidden_state, gain_hidden, 0)
+    grad_embed, gain_e = finish(embed_backs, embedded_next, gain_embed, 1)
+    gain_h, gain_e = lax.psum((gain_h, gain_e), "ctx")
     return (
         mean_loss,
-        finish(hidden_backs, hidden_state, gain_hidden, 0),
-        finish(embed_backs, embedded_next, gain_embed, 1),
-        gains[0],
-        gains[1],
+        grad_hidden,
+        grad_embed,
+        gain_h,
+        gain_e,
         grad_proj_hidden,
         grad_proj_embed,
         grad_final_gain,

time: 665 us -> 591 us (0.89)
  starting transfers between devices: 246 us -> 29.4 us
  waiting for transfers between devices: 133 us -> 315 us
  local copies, waits for them, and re-layouts: 103 us -> 49.4 us
  blocking collectives: 0 us -> 38.2 us
  other arithmetic: 57.4 us -> 33.4 us
  between operations: 5.65 us -> 17.4 us
  matrix products: 110 us -> 102 us
    ppermute x127 -> x18, starting transfers between devices: 218 us -> 10.2 us  [move(): return lax.ppermute(value, self.axis, pairs)]
    reduce_scatter x0 -> x1, waiting for transfers between devices: none -> 162 us  [collect(): lax.psum_scatter(pieces, ('ctx', 'vocab'), scatter_dimension=0, tiled=False)]
    unnamed x203 -> x74, local copies, waits for them, and re-layouts: 72.8 us -> 18.7 us
    all_gather x0 -> x1, waiting for transfers between devices: none -> 42.8 us  [spread(): pieces = lax.all_gather(piece, ('ctx', 'vocab'))]
    all_gather x0 -> x1, blocking collectives: none -> 31.8 us  [local(): gain_all = lax.all_gather(final_gain, 'vocab', tiled=True)]
    ppermute x127 -> x18, waiting for transfers between devices: 123 us -> 92.4 us  [move(): return lax.ppermute(value, self.axis, pairs)]
    ppermute x5 -> x2, starting transfers between devices: 28.2 us -> 11.3 us  [final_move(): return lax.ppermute(value, ('ctx', 'vocab'), pairs)]
    dynamic_slice x0 -> x3, local copies, waits for them, and re-layouts: none -> 11.2 us  [the longest x1 6.32 us: collect(): lax.dynamic_index_in_dim(partial, relative_place(index), 0, keepdims=False)]
  transfers between devices with their start and end apart: 132 -> 24, of which waited for: 48 -> 15; matrix products, arithmetic and copies ran while one was open for 30% -> 13% of each run, Pallas kernels for 0% -> 0%
where the time goes in v2:
time: 591 us; the launch traced here: 585 us
  waiting for transfers between devices  315 us (53%)
  matrix products  102 us (17%)
  local copies, waits for them, and re-layouts  49.4 us (8%)
  blocking collectives  38.2 us (6%)
  other arithmetic  33.4 us (6%)
  starting transfers between devices  29.4 us (5%)
  between operations  17.4 us (3%)
    reduce_scatter x1, waiting for transfers between devices, collect(): lax.psum_scatter(pieces, ('ctx', 'vocab'), scatter_dimension=0, tiled=False)  162 us
    ppermute x18, waiting for transfers between devices, move(): return lax.ppermute(value, self.axis, pairs)  92.4 us
    all_gather x1, waiting for transfers between devices, spread(): pieces = lax.all_gather(piece, ('ctx', 'vocab'))  42.8 us
    dot_general x3, matrix products, contract_first(): lax.dot_general(left, right, (((0,), (0,)), ((), ())), preferred_element_...  36.1 us
    dot_general x3, matrix products, dot(): return jnp.dot(left, right, preferred_element_type=F32)  33.1 us
    dot_general x5, matrix products, contract_last(): lax.dot_general(left, right, (((1,), (1,)), ((), ())), preferred_element_...  32.5 us
    all_gather x1, blocking collectives, local(): gain_all = lax.all_gather(final_gain, 'vocab', tiled=True)  31.8 us
    unnamed x74, local copies, waits for them, and re-layouts  18.7 us
  transfers between devices with their start and end apart: 24, of which 15 were waited for; matrix products, arithmetic and copies ran while one was open for 13% of the time, Pallas kernels for 0%

profile of v2, /device:TPU:2, one launch (start us, length us, event | category | flops | bytes accessed | tf_op | source)
XLA Modules:
  0.0 584.6 jit_solution(711231198229960322)
XLA Ops:
  7.2 2.1 multiply_reduce_fusion.3
  11.4 2.5 constant_dynamic-slice_fusion.29
  13.9 2.3 constant_dynamic-slice_fusion.23
  18.2 2.2 constant_dynamic-slice_fusion.28
  24.2 15.5 %collective-permute-done.5 = bf16[128,3584]{1,0:T(8,128)(2,1)} collective-permute-done((bf16[128,3584]{1,0:T(8,128)(2,1)}, bf16[128,3584]{1,0:T(8,128)(2,1)}, u32[]{:S(2)}, u32[]{:S(2)}) %collective-permute-start.5) | collective-permute-done | bytes 917536 | tf_op jit(solution)/shard_map/ppermute | solution.py:26
  41.1 18.1 %collective-permute-done = bf16[128,3584]{1,0:T(8,128)(2,1)} collective-permute-done((bf16[128,3584]{1,0:T(8,128)(2,1)}, bf16[128,3584]{1,0:T(8,128)(2,1)}, u32[]{:S(2)}, u32[]{:S(2)}) %collective-permute-start) | collective-permute-done | bytes 917536 | tf_op jit(solution)/shard_map/ppermute | solution.py:26
  60.6 3.3 fusion.60
  64.0 4.7 fusion.65
  72.7 6.1 %collective-permute-done.9 = bf16[128,896]{1,0:T(8,128)(2,1)S(1)} collective-permute-done((bf16[128,896]{1,0:T(8,128)(2,1)S(1)}, bf16[128,896]{1,0:T(8,128)(2,1)S(1)}, u32[]{:S(2)}, u32[]{:S(2)}) %collective-permute-start.9) | collective-permute-done | bytes 229408 | tf_op jit(solution)/shard_map/ppermute | solution.py:26
  79.7 31.8 %all-gather.1 = f32[8,1,896]{2,1,0:T(1,128)S(1)} all-gather(f32[1,1,896]{2,1,0:T(1,128)S(1)} %reshape.302), channel_id=1, replica_groups=mesh['ctx'=4,'vocab'=8] {'vocab'}, dimensions={0}, use_global_device_ids=true | all-gather | bytes 32256 | tf_op jit(solution)/shard_map/all_gather | solution.py:134
  111.7 42.8 %all-gather.4.cloned.1.call-done = bf16[4096,896]{1,0:T(8,128)(2,1)} async-done(((bf16[128,896]{1,0:T(8,128)(2,1)}), bf16[4096,896]{1,0:T(8,128)(2,1)}) %all-gather.4.cloned.1.call-update) | async-done | bytes 7340048 | tf_op jit(solution)/shard_map/all_gather | solution.py:169
  154.5 4.0 constant_dynamic-slice_fusion.16
  160.2 2.0 multiply_reduce_fusion
  163.1 21.3 %exponential_reduce_fusion = (f32[512]{0:T(512)S(1)}, f32[512]{0:T(512)S(1)}, f32[512]{0:T(512)S(1)}, f32[512,2048]{1,0:T(8,128)}) fusion(f32[512]{0:T(512)S(1)} %add_rsqrt_fusion, s32[2048]{0:T(1024)S(1)} %iota_add_fusion, s32[512]{0:T(512)S(1)} %bitcast.157, bf16[512,7168]{1,0:T(8,128)(2,1)S(1)} %constant_dynamic-update-slice_fusion, ...), kind=kOutput, calls=%fused_computation.11 | convolution fusion | flops 15040774144 | bytes 40912896 | tf_op jit(solution)/shard_map/dot_general | solution.py:68
  185.3 3.7 all-to-all-start
  189.2 7.4 %all-to-all-done = f32[32,3,4,128]{3,2,1,0:T(4,128)S(1)} async-done(((f32[32,3,4,128]{3,2,1,0:T(4,128)}), f32[32,3,4,128]{3,2,1,0:T(4,128)S(1)}, u32[]{:S(2)}, u32[]{:S(2)}) %all-to-all-start) | async-done | bytes 196640 | tf_op jit(solution)/shard_map/all_to_all | solution.py:60
  196.8 25.1 %convolution_convert_fusion.1 = bf16[512,7168]{1,0:T(8,128)(2,1)} fusion(bf16[2048,7168]{1,0:T(8,128)(2,1)} %param.17, f32[512,2048]{1,0:T(8,128)} %get-tuple-element.71, f32[512]{0:T(512)S(1)} %bitcast.154, f32[512]{0:T(512)S(1)} %get-tuple-element.55, s32[2048]{0:T(1024)S(1)} %iota_add_fusion, f32[512]{0:T(512)S(1)} %add_rsqrt_fusion, s32[512]{0:T(512)S(1)} %bitcast.158), kind=kOutput, calls=%fused_computation.2 | convolution fusion | flops 15043395584 | bytes 40910848 | tf_op jit(solution)/shard_map/dot_general | solution.py:72
  221.9 6.3 %constant_dynamic-slice_fusion.15 = (bf16[1,128,7168]{2,1,0:T(8,128)(2,1)}, bf16[1,128,7168]{2,1,0:T(8,128)(2,1)}, bf16[1,128,7168]{2,1,0:T(8,128)(2,1)}, bf16[1,128,7168]{2,1,0:T(8,128)(2,1)}) fusion(bf16[4,128,7168]{2,1,0:T(8,128)(2,1)} %bitcast.134, s32[]{:T(128)S(6)} %select_n.409, s32[]{:T(128)S(6)} %select_n.411, s32[]{:T(128)S(6)} %select_n.410, ...), kind=kLoop, calls=%fused_computation.99 | loop fusion | bytes 14680080 | tf_op jit(solution)/shard_map/jit(dynamic_index_in_dim)/dynamic_slice | solution.py:214
  228.2 3.9 copy.69
  232.1 3.9 copy.71
  235.9 3.9 copy.70
  239.8 3.9 copy.72
  243.7 6.6 %pad_maximum_fusion = bf16[32,128,896]{1,2,0:T(8,128)(2,1)} fusion(bf16[8,128,896]{1,2,0:T(8,128)(2,1)} %bitcast.128, bf16[8,128,896]{1,2,0:T(8,128)(2,1)} %bitcast.126, bf16[8,128,896]{1,2,0:T(8,128)(2,1)} %bitcast.127, bf16[8,128,896]{1,2,0:T(8,128)(2,1)} %bitcast.125), kind=kLoop, calls=%fused_computation.3 | loop fusion | flops 11010048 | bytes 14680064 | tf_op jit(solution)/shard_map/concatenate | solution.py:216
  250.8 162.2 %reduce-scatter.2.cloned.1.call-done = bf16[1,128,896]{1,2,0:T(8,128)(2,1)} async-done(((bf16[32,128,896]{1,2,0:T(8,128)(2,1)}), bf16[1,128,896]{1,2,0:T(8,128)(2,1)}) %reduce-scatter.2.cloned.1.call-update) | async-done | bytes 229392 | tf_op jit(solution)/shard_map/reduce_scatter | solution.py:217
  415.3 5.5 collective-permute-done.10
  423.3 25.5 %convolution_convert_fusion = bf16[2048,7168]{1,0:T(8,128)(2,1)} fusion(bf16[512,7168]{1,0:T(8,128)(2,1)} %copy-done.1, f32[512,2048]{1,0:T(8,128)} %get-tuple-element.71, f32[512]{0:T(512)S(1)} %bitcast.155, f32[512]{0:T(512)S(1)} %get-tuple-element.55, s32[2048]{0:T(1024)S(1)} %iota_add_fusion, f32[512]{0:T(512)S(1)} %add_rsqrt_fusion, s32[512]{0:T(512)S(1)} %bitcast.159), kind=kOutput, calls=%fused_computation | convolution fusion | flops 15054405632 | bytes 40910848 | tf_op jit(solution)/shard_map/dot_general | solution.py:64
  448.8 2.5 maximum_convert_fusion
  451.4 2.7 copy.62
  454.1 4.4 fusion.4
  459.5 2.2 fusion.19
  463.1 4.0 fusion.24
  467.1 2.0 collective-permute-start.16
  469.8 4.0 all-to-all-start.1
  473.8 5.7 convolution_convert_fusion.2
  479.5 6.0 %collective-permute-done.12 = bf16[512,896]{1,0:T(8,128)(2,1)} collective-permute-done((bf16[512,896]{1,0:T(8,128)(2,1)}, bf16[512,896]{1,0:T(8,128)(2,1)}, u32[]{:S(2)}, u32[]{:S(2)}) %collective-permute-start.12) | collective-permute-done | bytes 917536 | tf_op jit(solution)/shard_map/ppermute | solution.py:26
  485.6 2.6 add_convert_fusion.1
  488.2 16.6 %collective-permute-done.16 = bf16[512,896]{1,0:T(8,128)(2,1)} collective-permute-done((bf16[512,896]{1,0:T(8,128)(2,1)}, bf16[512,896]{1,0:T(8,128)(2,1)}, u32[]{:S(2)}, u32[]{:S(2)}) %collective-permute-start.16) | collective-permute-done | bytes 917536 | tf_op jit(solution)/shard_map/ppermute | solution.py:26
  504.9 2.4 add_convert_fusion
  509.0 4.9 convolution_convert_fusion.3
  515.0 2.1 collective-permute-start.17
  517.1 5.7 collective-permute-done.13
  523.9 12.1 %collective-permute-done.17 = bf16[2,128,896]{2,1,0:T(8,128)(2,1)S(1)} collective-permute-done((bf16[2,128,896]{2,1,0:T(8,128)(2,1)S(1)}, bf16[2,128,896]{2,1,0:T(8,128)(2,1)S(1)}, u32[]{:S(2)}, u32[]{:S(2)}) %collective-permute-start.17) | collective-permute-done | bytes 458784 | tf_op jit(solution)/shard_map/ppermute | solution.py:26
  538.3 4.5 collective-permute-start.15
  542.8 5.1 collective-permute-done.18
  549.0 6.8 %collective-permute-start.19 = (bf16[128,896]{1,0:T(8,128)(2,1)S(1)}, bf16[128,896]{1,0:T(8,128)(2,1)S(1)}, u32[]{:S(2)}, u32[]{:S(2)}) collective-permute-start(bf16[128,896]{1,0:T(8,128)(2,1)S(1)} %fusion.42), channel_id=1, source_target_pairs={{0,0},{1,1},{2,8},{3,9},{4,16},{5,17},{6,24},{7,25},{8,2},{9,3},{1... | collective-permute-start | bytes 688136 | tf_op jit(solution)/shard_map/ppermute | solution.py:228
  555.8 7.3 %collective-permute-done.15 = bf16[128,896]{1,0:T(8,128)(2,1)S(1)} collective-permute-done((bf16[128,896]{1,0:T(8,128)(2,1)S(1)}, bf16[128,896]{1,0:T(8,128)(2,1)S(1)}, u32[]{:S(2)}, u32[]{:S(2)}) %collective-permute-start.15) | collective-permute-done | bytes 229408 | tf_op jit(solution)/shard_map/ppermute | solution.py:228
  565.1 2.9 collective-permute-done.19
  569.9 6.4 %all-reduce = (f32[896]{0:T(1024)}, f32[896]{0:T(1024)}) all-reduce(f32[896]{0:T(1024)S(1)} %get-tuple-element.31, f32[896]{0:T(1024)S(1)} %get-tuple-element.29), channel_id=1, replica_groups=mesh['ctx'=4,'vocab'=8] {'ctx'}, use_global_device_ids=true, to_apply=%region_19.20 | all-reduce | flops 1792 | bytes 14336 | tf_op jit(solution)/shard_map/psum | solution.py:304
  (153 shorter events, 37.6 us)
Async XLA Ops:
  7.2 56.8 %copy-start = (bf16[1792,896]{1,0:T(8,128)(2,1)S(1)}, bf16[1792,896]{1,0:T(8,128)(2,1)}, u32[]{:S(2)}) copy-start(bf16[1792,896]{1,0:T(8,128)(2,1)} %param.14) | copy-start | bytes 9633796
  7.2 147.3 %all-gather.4.cloned.1.call-start = ((), (), s32[]{:S(2)}) async-start(), calls=%async_computation.4 | async-start | bytes 7569408 | tf_op jit(solution)/shard_map/all_gather | solution.py:169
  11.3 9.1 %collective-permute-start.3 = (f32[2,128]{1,0:T(2,128)S(1)}, f32[2,128]{1,0:T(2,128)S(1)}, u32[]{:S(2)}, u32[]{:S(2)}) collective-permute-start(f32[2,128]{1,0:T(2,128)S(1)} %fusion.52), channel_id=1, source_target_pairs={{0,16},{8,24},{16,0},{24,8},{1,17},{9,25},{17,1},{25,9},{2,18},{10... | collective-permute-start | bytes 3080 | tf_op jit(solution)/shard_map/ppermute | solution.py:26
  13.9 50.0 %collective-permute-start.1 = (bf16[128,1792]{1,0:T(8,128)(2,1)}, bf16[128,1792]{1,0:T(8,128)(2,1)}, u32[]{:S(2)}, u32[]{:S(2)}) collective-permute-start(bf16[128,1792]{1,0:T(8,128)(2,1)} %get-tuple-element.36), channel_id=1, source_target_pairs={{0,8},{8,0},{16,24},{24,16},{1,9},{9,1},{17,25},{25,17},{2,10},{10... | collective-permute-start | bytes 1376264 | tf_op jit(solution)/shard_map/ppermute | solution.py:26
  13.9 6.8 %copy-start.2 = (bf16[128,7168]{1,0:T(8,128)(2,1)S(1)}, bf16[128,7168]{1,0:T(8,128)(2,1)}, u32[]{:S(2)}) copy-start(bf16[128,7168]{1,0:T(8,128)(2,1)} %param.11) | copy-start | bytes 5505028
  16.2 23.5 %collective-permute-start.5 = (bf16[128,3584]{1,0:T(8,128)(2,1)}, bf16[128,3584]{1,0:T(8,128)(2,1)}, u32[]{:S(2)}, u32[]{:S(2)}) collective-permute-start(bf16[128,3584]{1,0:T(8,128)(2,1)} %constant_dynamic-slice_fusion.23), channel_id=1, source_target_pairs={{0,16},{8,24},{16,0},{24,8},{1,17},{9,25},{17,1},{25,9},{2,18},{10... | collective-permute-start | bytes 2752520 | tf_op jit(solution)/shard_map/ppermute | solution.py:26
  20.4 38.8 %collective-permute-start = (bf16[128,3584]{1,0:T(8,128)(2,1)}, bf16[128,3584]{1,0:T(8,128)(2,1)}, u32[]{:S(2)}, u32[]{:S(2)}) collective-permute-start(bf16[128,3584]{1,0:T(8,128)(2,1)} %constant_dynamic-slice_fusion.28), channel_id=1, source_target_pairs={{0,16},{8,24},{16,0},{24,8},{1,17},{9,25},{17,1},{25,9},{2,18},{10... | collective-permute-start | bytes 2752520 | tf_op jit(solution)/shard_map/ppermute | solution.py:26
  20.4 3.8 collective-permute-start.4
  22.0 38.5 %collective-permute-start.6 = (bf16[128,1792]{1,0:T(8,128)(2,1)}, bf16[128,1792]{1,0:T(8,128)(2,1)}, u32[]{:S(2)}, u32[]{:S(2)}) collective-permute-start(bf16[128,1792]{1,0:T(8,128)(2,1)} %get-tuple-element.34), channel_id=1, source_target_pairs={{0,8},{8,0},{16,24},{24,16},{1,9},{9,1},{17,25},{25,17},{2,10},{10... | collective-permute-start | bytes 1376264 | tf_op jit(solution)/shard_map/ppermute | solution.py:26
  22.3 38.2 %copy-start.12 = (bf16[128,1792]{1,0:T(8,128)(2,1)S(1)}, bf16[128,1792]{1,0:T(8,128)(2,1)}, u32[]{:S(2)}) copy-start(bf16[128,1792]{1,0:T(8,128)(2,1)} %get-tuple-element.33) | copy-start | bytes 1376260
  22.3 38.2 %copy-start.26 = (bf16[1792,896]{1,0:T(8,128)(2,1)S(1)}, bf16[1792,896]{1,0:T(8,128)(2,1)}, u32[]{:S(2)}) copy-start(bf16[1792,896]{1,0:T(8,128)(2,1)} %param.15) | copy-start | bytes 9633796
  41.0 22.9 %copy-start.15 = (bf16[128,1792]{1,0:T(8,128)(2,1)}, bf16[128,1792]{1,0:T(8,128)(2,1)S(1)}, u32[]{:S(2)}) copy-start(bf16[128,1792]{1,0:T(8,128)(2,1)S(1)} %get-tuple-element.49) | copy-start | bytes 1376260
  41.0 19.5 %collective-permute-start.7 = (bf16[128,1792]{1,0:T(8,128)(2,1)S(1)}, bf16[128,1792]{1,0:T(8,128)(2,1)S(1)}, u32[]{:S(2)}, u32[]{:S(2)}) collective-permute-start(bf16[128,1792]{1,0:T(8,128)(2,1)S(1)} %get-tuple-element.50), channel_id=1, source_target_pairs={{0,8},{8,0},{16,24},{24,16},{1,9},{9,1},{17,25},{25,17},{2,10},{10... | collective-permute-start | bytes 1376264 | tf_op jit(solution)/shard_map/ppermute | solution.py:26
  60.4 3.6 copy-start.13
  60.4 3.5 collective-permute-start.2
  60.5 3.4 copy-start.30
  60.5 3.4 copy-start.10
  63.9 4.8 copy-start.5
  64.0 4.7 copy-start.28
  68.7 10.1 %copy-start.23 = (f32[896]{0:T(1024)S(1)}, f32[896]{0:T(1024)}, u32[]{:S(2)}) copy-start(f32[896]{0:T(1024)} %param.16) | copy-start | bytes 10756
  68.7 42.9 %copy-start.25 = (s32[512]{0:T(512)S(1)}, s32[512]{0:T(512)}, u32[]{:S(2)}) copy-start(s32[512]{0:T(512)} %param.18) | copy-start | bytes 6148
  68.8 1.9 collective-permute-start.8
  70.8 8.0 %collective-permute-start.9 = (bf16[128,896]{1,0:T(8,128)(2,1)S(1)}, bf16[128,896]{1,0:T(8,128)(2,1)S(1)}, u32[]{:S(2)}, u32[]{:S(2)}) collective-permute-start(bf16[128,896]{1,0:T(8,128)(2,1)S(1)} %slice.115), channel_id=1, source_target_pairs={{0,16},{8,24},{16,0},{24,8},{1,17},{9,25},{17,1},{25,9},{2,18},{10... | collective-permute-start | bytes 688136 | tf_op jit(solution)/shard_map/ppermute | solution.py:26
  163.1 26.1 %copy-start.24 = (s32[512]{0:T(512)S(1)}, s32[512]{0:T(512)}, u32[]{:S(2)}) copy-start(s32[512]{0:T(512)} %param.19) | copy-start | bytes 6148
  185.3 11.3 %all-to-all-start = ((f32[32,3,4,128]{3,2,1,0:T(4,128)}), f32[32,3,4,128]{3,2,1,0:T(4,128)S(1)}, u32[]{:S(2)}, u32[]{:S(2)}) async-start(f32[32,3,4,128]{3,2,1,0:T(4,128)} %broadcast_in_dim.151), calls=%async_computation | async-start | bytes 393216 | tf_op jit(solution)/shard_map/all_to_all | solution.py:60
  188.9 224.1 %reduce-scatter.2.cloned.1.call-start = ((), (), s32[]{:S(2)}) async-start(), calls=%async_computation.3 | async-start | bytes 7569408 | tf_op jit(solution)/shard_map/reduce_scatter | solution.py:217
  413.0 7.8 %collective-permute-start.10 = (bf16[128,896]{0,1:T(8,128)(2,1)}, bf16[128,896]{0,1:T(8,128)(2,1)S(1)}, u32[]{:S(2)}, u32[]{:S(2)}) collective-permute-start(bf16[128,896]{0,1:T(8,128)(2,1)} %bitcast.145), channel_id=1, source_target_pairs={{0,16},{8,24},{16,0},{24,8},{1,17},{9,25},{17,1},{25,9},{2,18},{10... | collective-permute-start | bytes 688136 | tf_op jit(solution)/shard_map/ppermute | solution.py:26
  423.3 25.5 %copy-start.8 = (bf16[1,128,896]{1,2,0:T(8,128)(2,1)S(1)}, bf16[1,128,896]{1,2,0:T(8,128)(2,1)}, u32[]{:S(2)}) copy-start(bf16[1,128,896]{1,2,0:T(8,128)(2,1)} %reduce-scatter.2.cloned.1.call-done) | copy-start | bytes 688132
  423.3 25.5 %collective-permute-start.11 = (bf16[2,128,896]{1,2,0:T(8,128)(2,1)}, bf16[2,128,896]{1,2,0:T(8,128)(2,1)}, u32[]{:S(2)}, u32[]{:S(2)}) collective-permute-start(bf16[2,128,896]{1,2,0:T(8,128)(2,1)} %pad_maximum_fusion.3), channel_id=1, source_target_pairs={{0,8},{8,0},{16,24},{24,16},{1,9},{9,1},{17,25},{25,17},{2,10},{10... | collective-permute-start | bytes 1376264 | tf_op jit(solution)/shard_map/ppermute | solution.py:26
  458.5 3.2 copy-start.3
  461.7 23.8 %collective-permute-start.12 = (bf16[512,896]{1,0:T(8,128)(2,1)}, bf16[512,896]{1,0:T(8,128)(2,1)}, u32[]{:S(2)}, u32[]{:S(2)}) collective-permute-start(bf16[512,896]{1,0:T(8,128)(2,1)} %fusion.19), channel_id=1, source_target_pairs={{0,1},{1,0},{2,3},{3,2},{4,5},{5,4},{6,7},{7,6},{8,9},{9,8},{10,11... | collective-permute-start | bytes 2752520 | tf_op jit(solution)/shard_map/ppermute | solution.py:26
  467.1 37.8 %collective-permute-start.16 = (bf16[512,896]{1,0:T(8,128)(2,1)}, bf16[512,896]{1,0:T(8,128)(2,1)}, u32[]{:S(2)}, u32[]{:S(2)}) collective-permute-start(bf16[512,896]{1,0:T(8,128)(2,1)} %fusion.24), channel_id=1, source_target_pairs={{0,1},{1,0},{2,3},{3,2},{4,5},{5,4},{6,7},{7,6},{8,9},{9,8},{10,11... | collective-permute-start | bytes 2752520 | tf_op jit(solution)/shard_map/ppermute | solution.py:26
  469.8 44.1 %all-to-all-start.1 = ((f32[32,2,128]{2,1,0:T(2,128)}), f32[32,2,128]{2,1,0:T(2,128)S(1)}, u32[]{:S(2)}, u32[]{:S(2)}) async-start(f32[32,2,128]{2,1,0:T(2,128)} %bitcast.53), calls=%async_computation.2 | async-start | bytes 65536 | tf_op jit(solution)/shard_map/all_to_all | solution.py:280
  473.8 11.8 %copy-start.16 = (bf16[128,896]{1,0:T(8,128)(2,1)S(1)}, bf16[128,896]{1,0:T(8,128)(2,1)}, u32[]{:S(2)}) copy-start(bf16[128,896]{1,0:T(8,128)(2,1)} %get-tuple-element.46) | copy-start | bytes 688132
  473.8 11.8 %copy-start.17 = (bf16[128,896]{1,0:T(8,128)(2,1)S(1)}, bf16[128,896]{1,0:T(8,128)(2,1)}, u32[]{:S(2)}) copy-start(bf16[128,896]{1,0:T(8,128)(2,1)} %get-tuple-element.47) | copy-start | bytes 688132
  473.8 11.7 %copy-start.18 = (bf16[128,896]{1,0:T(8,128)(2,1)S(1)}, bf16[128,896]{1,0:T(8,128)(2,1)}, u32[]{:S(2)}) copy-start(bf16[128,896]{1,0:T(8,128)(2,1)} %get-tuple-element.48) | copy-start | bytes 688132
  485.6 19.3 %copy-start.27 = (bf16[1792,896]{1,0:T(8,128)(2,1)S(1)}, bf16[1792,896]{1,0:T(8,128)(2,1)}, u32[]{:S(2)}) copy-start(bf16[1792,896]{1,0:T(8,128)(2,1)} %param.15) | copy-start | bytes 9633796
  488.2 19.1 %copy-start.7 = (bf16[512,896]{1,0:T(8,128)(2,1)}, bf16[512,896]{1,0:T(8,128)(2,1)S(1)}, u32[]{:S(2)}) copy-start(bf16[512,896]{1,0:T(8,128)(2,1)S(1)} %add_convert_fusion.1) | copy-start | bytes 2752516
  488.2 20.9 %copy-start.4 = (bf16[512,896]{1,0:T(8,128)(2,1)S(1)}, bf16[512,896]{1,0:T(8,128)(2,1)}, u32[]{:S(2)}) copy-start(bf16[512,896]{1,0:T(8,128)(2,1)} %copy-done.3) | copy-start | bytes 2752516
  488.2 20.8 %copy-start.11 = (bf16[128,1792]{1,0:T(8,128)(2,1)S(1)}, bf16[128,1792]{1,0:T(8,128)(2,1)}, u32[]{:S(2)}) copy-start(bf16[128,1792]{1,0:T(8,128)(2,1)} %get-tuple-element.35) | copy-start | bytes 1376260
  488.2 20.8 %copy-start.14 = (bf16[128,1792]{1,0:T(8,128)(2,1)S(1)}, bf16[128,1792]{1,0:T(8,128)(2,1)}, u32[]{:S(2)}) copy-start(bf16[128,1792]{1,0:T(8,128)(2,1)} %copy-done.13) | copy-start | bytes 1376260
  488.2 20.8 %copy-start.29 = (bf16[128,1792]{1,0:T(8,128)(2,1)S(1)}, bf16[128,1792]{1,0:T(8,128)(2,1)}, u32[]{:S(2)}) copy-start(bf16[128,1792]{1,0:T(8,128)(2,1)} %copy-done.28) | copy-start | bytes 1376260
  509.0 13.7 %collective-permute-start.13 = (bf16[2,128,896]{2,1,0:T(8,128)(2,1)}, bf16[2,128,896]{2,1,0:T(8,128)(2,1)}, u32[]{:S(2)}, u32[]{:S(2)}) collective-permute-start(bf16[2,128,896]{2,1,0:T(8,128)(2,1)} %pad_maximum_fusion.4), channel_id=1, source_target_pairs={{0,2},{1,3},{2,0},{3,1},{4,6},{5,7},{6,4},{7,5},{8,10},{9,11},{10,... | collective-permute-start | bytes 1376264 | tf_op jit(solution)/shard_map/ppermute | solution.py:26
  515.0 21.1 %collective-permute-start.17 = (bf16[2,128,896]{2,1,0:T(8,128)(2,1)S(1)}, bf16[2,128,896]{2,1,0:T(8,128)(2,1)S(1)}, u32[]{:S(2)}, u32[]{:S(2)}) collective-permute-start(bf16[2,128,896]{2,1,0:T(8,128)(2,1)S(1)} %pad_maximum_fusion.5), channel_id=1, source_target_pairs={{0,2},{1,3},{2,0},{3,1},{4,6},{5,7},{6,4},{7,5},{8,10},{9,11},{10,... | collective-permute-start | bytes 1376264 | tf_op jit(solution)/shard_map/ppermute | solution.py:26
  523.9 13.3 %collective-permute-start.14 = (bf16[1,128,896]{2,1,0:T(8,128)(2,1)S(1)}, bf16[1,128,896]{2,1,0:T(8,128)(2,1)S(1)}, u32[]{:S(2)}, u32[]{:S(2)}) collective-permute-start(bf16[1,128,896]{2,1,0:T(8,128)(2,1)S(1)} %add_convert_fusion.6), channel_id=1, source_target_pairs={{0,4},{1,5},{2,6},{3,7},{4,0},{5,1},{6,2},{7,3},{8,12},{9,13},{10,... | collective-permute-start | bytes 688136 | tf_op jit(solution)/shard_map/ppermute | solution.py:26
  537.1 10.9 %collective-permute-start.18 = (bf16[1,128,896]{2,1,0:T(8,128)(2,1)S(1)}, bf16[1,128,896]{2,1,0:T(8,128)(2,1)S(1)}, u32[]{:S(2)}, u32[]{:S(2)}) collective-permute-start(bf16[1,128,896]{2,1,0:T(8,128)(2,1)S(1)} %add_convert_fusion.4), channel_id=1, source_target_pairs={{0,4},{1,5},{2,6},{3,7},{4,0},{5,1},{6,2},{7,3},{8,12},{9,13},{10,... | collective-permute-start | bytes 688136 | tf_op jit(solution)/shard_map/ppermute | solution.py:26
  538.3 24.8 %collective-permute-start.15 = (bf16[128,896]{1,0:T(8,128)(2,1)S(1)}, bf16[128,896]{1,0:T(8,128)(2,1)S(1)}, u32[]{:S(2)}, u32[]{:S(2)}) collective-permute-start(bf16[128,896]{1,0:T(8,128)(2,1)S(1)} %fusion.41), channel_id=1, source_target_pairs={{0,0},{1,1},{2,8},{3,9},{4,16},{5,17},{6,24},{7,25},{8,2},{9,3},{1... | collective-permute-start | bytes 688136 | tf_op jit(solution)/shard_map/ppermute | solution.py:228
  549.0 19.0 %collective-permute-start.19 = (bf16[128,896]{1,0:T(8,128)(2,1)S(1)}, bf16[128,896]{1,0:T(8,128)(2,1)S(1)}, u32[]{:S(2)}, u32[]{:S(2)}) collective-permute-start(bf16[128,896]{1,0:T(8,128)(2,1)S(1)} %fusion.42), channel_id=1, source_target_pairs={{0,0},{1,1},{2,8},{3,9},{4,16},{5,17},{6,24},{7,25},{8,2},{9,3},{1... | collective-permute-start | bytes 688136 | tf_op jit(solution)/shard_map/ppermute | solution.py:228
  (7 other events, 14.1 us)
Sparse Core Ops, SparseCore 0:
  79.7 74.7 all-gather.3
  250.4 162.5 reduce-scatter.1

commit v3 on v2

v3 whole, which is shorter than its diff:
```python
import jax
import jax.numpy as jnp
from jax import lax
from jax.sharding import PartitionSpec as P

EPSILON = 1e-06
PARTS = 2
F32 = jnp.float32
BF16 = jnp.bfloat16


class Dim:
    def __init__(self, axis, size, n, stride):
        self.axis, self.size, self.n, self.stride = axis, size, n, stride

    def place(self):
        return (lax.axis_index(self.axis) // self.stride) % self.n

    def move(self, value, target):
        pairs = []
        for index in range(self.size):
            here = (index // self.stride) % self.n
            there = target(here)
            if there is not None and 0 <= there < self.n:
                pairs.append((index, index + (there - here) * self.stride))
        return lax.ppermute(value, self.axis, pairs)

    def swap(self, value, bit):
        return self.move(value, lambda here: here ^ bit)

    def turn(self, value, by):
        return self.move(value, lambda here: (here + by) % self.n)


def halving_scatter(chunks, dim):
    here = dim.place()
    held = {
        offset: lax.dynamic_index_in_dim(chunks, here ^ offset, 0, keepdims=False)
        for offset in range(dim.n)
    }
    bit = 1
    while bit < dim.n:
        send = jnp.stack([held[offset] for offset in range(dim.n) if offset in held and offset & bit])
        got = dim.swap(send, bit)
        keep = [offset for offset in sorted(held) if not offset & bit]
        held = {
            offset: (held[offset].astype(F32) + got[index].astype(F32))
            for index, offset in enumerate(keep)
        }
        bit *= 2
        if bit < dim.n:
            held = {offset: piece.astype(BF16) for offset, piece in held.items()}
    return held[0]


def sum_everywhere(value):
    axes = ("ctx", "vocab")
    count = lax.axis_size("ctx") * lax.axis_size("vocab")
    copies = jnp.broadcast_to(value[None], (count,) + value.shape)
    return jnp.sum(lax.all_to_all(copies, axes, 0, 0, tiled=True), axis=0)


def contract_first(left, right):
    return lax.dot_general(left, right, (((0,), (0,)), ((), ())), preferred_element_type=F32)


def contract_last(left, right):
    return lax.dot_general(left, right, (((1,), (1,)), ((), ())), preferred_element_type=F32)


def dot(left, right):
    return jnp.dot(left, right, preferred_element_type=F32)


def cut(array, start, width, axis):
    return lax.dynamic_slice_in_dim(array, start, width, axis)


def local(
    hidden_state,
    embedded_next,
    gain_hidden,
    gain_embed,
    proj_hidden,
    proj_embed,
    final_gain,
    head,
    targets,
    loss_mask,
):
    nc, nv = lax.axis_size("ctx"), lax.axis_size("vocab")
    nx, va = nc // 2, 4
    vb = nv // va
    core = Dim("ctx", nc, 2, 1)
    dim_x = Dim("ctx", nc, nx, 2)
    dim_b = Dim("vocab", nv, vb, 1)
    dim_a = Dim("vocab", nv, va, vb)
    own, slot = lax.axis_index("ctx"), lax.axis_index("vocab")
    x, c, b = own // 2, own % 2, slot % vb

    width = hidden_state.shape[1]
    block = hidden_state.shape[0]
    token_total = targets.shape[0]
    feat, cols = proj_hidden.shape
    rows = block // PARTS
    part_rows = nc * rows
    vocab_local = head.shape[0]

    def relative_place(block_index):
        return (c ^ (block_index % 2)) * nx + (x - block_index // 2) % nx

    def block_at(place):
        return ((x - place % nx) % nx) * 2 + (c ^ (place // nx))

    order = jnp.stack([relative_place(jnp.int32(i)) for i in range(nc)])
    to_absolute = (order[:, None] == jnp.arange(nc, dtype=jnp.int32)[None, :])[:, :, None, None]

    def absolute(value):
        value = value.reshape(value.shape[:-1] + (PARTS, nc, rows))
        value = jnp.swapaxes(value, -3, -2)[..., None, :, :, :]
        return jnp.sum(jnp.where(to_absolute, value, 0), axis=-3).reshape(
            value.shape[:-4] + (nc, block)
        )

    def relative(value):
        value = value.reshape(value.shape[:-1] + (PARTS, rows))[..., :, None, :, :]
        value = jnp.sum(jnp.where(to_absolute, value, 0), axis=-4)
        return jnp.swapaxes(value, -3, -2).reshape(value.shape[:-3] + (token_total,))

    def by_part(pieces):
        return jnp.concatenate(
            [piece[part * rows : (part + 1) * rows] for part in range(PARTS) for piece in pieces]
        )

    def gather_x(value):
        return jnp.stack([value] + [dim_x.turn(value, r) for r in range(1, nx)])

    def x_sends(wide):
        return [cut(wide, ((x + r) % nx) * 2 * feat, 2 * feat, 1) for r in range(1, nx)]

    hidden_sends, embed_sends = x_sends(hidden_state), x_sends(embedded_next)
    hidden_sends, embed_sends, hidden_state, embedded_next = lax.optimization_barrier(
        (hidden_sends, embed_sends, hidden_state, embedded_next)
    )
    hidden_x = [dim_x.turn(send, r + 1) for r, send in enumerate(hidden_sends)]
    embed_x = [dim_x.turn(send, r + 1) for r, send in enumerate(embed_sends)]

    hidden_wide, embed_wide = hidden_state.astype(F32), embedded_next.astype(F32)
    scales = lax.rsqrt(
        jnp.stack(
            [jnp.mean(hidden_wide * hidden_wide, axis=-1), jnp.mean(embed_wide * embed_wide, axis=-1)]
        )
        + EPSILON
    )
    scales_x = gather_x(scales)
    scales_all = jnp.concatenate([scales_x, core.swap(scales_x, 1)])

    def normed_inputs(wide, from_x, gain, kind):
        pieces = [cut(wide, x * 2 * feat, 2 * feat, 1)] + from_x
        mine = [cut(piece, c * feat, feat, 1) for piece in pieces]
        theirs = [core.swap(cut(piece, (1 - c) * feat, feat, 1), 1) for piece in pieces]
        raw = by_part(mine + theirs).astype(F32)
        scale = by_part([scales_all[place, kind][:, None] for place in range(nc)])
        return (raw * scale * cut(gain, own * feat, feat, 0)).astype(BF16)

    normed_h = normed_inputs(hidden_state, hidden_x, gain_hidden, 0)
    normed_e = normed_inputs(embedded_next, embed_x, gain_embed, 1)

    half_h, half_e = dot(normed_h, proj_hidden), dot(normed_e, proj_embed)
    total = (half_h + half_e).reshape(PARTS, 2, nx, rows, cols)
    mine = total[:, 0] + core.swap(total[:, 1].astype(BF16), 1).astype(F32)
    projected = mine[:, 0]
    for r in range(1, nx):
        projected = projected + dim_x.turn(mine[:, r].astype(BF16), -r).astype(F32)
    projected = projected.reshape(block, cols)

    pieces = lax.all_gather((projected * final_gain).astype(BF16), ("ctx", "vocab"))
    squares = jnp.sum(projected * projected, axis=-1)
    squares = lax.all_to_all(
        jnp.broadcast_to(squares, (nc * nv, block)), ("ctx", "vocab"), 0, 0, tiled=True
    )
    squares = jnp.sum(squares.reshape(nc, nv, block), axis=1)
    row_scale = relative(lax.rsqrt(squares / width + EPSILON))
    pieces = pieces.reshape(nc, nv, block, cols)
    gathered = by_part(
        [
            lax.dynamic_index_in_dim(pieces, block_at(place), 0, keepdims=False)
            .transpose(1, 0, 2)
            .reshape(block, width)
            for place in range(nc)
        ]
    )

    vocab_ids = (own * nv + slot) * vocab_local + lax.iota(jnp.int32, vocab_local)
    logits = contract_last(gathered, head) * row_scale[:, None]
    target = relative(targets.reshape(nc, block))
    mask_weight = loss_mask.astype(F32).reshape(nc, block)
    mask = relative(mask_weight)
    is_target = target[:, None] == vocab_ids[None, :]
    power = jnp.exp(logits)
    sums = jnp.stack(
        [
            jnp.sum(power, axis=-1),
            jnp.sum(power * (logits * F32(1.0 / 256.0)), axis=-1),
            jnp.sum(jnp.where(is_target, logits, F32(0.0)), axis=-1),
        ]
    )
    sums = sum_everywhere(absolute(sums))
    exp_total, weighted, target_logit = sums[0], sums[1], sums[2]
    log_total = jnp.log(exp_total)
    mean_loss = jnp.sum(mask_weight * (log_total - target_logit)) / token_total
    scaled_dot = mask * relative(weighted / exp_total * F32(256.0) - target_logit)
    probs = jnp.exp(logits - relative(log_total)[:, None])
    scaled_grad = ((mask * row_scale)[:, None] * (probs - is_target.astype(F32))).astype(BF16)
    coefficient = row_scale * row_scale * scaled_dot / width

    def column_chunk(value, place):
        return jnp.stack([cut(value, (p * vb + place) * cols, cols, 1) for p in range(va)])

    def collect(part_grad):
        partial = dot(part_grad, head).astype(BF16)
        mine, theirs = partial[: nx * rows], partial[nx * rows :]
        mine = (mine.astype(F32) + core.swap(theirs, 1).astype(F32)).astype(BF16)
        mine = mine.reshape(nx, rows, width)
        summed = mine[0].astype(F32)
        for r in range(1, nx):
            summed = summed + dim_x.turn(mine[r], -r).astype(F32)
        summed = summed.astype(BF16)
        kept = column_chunk(summed, b).astype(F32)
        for r in range(1, vb):
            kept = kept + dim_b.turn(column_chunk(summed, (b + r) % vb), r).astype(F32)
        summed = halving_scatter(kept.astype(BF16), dim_a).astype(BF16)
        along = gather_x(summed)
        along = jnp.concatenate([along, core.swap(along, 1)])
        return along.reshape(part_rows, cols)

    def final_move(value):
        pairs = []
        ratio = nv // nc
        for i in range(nc):
            for j in range(nv):
                pairs.append((i * nv + j, (j // ratio) * nv + i * ratio + j % ratio))
        return lax.ppermute(value, ("ctx", "vocab"), pairs)

    def back(part_grad):
        def products(place):
            picked = jnp.concatenate(
                [
                    cut(part_grad, relative_place((p * vb + place) // 2) * rows, rows, 0)
                    for p in range(va)
                ]
            )
            return [
                contract_last(picked, cut(weight, (place % 2) * cols, cols, 0)).reshape(
                    va, rows, cols
                )
                for weight in (proj_hidden, proj_embed)
            ]

        sends = [
            dim_b.swap(jnp.concatenate(products(b ^ r), axis=1).astype(BF16), r)
            for r in range(1, vb)
        ]
        kept = jnp.concatenate(products(b), axis=1)
        for got in sends:
            kept = kept + got.astype(F32)
        moved = final_move(halving_scatter(kept.astype(BF16), dim_a).astype(BF16))
        return moved.astype(F32)

    grad_final_gain = jnp.zeros((cols,), F32)
    proj_grads, backs = [], []
    for part in range(PARTS):
        span = slice(part * part_rows, (part + 1) * part_rows)
        scaled = collect(scaled_grad[span]).astype(F32)
        plain = cut(gathered[span], slot * cols, cols, 1).astype(F32) / final_gain
        grad_final_gain = grad_final_gain + jnp.sum(scaled * plain, axis=0)
        part_grad = (scaled * final_gain - plain * coefficient[span][:, None]).astype(BF16)
        proj_grads.append(part_grad)
        backs.append(back(part_grad))

    grad_head = contract_first(scaled_grad, gathered).astype(BF16)
    proj_grad = jnp.concatenate(proj_grads)
    wide_h, wide_e = contract_first(normed_h, proj_grad), contract_first(normed_e, proj_grad)
    grad_proj_hidden, grad_proj_embed = wide_h.astype(BF16), wide_e.astype(BF16)

    wide = proj_grad.astype(F32)
    dots = absolute(jnp.stack([jnp.sum(wide * half_h, axis=-1), jnp.sum(wide * half_e, axis=-1)]))
    dots = jnp.broadcast_to(dots.transpose(1, 0, 2)[:, None], (nc, nv, 2, block))
    gains = jnp.stack(
        [
            jnp.sum(wide_h * proj_hidden.astype(F32), axis=1),
            jnp.sum(wide_e * proj_embed.astype(F32), axis=1),
        ]
    )
    ratio = nv // nc
    gains = gains.reshape(2, ratio, cols).transpose(1, 0, 2)[None]
    holder = jnp.arange(nc, dtype=jnp.int32)[:, None, None, None] == own
    gains = jnp.where(holder, gains, F32(0.0)).reshape(nv, 2, cols)
    gains = jnp.broadcast_to(gains[None], (nc, nv, 2, cols))
    ends = jnp.concatenate([dots, gains], axis=-1).reshape(nc * nv, 2, block + cols)
    ends = jnp.sum(lax.all_to_all(ends, ("ctx", "vocab"), 0, 0, tiled=True), axis=0)

    def finish(kind, source, gain):
        back_all = jnp.concatenate([moved[kind * rows : (kind + 1) * rows] for moved in backs])
        scale = scales[kind][:, None]
        dot_all = ends[kind, :block][:, None]
        source = cut(source, slot * cols, cols, 1).astype(F32)
        gain = cut(gain, slot * cols, cols, 0)
        grad = scale * (back_all * gain) - source * (scale * scale) * (dot_all / width)
        return grad.astype(BF16), ends[kind, block:] / gain

    grad_hidden, grad_gain_hidden = finish(0, hidden_state, gain_hidden)
    grad_embed, grad_gain_embed = finish(1, embedded_next, gain_embed)
    return (
        mean_loss,
        grad_hidden,
        grad_embed,
        grad_gain_hidden,
        grad_gain_embed,
        grad_proj_hidden,
        grad_proj_embed,
        grad_final_gain,
        grad_head,
    )


def solution(mesh):
    in_specs = (
        P("ctx", None),
        P("ctx", None),
        P(),
        P(),
        P("ctx", "vocab"),
        P("ctx", "vocab"),
        P("vocab"),
        P(("ctx", "vocab"), None),
        P(),
        P(),
    )
    out_specs = (
        P(),
        P("ctx", "vocab"),
        P("ctx", "vocab"),
        P("vocab"),
        P("vocab"),
        P("ctx", "vocab"),
        P("ctx", "vocab"),
        P("vocab"),
        P(("ctx", "vocab"), None),
    )
    return jax.shard_map(local, mesh=mesh, in_specs=in_specs, out_specs=out_specs, check_vma=False)
```

time: 591 us -> 497 us (0.84)
  waiting for transfers between devices: 315 us -> 233 us
  blocking collectives: 38.2 us -> 0 us
  starting transfers between devices: 29.4 us -> 45.4 us
  local copies, waits for them, and re-layouts: 49.4 us -> 61.8 us
    reduce_scatter x1 -> x0, waiting for transfers between devices: 162 us -> none  [collect(): lax.psum_scatter(pieces, ('ctx', 'vocab'), scatter_dimension=0, tiled=False)]
    ppermute x18 -> x30, waiting for transfers between devices: 92.4 us -> 156 us  [move(): return lax.ppermute(value, self.axis, pairs)]
    all_gather x1 -> x0, blocking collectives: 31.8 us -> none  [local(): gain_all = lax.all_gather(final_gain, 'vocab', tiled=True)]
    unnamed x74 -> x119, local copies, waits for them, and re-layouts: 18.7 us -> 39.6 us
    all_gather x1, waiting for transfers between devices: 42.8 us -> 56.5 us  [local(): lax.all_gather((projected * final_gain).astype(BF16), ('ctx', 'vocab'))]
    ppermute x18 -> x30, starting transfers between devices: 10.2 us -> 21 us  [move(): return lax.ppermute(value, self.axis, pairs)]
    convert_element_type x4 -> x18, other arithmetic: 5.45 us -> 16.2 us  [the longest x2 4.44 us: collect(): mine = (mine.astype(F32) + core.swap(theirs, 1).astype(F32)).astype(BF16)]
    dynamic_slice x2 -> x0, local copies, waits for them, and re-layouts: 10.3 us -> none  [the longest x1 6.32 us: collect(): lax.dynamic_index_in_dim(partial, relative_place(index), 0, keepdims=False)]
  transfers between devices with their start and end apart: 24 -> 36, of which waited for: 15 -> 20; matrix products, arithmetic and copies ran while one was open for 13% -> 15% of each run, Pallas kernels for 0% -> 0%
where the time goes in v3:
time: 497 us; the launch traced here: 491 us
  waiting for transfers between devices  233 us (47%)
  matrix products  101 us (20%)
  local copies, waits for them, and re-layouts  61.8 us (12%)
  starting transfers between devices  45.4 us (9%)
  other arithmetic  31.3 us (6%)
  between operations  18 us (4%)
    ppermute x30, waiting for transfers between devices, move(): return lax.ppermute(value, self.axis, pairs)  156 us
    all_gather x1, waiting for transfers between devices, local(): lax.all_gather((projected * final_gain).astype(BF16), ('ctx', 'vocab'))  56.5 us
    unnamed x119, local copies, waits for them, and re-layouts  39.6 us
    dot_general x9, matrix products, contract_last(): lax.dot_general(left, right, (((1,), (1,)), ((), ())), preferred_element_...  35.9 us
    dot_general x4, matrix products, dot(): return jnp.dot(left, right, preferred_element_type=F32)  34.2 us
    dot_general x3, matrix products, contract_first(): lax.dot_general(left, right, (((0,), (0,)), ((), ())), preferred_element_...  31.2 us
    ppermute x30, starting transfers between devices, move(): return lax.ppermute(value, self.axis, pairs)  21 us
    ppermute x2, waiting for transfers between devices, final_move(): return lax.ppermute(value, ('ctx', 'vocab'), pairs)  13 us
  transfers between devices with their start and end apart: 36, of which 20 were waited for; matrix products, arithmetic and copies ran while one was open for 15% of the time, Pallas kernels for 0%

profile of v3, /device:TPU:2, one launch (start us, length us, event | category | flops | bytes accessed | tf_op | source)
XLA Modules:
  0.0 490.6 jit_solution(17323848790618706259)
XLA Ops:
  7.3 3.0 constant_dynamic-slice_fusion.28
  12.3 2.0 constant_dynamic-slice_fusion.25
  15.8 2.0 collective-permute-start
  18.6 1.8 dynamic-slice_dynamic-update-slice_fusion.3
  23.6 15.6 %collective-permute-done = bf16[128,3584]{1,0:T(8,128)(2,1)S(1)} collective-permute-done((bf16[128,3584]{1,0:T(8,128)(2,1)}, bf16[128,3584]{1,0:T(8,128)(2,1)S(1)}, u32[]{:S(2)}, u32[]{:S(2)}) %collective-permute-start) | collective-permute-done | bytes 917536 | tf_op jit(solution)/shard_map/ppermute | solution.py:26
  39.3 19.0 %collective-permute-done.5 = bf16[128,3584]{1,0:T(8,128)(2,1)} collective-permute-done((bf16[128,3584]{1,0:T(8,128)(2,1)}, bf16[128,3584]{1,0:T(8,128)(2,1)}, u32[]{:S(2)}, u32[]{:S(2)}) %collective-permute-start.5) | collective-permute-done | bytes 917536 | tf_op jit(solution)/shard_map/ppermute | solution.py:26
  67.6 2.1 fusion.48
  70.7 3.4 fusion.100
  76.2 1.8 collective-permute-start.9
  78.1 6.1 %collective-permute-done.9 = bf16[2,64,896]{2,1,0:T(8,128)(2,1)S(1)} collective-permute-done((bf16[2,64,896]{2,1,0:T(8,128)(2,1)S(1)}, bf16[2,64,896]{2,1,0:T(8,128)(2,1)S(1)}, u32[]{:S(2)}, u32[]{:S(2)}) %collective-permute-start.9) | collective-permute-done | bytes 229408 | tf_op jit(solution)/shard_map/ppermute | solution.py:26
  86.2 6.7 %all-to-all-start = ((f32[32,1,128]{2,1,0:T(1,128)}), f32[32,1,128]{2,1,0:T(1,128)S(1)}, u32[]{:S(2)}, u32[]{:S(2)}) async-start(f32[32,1,128]{2,1,0:T(1,128)} %broadcast_in_dim.185), calls=%async_computation | async-start | bytes 32768 | tf_op jit(solution)/shard_map/all_to_all | solution.py:179
  93.7 5.8 %copy.95 = bf16[1792,896]{0,1:T(8,128)(2,1)} copy(bf16[1792,896]{1,0:T(8,128)(2,1)} %param.14) | data formatting | bytes 6422528 | tf_op args[4]
  99.5 3.6 copy.96
  103.7 56.5 %all-gather.2.cloned.1.call-done = bf16[32,128,896]{2,1,0:T(8,128)(2,1)} async-done(((bf16[1,128,896]{2,1,0:T(8,128)(2,1)}), bf16[32,128,896]{2,1,0:T(8,128)(2,1)}) %all-gather.2.cloned.1.call-update) | async-done | bytes 7340048 | tf_op jit(solution)/shard_map/all_gather | solution.py:177
  160.2 4.0 dynamic-slice_bitcast_fusion
  167.6 23.9 %exponential_reduce_fusion = (f32[512]{0:T(512)S(1)}, f32[512]{0:T(512)S(1)}, f32[512]{0:T(512)S(1)}, f32[512,2048]{1,0:T(8,128)}) fusion(f32[512]{0:T(512)S(1)} %mul.441, s32[2048]{0:T(1024)S(1)} %iota_add_fusion, s32[512]{0:T(512)S(1)} %eq.109, bf16[512,7168]{1,0:T(8,128)(2,1)S(1)} %constant_dynamic-update-slice_fusion, bf16[2048,7168]{1,0:T(8,128)(2,1)} %param.17), kind=kOutput, calls=%fused_computation.12 | convolution fusion | flops 15040774144 | bytes 40912896 | tf_op jit(solution)/shard_map/dot_general | solution.py:68
  192.7 4.2 all-to-all-start.1
  196.9 7.5 %all-to-all-done.1 = f32[32,3,4,128]{3,2,1,0:T(4,128)S(1)} async-done(((f32[32,3,4,128]{3,2,1,0:T(4,128)}), f32[32,3,4,128]{3,2,1,0:T(4,128)S(1)}, u32[]{:S(2)}, u32[]{:S(2)}) %all-to-all-start.1) | async-done | bytes 196640 | tf_op jit(solution)/shard_map/all_to_all | solution.py:60
  205.0 3.2 fusion.3
  208.2 14.1 %convolution_convert_fusion.1 = bf16[256,7168]{1,0:T(8,128)(2,1)S(1)} fusion(bf16[2048,7168]{1,0:T(8,128)(2,1)} %param.17, bf16[512,2048]{1,0:T(8,128)(2,1)S(1)} %fusion.3), kind=kOutput, calls=%fused_computation.1 | convolution fusion | flops 7518027776 | bytes 34078720 | tf_op jit(solution)/shard_map/dot_general | solution.py:72
  222.3 14.7 %convolution_convert_fusion.2 = bf16[256,7168]{1,0:T(8,128)(2,1)S(1)} fusion(bf16[2048,7168]{1,0:T(8,128)(2,1)} %param.17, bf16[512,2048]{1,0:T(8,128)(2,1)S(1)} %fusion.3), kind=kOutput, calls=%fused_computation.2 | convolution fusion | flops 7518027776 | bytes 34078720 | tf_op jit(solution)/shard_map/dot_general | solution.py:72
  240.5 23.3 %convolution_convert_fusion = bf16[2048,7168]{1,0:T(8,128)(2,1)} fusion(bf16[512,2048]{1,0:T(8,128)(2,1)} %copy-done.18, bf16[512,7168]{1,0:T(8,128)(2,1)} %copy-done.35), kind=kOutput, calls=%fused_computation | convolution fusion | flops 15047065600 | bytes 38797312 | tf_op jit(solution)/shard_map/dot_general | solution.py:64
  263.7 2.5 add_convert_fusion
  267.3 1.9 add_convert_fusion.1
  270.5 19.0 %collective-permute-done.22 = bf16[64,7168]{1,0:T(8,128)(2,1)S(1)} collective-permute-done((bf16[64,7168]{1,0:T(8,128)(2,1)S(1)}, bf16[64,7168]{1,0:T(8,128)(2,1)S(1)}, u32[]{:S(2)}, u32[]{:S(2)}) %collective-permute-start.22) | collective-permute-done | bytes 917536 | tf_op jit(solution)/shard_map/ppermute | solution.py:26
  291.2 17.6 %collective-permute-done.11 = bf16[64,7168]{1,0:T(8,128)(2,1)S(1)} collective-permute-done((bf16[64,7168]{1,0:T(8,128)(2,1)S(1)}, bf16[64,7168]{1,0:T(8,128)(2,1)S(1)}, u32[]{:S(2)}, u32[]{:S(2)}) %collective-permute-start.11) | collective-permute-done | bytes 917536 | tf_op jit(solution)/shard_map/ppermute | solution.py:26
  310.6 10.8 %collective-permute-done.12 = bf16[4,64,896]{2,1,0:T(8,128)(2,1)S(1)} collective-permute-done((bf16[4,64,896]{2,1,0:T(8,128)(2,1)S(1)}, bf16[4,64,896]{2,1,0:T(8,128)(2,1)S(1)}, u32[]{:S(2)}, u32[]{:S(2)}) %collective-permute-start.12) | collective-permute-done | bytes 458784 | tf_op jit(solution)/shard_map/ppermute | solution.py:26
  323.4 7.1 %collective-permute-done.13 = bf16[2,64,896]{2,1,0:T(8,128)(2,1)S(1)} collective-permute-done((bf16[2,64,896]{2,1,0:T(8,128)(2,1)S(1)}, bf16[2,64,896]{2,1,0:T(8,128)(2,1)S(1)}, u32[]{:S(2)}, u32[]{:S(2)}) %collective-permute-start.13) | collective-permute-done | bytes 229408 | tf_op jit(solution)/shard_map/ppermute | solution.py:26
  330.8 6.1 %collective-permute-done.14 = bf16[1,64,896]{2,1,0:T(8,128)(2,1)S(1)} collective-permute-done((bf16[1,64,896]{2,1,0:T(8,128)(2,1)S(1)}, bf16[1,64,896]{2,1,0:T(8,128)(2,1)S(1)}, u32[]{:S(2)}, u32[]{:S(2)}) %collective-permute-start.14) | collective-permute-done | bytes 114720 | tf_op jit(solution)/shard_map/ppermute | solution.py:26
  338.1 3.7 collective-permute-done.15
  359.0 4.0 fusion.95
  363.0 4.0 fusion.96
  367.0 5.6 %copy.98 = bf16[1792,896]{1,0:T(8,128)(2,1)} copy(bf16[1792,896]{0,1:T(8,128)(2,1)} %get-tuple-element.97) | data formatting | bytes 6422528
  372.6 5.8 %copy.99 = bf16[1792,896]{1,0:T(8,128)(2,1)} copy(bf16[1792,896]{0,1:T(8,128)(2,1)} %get-tuple-element.95) | data formatting | bytes 6422528
  379.8 2.7 all-to-all-start.2
  382.6 2.3 pad_maximum_fusion
  390.8 1.7 fusion.20
  397.8 11.4 %collective-permute-done.17 = bf16[4,128,896]{2,1,0:T(8,128)(2,1)} collective-permute-done((bf16[4,128,896]{2,1,0:T(8,128)(2,1)}, bf16[4,128,896]{2,1,0:T(8,128)(2,1)}, u32[]{:S(2)}, u32[]{:S(2)}) %collective-permute-start.17) | collective-permute-done | bytes 917536 | tf_op jit(solution)/shard_map/ppermute | solution.py:26
  412.1 16.2 %collective-permute-done.28 = bf16[4,128,896]{2,1,0:T(8,128)(2,1)} collective-permute-done((bf16[4,128,896]{2,1,0:T(8,128)(2,1)}, bf16[4,128,896]{2,1,0:T(8,128)(2,1)}, u32[]{:S(2)}, u32[]{:S(2)}) %collective-permute-start.28) | collective-permute-done | bytes 917536 | tf_op jit(solution)/shard_map/ppermute | solution.py:26
  431.4 2.2 collective-permute-start.19
  433.5 13.2 %collective-permute-done.29 = bf16[2,128,896]{2,1,0:T(8,128)(2,1)S(1)} collective-permute-done((bf16[2,128,896]{2,1,0:T(8,128)(2,1)S(1)}, bf16[2,128,896]{2,1,0:T(8,128)(2,1)S(1)}, u32[]{:S(2)}, u32[]{:S(2)}) %collective-permute-start.29) | collective-permute-done | bytes 458784 | tf_op jit(solution)/shard_map/ppermute | solution.py:26
  448.0 4.0 collective-permute-start.20
  452.0 6.8 %collective-permute-done.30 = bf16[1,128,896]{2,1,0:T(8,128)(2,1)S(1)} collective-permute-done((bf16[1,128,896]{2,1,0:T(8,128)(2,1)S(1)}, bf16[1,128,896]{2,1,0:T(8,128)(2,1)S(1)}, u32[]{:S(2)}, u32[]{:S(2)}) %collective-permute-start.30) | collective-permute-done | bytes 229408 | tf_op jit(solution)/shard_map/ppermute | solution.py:26
  458.9 6.8 %collective-permute-start.31 = (bf16[128,896]{1,0:T(8,128)(2,1)S(1)}, bf16[128,896]{1,0:T(8,128)(2,1)S(1)}, u32[]{:S(2)}, u32[]{:S(2)}) collective-permute-start(bf16[128,896]{1,0:T(8,128)(2,1)S(1)} %fusion.65), channel_id=1, source_target_pairs={{0,0},{1,1},{2,8},{3,9},{4,16},{5,17},{6,24},{7,25},{8,2},{9,3},{1... | collective-permute-start | bytes 688136 | tf_op jit(solution)/shard_map/ppermute | solution.py:243
  465.7 8.3 %collective-permute-done.20 = bf16[128,896]{1,0:T(8,128)(2,1)S(1)} collective-permute-done((bf16[128,896]{1,0:T(8,128)(2,1)S(1)}, bf16[128,896]{1,0:T(8,128)(2,1)S(1)}, u32[]{:S(2)}, u32[]{:S(2)}) %collective-permute-start.20) | collective-permute-done | bytes 229408 | tf_op jit(solution)/shard_map/ppermute | solution.py:243
  474.0 4.7 collective-permute-done.31
  478.7 1.8 fusion.59
  480.5 1.8 fusion.62
  (301 shorter events, 76.3 us)
Async XLA Ops:
  7.2 153.0 %all-gather.2.cloned.1.call-start = ((), (), s32[]{:S(2)}) async-start(), calls=%async_computation.3 | async-start | bytes 7569408 | tf_op jit(solution)/shard_map/all_gather | solution.py:177
  12.2 9.8 %collective-permute-start.3 = (f32[2,128]{1,0:T(2,128)S(1)}, f32[2,128]{1,0:T(2,128)S(1)}, u32[]{:S(2)}, u32[]{:S(2)}) collective-permute-start(f32[2,128]{1,0:T(2,128)S(1)} %fusion.77), channel_id=1, source_target_pairs={{0,16},{8,24},{16,0},{24,8},{1,17},{9,25},{17,1},{25,9},{2,18},{10... | collective-permute-start | bytes 3080 | tf_op jit(solution)/shard_map/ppermute | solution.py:26
  14.3 47.5 %collective-permute-start.6 = (bf16[128,1792]{1,0:T(8,128)(2,1)}, bf16[128,1792]{1,0:T(8,128)(2,1)}, u32[]{:S(2)}, u32[]{:S(2)}) collective-permute-start(bf16[128,1792]{1,0:T(8,128)(2,1)} %constant_dynamic-slice_fusion.25), channel_id=1, source_target_pairs={{0,8},{8,0},{16,24},{24,16},{1,9},{9,1},{17,25},{25,17},{2,10},{10... | collective-permute-start | bytes 1376264 | tf_op jit(solution)/shard_map/ppermute | solution.py:26
  15.3 45.8 %collective-permute-start.1 = (bf16[128,1792]{1,0:T(8,128)(2,1)}, bf16[128,1792]{1,0:T(8,128)(2,1)S(1)}, u32[]{:S(2)}, u32[]{:S(2)}) collective-permute-start(bf16[128,1792]{1,0:T(8,128)(2,1)} %constant_dynamic-slice_fusion.27), channel_id=1, source_target_pairs={{0,8},{8,0},{16,24},{24,16},{1,9},{9,1},{17,25},{25,17},{2,10},{10... | collective-permute-start | bytes 1376264 | tf_op jit(solution)/shard_map/ppermute | solution.py:26
  15.8 23.4 %collective-permute-start = (bf16[128,3584]{1,0:T(8,128)(2,1)}, bf16[128,3584]{1,0:T(8,128)(2,1)S(1)}, u32[]{:S(2)}, u32[]{:S(2)}) collective-permute-start(bf16[128,3584]{1,0:T(8,128)(2,1)} %get-tuple-element.14), channel_id=1, source_target_pairs={{0,16},{8,24},{16,0},{24,8},{1,17},{9,25},{17,1},{25,9},{2,18},{10... | collective-permute-start | bytes 2752520 | tf_op jit(solution)/shard_map/ppermute | solution.py:26
  17.8 40.5 %collective-permute-start.5 = (bf16[128,3584]{1,0:T(8,128)(2,1)}, bf16[128,3584]{1,0:T(8,128)(2,1)}, u32[]{:S(2)}, u32[]{:S(2)}) collective-permute-start(bf16[128,3584]{1,0:T(8,128)(2,1)} %get-tuple-element.16), channel_id=1, source_target_pairs={{0,16},{8,24},{16,0},{24,8},{1,17},{9,25},{17,1},{25,9},{2,18},{10... | collective-permute-start | bytes 2752520 | tf_op jit(solution)/shard_map/ppermute | solution.py:26
  22.1 1.2 collective-permute-start.4
  23.6 36.6 %copy-start.37 = (bf16[512,1792]{1,0:T(8,128)(2,1)S(1)}, bf16[512,1792]{1,0:T(8,128)(2,1)}, u32[]{:S(2)}) copy-start(bf16[512,1792]{1,0:T(8,128)(2,1)} %dynamic-slice_dynamic-update-slice_fusion.3) | copy-start | bytes 5505028
  39.2 23.7 %collective-permute-start.2 = (bf16[128,1792]{1,0:T(8,128)(2,1)S(1)}, bf16[128,1792]{1,0:T(8,128)(2,1)S(1)}, u32[]{:S(2)}, u32[]{:S(2)}) collective-permute-start(bf16[128,1792]{1,0:T(8,128)(2,1)S(1)} %constant_dynamic-slice_fusion.26), channel_id=1, source_target_pairs={{0,8},{8,0},{16,24},{24,16},{1,9},{9,1},{17,25},{25,17},{2,10},{10... | collective-permute-start | bytes 1376264 | tf_op jit(solution)/shard_map/ppermute | solution.py:26
  59.3 5.1 %collective-permute-start.7 = (bf16[128,1792]{1,0:T(8,128)(2,1)S(1)}, bf16[128,1792]{1,0:T(8,128)(2,1)S(1)}, u32[]{:S(2)}, u32[]{:S(2)}) collective-permute-start(bf16[128,1792]{1,0:T(8,128)(2,1)S(1)} %constant_dynamic-slice_fusion.24), channel_id=1, source_target_pairs={{0,8},{8,0},{16,24},{24,16},{1,9},{9,1},{17,25},{25,17},{2,10},{10... | collective-permute-start | bytes 1376264 | tf_op jit(solution)/shard_map/ppermute | solution.py:26
  74.1 10.3 %copy-start.36 = (f32[896]{0:T(1024)S(1)}, f32[896]{0:T(1024)}, u32[]{:S(2)}) copy-start(f32[896]{0:T(1024)} %param.16) | copy-start | bytes 10756
  74.1 2.0 collective-permute-start.8
  76.2 9.0 %copy-start.44 = (s32[512]{0:T(512)S(1)}, s32[512]{0:T(512)}, u32[]{:S(2)}) copy-start(s32[512]{0:T(512)} %param.18) | copy-start | bytes 6148
  76.2 8.0 %collective-permute-start.9 = (bf16[2,64,896]{2,1,0:T(8,128)(2,1)S(1)}, bf16[2,64,896]{2,1,0:T(8,128)(2,1)S(1)}, u32[]{:S(2)}, u32[]{:S(2)}) collective-permute-start(bf16[2,64,896]{2,1,0:T(8,128)(2,1)S(1)} %fusion.66), channel_id=1, source_target_pairs={{0,16},{8,24},{16,0},{24,8},{1,17},{9,25},{17,1},{25,9},{2,18},{10... | collective-permute-start | bytes 688136 | tf_op jit(solution)/shard_map/ppermute | solution.py:26
  86.2 17.2 %all-to-all-start = ((f32[32,1,128]{2,1,0:T(1,128)}), f32[32,1,128]{2,1,0:T(1,128)S(1)}, u32[]{:S(2)}, u32[]{:S(2)}) async-start(f32[32,1,128]{2,1,0:T(1,128)} %broadcast_in_dim.185), calls=%async_computation | async-start | bytes 32768 | tf_op jit(solution)/shard_map/all_to_all | solution.py:179
  167.6 24.0 %copy-start.35 = (bf16[512,7168]{1,0:T(8,128)(2,1)}, bf16[512,7168]{1,0:T(8,128)(2,1)S(1)}, u32[]{:S(2)}) copy-start(bf16[512,7168]{1,0:T(8,128)(2,1)S(1)} %constant_dynamic-update-slice_fusion) | copy-start | bytes 22020100
  192.7 11.7 %all-to-all-start.1 = ((f32[32,3,4,128]{3,2,1,0:T(4,128)}), f32[32,3,4,128]{3,2,1,0:T(4,128)S(1)}, u32[]{:S(2)}, u32[]{:S(2)}) async-start(f32[32,3,4,128]{3,2,1,0:T(4,128)} %broadcast_in_dim.195), calls=%async_computation.1 | async-start | bytes 393216 | tf_op jit(solution)/shard_map/all_to_all | solution.py:60
  208.2 14.1 %copy-start.18 = (bf16[512,2048]{1,0:T(8,128)(2,1)}, bf16[512,2048]{1,0:T(8,128)(2,1)S(1)}, u32[]{:S(2)}) copy-start(bf16[512,2048]{1,0:T(8,128)(2,1)S(1)} %fusion.3) | copy-start | bytes 6291460
  222.3 14.7 %copy-start.9 = (bf16[256,7168]{1,0:T(8,128)(2,1)}, bf16[256,7168]{1,0:T(8,128)(2,1)S(1)}, u32[]{:S(2)}) copy-start(bf16[256,7168]{1,0:T(8,128)(2,1)S(1)} %convolution_convert_fusion.1) | copy-start | bytes 11010052
  238.4 25.4 %collective-permute-start.21 = (bf16[128,7168]{1,0:T(8,128)(2,1)}, bf16[128,7168]{1,0:T(8,128)(2,1)}, u32[]{:S(2)}, u32[]{:S(2)}) collective-permute-start(bf16[128,7168]{1,0:T(8,128)(2,1)} %slice.481), channel_id=1, source_target_pairs={{0,8},{8,0},{16,24},{24,16},{1,9},{9,1},{17,25},{25,17},{2,10},{10... | collective-permute-start | bytes 5505032 | tf_op jit(solution)/shard_map/ppermute | solution.py:26
  240.5 26.8 %collective-permute-start.10 = (bf16[128,7168]{1,0:T(8,128)(2,1)}, bf16[128,7168]{1,0:T(8,128)(2,1)}, u32[]{:S(2)}, u32[]{:S(2)}) collective-permute-start(bf16[128,7168]{1,0:T(8,128)(2,1)} %slice.470), channel_id=1, source_target_pairs={{0,8},{8,0},{16,24},{24,16},{1,9},{9,1},{17,25},{25,17},{2,10},{10... | collective-permute-start | bytes 5505032 | tf_op jit(solution)/shard_map/ppermute | solution.py:26
  266.3 23.2 %collective-permute-start.22 = (bf16[64,7168]{1,0:T(8,128)(2,1)S(1)}, bf16[64,7168]{1,0:T(8,128)(2,1)S(1)}, u32[]{:S(2)}, u32[]{:S(2)}) collective-permute-start(bf16[64,7168]{1,0:T(8,128)(2,1)S(1)} %slice.483), channel_id=1, source_target_pairs={{0,16},{8,24},{16,0},{24,8},{1,17},{9,25},{17,1},{25,9},{2,18},{10... | collective-permute-start | bytes 2752520 | tf_op jit(solution)/shard_map/ppermute | solution.py:26
  269.3 39.5 %collective-permute-start.11 = (bf16[64,7168]{1,0:T(8,128)(2,1)S(1)}, bf16[64,7168]{1,0:T(8,128)(2,1)S(1)}, u32[]{:S(2)}, u32[]{:S(2)}) collective-permute-start(bf16[64,7168]{1,0:T(8,128)(2,1)S(1)} %slice.472), channel_id=1, source_target_pairs={{0,16},{8,24},{16,0},{24,8},{1,17},{9,25},{17,1},{25,9},{2,18},{10... | collective-permute-start | bytes 2752520 | tf_op jit(solution)/shard_map/ppermute | solution.py:26
  289.9 20.1 %collective-permute-start.23 = (bf16[4,64,896]{2,1,0:T(8,128)(2,1)S(1)}, bf16[4,64,896]{2,1,0:T(8,128)(2,1)S(1)}, u32[]{:S(2)}, u32[]{:S(2)}) collective-permute-start(bf16[4,64,896]{2,1,0:T(8,128)(2,1)S(1)} %pad_maximum_fusion.8), channel_id=1, source_target_pairs={{0,1},{1,0},{2,3},{3,2},{4,5},{5,4},{6,7},{7,6},{8,9},{9,8},{10,11... | collective-permute-start | bytes 1376264 | tf_op jit(solution)/shard_map/ppermute | solution.py:26
  309.2 12.2 %collective-permute-start.12 = (bf16[4,64,896]{2,1,0:T(8,128)(2,1)S(1)}, bf16[4,64,896]{2,1,0:T(8,128)(2,1)S(1)}, u32[]{:S(2)}, u32[]{:S(2)}) collective-permute-start(bf16[4,64,896]{2,1,0:T(8,128)(2,1)S(1)} %pad_maximum_fusion.3), channel_id=1, source_target_pairs={{0,1},{1,0},{2,3},{3,2},{4,5},{5,4},{6,7},{7,6},{8,9},{9,8},{10,11... | collective-permute-start | bytes 1376264 | tf_op jit(solution)/shard_map/ppermute | solution.py:26
  310.2 11.6 %collective-permute-start.24 = (bf16[2,64,896]{2,1,0:T(8,128)(2,1)S(1)}, bf16[2,64,896]{2,1,0:T(8,128)(2,1)S(1)}, u32[]{:S(2)}, u32[]{:S(2)}) collective-permute-start(bf16[2,64,896]{2,1,0:T(8,128)(2,1)S(1)} %pad_maximum_fusion.16), channel_id=1, source_target_pairs={{0,2},{1,3},{2,0},{3,1},{4,6},{5,7},{6,4},{7,5},{8,10},{9,11},{10,... | collective-permute-start | bytes 688136 | tf_op jit(solution)/shard_map/ppermute | solution.py:26
  321.6 8.9 %collective-permute-start.13 = (bf16[2,64,896]{2,1,0:T(8,128)(2,1)S(1)}, bf16[2,64,896]{2,1,0:T(8,128)(2,1)S(1)}, u32[]{:S(2)}, u32[]{:S(2)}) collective-permute-start(bf16[2,64,896]{2,1,0:T(8,128)(2,1)S(1)} %pad_maximum_fusion.14), channel_id=1, source_target_pairs={{0,2},{1,3},{2,0},{3,1},{4,6},{5,7},{6,4},{7,5},{8,10},{9,11},{10,... | collective-permute-start | bytes 688136 | tf_op jit(solution)/shard_map/ppermute | solution.py:26
  321.9 8.7 %collective-permute-start.25 = (bf16[1,64,896]{2,1,0:T(8,128)(2,1)S(1)}, bf16[1,64,896]{2,1,0:T(8,128)(2,1)S(1)}, u32[]{:S(2)}, u32[]{:S(2)}) collective-permute-start(bf16[1,64,896]{2,1,0:T(8,128)(2,1)S(1)} %add_convert_fusion.13), channel_id=1, source_target_pairs={{0,4},{1,5},{2,6},{3,7},{4,0},{5,1},{6,2},{7,3},{8,12},{9,13},{10,... | collective-permute-start | bytes 344072 | tf_op jit(solution)/shard_map/ppermute | solution.py:26
  330.5 6.4 %collective-permute-start.14 = (bf16[1,64,896]{2,1,0:T(8,128)(2,1)S(1)}, bf16[1,64,896]{2,1,0:T(8,128)(2,1)S(1)}, u32[]{:S(2)}, u32[]{:S(2)}) collective-permute-start(bf16[1,64,896]{2,1,0:T(8,128)(2,1)S(1)} %add_convert_fusion.16), channel_id=1, source_target_pairs={{0,4},{1,5},{2,6},{3,7},{4,0},{5,1},{6,2},{7,3},{8,12},{9,13},{10,... | collective-permute-start | bytes 344072 | tf_op jit(solution)/shard_map/ppermute | solution.py:26
  330.7 6.7 %collective-permute-start.26 = (bf16[64,896]{1,0:T(8,128)(2,1)S(1)}, bf16[64,896]{1,0:T(8,128)(2,1)S(1)}, u32[]{:S(2)}, u32[]{:S(2)}) collective-permute-start(bf16[64,896]{1,0:T(8,128)(2,1)S(1)} %bitcast.228), channel_id=1, source_target_pairs={{0,16},{8,24},{16,0},{24,8},{1,17},{9,25},{17,1},{25,9},{2,18},{10... | collective-permute-start | bytes 344072 | tf_op jit(solution)/shard_map/ppermute | solution.py:26
  337.0 4.9 collective-permute-start.15
  338.1 5.7 %collective-permute-start.27 = (bf16[2,64,896]{2,1,0:T(8,128)(2,1)}, bf16[2,64,896]{2,1,0:T(8,128)(2,1)S(1)}, u32[]{:S(2)}, u32[]{:S(2)}) collective-permute-start(bf16[2,64,896]{2,1,0:T(8,128)(2,1)} %pad_maximum_fusion.17), channel_id=1, source_target_pairs={{0,8},{8,0},{16,24},{24,16},{1,9},{9,1},{17,25},{25,17},{2,10},{10... | collective-permute-start | bytes 688136 | tf_op jit(solution)/shard_map/ppermute | solution.py:26
  342.5 1.8 collective-permute-start.16
  379.8 15.1 %all-to-all-start.2 = ((f32[32,2,1024]{2,1,0:T(2,128)}), f32[32,2,1024]{2,1,0:T(2,128)S(1)}, u32[]{:S(2)}, u32[]{:S(2)}) async-start(f32[32,2,1024]{2,1,0:T(2,128)} %bitcast.227), calls=%async_computation.2 | async-start | bytes 524288 | tf_op jit(solution)/shard_map/all_to_all | solution.py:301
  382.5 6.0 %copy-start.27 = (bf16[64,896]{1,0:T(8,128)(2,1)S(1)}, bf16[64,896]{1,0:T(8,128)(2,1)}, u32[]{:S(2)}) copy-start(bf16[64,896]{1,0:T(8,128)(2,1)} %get-tuple-element.139) | copy-start | bytes 344068
  382.5 6.0 %copy-start.28 = (bf16[64,896]{1,0:T(8,128)(2,1)S(1)}, bf16[64,896]{1,0:T(8,128)(2,1)}, u32[]{:S(2)}) copy-start(bf16[64,896]{1,0:T(8,128)(2,1)} %get-tuple-element.140) | copy-start | bytes 344068
  382.5 6.0 %copy-start.29 = (bf16[64,896]{1,0:T(8,128)(2,1)S(1)}, bf16[64,896]{1,0:T(8,128)(2,1)}, u32[]{:S(2)}) copy-start(bf16[64,896]{1,0:T(8,128)(2,1)} %get-tuple-element.141) | copy-start | bytes 344068
  384.8 24.4 %collective-permute-start.17 = (bf16[4,128,896]{2,1,0:T(8,128)(2,1)}, bf16[4,128,896]{2,1,0:T(8,128)(2,1)}, u32[]{:S(2)}, u32[]{:S(2)}) collective-permute-start(bf16[4,128,896]{2,1,0:T(8,128)(2,1)} %pad_maximum_fusion), channel_id=1, source_target_pairs={{0,1},{1,0},{2,3},{3,2},{4,5},{5,4},{6,7},{7,6},{8,9},{9,8},{10,11... | collective-permute-start | bytes 2752520 | tf_op jit(solution)/shard_map/ppermute | solution.py:26
  387.3 40.9 %collective-permute-start.28 = (bf16[4,128,896]{2,1,0:T(8,128)(2,1)}, bf16[4,128,896]{2,1,0:T(8,128)(2,1)}, u32[]{:S(2)}, u32[]{:S(2)}) collective-permute-start(bf16[4,128,896]{2,1,0:T(8,128)(2,1)} %pad_maximum_fusion.1), channel_id=1, source_target_pairs={{0,1},{1,0},{2,3},{3,2},{4,5},{5,4},{6,7},{7,6},{8,9},{9,8},{10,11... | collective-permute-start | bytes 2752520 | tf_op jit(solution)/shard_map/ppermute | solution.py:26
  394.2 15.0 %copy-start.24 = (f32[256,896]{1,0:T(8,128)S(1)}, f32[256,896]{1,0:T(8,128)}, u32[]{:S(2)}) copy-start(f32[256,896]{1,0:T(8,128)} %fusion.18) | copy-start | bytes 2752516
  410.6 17.7 %copy-start.22 = (f32[256,896]{1,0:T(8,128)S(1)}, f32[256,896]{1,0:T(8,128)}, u32[]{:S(2)}) copy-start(f32[256,896]{1,0:T(8,128)} %fusion.16) | copy-start | bytes 2752516
  410.6 17.7 %copy-start.23 = (f32[256,896]{1,0:T(8,128)S(1)}, f32[256,896]{1,0:T(8,128)}, u32[]{:S(2)}) copy-start(f32[256,896]{1,0:T(8,128)} %fusion.20) | copy-start | bytes 2752516
  410.7 20.6 %collective-permute-start.18 = (bf16[2,128,896]{2,1,0:T(8,128)(2,1)S(1)}, bf16[2,128,896]{2,1,0:T(8,128)(2,1)S(1)}, u32[]{:S(2)}, u32[]{:S(2)}) collective-permute-start(bf16[2,128,896]{2,1,0:T(8,128)(2,1)S(1)} %pad_maximum_fusion.7), channel_id=1, source_target_pairs={{0,2},{1,3},{2,0},{3,1},{4,6},{5,7},{6,4},{7,5},{8,10},{9,11},{10,... | collective-permute-start | bytes 1376264 | tf_op jit(solution)/shard_map/ppermute | solution.py:26
  429.8 16.9 %collective-permute-start.29 = (bf16[2,128,896]{2,1,0:T(8,128)(2,1)S(1)}, bf16[2,128,896]{2,1,0:T(8,128)(2,1)S(1)}, u32[]{:S(2)}, u32[]{:S(2)}) collective-permute-start(bf16[2,128,896]{2,1,0:T(8,128)(2,1)S(1)} %pad_maximum_fusion.12), channel_id=1, source_target_pairs={{0,2},{1,3},{2,0},{3,1},{4,6},{5,7},{6,4},{7,5},{8,10},{9,11},{10,... | collective-permute-start | bytes 1376264 | tf_op jit(solution)/shard_map/ppermute | solution.py:26
  431.4 16.5 %collective-permute-start.19 = (bf16[1,128,896]{2,1,0:T(8,128)(2,1)S(1)}, bf16[1,128,896]{2,1,0:T(8,128)(2,1)S(1)}, u32[]{:S(2)}, u32[]{:S(2)}) collective-permute-start(bf16[1,128,896]{2,1,0:T(8,128)(2,1)S(1)} %add_convert_fusion.10), channel_id=1, source_target_pairs={{0,4},{1,5},{2,6},{3,7},{4,0},{5,1},{6,2},{7,3},{8,12},{9,13},{10,... | collective-permute-start | bytes 688136 | tf_op jit(solution)/shard_map/ppermute | solution.py:26
  446.8 12.0 %collective-permute-start.30 = (bf16[1,128,896]{2,1,0:T(8,128)(2,1)S(1)}, bf16[1,128,896]{2,1,0:T(8,128)(2,1)S(1)}, u32[]{:S(2)}, u32[]{:S(2)}) collective-permute-start(bf16[1,128,896]{2,1,0:T(8,128)(2,1)S(1)} %add_convert_fusion.8), channel_id=1, source_target_pairs={{0,4},{1,5},{2,6},{3,7},{4,0},{5,1},{6,2},{7,3},{8,12},{9,13},{10,... | collective-permute-start | bytes 688136 | tf_op jit(solution)/shard_map/ppermute | solution.py:26
  448.0 26.0 %collective-permute-start.20 = (bf16[128,896]{1,0:T(8,128)(2,1)S(1)}, bf16[128,896]{1,0:T(8,128)(2,1)S(1)}, u32[]{:S(2)}, u32[]{:S(2)}) collective-permute-start(bf16[128,896]{1,0:T(8,128)(2,1)S(1)} %fusion.64), channel_id=1, source_target_pairs={{0,0},{1,1},{2,8},{3,9},{4,16},{5,17},{6,24},{7,25},{8,2},{9,3},{1... | collective-permute-start | bytes 688136 | tf_op jit(solution)/shard_map/ppermute | solution.py:243
  458.9 19.8 %collective-permute-start.31 = (bf16[128,896]{1,0:T(8,128)(2,1)S(1)}, bf16[128,896]{1,0:T(8,128)(2,1)S(1)}, u32[]{:S(2)}, u32[]{:S(2)}) collective-permute-start(bf16[128,896]{1,0:T(8,128)(2,1)S(1)} %fusion.65), channel_id=1, source_target_pairs={{0,0},{1,1},{2,8},{3,9},{4,16},{5,17},{6,24},{7,25},{8,2},{9,3},{1... | collective-permute-start | bytes 688136 | tf_op jit(solution)/shard_map/ppermute | solution.py:243
  (33 other events, 91.5 us)
Sparse Core Ops, SparseCore 0:
  85.2 74.9 all-gather.1

commit v4 on v3

--- a/solution.py
+++ b/solution.py
@@ -1,6 +1,8 @@
 import jax
 import jax.numpy as jnp
 from jax import lax
+from jax.experimental import pallas as pl
+from jax.experimental.pallas import tpu as pltpu
 from jax.sharding import PartitionSpec as P
 
 EPSILON = 1e-06
@@ -66,6 +68,149 @@
 
 def contract_last(left, right):
     return lax.dot_general(left, right, (((1,), (1,)), ((), ())), preferred_element_type=F32)
+
+
+def whole_block(shape):
+    return pl.BlockSpec(shape, lambda *step: (0,) * len(shape), pipeline_mode=pl.Buffered(1))
+
+
+def kernel_call(body, grid, in_specs, out_specs, out_shape, flops, moved, exps=0):
+    return pl.pallas_call(
+        body,
+        grid=grid,
+        in_specs=in_specs,
+        out_specs=out_specs,
+        out_shape=out_shape,
+        compiler_params=pltpu.CompilerParams(vmem_limit_bytes=48 * 1024 * 1024),
+        cost_estimate=pl.CostEstimate(flops=flops, bytes_accessed=moved, transcendentals=exps),
+    )
+
+
+def logits_with_sums(rows_all, head, row_scale, target):
+    tokens, width = rows_all.shape
+    entries = head.shape[0]
+    tile = 256
+
+    def body(rows_ref, head_ref, scale_ref, target_ref, logits_ref, sums_ref):
+        step = pl.program_id(0)
+        logits = contract_last(rows_ref[...], head_ref[...]) * scale_ref[...]
+        logits_ref[...] = logits
+        power = jnp.exp(logits)
+        ids = lax.broadcasted_iota(jnp.int32, logits.shape, 1) + step * tile
+        chosen = jnp.where(ids == target_ref[...], logits, 0.0)
+        terms = (power, power * (logits * F32(1.0 / 256.0)), chosen)
+
+        @pl.when(step == 0)
+        def _():
+            sums_ref[...] = jnp.zeros_like(sums_ref)
+
+        for index, term in enumerate(terms):
+            folded = term[:, :128]
+            for lane in range(128, tile, 128):
+                folded = folded + term[:, lane : lane + 128]
+            sums_ref[index] += folded
+
+    return kernel_call(
+        body,
+        (entries // tile,),
+        [
+            whole_block((tokens, width)),
+            pl.BlockSpec((tile, width), lambda step: (step, 0)),
+            whole_block((tokens, 1)),
+            whole_block((tokens, 1)),
+        ],
+        [
+            pl.BlockSpec((tokens, tile), lambda step: (0, step)),
+            pl.BlockSpec((3, tokens, 128), lambda step: (0, 0, 0)),
+        ],
+        [
+            jax.ShapeDtypeStruct((tokens, entries), F32),
+            jax.ShapeDtypeStruct((3, tokens, 128), F32),
+        ],
+        2 * tokens * width * entries,
+        2 * entries * width + 2 * tokens * width + 4 * tokens * entries,
+        tokens * entries,
+    )(rows_all, head, row_scale[:, None], target[:, None])
+
+
+def times_head(grad, head):
+    tokens, entries = grad.shape
+    width = head.shape[1]
+    tile = 512
+
+    def body(grad_ref, head_ref, out_ref):
+        out_ref[...] = dot(grad_ref[...], head_ref[...]).astype(BF16)
+
+    return kernel_call(
+        body,
+        (width // tile,),
+        [whole_block((tokens, entries)), pl.BlockSpec((entries, tile), lambda step: (0, step))],
+        pl.BlockSpec((tokens, tile), lambda step: (0, step)),
+        jax.ShapeDtypeStruct((tokens, width), BF16),
+        2 * tokens * width * entries,
+        2 * entries * width + 2 * tokens * width + 2 * tokens * entries,
+    )(grad, head)
+
+
+def head_gradient(grads, rows_all, after):
+    tokens, entries = grads[0].shape
+    width = rows_all[0].shape[1]
+    tile, chunk = 256, 1024
+    parts = len(grads)
+
+    def body(*refs):
+        grad_refs, row_refs, out_ref = refs[:parts], refs[parts : 2 * parts], refs[-1]
+        for start in range(0, width, chunk):
+            total = None
+            for grad_ref, row_ref in zip(grad_refs, row_refs):
+                term = contract_first(grad_ref[...], row_ref[:, start : start + chunk])
+                total = term if total is None else total + term
+            out_ref[:, start : start + chunk] = total.astype(BF16)
+
+    return kernel_call(
+        body,
+        (entries // tile,),
+        [pl.BlockSpec((tokens, tile), lambda step: (0, step))] * parts
+        + [whole_block((tokens, width))] * parts
+        + [pl.BlockSpec(memory_space=pl.ANY)] * len(after),
+        pl.BlockSpec((tile, width), lambda step: (step, 0)),
+        jax.ShapeDtypeStruct((entries, width), BF16),
+        2 * parts * tokens * width * entries,
+        2 * entries * width + 2 * parts * tokens * (width + entries),
+    )(*grads, *rows_all, *after)
+
+
+def weight_gradient(normed, proj_grad, weight):
+    tokens, feat = normed.shape
+    cols = proj_grad.shape[1]
+    tile = 256 if feat % 256 == 0 else 128
+
+    def body(normed_ref, grad_ref, weight_ref, out_ref, sum_ref):
+        grad = contract_first(normed_ref[...], grad_ref[...])
+        out_ref[...] = grad.astype(BF16)
+        total = jnp.sum(grad * weight_ref[...].astype(F32), axis=1, keepdims=True)
+        sum_ref[...] = jnp.broadcast_to(total, sum_ref.shape)
+
+    out, sums = kernel_call(
+        body,
+        (feat // tile,),
+        [
+            pl.BlockSpec((tokens, tile), lambda step: (0, step)),
+            whole_block((tokens, cols)),
+            pl.BlockSpec((tile, cols), lambda step: (step, 0)),
+        ],
+        [
+            pl.BlockSpec((tile, cols), lambda step: (step, 0)),
+            pl.BlockSpec((tile, 128), lambda step: (step, 0)),
+        ],
+        [
+            jax.ShapeDtypeStruct((feat, cols), BF16),
+            jax.ShapeDtypeStruct((feat, 128), F32),
+        ],
+        2 * tokens * feat * cols,
+        4 * feat * cols + 2 * tokens * (feat + cols),
+    )(normed, proj_grad, weight)
+    return out, sums[:, 0]
 
 
 def dot(left, right):
@@ -127,100 +272,103 @@
         value = jnp.sum(jnp.where(to_absolute, value, 0), axis=-4)
         return jnp.swapaxes(value, -3, -2).reshape(value.shape[:-3] + (token_total,))
 
-    def by_part(pieces):
-        return jnp.concatenate(
-            [piece[part * rows : (part + 1) * rows] for part in range(PARTS) for piece in pieces]
-        )
-
-    def gather_x(value):
-        return jnp.stack([value] + [dim_x.turn(value, r) for r in range(1, nx)])
-
-    def x_sends(wide):
-        return [cut(wide, ((x + r) % nx) * 2 * feat, 2 * feat, 1) for r in range(1, nx)]
-
-    hidden_sends, embed_sends = x_sends(hidden_state), x_sends(embedded_next)
-    hidden_sends, embed_sends, hidden_state, embedded_next = lax.optimization_barrier(
-        (hidden_sends, embed_sends, hidden_state, embedded_next)
-    )
-    hidden_x = [dim_x.turn(send, r + 1) for r, send in enumerate(hidden_sends)]
-    embed_x = [dim_x.turn(send, r + 1) for r, send in enumerate(embed_sends)]
-
-    hidden_wide, embed_wide = hidden_state.astype(F32), embedded_next.astype(F32)
-    scales = lax.rsqrt(
-        jnp.stack(
-            [jnp.mean(hidden_wide * hidden_wide, axis=-1), jnp.mean(embed_wide * embed_wide, axis=-1)]
-        )
-        + EPSILON
-    )
-    scales_x = gather_x(scales)
-    scales_all = jnp.concatenate([scales_x, core.swap(scales_x, 1)])
-
-    def normed_inputs(wide, from_x, gain, kind):
-        pieces = [cut(wide, x * 2 * feat, 2 * feat, 1)] + from_x
-        mine = [cut(piece, c * feat, feat, 1) for piece in pieces]
-        theirs = [core.swap(cut(piece, (1 - c) * feat, feat, 1), 1) for piece in pieces]
-        raw = by_part(mine + theirs).astype(F32)
-        scale = by_part([scales_all[place, kind][:, None] for place in range(nc)])
-        return (raw * scale * cut(gain, own * feat, feat, 0)).astype(BF16)
-
-    normed_h = normed_inputs(hidden_state, hidden_x, gain_hidden, 0)
-    normed_e = normed_inputs(embedded_next, embed_x, gain_embed, 1)
-
-    half_h, half_e = dot(normed_h, proj_hidden), dot(normed_e, proj_embed)
-    total = (half_h + half_e).reshape(PARTS, 2, nx, rows, cols)
-    mine = total[:, 0] + core.swap(total[:, 1].astype(BF16), 1).astype(F32)
-    projected = mine[:, 0]
-    for r in range(1, nx):
-        projected = projected + dim_x.turn(mine[:, r].astype(BF16), -r).astype(F32)
-    projected = projected.reshape(block, cols)
-
-    pieces = lax.all_gather((projected * final_gain).astype(BF16), ("ctx", "vocab"))
+    def absolute_part(value):
+        value = value.reshape(value.shape[0], nc, rows, value.shape[-1])[:, None]
+        return jnp.sum(jnp.where(to_absolute[..., 0, :, None], value, 0), axis=2)
+
+    def relative_part(value):
+        return jnp.sum(jnp.where(to_absolute[..., 0], value[:, None], 0), axis=0).reshape(part_rows)
+
+    places = [(rc, rx) for rc in range(2) for rx in range(nx)]
+
+    def send(value, rc, rx):
+        pairs = []
+        for i in range(nc):
+            pairs.append((i, ((i // 2 + rx) % nx) * 2 + ((i % 2) ^ rc)))
+        return lax.ppermute(value, "ctx", pairs)
+
+    def scale_of(wide):
+        wide = wide.astype(F32)
+        return lax.rsqrt(jnp.mean(wide * wide, axis=-1, keepdims=True) + EPSILON)
+
+    def normed_blocks(wide, scale, gain):
+        def piece(rc, rx):
+            start = (((x + rx) % nx) * 2 + (c ^ rc)) * feat
+            value = cut(wide, start, feat, 1).astype(F32)
+            return (value * scale * cut(gain, start, feat, 0)).astype(BF16)
+
+        far = {(rc, rx): send(piece(rc, rx), rc, rx) for rx in range(1, nx) for rc in range(2)}
+        far[1, 0] = send(piece(1, 0), 1, 0)
+        far[0, 0] = piece(0, 0)
+        return [far[place] for place in places]
+
+    hidden_scale, embed_scale = scale_of(hidden_state), scale_of(embedded_next)
+    blocks_h = normed_blocks(hidden_state, hidden_scale, gain_hidden)
+    blocks_e = normed_blocks(embedded_next, embed_scale, gain_embed)
+
+    halves_h = [dot(piece, proj_hidden) for piece in blocks_h]
+    halves_e = [dot(piece, proj_embed) for piece in blocks_e]
+    projected = halves_h[0] + halves_e[0]
+    for index, (rc, rx) in enumerate(places[1:], 1):
+        term = (halves_h[index] + halves_e[index]).astype(BF16)
+        projected = projected + send(term, rc, (nx - rx) % nx).astype(F32)
+
+    piece = (projected * final_gain).astype(BF16)
     squares = jnp.sum(projected * projected, axis=-1)
     squares = lax.all_to_all(
         jnp.broadcast_to(squares, (nc * nv, block)), ("ctx", "vocab"), 0, 0, tiled=True
     )
     squares = jnp.sum(squares.reshape(nc, nv, block), axis=1)
-    row_scale = relative(lax.rsqrt(squares / width + EPSILON))
-    pieces = pieces.reshape(nc, nv, block, cols)
-    gathered = by_part(
-        [
-            lax.dynamic_index_in_dim(pieces, block_at(place), 0, keepdims=False)
-            .transpose(1, 0, 2)
-            .reshape(block, width)
-            for place in range(nc)
-        ]
-    )
-
-    vocab_ids = (own * nv + slot) * vocab_local + lax.iota(jnp.int32, vocab_local)
-    logits = contract_last(gathered, head) * row_scale[:, None]
-    target = relative(targets.reshape(nc, block))
+    row_scales = relative(lax.rsqrt(squares / width + EPSILON))
+    target_local = relative(targets.reshape(nc, block)) - (own * nv + slot) * vocab_local
     mask_weight = loss_mask.astype(F32).reshape(nc, block)
     mask = relative(mask_weight)
-    is_target = target[:, None] == vocab_ids[None, :]
-    power = jnp.exp(logits)
-    sums = jnp.stack(
-        [
-            jnp.sum(power, axis=-1),
-            jnp.sum(power * (logits * F32(1.0 / 256.0)), axis=-1),
-            jnp.sum(jnp.where(is_target, logits, F32(0.0)), axis=-1),
-        ]
-    )
-    sums = sum_everywhere(absolute(sums))
-    exp_total, weighted, target_logit = sums[0], sums[1], sums[2]
-    log_total = jnp.log(exp_total)
-    mean_loss = jnp.sum(mask_weight * (log_total - target_logit)) / token_total
-    scaled_dot = mask * relative(weighted / exp_total * F32(256.0) - target_logit)
-    probs = jnp.exp(logits - relative(log_total)[:, None])
-    scaled_grad = ((mask * row_scale)[:, None] * (probs - is_target.astype(F32))).astype(BF16)
-    coefficient = row_scale * row_scale * scaled_dot / width
+    gathered, logit_list, sum_list = [], [], []
+    for part in range(PARTS):
+        span = slice(part * part_rows, (part + 1) * part_rows)
+        pieces = lax.all_gather(piece[part * rows : (part + 1) * rows], ("ctx", "vocab"))
+        pieces = pieces.reshape(nc, nv, rows, cols)
+        gathered.append(
+            jnp.concatenate(
+                [
+                    lax.dynamic_index_in_dim(pieces, block_at(place), 0, keepdims=False)
+                    .transpose(1, 0, 2)
+                    .reshape(rows, width)
+                    for place in range(nc)
+                ]
+            )
+        )
+        logits, sums = logits_with_sums(gathered[part], head, row_scales[span], target_local[span])
+        logit_list.append(logits)
+        sum_list.append(sum_everywhere(jnp.sum(absolute_part(sums), axis=-1)))
+
+    mean_loss = F32(0.0)
+    logit_grads, coefficients = [], []
+    vocab_ids = lax.iota(jnp.int32, vocab_local)[None, :]
+    for part in range(PARTS):
+        span = slice(part * part_rows, (part + 1) * part_rows)
+        exp_total, weighted, target_logit = sum_list[part]
+        log_total = jnp.log(exp_total)
+        part_mask = mask_weight[:, part * rows : (part + 1) * rows]
+        mean_loss = mean_loss + jnp.sum(part_mask * (log_total - target_logit))
+        scaled_dot = mask[span] * relative_part(weighted / exp_total * F32(256.0) - target_logit)
+        row_scale = row_scales[span]
+        probs = jnp.exp(logit_list[part] - relative_part(log_total)[:, None])
+        is_target = target_local[span][:, None] == vocab_ids
+        logit_grads.append(
+            ((mask[span] * row_scale)[:, None] * (probs - is_target.astype(F32))).astype(BF16)
+        )
+        coefficients.append(row_scale * row_scale * scaled_dot / width)
+    mean_loss = mean_loss / token_total
 
     def column_chunk(value, place):
         return jnp.stack([cut(value, (p * vb + place) * cols, cols, 1) for p in range(va)])
 
-    def collect(part_grad):
-        partial = dot(part_grad, head).astype(BF16)
+    def core_sum(partial):
         mine, theirs = partial[: nx * rows], partial[nx * rows :]
-        mine = (mine.astype(F32) + core.swap(theirs, 1).astype(F32)).astype(BF16)
+        return (mine.astype(F32) + core.swap(theirs, 1).astype(F32)).astype(BF16)
+
+    def collect(mine):
         mine = mine.reshape(nx, rows, width)
         summed = mine[0].astype(F32)
         for r in range(1, nx):
@@ -230,9 +378,7 @@
         for r in range(1, vb):
             kept = kept + dim_b.turn(column_chunk(summed, (b + r) % vb), r).astype(F32)
         summed = halving_scatter(kept.astype(BF16), dim_a).astype(BF16)
-        along = gather_x(summed)
-        along = jnp.concatenate([along, core.swap(along, 1)])
-        return along.reshape(part_rows, cols)
+        return jnp.concatenate([summed] + [send(summed, rc, rx) for rc, rx in places[1:]])
 
     def final_move(value):
         pairs = []
@@ -267,31 +413,33 @@
         moved = final_move(halving_scatter(kept.astype(BF16), dim_a).astype(BF16))
         return moved.astype(F32)
 
+    core_sums = [core_sum(times_head(part_grad, head)) for part_grad in logit_grads]
+    grad_head = head_gradient(logit_grads, gathered, core_sums)
     grad_final_gain = jnp.zeros((cols,), F32)
     proj_grads, backs = [], []
     for part in range(PARTS):
-        span = slice(part * part_rows, (part + 1) * part_rows)
-        scaled = collect(scaled_grad[span]).astype(F32)
-        plain = cut(gathered[span], slot * cols, cols, 1).astype(F32) / final_gain
+        scaled = collect(core_sums[part]).astype(F32)
+        plain = cut(gathered[part], slot * cols, cols, 1).astype(F32) / final_gain
         grad_final_gain = grad_final_gain + jnp.sum(scaled * plain, axis=0)
-        part_grad = (scaled * final_gain - plain * coefficient[span][:, None]).astype(BF16)
-        proj_grads.append(part_grad)
-        backs.append(back(part_grad))
-
-    grad_head = contract_first(scaled_grad, gathered).astype(BF16)
-    proj_grad = jnp.concatenate(proj_grads)
-    wide_h, wide_e = contract_first(normed_h, proj_grad), contract_first(normed_e, proj_grad)
-    grad_proj_hidden, grad_proj_embed = wide_h.astype(BF16), wide_e.astype(BF16)
-
-    wide = proj_grad.astype(F32)
-    dots = absolute(jnp.stack([jnp.sum(wide * half_h, axis=-1), jnp.sum(wide * half_e, axis=-1)]))
+        part_grad = scaled * final_gain - plain * coefficients[part][:, None]
+        proj_grads.append(part_grad.astype(BF16))
+        backs.append(back(proj_grads[part]))
+
+    proj_grad = jnp.stack([grad.reshape(nc, rows, cols) for grad in proj_grads], axis=1)
+    grad_proj_hidden, gain_h = weight_gradient(
+        jnp.concatenate(blocks_h), proj_grad.reshape(token_total, cols), proj_hidden
+    )
+    grad_proj_embed, gain_e = weight_gradient(
+        jnp.concatenate(blocks_e), proj_grad.reshape(token_total, cols), proj_embed
+    )
+
+    wide = proj_grad.astype(F32).reshape(nc, block, cols)
+    dots = jnp.stack(
+        [jnp.sum(wide * jnp.stack(halves), axis=-1) for halves in (halves_h, halves_e)]
+    )
+    dots = jnp.sum(jnp.where(to_absolute[..., 0], dots[:, None], 0), axis=2)
     dots = jnp.broadcast_to(dots.transpose(1, 0, 2)[:, None], (nc, nv, 2, block))
-    gains = jnp.stack(
-        [
-            jnp.sum(wide_h * proj_hidden.astype(F32), axis=1),
-            jnp.sum(wide_e * proj_embed.astype(F32), axis=1),
-        ]
-    )
+    gains = jnp.stack([gain_h, gain_e])
     ratio = nv // nc
     gains = gains.reshape(2, ratio, cols).transpose(1, 0, 2)[None]
     holder = jnp.arange(nc, dtype=jnp.int32)[:, None, None, None] == own
@@ -302,7 +450,7 @@
 
     def finish(kind, source, gain):
         back_all = jnp.concatenate([moved[kind * rows : (kind + 1) * rows] for moved in backs])
-        scale = scales[kind][:, None]
+        scale = (hidden_scale, embed_scale)[kind]
         dot_all = ends[kind, :block][:, None]
         source = cut(source, slot * cols, cols, 1).astype(F32)
         gain = cut(gain, slot * cols, cols, 0)

time: 497 us -> 527 us (1.060)
  Pallas kernels: 0 us -> 106 us
  matrix products: 101 us -> 19.7 us
  local copies, waits for them, and re-layouts: 61.8 us -> 30.2 us
  waiting for transfers between devices: 233 us -> 260 us
  other arithmetic: 31.3 us -> 39.8 us
  starting transfers between devices: 45.4 us -> 51.7 us
    pallas_call x0 -> x7, Pallas kernels: none -> 106 us  [the longest x2 35.6 us: times_head(): kernel_call(body, (width // tile,), [whole_block((tokens, entries)), pl.B...]
    ppermute x30 -> x16, waiting for transfers between devices: 156 us -> 72.1 us  [move(): return lax.ppermute(value, self.axis, pairs)]
    all_gather x1 -> x2, waiting for transfers between devices: 56.5 us -> 110 us  [local(): lax.all_gather(piece[part * rows:(part + 1) * rows], ('ctx', 'vocab'))]
    ppermute x0 -> x15, waiting for transfers between devices: none -> 38.2 us  [send(): return lax.ppermute(value, 'ctx', pairs)]
    dot_general x3 -> x0, matrix products: 31.2 us -> none  [contract_first(): lax.dot_general(left, right, (((0,), (0,)), ((), ())), preferred_element_...]
    dot_general x4 -> x8, matrix products: 34.2 us -> 7.53 us  [dot(): return jnp.dot(left, right, preferred_element_type=F32)]
    unnamed x119 -> x154, local copies, waits for them, and re-layouts: 39.6 us -> 13 us
    dot_general x9 -> x8, matrix products: 35.9 us -> 12.2 us  [contract_last(): lax.dot_general(left, right, (((1,), (1,)), ((), ())), preferred_element_...]
  transfers between devices with their start and end apart: 36 -> 39, of which waited for: 20 -> 22; matrix products, arithmetic and copies ran while one was open for 15% -> 10% of each run, Pallas kernels for 0% -> 10%
where the time goes in v4:
time: 527 us; the launch traced here: 525 us
  waiting for transfers between devices  260 us (49%)
  Pallas kernels  106 us (20%)
  starting transfers between devices  51.7 us (10%)
  other arithmetic  39.8 us (8%)
  local copies, waits for them, and re-layouts  30.2 us (6%)
  matrix products  19.7 us (4%)
  between operations  18.8 us (4%)
    all_gather x2, waiting for transfers between devices, local(): lax.all_gather(piece[part * rows:(part + 1) * rows], ('ctx', 'vocab'))  110 us
    ppermute x16, waiting for transfers between devices, move(): return lax.ppermute(value, self.axis, pairs)  72.1 us
    ppermute x15, waiting for transfers between devices, send(): return lax.ppermute(value, 'ctx', pairs)  38.2 us
    pallas_call x2, Pallas kernels, times_head(): kernel_call(body, (width // tile,), [whole_block((tokens, entries)), pl.B...  35.6 us
    pallas_call x2, Pallas kernels, logits_with_sums(): kernel_call(body, (entries // tile,), [whole_block((tokens, width)), pl.B...  33.2 us
    pallas_call x1, Pallas kernels, head_gradient(): kernel_call(body, (entries // tile,), [pl.BlockSpec((tokens, tile), lambd...  22.1 us
    pallas_call x2, Pallas kernels, weight_gradient(): kernel_call(body, (feat // tile,), [pl.BlockSpec((tokens, tile), lambda s...  14.7 us
    ppermute x16, starting transfers between devices, move(): return lax.ppermute(value, self.axis, pairs)  13.5 us
  transfers between devices with their start and end apart: 39, of which 22 were waited for; matrix products, arithmetic and copies ran while one was open for 10% of the time, Pallas kernels for 10%

profile of v4, /device:TPU:2, one launch (start us, length us, event | category | flops | bytes accessed | tf_op | source)
XLA Modules:
  0.0 525.2 jit_solution(18368373687038729647)
XLA Ops:
  7.3 2.0 multiply_reduce_fusion
  11.6 2.1 collective-permute-start.1
  16.7 18.1 %collective-permute-done.1 = bf16[128,1792]{1,0:T(8,128)(2,1)S(1)} collective-permute-done((bf16[128,1792]{1,0:T(8,128)(2,1)S(1)}, bf16[128,1792]{1,0:T(8,128)(2,1)S(1)}, u32[]{:S(2)}, u32[]{:S(2)}) %collective-permute-start.1) | collective-permute-done | bytes 458784 | tf_op jit(solution)/shard_map/ppermute | solution.py:288
  35.5 9.2 %collective-permute-done = bf16[128,1792]{1,0:T(8,128)(2,1)S(1)} collective-permute-done((bf16[128,1792]{1,0:T(8,128)(2,1)S(1)}, bf16[128,1792]{1,0:T(8,128)(2,1)S(1)}, u32[]{:S(2)}, u32[]{:S(2)}) %collective-permute-start) | collective-permute-done | bytes 458784 | tf_op jit(solution)/shard_map/ppermute | solution.py:288
  46.9 6.5 %collective-permute-done.6 = bf16[128,1792]{1,0:T(8,128)(2,1)S(1)} collective-permute-done((bf16[128,1792]{1,0:T(8,128)(2,1)S(1)}, bf16[128,1792]{1,0:T(8,128)(2,1)S(1)}, u32[]{:S(2)}, u32[]{:S(2)}) %collective-permute-start.6) | collective-permute-done | bytes 458784 | tf_op jit(solution)/shard_map/ppermute | solution.py:288
  59.4 3.8 collective-permute-done.8
  66.0 6.2 %all-to-all-start = ((f32[32,1,128]{2,1,0:T(1,128)}), f32[32,1,128]{2,1,0:T(1,128)S(1)}, u32[]{:S(2)}, u32[]{:S(2)}) async-start(f32[32,1,128]{2,1,0:T(1,128)} %broadcast_in_dim.255), calls=%async_computation | async-start | bytes 32768 | tf_op jit(solution)/shard_map/all_to_all | solution.py:318
  75.3 2.7 all-to-all-done
  78.6 47.5 %all-gather.5.cloned.1.call-done = bf16[2048,896]{1,0:T(8,128)(2,1)} async-done(((bf16[64,896]{1,0:T(8,128)(2,1)}), bf16[2048,896]{1,0:T(8,128)(2,1)}) %all-gather.5.cloned.1.call-update) | async-done | bytes 3670032 | tf_op jit(solution)/shard_map/all_gather | solution.py:329
  126.1 62.9 %all-gather.7.cloned.1.call-done = bf16[2048,896]{1,0:T(8,128)(2,1)} async-done(((bf16[64,896]{1,0:T(8,128)(2,1)}), bf16[2048,896]{1,0:T(8,128)(2,1)}) %all-gather.7.cloned.1.call-update) | async-done | bytes 3670032 | tf_op jit(solution)/shard_map/all_gather | solution.py:329
  189.0 4.6 constant_dynamic-slice_fusion.24
  196.9 17.3 %shard_map.169 = (f32[256,2048]{1,0:T(8,128)S(1)}, f32[3,256,128]{2,1,0:T(8,128)S(1)}) custom-call(bf16[256,7168]{1,0:T(8,128)(2,1)} %copy-done.14, bf16[2048,7168]{1,0:T(8,128)(2,1)} %head_ref.7, f32[256,1]{1,0:T(8,128)S(1)} %broadcast_in_dim.293.scale_ref, s32[256,1]{1,0:T(8,128)S(1)} %broadcast_in_dim.294.target_ref), custom_call_target="tpu_custom_call" | custom-call | flops 7516192768 | bytes 35127296 | tf_op jit(solution)/shard_map/pallas_call | solution.py:113
  215.5 16.0 %shard_map.170 = (f32[256,2048]{1,0:T(8,128)S(1)}, f32[3,256,128]{2,1,0:T(8,128)S(1)}) custom-call(bf16[256,7168]{1,0:T(8,128)(2,1)} %copy-done.15, bf16[2048,7168]{1,0:T(8,128)(2,1)} %head_ref.7, f32[256,1]{1,0:T(8,128)S(1)} %broadcast_in_dim.295.scale_ref, s32[256,1]{1,0:T(8,128)S(1)} %broadcast_in_dim.296.target_ref), custom_call_target="tpu_custom_call" | custom-call | flops 7516192768 | bytes 35127296 | tf_op jit(solution)/shard_map/pallas_call | solution.py:113
  232.7 3.8 all-to-all-start.2
  237.5 5.7 %all-to-all-done.2 = f32[32,1,768]{2,1,0:T(1,128)S(1)} async-done(((f32[32,1,768]{2,1,0:T(1,128)}), f32[32,1,768]{2,1,0:T(1,128)S(1)}, u32[]{:S(2)}, u32[]{:S(2)}) %all-to-all-start.2) | async-done | bytes 98336 | tf_op jit(solution)/shard_map/all_to_all | solution.py:62
  243.1 3.4 all-to-all-start.1
  248.1 5.1 all-to-all-done.1
  257.4 17.8 %shard_map.172 = bf16[256,7168]{1,0:T(8,128)(2,1)S(1)} custom-call(bf16[256,2048]{1,0:T(8,128)(2,1)S(1)} %multiply_convert_fusion.grad_ref.refs_1_, bf16[2048,7168]{1,0:T(8,128)(2,1)} %head_ref.7), custom_call_target="tpu_custom_call" | custom-call | flops 7516192768 | bytes 34078720 | tf_op jit(solution)/shard_map/pallas_call | solution.py:144
  275.2 1.8 copy-done
  280.9 2.4 multiply_convert_fusion.1.grad_ref.refs_0_
  283.3 17.8 %shard_map.171 = bf16[256,7168]{1,0:T(8,128)(2,1)S(1)} custom-call(bf16[256,2048]{1,0:T(8,128)(2,1)S(1)} %multiply_convert_fusion.1.grad_ref.refs_0_, bf16[2048,7168]{1,0:T(8,128)(2,1)} %head_ref.7), custom_call_target="tpu_custom_call" | custom-call | flops 7516192768 | bytes 34078720 | tf_op jit(solution)/shard_map/pallas_call | solution.py:144
  306.5 2.6 add_convert_fusion.refs_5_
  310.5 1.9 add_convert_fusion.1.refs_4_
  313.4 22.1 %shard_map.175 = bf16[2048,7168]{1,0:T(8,128)(2,1)} custom-call(bf16[256,2048]{1,0:T(8,128)(2,1)S(1)} %multiply_convert_fusion.1.grad_ref.refs_0_, bf16[256,2048]{1,0:T(8,128)(2,1)S(1)} %multiply_convert_fusion.grad_ref.refs_1_, bf16[256,7168]{1,0:T(8,128)(2,1)} %copy-done.14, bf16[256,7168]{1,0:T(8,128)(2,1)} %copy-done.15, ...), custom_call_target="tpu_custom_call" | custom-call | flops 15032385536 | bytes 38797312 | tf_op jit(solution)/shard_map/pallas_call | solution.py:170
  335.6 15.5 %collective-permute-done.10 = bf16[64,7168]{1,0:T(8,128)(2,1)S(1)} collective-permute-done((bf16[64,7168]{1,0:T(8,128)(2,1)S(1)}, bf16[64,7168]{1,0:T(8,128)(2,1)S(1)}, u32[]{:S(2)}, u32[]{:S(2)}) %collective-permute-start.10) | collective-permute-done | bytes 917536 | tf_op jit(solution)/shard_map/ppermute | solution.py:28
  354.1 11.0 %collective-permute-done.11 = bf16[4,64,896]{2,1,0:T(8,128)(2,1)S(1)} collective-permute-done((bf16[4,64,896]{2,1,0:T(8,128)(2,1)S(1)}, bf16[4,64,896]{2,1,0:T(8,128)(2,1)S(1)}, u32[]{:S(2)}, u32[]{:S(2)}) %collective-permute-start.11) | collective-permute-done | bytes 458784 | tf_op jit(solution)/shard_map/ppermute | solution.py:28
  366.1 6.7 %collective-permute-done.23 = bf16[4,64,896]{2,1,0:T(8,128)(2,1)S(1)} collective-permute-done((bf16[4,64,896]{2,1,0:T(8,128)(2,1)S(1)}, bf16[4,64,896]{2,1,0:T(8,128)(2,1)S(1)}, u32[]{:S(2)}, u32[]{:S(2)}) %collective-permute-start.23) | collective-permute-done | bytes 458784 | tf_op jit(solution)/shard_map/ppermute | solution.py:28
  374.8 7.0 %collective-permute-done.24 = bf16[2,64,896]{2,1,0:T(8,128)(2,1)S(1)} collective-permute-done((bf16[2,64,896]{2,1,0:T(8,128)(2,1)S(1)}, bf16[2,64,896]{2,1,0:T(8,128)(2,1)S(1)}, u32[]{:S(2)}, u32[]{:S(2)}) %collective-permute-start.24) | collective-permute-done | bytes 229408 | tf_op jit(solution)/shard_map/ppermute | solution.py:28
  381.9 1.8 collective-permute-done.13
  383.9 2.0 collective-permute-start.14
  386.0 2.8 collective-permute-done.25
  402.1 2.2 pad_maximum_fusion.3
  407.3 7.4 %shard_map.174 = (bf16[1792,896]{1,0:T(8,128)(2,1)}, f32[1792,128]{1,0:T(8,128)S(1)}) custom-call(bf16[512,1792]{1,0:T(8,128)(2,1)S(1)} %copy-done.4, bf16[512,896]{1,0:T(8,128)(2,1)S(1)} %bitcast.190, bf16[1792,896]{1,0:T(8,128)(2,1)} %weight_ref.3), custom_call_target="tpu_custom_call" | custom-call | flops 1644167168 | bytes 9175040 | tf_op jit(solution)/shard_map/pallas_call | solution.py:194
  415.1 7.3 %shard_map.173 = (bf16[1792,896]{1,0:T(8,128)(2,1)}, f32[1792,128]{1,0:T(8,128)S(1)}) custom-call(bf16[512,1792]{1,0:T(8,128)(2,1)S(1)} %copy-done.5, bf16[512,896]{1,0:T(8,128)(2,1)S(1)} %bitcast.191, bf16[1792,896]{1,0:T(8,128)(2,1)} %weight_ref.2), custom_call_target="tpu_custom_call" | custom-call | flops 1644167168 | bytes 9175040 | tf_op jit(solution)/shard_map/pallas_call | solution.py:194
  423.7 3.8 all-to-all-start.3
  428.2 3.4 fusion.14
  437.3 11.6 %all-to-all-done.3 = f32[32,2,1024]{2,1,0:T(2,128)S(1)} async-done(((f32[32,2,1024]{2,1,0:T(2,128)}), f32[32,2,1024]{2,1,0:T(2,128)S(1)}, u32[]{:S(2)}, u32[]{:S(2)}) %all-to-all-start.3) | async-done | bytes 262176 | tf_op jit(solution)/shard_map/all_to_all | solution.py:449
  451.8 2.0 fusion.3
  457.7 9.7 %collective-permute-done.30 = bf16[2,128,896]{2,1,0:T(8,128)(2,1)S(1)} collective-permute-done((bf16[2,128,896]{2,1,0:T(8,128)(2,1)S(1)}, bf16[2,128,896]{2,1,0:T(8,128)(2,1)S(1)}, u32[]{:S(2)}, u32[]{:S(2)}) %collective-permute-start.30) | collective-permute-done | bytes 458784 | tf_op jit(solution)/shard_map/ppermute | solution.py:28
  467.5 2.1 collective-permute-start.31
  469.6 11.6 %collective-permute-done.18 = bf16[2,128,896]{2,1,0:T(8,128)(2,1)S(1)} collective-permute-done((bf16[2,128,896]{2,1,0:T(8,128)(2,1)S(1)}, bf16[2,128,896]{2,1,0:T(8,128)(2,1)S(1)}, u32[]{:S(2)}, u32[]{:S(2)}) %collective-permute-start.18) | collective-permute-done | bytes 458784 | tf_op jit(solution)/shard_map/ppermute | solution.py:28
  481.5 5.7 %collective-permute-start.32 = (bf16[128,896]{1,0:T(8,128)(2,1)S(1)}, bf16[128,896]{1,0:T(8,128)(2,1)S(1)}, u32[]{:S(2)}, u32[]{:S(2)}) collective-permute-start(bf16[128,896]{1,0:T(8,128)(2,1)S(1)} %fusion.45), channel_id=1, source_target_pairs={{0,0},{1,1},{2,8},{3,9},{4,16},{5,17},{6,24},{7,25},{8,2},{9,3},{1... | collective-permute-start | bytes 688136 | tf_op jit(solution)/shard_map/ppermute | solution.py:389
  487.3 5.9 %collective-permute-done.19 = bf16[1,128,896]{2,1,0:T(8,128)(2,1)S(1)} collective-permute-done((bf16[1,128,896]{2,1,0:T(8,128)(2,1)S(1)}, bf16[1,128,896]{2,1,0:T(8,128)(2,1)S(1)}, u32[]{:S(2)}, u32[]{:S(2)}) %collective-permute-start.19) | collective-permute-done | bytes 229408 | tf_op jit(solution)/shard_map/ppermute | solution.py:28
  493.3 7.2 %collective-permute-start.20 = (bf16[128,896]{1,0:T(8,128)(2,1)S(1)}, bf16[128,896]{1,0:T(8,128)(2,1)S(1)}, u32[]{:S(2)}, u32[]{:S(2)}) collective-permute-start(bf16[128,896]{1,0:T(8,128)(2,1)S(1)} %fusion.44), channel_id=1, source_target_pairs={{0,0},{1,1},{2,8},{3,9},{4,16},{5,17},{6,24},{7,25},{8,2},{9,3},{1... | collective-permute-start | bytes 688136 | tf_op jit(solution)/shard_map/ppermute | solution.py:389
  500.5 8.3 %collective-permute-done.32 = bf16[128,896]{1,0:T(8,128)(2,1)S(1)} collective-permute-done((bf16[128,896]{1,0:T(8,128)(2,1)S(1)}, bf16[128,896]{1,0:T(8,128)(2,1)S(1)}, u32[]{:S(2)}, u32[]{:S(2)}) %collective-permute-start.32) | collective-permute-done | bytes 229408 | tf_op jit(solution)/shard_map/ppermute | solution.py:389
  508.8 4.8 collective-permute-done.20
  513.6 1.8 fusion.43
  515.5 1.8 fusion.40
  (341 shorter events, 79.7 us)
Async XLA Ops:
  7.2 119.0 %all-gather.5.cloned.1.call-start = ((), (), s32[]{:S(2)}) async-start(), calls=%async_computation.4 | async-start | bytes 3784704 | tf_op jit(solution)/shard_map/all_gather | solution.py:329
  11.5 44.0 %collective-permute-start.4 = (bf16[128,1792]{1,0:T(8,128)(2,1)S(1)}, bf16[128,1792]{1,0:T(8,128)(2,1)S(1)}, u32[]{:S(2)}, u32[]{:S(2)}) collective-permute-start(bf16[128,1792]{1,0:T(8,128)(2,1)S(1)} %get-tuple-element.57), channel_id=1, source_target_pairs={{0,8},{8,0},{16,24},{24,16},{1,9},{9,1},{17,25},{25,17},{2,10},{10... | collective-permute-start | bytes 1376264 | tf_op jit(solution)/shard_map/ppermute | solution.py:288
  11.6 34.6 %collective-permute-start.7 = (bf16[128,1792]{1,0:T(8,128)(2,1)S(1)}, bf16[128,1792]{1,0:T(8,128)(2,1)S(1)}, u32[]{:S(2)}, u32[]{:S(2)}) collective-permute-start(bf16[128,1792]{1,0:T(8,128)(2,1)S(1)} %get-tuple-element.58), channel_id=1, source_target_pairs={{0,24},{8,16},{16,8},{24,0},{1,25},{9,17},{17,9},{25,1},{2,26},{10... | collective-permute-start | bytes 1376264 | tf_op jit(solution)/shard_map/ppermute | solution.py:288
  11.6 23.2 %collective-permute-start.1 = (bf16[128,1792]{1,0:T(8,128)(2,1)S(1)}, bf16[128,1792]{1,0:T(8,128)(2,1)S(1)}, u32[]{:S(2)}, u32[]{:S(2)}) collective-permute-start(bf16[128,1792]{1,0:T(8,128)(2,1)S(1)} %get-tuple-element.59), channel_id=1, source_target_pairs={{0,16},{8,24},{16,0},{24,8},{1,17},{9,25},{17,1},{25,9},{2,18},{10... | collective-permute-start | bytes 1376264 | tf_op jit(solution)/shard_map/ppermute | solution.py:288
  15.3 42.8 %copy-start.26 = (bf16[128,1792]{1,0:T(8,128)(2,1)}, bf16[128,1792]{1,0:T(8,128)(2,1)S(1)}, u32[]{:S(2)}) copy-start(bf16[128,1792]{1,0:T(8,128)(2,1)S(1)} %get-tuple-element.60) | copy-start | bytes 1376260
  15.3 40.8 %collective-permute-start.3 = (bf16[128,1792]{1,0:T(8,128)(2,1)S(1)}, bf16[128,1792]{1,0:T(8,128)(2,1)S(1)}, u32[]{:S(2)}, u32[]{:S(2)}) collective-permute-start(bf16[128,1792]{1,0:T(8,128)(2,1)S(1)} %get-tuple-element.61), channel_id=1, source_target_pairs={{0,8},{8,0},{16,24},{24,16},{1,9},{9,1},{17,25},{25,17},{2,10},{10... | collective-permute-start | bytes 1376264 | tf_op jit(solution)/shard_map/ppermute | solution.py:288
  15.4 29.3 %collective-permute-start = (bf16[128,1792]{1,0:T(8,128)(2,1)S(1)}, bf16[128,1792]{1,0:T(8,128)(2,1)S(1)}, u32[]{:S(2)}, u32[]{:S(2)}) collective-permute-start(bf16[128,1792]{1,0:T(8,128)(2,1)S(1)} %get-tuple-element.63), channel_id=1, source_target_pairs={{0,16},{8,24},{16,0},{24,8},{1,17},{9,25},{17,1},{25,9},{2,18},{10... | collective-permute-start | bytes 1376264 | tf_op jit(solution)/shard_map/ppermute | solution.py:288
  16.7 46.5 %copy-start.22 = (f32[128,896]{1,0:T(8,128)}, f32[128,896]{1,0:T(8,128)S(1)}, u32[]{:S(2)}) copy-start(f32[128,896]{1,0:T(8,128)S(1)} %fusion.82) | copy-start | bytes 1376260
  16.7 28.0 %copy-start.9 = (bf16[1792,896]{1,0:T(8,128)(2,1)S(1)}, bf16[1792,896]{1,0:T(8,128)(2,1)}, u32[]{:S(2)}) copy-start(bf16[1792,896]{1,0:T(8,128)(2,1)} %weight_ref.2) | copy-start | bytes 9633796
  34.8 18.5 %collective-permute-start.6 = (bf16[128,1792]{1,0:T(8,128)(2,1)S(1)}, bf16[128,1792]{1,0:T(8,128)(2,1)S(1)}, u32[]{:S(2)}, u32[]{:S(2)}) collective-permute-start(bf16[128,1792]{1,0:T(8,128)(2,1)S(1)} %get-tuple-element.62), channel_id=1, source_target_pairs={{0,24},{8,16},{16,8},{24,0},{1,25},{9,17},{17,9},{25,1},{2,26},{10... | collective-permute-start | bytes 1376264 | tf_op jit(solution)/shard_map/ppermute | solution.py:288
  46.1 13.3 %collective-permute-start.2 = (bf16[128,896]{1,0:T(8,128)(2,1)S(1)}, bf16[128,896]{1,0:T(8,128)(2,1)S(1)}, u32[]{:S(2)}, u32[]{:S(2)}) collective-permute-start(bf16[128,896]{1,0:T(8,128)(2,1)S(1)} %get-tuple-element.142), channel_id=1, source_target_pairs={{0,16},{8,24},{16,0},{24,8},{1,17},{9,25},{17,1},{25,9},{2,18},{10... | collective-permute-start | bytes 688136 | tf_op jit(solution)/shard_map/ppermute | solution.py:288
  54.8 8.4 %collective-permute-start.8 = (bf16[128,896]{1,0:T(8,128)(2,1)S(1)}, bf16[128,896]{1,0:T(8,128)(2,1)S(1)}, u32[]{:S(2)}, u32[]{:S(2)}) collective-permute-start(bf16[128,896]{1,0:T(8,128)(2,1)S(1)} %get-tuple-element.138), channel_id=1, source_target_pairs={{0,24},{8,16},{16,8},{24,0},{1,25},{9,17},{17,9},{25,1},{2,26},{10... | collective-permute-start | bytes 688136 | tf_op jit(solution)/shard_map/ppermute | solution.py:288
  57.6 5.6 %collective-permute-start.5 = (bf16[128,896]{1,0:T(8,128)(2,1)S(1)}, bf16[128,896]{1,0:T(8,128)(2,1)S(1)}, u32[]{:S(2)}, u32[]{:S(2)}) collective-permute-start(bf16[128,896]{1,0:T(8,128)(2,1)S(1)} %get-tuple-element.140), channel_id=1, source_target_pairs={{0,8},{8,0},{16,24},{24,16},{1,9},{9,1},{17,25},{25,17},{2,10},{10... | collective-permute-start | bytes 688136 | tf_op jit(solution)/shard_map/ppermute | solution.py:288
  64.2 124.8 %all-gather.7.cloned.1.call-start = ((), (), s32[]{:S(2)}) async-start(), calls=%async_computation.5 | async-start | bytes 3784704 | tf_op jit(solution)/shard_map/all_gather | solution.py:329
  66.0 12.0 %all-to-all-start = ((f32[32,1,128]{2,1,0:T(1,128)}), f32[32,1,128]{2,1,0:T(1,128)S(1)}, u32[]{:S(2)}, u32[]{:S(2)}) async-start(f32[32,1,128]{2,1,0:T(1,128)} %broadcast_in_dim.255), calls=%async_computation | async-start | bytes 32768 | tf_op jit(solution)/shard_map/all_to_all | solution.py:318
  196.9 17.3 %copy-start.15 = (bf16[256,7168]{1,0:T(8,128)(2,1)}, bf16[256,7168]{1,0:T(8,128)(2,1)S(1)}, u32[]{:S(2)}) copy-start(bf16[256,7168]{1,0:T(8,128)(2,1)S(1)} %constant_dynamic-update-slice_fusion.4.rows_ref.refs_3_) | copy-start | bytes 11010052
  232.7 10.4 %all-to-all-start.2 = ((f32[32,1,768]{2,1,0:T(1,128)}), f32[32,1,768]{2,1,0:T(1,128)S(1)}, u32[]{:S(2)}, u32[]{:S(2)}) async-start(f32[32,1,768]{2,1,0:T(1,128)} %reshape.460), calls=%async_computation.2 | async-start | bytes 196608 | tf_op jit(solution)/shard_map/all_to_all | solution.py:62
  243.1 10.1 %all-to-all-start.1 = ((f32[32,1,768]{2,1,0:T(1,128)}), f32[32,1,768]{2,1,0:T(1,128)S(1)}, u32[]{:S(2)}, u32[]{:S(2)}) async-start(f32[32,1,768]{2,1,0:T(1,128)} %reshape.462), calls=%async_computation.1 | async-start | bytes 196608 | tf_op jit(solution)/shard_map/all_to_all | solution.py:62
  278.4 28.2 %collective-permute-start.21 = (bf16[128,7168]{1,0:T(8,128)(2,1)}, bf16[128,7168]{1,0:T(8,128)(2,1)}, u32[]{:S(2)}, u32[]{:S(2)}) collective-permute-start(bf16[128,7168]{1,0:T(8,128)(2,1)} %slice.190), channel_id=1, source_target_pairs={{0,8},{8,0},{16,24},{24,16},{1,9},{9,1},{17,25},{25,17},{2,10},{10... | collective-permute-start | bytes 5505032 | tf_op jit(solution)/shard_map/ppermute | solution.py:28
  302.5 8.1 %collective-permute-start.9 = (bf16[128,7168]{1,0:T(8,128)(2,1)}, bf16[128,7168]{1,0:T(8,128)(2,1)}, u32[]{:S(2)}, u32[]{:S(2)}) collective-permute-start(bf16[128,7168]{1,0:T(8,128)(2,1)} %slice.180), channel_id=1, source_target_pairs={{0,8},{8,0},{16,24},{24,16},{1,9},{9,1},{17,25},{25,17},{2,10},{10... | collective-permute-start | bytes 5505032 | tf_op jit(solution)/shard_map/ppermute | solution.py:28
  309.3 43.3 %collective-permute-start.22 = (bf16[64,7168]{1,0:T(8,128)(2,1)S(1)}, bf16[64,7168]{1,0:T(8,128)(2,1)S(1)}, u32[]{:S(2)}, u32[]{:S(2)}) collective-permute-start(bf16[64,7168]{1,0:T(8,128)(2,1)S(1)} %slice.192), channel_id=1, source_target_pairs={{0,16},{8,24},{16,0},{24,8},{1,17},{9,25},{17,1},{25,9},{2,18},{10... | collective-permute-start | bytes 2752520 | tf_op jit(solution)/shard_map/ppermute | solution.py:28
  312.5 38.5 %collective-permute-start.10 = (bf16[64,7168]{1,0:T(8,128)(2,1)S(1)}, bf16[64,7168]{1,0:T(8,128)(2,1)S(1)}, u32[]{:S(2)}, u32[]{:S(2)}) collective-permute-start(bf16[64,7168]{1,0:T(8,128)(2,1)S(1)} %slice.182), channel_id=1, source_target_pairs={{0,16},{8,24},{16,0},{24,8},{1,17},{9,25},{17,1},{25,9},{2,18},{10... | collective-permute-start | bytes 2752520 | tf_op jit(solution)/shard_map/ppermute | solution.py:28
  351.5 13.5 %collective-permute-start.11 = (bf16[4,64,896]{2,1,0:T(8,128)(2,1)S(1)}, bf16[4,64,896]{2,1,0:T(8,128)(2,1)S(1)}, u32[]{:S(2)}, u32[]{:S(2)}) collective-permute-start(bf16[4,64,896]{2,1,0:T(8,128)(2,1)S(1)} %pad_maximum_fusion.5), channel_id=1, source_target_pairs={{0,1},{1,0},{2,3},{3,2},{4,5},{5,4},{6,7},{7,6},{8,9},{9,8},{10,11... | collective-permute-start | bytes 1376264 | tf_op jit(solution)/shard_map/ppermute | solution.py:28
  352.9 19.9 %collective-permute-start.23 = (bf16[4,64,896]{2,1,0:T(8,128)(2,1)S(1)}, bf16[4,64,896]{2,1,0:T(8,128)(2,1)S(1)}, u32[]{:S(2)}, u32[]{:S(2)}) collective-permute-start(bf16[4,64,896]{2,1,0:T(8,128)(2,1)S(1)} %pad_maximum_fusion.10), channel_id=1, source_target_pairs={{0,1},{1,0},{2,3},{3,2},{4,5},{5,4},{6,7},{7,6},{8,9},{9,8},{10,11... | collective-permute-start | bytes 1376264 | tf_op jit(solution)/shard_map/ppermute | solution.py:28
  365.2 9.2 %collective-permute-start.12 = (bf16[2,64,896]{2,1,0:T(8,128)(2,1)S(1)}, bf16[2,64,896]{2,1,0:T(8,128)(2,1)S(1)}, u32[]{:S(2)}, u32[]{:S(2)}) collective-permute-start(bf16[2,64,896]{2,1,0:T(8,128)(2,1)S(1)} %pad_maximum_fusion.16), channel_id=1, source_target_pairs={{0,2},{1,3},{2,0},{3,1},{4,6},{5,7},{6,4},{7,5},{8,10},{9,11},{10,... | collective-permute-start | bytes 688136 | tf_op jit(solution)/shard_map/ppermute | solution.py:28
  373.0 8.8 %collective-permute-start.24 = (bf16[2,64,896]{2,1,0:T(8,128)(2,1)S(1)}, bf16[2,64,896]{2,1,0:T(8,128)(2,1)S(1)}, u32[]{:S(2)}, u32[]{:S(2)}) collective-permute-start(bf16[2,64,896]{2,1,0:T(8,128)(2,1)S(1)} %pad_maximum_fusion.17), channel_id=1, source_target_pairs={{0,2},{1,3},{2,0},{3,1},{4,6},{5,7},{6,4},{7,5},{8,10},{9,11},{10,... | collective-permute-start | bytes 688136 | tf_op jit(solution)/shard_map/ppermute | solution.py:28
  374.5 9.2 %collective-permute-start.13 = (bf16[1,64,896]{2,1,0:T(8,128)(2,1)S(1)}, bf16[1,64,896]{2,1,0:T(8,128)(2,1)S(1)}, u32[]{:S(2)}, u32[]{:S(2)}) collective-permute-start(bf16[1,64,896]{2,1,0:T(8,128)(2,1)S(1)} %add_convert_fusion.19), channel_id=1, source_target_pairs={{0,4},{1,5},{2,6},{3,7},{4,0},{5,1},{6,2},{7,3},{8,12},{9,13},{10,... | collective-permute-start | bytes 344072 | tf_op jit(solution)/shard_map/ppermute | solution.py:28
  381.8 11.4 %copy-start.7 = (bf16[1792,896]{1,0:T(8,128)(2,1)S(1)}, bf16[1792,896]{1,0:T(8,128)(2,1)}, u32[]{:S(2)}) copy-start(bf16[1792,896]{1,0:T(8,128)(2,1)} %weight_ref.3) | copy-start | bytes 9633796
  381.8 7.0 %collective-permute-start.25 = (bf16[1,64,896]{2,1,0:T(8,128)(2,1)S(1)}, bf16[1,64,896]{2,1,0:T(8,128)(2,1)S(1)}, u32[]{:S(2)}, u32[]{:S(2)}) collective-permute-start(bf16[1,64,896]{2,1,0:T(8,128)(2,1)S(1)} %add_convert_fusion.17), channel_id=1, source_target_pairs={{0,4},{1,5},{2,6},{3,7},{4,0},{5,1},{6,2},{7,3},{8,12},{9,13},{10,... | collective-permute-start | bytes 344072 | tf_op jit(solution)/shard_map/ppermute | solution.py:28
  383.8 5.6 %collective-permute-start.16 = (bf16[64,896]{1,0:T(8,128)(2,1)S(1)}, bf16[64,896]{1,0:T(8,128)(2,1)S(1)}, u32[]{:S(2)}, u32[]{:S(2)}) collective-permute-start(bf16[64,896]{1,0:T(8,128)(2,1)S(1)} %fusion.46), channel_id=1, source_target_pairs={{0,24},{8,16},{16,8},{24,0},{1,25},{9,17},{17,9},{25,1},{2,26},{10... | collective-permute-start | bytes 344072 | tf_op jit(solution)/shard_map/ppermute | solution.py:288
  383.9 7.2 %collective-permute-start.15 = (bf16[64,896]{1,0:T(8,128)(2,1)S(1)}, bf16[64,896]{1,0:T(8,128)(2,1)S(1)}, u32[]{:S(2)}, u32[]{:S(2)}) collective-permute-start(bf16[64,896]{1,0:T(8,128)(2,1)S(1)} %fusion.46), channel_id=1, source_target_pairs={{0,8},{8,0},{16,24},{24,16},{1,9},{9,1},{17,25},{25,17},{2,10},{10... | collective-permute-start | bytes 344072 | tf_op jit(solution)/shard_map/ppermute | solution.py:288
  383.9 7.1 %collective-permute-start.14 = (bf16[64,896]{1,0:T(8,128)(2,1)S(1)}, bf16[64,896]{1,0:T(8,128)(2,1)S(1)}, u32[]{:S(2)}, u32[]{:S(2)}) collective-permute-start(bf16[64,896]{1,0:T(8,128)(2,1)S(1)} %fusion.46), channel_id=1, source_target_pairs={{0,16},{8,24},{16,0},{24,8},{1,17},{9,25},{17,1},{25,9},{2,18},{10... | collective-permute-start | bytes 344072 | tf_op jit(solution)/shard_map/ppermute | solution.py:288
  388.9 7.0 %collective-permute-start.28 = (bf16[64,896]{1,0:T(8,128)(2,1)S(1)}, bf16[64,896]{1,0:T(8,128)(2,1)S(1)}, u32[]{:S(2)}, u32[]{:S(2)}) collective-permute-start(bf16[64,896]{1,0:T(8,128)(2,1)S(1)} %fusion.47), channel_id=1, source_target_pairs={{0,24},{8,16},{16,8},{24,0},{1,25},{9,17},{17,9},{25,1},{2,26},{10... | collective-permute-start | bytes 344072 | tf_op jit(solution)/shard_map/ppermute | solution.py:288
  388.9 6.9 %collective-permute-start.27 = (bf16[64,896]{1,0:T(8,128)(2,1)S(1)}, bf16[64,896]{1,0:T(8,128)(2,1)S(1)}, u32[]{:S(2)}, u32[]{:S(2)}) collective-permute-start(bf16[64,896]{1,0:T(8,128)(2,1)S(1)} %fusion.47), channel_id=1, source_target_pairs={{0,8},{8,0},{16,24},{24,16},{1,9},{9,1},{17,25},{25,17},{2,10},{10... | collective-permute-start | bytes 344072 | tf_op jit(solution)/shard_map/ppermute | solution.py:288
  389.4 6.4 %collective-permute-start.26 = (bf16[64,896]{1,0:T(8,128)(2,1)S(1)}, bf16[64,896]{1,0:T(8,128)(2,1)S(1)}, u32[]{:S(2)}, u32[]{:S(2)}) collective-permute-start(bf16[64,896]{1,0:T(8,128)(2,1)S(1)} %fusion.47), channel_id=1, source_target_pairs={{0,16},{8,24},{16,0},{24,8},{1,17},{9,25},{17,1},{25,9},{2,18},{10... | collective-permute-start | bytes 344072 | tf_op jit(solution)/shard_map/ppermute | solution.py:288
  404.3 47.5 %collective-permute-start.29 = (bf16[4,128,896]{2,1,0:T(8,128)(2,1)}, bf16[4,128,896]{2,1,0:T(8,128)(2,1)}, u32[]{:S(2)}, u32[]{:S(2)}) collective-permute-start(bf16[4,128,896]{2,1,0:T(8,128)(2,1)} %pad_maximum_fusion.3), channel_id=1, source_target_pairs={{0,1},{1,0},{2,3},{3,2},{4,5},{5,4},{6,7},{7,6},{8,9},{9,8},{10,11... | collective-permute-start | bytes 2752520 | tf_op jit(solution)/shard_map/ppermute | solution.py:28
  405.9 48.6 %collective-permute-start.17 = (bf16[4,128,896]{2,1,0:T(8,128)(2,1)}, bf16[4,128,896]{2,1,0:T(8,128)(2,1)}, u32[]{:S(2)}, u32[]{:S(2)}) collective-permute-start(bf16[4,128,896]{2,1,0:T(8,128)(2,1)} %pad_maximum_fusion.2), channel_id=1, source_target_pairs={{0,1},{1,0},{2,3},{3,2},{4,5},{5,4},{6,7},{7,6},{8,9},{9,8},{10,11... | collective-permute-start | bytes 2752520 | tf_op jit(solution)/shard_map/ppermute | solution.py:28
  423.7 25.2 %all-to-all-start.3 = ((f32[32,2,1024]{2,1,0:T(2,128)}), f32[32,2,1024]{2,1,0:T(2,128)S(1)}, u32[]{:S(2)}, u32[]{:S(2)}) async-start(f32[32,2,1024]{2,1,0:T(2,128)} %bitcast.224), calls=%async_computation.3 | async-start | bytes 524288 | tf_op jit(solution)/shard_map/all_to_all | solution.py:449
  454.0 13.4 %collective-permute-start.30 = (bf16[2,128,896]{2,1,0:T(8,128)(2,1)S(1)}, bf16[2,128,896]{2,1,0:T(8,128)(2,1)S(1)}, u32[]{:S(2)}, u32[]{:S(2)}) collective-permute-start(bf16[2,128,896]{2,1,0:T(8,128)(2,1)S(1)} %pad_maximum_fusion.14), channel_id=1, source_target_pairs={{0,2},{1,3},{2,0},{3,1},{4,6},{5,7},{6,4},{7,5},{8,10},{9,11},{10,... | collective-permute-start | bytes 1376264 | tf_op jit(solution)/shard_map/ppermute | solution.py:28
  456.0 25.2 %collective-permute-start.18 = (bf16[2,128,896]{2,1,0:T(8,128)(2,1)S(1)}, bf16[2,128,896]{2,1,0:T(8,128)(2,1)S(1)}, u32[]{:S(2)}, u32[]{:S(2)}) collective-permute-start(bf16[2,128,896]{2,1,0:T(8,128)(2,1)S(1)} %pad_maximum_fusion.9), channel_id=1, source_target_pairs={{0,2},{1,3},{2,0},{3,1},{4,6},{5,7},{6,4},{7,5},{8,10},{9,11},{10,... | collective-permute-start | bytes 1376264 | tf_op jit(solution)/shard_map/ppermute | solution.py:28
  467.5 46.1 %copy-start.60 = (f32[128]{0:T(128)S(1)}, f32[128]{0:T(128)}, u32[]{:S(2)}) copy-start(f32[128]{0:T(128)} %copy-done.59) | copy-start | bytes 1540
  467.5 46.1 %copy-start.65 = (f32[128]{0:T(128)S(1)}, f32[128]{0:T(128)}, u32[]{:S(2)}) copy-start(f32[128]{0:T(128)} %get-tuple-element.134) | copy-start | bytes 1540
  467.5 13.9 %collective-permute-start.31 = (bf16[1,128,896]{2,1,0:T(8,128)(2,1)S(1)}, bf16[1,128,896]{2,1,0:T(8,128)(2,1)S(1)}, u32[]{:S(2)}, u32[]{:S(2)}) collective-permute-start(bf16[1,128,896]{2,1,0:T(8,128)(2,1)S(1)} %add_convert_fusion.8), channel_id=1, source_target_pairs={{0,4},{1,5},{2,6},{3,7},{4,0},{5,1},{6,2},{7,3},{8,12},{9,13},{10,... | collective-permute-start | bytes 688136 | tf_op jit(solution)/shard_map/ppermute | solution.py:28
  481.3 34.1 %copy-start.62 = (f32[128]{0:T(128)S(1)}, f32[128]{0:T(128)}, u32[]{:S(2)}) copy-start(f32[128]{0:T(128)} %copy-done.61) | copy-start | bytes 1540
  481.3 34.1 %copy-start.66 = (f32[128]{0:T(128)S(1)}, f32[128]{0:T(128)}, u32[]{:S(2)}) copy-start(f32[128]{0:T(128)} %get-tuple-element.136) | copy-start | bytes 1540
  481.3 11.9 %collective-permute-start.19 = (bf16[1,128,896]{2,1,0:T(8,128)(2,1)S(1)}, bf16[1,128,896]{2,1,0:T(8,128)(2,1)S(1)}, u32[]{:S(2)}, u32[]{:S(2)}) collective-permute-start(bf16[1,128,896]{2,1,0:T(8,128)(2,1)S(1)} %add_convert_fusion.10), channel_id=1, source_target_pairs={{0,4},{1,5},{2,6},{3,7},{4,0},{5,1},{6,2},{7,3},{8,12},{9,13},{10,... | collective-permute-start | bytes 688136 | tf_op jit(solution)/shard_map/ppermute | solution.py:28
  481.5 27.2 %collective-permute-start.32 = (bf16[128,896]{1,0:T(8,128)(2,1)S(1)}, bf16[128,896]{1,0:T(8,128)(2,1)S(1)}, u32[]{:S(2)}, u32[]{:S(2)}) collective-permute-start(bf16[128,896]{1,0:T(8,128)(2,1)S(1)} %fusion.45), channel_id=1, source_target_pairs={{0,0},{1,1},{2,8},{3,9},{4,16},{5,17},{6,24},{7,25},{8,2},{9,3},{1... | collective-permute-start | bytes 688136 | tf_op jit(solution)/shard_map/ppermute | solution.py:389
  493.3 20.2 %collective-permute-start.20 = (bf16[128,896]{1,0:T(8,128)(2,1)S(1)}, bf16[128,896]{1,0:T(8,128)(2,1)S(1)}, u32[]{:S(2)}, u32[]{:S(2)}) collective-permute-start(bf16[128,896]{1,0:T(8,128)(2,1)S(1)} %fusion.44), channel_id=1, source_target_pairs={{0,0},{1,1},{2,8},{3,9},{4,16},{5,17},{6,24},{7,25},{8,2},{9,3},{1... | collective-permute-start | bytes 688136 | tf_op jit(solution)/shard_map/ppermute | solution.py:389
  (59 other events, 200.3 us)
Sparse Core Ops, SparseCore 0:
  64.3 61.7 all-gather.4
  129.6 59.3 all-gather.6

commit v5 on v3

v5 whole, which is shorter than its diff:
```python
import jax
import jax.numpy as jnp
from jax import lax
from jax.experimental import pallas as pl
from jax.experimental.pallas import tpu as pltpu
from jax.sharding import PartitionSpec as P

EPSILON = 1e-06
TILE = 256
F32 = jnp.float32
BF16 = jnp.bfloat16


class Dim:
    def __init__(self, axis, size, n, stride):
        self.axis, self.size, self.n, self.stride = axis, size, n, stride

    def place(self):
        return (lax.axis_index(self.axis) // self.stride) % self.n

    def move(self, value, target):
        pairs = []
        for index in range(self.size):
            here = (index // self.stride) % self.n
            there = target(here)
            if there is not None and 0 <= there < self.n:
                pairs.append((index, index + (there - here) * self.stride))
        return lax.ppermute(value, self.axis, pairs)

    def swap(self, value, bit):
        return self.move(value, lambda here: here ^ bit)

    def turn(self, value, by):
        return self.move(value, lambda here: (here + by) % self.n)


def exchange_near(chunks, dim):
    here = dim.place()
    pick = [lax.dynamic_index_in_dim(chunks, here ^ bit, 0, keepdims=False) for bit in range(4)]
    got = dim.swap(jnp.stack([pick[1], pick[3]]), 1).astype(F32)
    return pick[0].astype(F32) + got[0], (pick[2].astype(F32) + got[1]).astype(BF16)


def exchange_far(pair, dim):
    near, far = pair
    return (near + dim.swap(far, 2).astype(F32)).astype(BF16)


def sum_everywhere(value):
    axes = ("ctx", "vocab")
    count = lax.axis_size("ctx") * lax.axis_size("vocab")
    copies = jnp.broadcast_to(value[None], (count,) + value.shape)
    return jnp.sum(lax.all_to_all(copies, axes, 0, 0, tiled=True), axis=0)


def contract_first(left, right):
    return lax.dot_general(left, right, (((0,), (0,)), ((), ())), preferred_element_type=F32)


def contract_last(left, right):
    return lax.dot_general(left, right, (((1,), (1,)), ((), ())), preferred_element_type=F32)


def whole_block(shape):
    return pl.BlockSpec(shape, lambda *step: (0,) * len(shape), pipeline_mode=pl.Buffered(1))


def kernel_call(body, grid, in_specs, out_specs, out_shape, flops, moved, exps=0):
    return pl.pallas_call(
        body,
        grid=grid,
        in_specs=in_specs,
        out_specs=out_specs,
        out_shape=out_shape,
        compiler_params=pltpu.CompilerParams(vmem_limit_bytes=48 * 1024 * 1024),
        cost_estimate=pl.CostEstimate(flops=flops, bytes_accessed=moved, transcendentals=exps),
    )


def head_gradient(grad, rows_all, span, after, base=None):
    tokens, entries = grad.shape
    width = rows_all.shape[1]
    chunk = 1024
    begin, end = span
    extra = ([] if base is None else [base]) + list(after)

    def body(grad_ref, rows_ref, *rest):
        out_ref, mark_ref = rest[-2:]
        for start in range(0, width, chunk):
            part = contract_first(grad_ref[...], rows_ref[:, start : start + chunk])
            out_ref[:, start : start + chunk] = part.astype(BF16)
        mark_ref[...] = jnp.zeros_like(mark_ref)

    return pl.pallas_call(
        body,
        grid=(end - begin,),
        in_specs=[
            pl.BlockSpec((tokens, TILE), lambda step: (0, step + begin)),
            whole_block((tokens, width)),
        ]
        + [pl.BlockSpec(memory_space=pl.ANY)] * len(extra),
        out_specs=[
            pl.BlockSpec((TILE, width), lambda step: (step + begin, 0)),
            pl.BlockSpec((8, 128), lambda step: (0, 0)),
        ],
        out_shape=[
            jax.ShapeDtypeStruct((entries, width), BF16),
            jax.ShapeDtypeStruct((8, 128), F32),
        ],
        input_output_aliases={} if base is None else {2: 0},
        compiler_params=pltpu.CompilerParams(vmem_limit_bytes=48 * 1024 * 1024),
        cost_estimate=pl.CostEstimate(
            flops=2 * tokens * width * TILE * (end - begin),
            bytes_accessed=2 * width * TILE * (end - begin) + 2 * tokens * width,
            transcendentals=0,
        ),
    )(grad, rows_all, *extra)


def add_after(left, right, after):
    def body(*refs):
        total = refs[0][...].astype(F32) + refs[1][...].astype(F32)
        refs[-1][...] = total.astype(BF16)

    return kernel_call(
        body,
        (1,),
        [whole_block(left.shape)] * 2 + [pl.BlockSpec(memory_space=pl.ANY)] * len(after),
        whole_block(left.shape),
        jax.ShapeDtypeStruct(left.shape, BF16),
        left.size,
        8 * left.size,
    )(left, right, *after)


def held_back(value, after):
    def body(*refs):
        refs[-1][...] = refs[0][...]

    return kernel_call(
        body,
        (1,),
        [whole_block(value.shape)] + [pl.BlockSpec(memory_space=pl.ANY)] * len(after),
        whole_block(value.shape),
        jax.ShapeDtypeStruct(value.shape, value.dtype),
        0,
        2 * value.size * value.dtype.itemsize,
    )(value, *after)


def weight_gradient(normed, proj_grad, weight):
    tokens, feat = normed.shape
    cols = proj_grad.shape[1]
    tile = 256 if feat % 256 == 0 else 128

    def body(normed_ref, grad_ref, weight_ref, out_ref, sum_ref):
        grad = contract_first(normed_ref[...], grad_ref[...])
        out_ref[...] = grad.astype(BF16)
        total = jnp.sum(grad * weight_ref[...].astype(F32), axis=1, keepdims=True)
        sum_ref[...] = jnp.broadcast_to(total, sum_ref.shape)

    out, sums = kernel_call(
        body,
        (feat // tile,),
        [
            pl.BlockSpec((tokens, tile), lambda step: (0, step)),
            whole_block((tokens, cols)),
            pl.BlockSpec((tile, cols), lambda step: (step, 0)),
        ],
        [
            pl.BlockSpec((tile, cols), lambda step: (step, 0)),
            pl.BlockSpec((tile, 128), lambda step: (step, 0)),
        ],
        [
            jax.ShapeDtypeStruct((feat, cols), BF16),
            jax.ShapeDtypeStruct((feat, 128), F32),
        ],
        2 * tokens * feat * cols,
        4 * feat * cols + 2 * tokens * (feat + cols),
    )(normed, proj_grad, weight)
    return out, sums[:, 0]


def dot(left, right):
    return jnp.dot(left, right, preferred_element_type=F32)


def cut(array, start, width, axis):
    return lax.dynamic_slice_in_dim(array, start, width, axis)


def local(
    hidden_state,
    embedded_next,
    gain_hidden,
    gain_embed,
    proj_hidden,
    proj_embed,
    final_gain,
    head,
    targets,
    loss_mask,
):
    nc, nv = lax.axis_size("ctx"), lax.axis_size("vocab")
    nx, va = nc // 2, 4
    vb = nv // va
    core = Dim("ctx", nc, 2, 1)
    dim_x = Dim("ctx", nc, nx, 2)
    dim_b = Dim("vocab", nv, vb, 1)
    dim_a = Dim("vocab", nv, va, vb)
    own, slot = lax.axis_index("ctx"), lax.axis_index("vocab")
    x, c, b = own // 2, own % 2, slot % vb

    width = hidden_state.shape[1]
    block = hidden_state.shape[0]
    token_total = targets.shape[0]
    feat, cols = proj_hidden.shape
    half = block // 2
    near = nx * block
    vocab_local = head.shape[0]

    def relative_place(block_index):
        return (c ^ (block_index % 2)) * nx + (x - block_index // 2) % nx

    def block_at(place):
        return ((x - place % nx) % nx) * 2 + (c ^ (place // nx))

    order = jnp.stack([relative_place(jnp.int32(i)) for i in range(nc)])
    to_absolute = (order[:, None] == jnp.arange(nc, dtype=jnp.int32)[None, :])[:, :, None]

    def absolute(value):
        value = value.reshape(value.shape[:-1] + (1, nc, block))
        return jnp.sum(jnp.where(to_absolute, value, 0), axis=-2)

    def relative(value):
        value = jnp.sum(jnp.where(to_absolute, value[..., :, None, :], 0), axis=-3)
        return value.reshape(value.shape[:-2] + (token_total,))

    places = [(rc, rx) for rc in range(2) for rx in range(nx)]

    def send(value, rc, rx):
        pairs = []
        for i in range(nc):
            pairs.append((i, ((i // 2 + rx) % nx) * 2 + ((i % 2) ^ rc)))
        return lax.ppermute(value, "ctx", pairs)

    def scale_of(wide):
        wide = wide.astype(F32)
        return lax.rsqrt(jnp.mean(wide * wide, axis=-1, keepdims=True) + EPSILON)

    def normed_blocks(wide, scale, gain):
        def piece(rc, rx):
            start = (((x + rx) % nx) * 2 + (c ^ rc)) * feat
            value = cut(wide, start, feat, 1).astype(F32)
            return (value * scale * cut(gain, start, feat, 0)).astype(BF16)

        far = {(rc, rx): send(piece(rc, rx), rc, rx) for rx in range(1, nx) for rc in range(2)}
        far[1, 0] = send(piece(1, 0), 1, 0)
        far[0, 0] = piece(0, 0)
        return [far[place] for place in places]

    hidden_scale, embed_scale = scale_of(hidden_state), scale_of(embedded_next)
    blocks_h = normed_blocks(hidden_state, hidden_scale, gain_hidden)
    blocks_e = normed_blocks(embedded_next, embed_scale, gain_embed)

    halves_h = [dot(piece, proj_hidden) for piece in blocks_h]
    halves_e = [dot(piece, proj_embed) for piece in blocks_e]
    projected = halves_h[0] + halves_e[0]
    for index, (rc, rx) in enumerate(places[1:], 1):
        term = (halves_h[index] + halves_e[index]).astype(BF16)
        projected = projected + send(term, rc, (nx - rx) % nx).astype(F32)

    piece = (projected * final_gain).astype(BF16)
    squares = jnp.sum(projected * projected, axis=-1)
    squares = lax.all_to_all(
        jnp.broadcast_to(squares, (nc * nv, block)), ("ctx", "vocab"), 0, 0, tiled=True
    )
    squares = jnp.sum(squares.reshape(nc, nv, block), axis=1)
    row_scale = relative(lax.rsqrt(squares / width + EPSILON))
    pieces = lax.all_gather(piece, ("ctx", "vocab")).reshape(nc, nv, block, cols)
    gathered = jnp.concatenate(
        [
            lax.dynamic_index_in_dim(pieces, block_at(place), 0, keepdims=False)
            .transpose(1, 0, 2)
            .reshape(block, width)
            for place in range(nc)
        ]
    )

    vocab_ids = (own * nv + slot) * vocab_local + lax.iota(jnp.int32, vocab_local)
    logits = contract_last(gathered, head) * row_scale[:, None]
    target = relative(targets.reshape(nc, block))
    mask_weight = loss_mask.astype(F32).reshape(nc, block)
    mask = relative(mask_weight)
    is_target = target[:, None] == vocab_ids[None, :]
    power = jnp.exp(logits)
    sums = jnp.stack(
        [
            jnp.sum(power, axis=-1),
            jnp.sum(power * (logits * F32(1.0 / 256.0)), axis=-1),
            jnp.sum(jnp.where(is_target, logits, F32(0.0)), axis=-1),
        ]
    )
    exp_total, weighted, target_logit = sum_everywhere(absolute(sums))
    log_total = jnp.log(exp_total)
    mean_loss = jnp.sum(mask_weight * (log_total - target_logit)) / token_total
    scaled_dot = mask * relative(weighted / exp_total * F32(256.0) - target_logit)
    probs = jnp.exp(logits - relative(log_total)[:, None])
    scaled_grad = ((mask * row_scale)[:, None] * (probs - is_target.astype(F32))).astype(BF16)
    coefficient = row_scale * row_scale * scaled_dot / width

    def column_chunk(value, place):
        return jnp.stack([cut(value, (p * vb + place) * cols, cols, 1) for p in range(va)])

    theirs = core.swap(dot(scaled_grad[near:], head).astype(BF16), 1)
    mine = lax.optimization_barrier(dot(scaled_grad[:near], head).astype(BF16))
    mine = (mine.astype(F32) + theirs.astype(F32)).astype(BF16)
    mine = mine.reshape(nx, block, width)
    first_sends = [mine[r, :half] for r in range(1, nx)]
    last = mine[:, half:].reshape(nx * half, width)
    last_sends = [column_chunk(last, (b + r) % vb) for r in range(1, vb)]
    first_got = [dim_x.turn(value, -r) for r, value in enumerate(first_sends, 1)]
    last = column_chunk(last, b).astype(F32)
    for r, value in enumerate(last_sends, 1):
        last = last + dim_b.turn(value, r).astype(F32)
    tiles = vocab_local // TILE
    most = max(1, tiles * 3 // 4)
    grad_head, mark = head_gradient(scaled_grad, gathered, (0, most), first_sends + last_sends)
    first = add_after(mine[0, :half], first_got[0], [mark])
    for value in first_got[1:]:
        first = (first.astype(F32) + value.astype(F32)).astype(BF16)
    kept = column_chunk(first, b).astype(F32)
    second_sends = [column_chunk(first, (b + r) % vb) for r in range(1, vb)]
    for r, value in enumerate(second_sends, 1):
        kept = kept + dim_b.turn(value, r).astype(F32)
    first = kept.astype(BF16)
    last = last.astype(BF16).reshape(va, nx, half, cols)
    kept = last[:, 0].astype(F32)
    for r in range(1, nx):
        kept = kept + dim_x.turn(last[:, r], -r).astype(F32)
    grad_head, mark = head_gradient(
        scaled_grad, gathered, (most, tiles), second_sends, base=grad_head
    )
    summed = jnp.concatenate([first, kept.astype(BF16)], axis=1)
    summed = exchange_far(exchange_near(summed, dim_a), dim_a)
    scaled = jnp.concatenate([summed] + [send(summed, rc, rx) for rc, rx in places[1:]])
    scaled = scaled.astype(F32)

    plain = cut(gathered, slot * cols, cols, 1).astype(F32) / final_gain
    grad_final_gain = jnp.sum(scaled * plain, axis=0)
    proj_grad = (scaled * final_gain - plain * coefficient[:, None]).astype(BF16)

    def final_move(value):
        pairs = []
        ratio = nv // nc
        for i in range(nc):
            for j in range(nv):
                pairs.append((i * nv + j, (j // ratio) * nv + i * ratio + j % ratio))
        return lax.ppermute(value, ("ctx", "vocab"), pairs)

    def products(weight, place):
        picked = jnp.concatenate(
            [
                cut(proj_grad, relative_place((p * vb + place) // 2) * block, block, 0)
                for p in range(va)
            ]
        )
        weight_half = cut(weight, (place % 2) * cols, cols, 0)
        return contract_last(picked, weight_half).reshape(va, block, cols)

    def exchanged(weight):
        return [dim_b.swap(products(weight, b ^ r).astype(BF16), r) for r in range(1, vb)]

    got_h, got_e = exchanged(proj_hidden), exchanged(proj_embed)
    kept_h = products(proj_hidden, b)
    for value in got_h:
        kept_h = kept_h + value.astype(F32)
    pair_h = exchange_near(kept_h.astype(BF16), dim_a)
    kept_e = products(proj_embed, b)
    for value in got_e[1:]:
        kept_e = kept_e + value.astype(F32)
    kept_e = add_after(kept_e, got_e[0], [pair_h[1]])
    hidden_moved = final_move(exchange_far(pair_h, dim_a))
    pair_e = exchange_near(kept_e, dim_a)
    hidden_back = hidden_moved.astype(F32)
    embed_back = final_move(exchange_far(pair_e, dim_a)).astype(F32)

    grad_proj_hidden, gain_h = weight_gradient(jnp.concatenate(blocks_h), proj_grad, proj_hidden)
    grad_proj_embed, gain_e = weight_gradient(jnp.concatenate(blocks_e), proj_grad, proj_embed)

    wide = proj_grad.astype(F32).reshape(nc, block, cols)
    dots = jnp.stack(
        [jnp.sum(wide * jnp.stack(halves), axis=-1) for halves in (halves_h, halves_e)]
    )
    dots = jnp.sum(jnp.where(to_absolute, dots[:, None], 0), axis=2)
    dots = jnp.broadcast_to(dots.transpose(1, 0, 2)[:, None], (nc, nv, 2, block))
    gains = jnp.stack([gain_h, gain_e])
    ratio = nv // nc
    gains = gains.reshape(2, ratio, cols).transpose(1, 0, 2)[None]
    holder = jnp.arange(nc, dtype=jnp.int32)[:, None, None, None] == own
    gains = jnp.where(holder, gains, F32(0.0)).reshape(nv, 2, cols)
    gains = jnp.broadcast_to(gains[None], (nc, nv, 2, cols))
    ends = jnp.concatenate([dots, gains], axis=-1).reshape(nc * nv, 2, block + cols)
    ends = held_back(ends, [hidden_moved, pair_e[1]])
    ends = jnp.sum(lax.all_to_all(ends, ("ctx", "vocab"), 0, 0, tiled=True), axis=0)

    def finish(kind, source, gain):
        back_all = (hidden_back, embed_back)[kind]
        scale = (hidden_scale, embed_scale)[kind]
        dot_all = ends[kind, :block][:, None]
        source = cut(source, slot * cols, cols, 1).astype(F32)
        gain = cut(gain, slot * cols, cols, 0)
        grad = scale * (back_all * gain) - source * (scale * scale) * (dot_all / width)
        return grad.astype(BF16), ends[kind, block:] / gain

    grad_hidden, grad_gain_hidden = finish(0, hidden_state, gain_hidden)
    grad_embed, grad_gain_embed = finish(1, embedded_next, gain_embed)
    return (
        mean_loss,
        grad_hidden,
        grad_embed,
        grad_gain_hidden,
        grad_gain_embed,
        grad_proj_hidden,
        grad_proj_embed,
        grad_final_gain,
        grad_head,
    )


def solution(mesh):
    in_specs = (
        P("ctx", None),
        P("ctx", None),
        P(),
        P(),
        P("ctx", "vocab"),
        P("ctx", "vocab"),
        P("vocab"),
        P(("ctx", "vocab"), None),
        P(),
        P(),
    )
    out_specs = (
        P(),
        P("ctx", "vocab"),
        P("ctx", "vocab"),
        P("vocab"),
        P("vocab"),
        P("ctx", "vocab"),
        P("ctx", "vocab"),
        P("vocab"),
        P(("ctx", "vocab"), None),
    )
    return jax.shard_map(local, mesh=mesh, in_specs=in_specs, out_specs=out_specs, check_vma=False)
```

time: 497 us -> 426 us (0.86)
  local copies, waits for them, and re-layouts: 61.8 us -> 14.5 us
  Pallas kernels: 0 us -> 43.6 us
  waiting for transfers between devices: 233 us -> 192 us
  matrix products: 101 us -> 69.9 us
  other arithmetic: 31.3 us -> 38.9 us
    ppermute x30 -> x13, waiting for transfers between devices: 156 us -> 50.5 us  [move(): return lax.ppermute(value, self.axis, pairs)]
    ppermute x0 -> x12, waiting for transfers between devices: none -> 47.1 us  [send(): return lax.ppermute(value, 'ctx', pairs)]
    pallas_call x0 -> x7, Pallas kernels: none -> 43.6 us  [the longest x2 27.2 us: head_gradient(): pl.pallas_call(body, grid=(end - begin,), in_specs=[pl.BlockSpec((tokens,...]
    unnamed x119 -> x129, local copies, waits for them, and re-layouts: 39.6 us -> 4.64 us
    dot_general x3 -> x0, matrix products: 31.2 us -> none  [contract_first(): lax.dot_general(left, right, (((0,), (0,)), ((), ())), preferred_element_...]
    dynamic_slice x9 -> x3, local copies, waits for them, and re-layouts: 10.2 us -> 2 us  [cut(): return lax.dynamic_slice_in_dim(array, start, width, axis)]
    ppermute x2, waiting for transfers between devices: 13 us -> 19.6 us  [final_move(): return lax.ppermute(value, ('ctx', 'vocab'), pairs)]
    convert_element_type x19 -> x17, other arithmetic: 9.53 us -> 15.9 us  [the longest x1 3.39 us: local(): mine = (mine.astype(F32) + theirs.astype(F32)).astype(BF16)]
  transfers between devices with their start and end apart: 36 -> 31, of which waited for: 20 -> 21; matrix products, arithmetic and copies ran while one was open for 15% -> 12% of each run, Pallas kernels for 0% -> 10%
where the time goes in v5:
time: 426 us; the launch traced here: 419 us
  waiting for transfers between devices  192 us (45%)
  matrix products  69.9 us (16%)
  Pallas kernels  43.6 us (10%)
  starting transfers between devices  42.7 us (10%)
  other arithmetic  38.9 us (9%)
  between operations  17.3 us (4%)
  local copies, waits for them, and re-layouts  14.5 us (3%)
    all_gather x1, waiting for transfers between devices, local(): lax.all_gather(piece, ('ctx', 'vocab')).reshape(nc, nv, block, cols)  61.2 us
    ppermute x13, waiting for transfers between devices, move(): return lax.ppermute(value, self.axis, pairs)  50.5 us
    ppermute x12, waiting for transfers between devices, send(): return lax.ppermute(value, 'ctx', pairs)  47.1 us
    dot_general x10, matrix products, dot(): return jnp.dot(left, right, preferred_element_type=F32)  35.4 us
    dot_general x5, matrix products, contract_last(): lax.dot_general(left, right, (((1,), (1,)), ((), ())), preferred_element_...  34.5 us
    pallas_call x2, Pallas kernels, head_gradient(): pl.pallas_call(body, grid=(end - begin,), in_specs=[pl.BlockSpec((tokens,...  27.2 us
    ppermute x2, waiting for transfers between devices, final_move(): return lax.ppermute(value, ('ctx', 'vocab'), pairs)  19.6 us
    ppermute x13, starting transfers between devices, move(): return lax.ppermute(value, self.axis, pairs)  15.9 us
  transfers between devices with their start and end apart: 31, of which 21 were waited for; matrix products, arithmetic and copies ran while one was open for 12% of the time, Pallas kernels for 10%

profile of v5, /device:TPU:2, one launch (start us, length us, event | category | flops | bytes accessed | tf_op | source)
XLA Modules:
  0.0 418.5 jit_solution(3594582488814574966)
XLA Ops:
  7.3 1.9 multiply_reduce_fusion.1
  10.7 2.0 multiply_convert_fusion.6
  14.3 1.8 collective-permute-start.6
  17.3 8.2 %collective-permute-done.7 = bf16[128,1792]{1,0:T(8,128)(2,1)S(1)} collective-permute-done((bf16[128,1792]{1,0:T(8,128)(2,1)S(1)}, bf16[128,1792]{1,0:T(8,128)(2,1)S(1)}, u32[]{:S(2)}, u32[]{:S(2)}) %collective-permute-start.7) | collective-permute-done | bytes 458784 | tf_op jit(solution)/shard_map/ppermute | solution.py:245
  26.2 9.1 %collective-permute-done.6 = bf16[128,1792]{1,0:T(8,128)(2,1)S(1)} collective-permute-done((bf16[128,1792]{1,0:T(8,128)(2,1)S(1)}, bf16[128,1792]{1,0:T(8,128)(2,1)S(1)}, u32[]{:S(2)}, u32[]{:S(2)}) %collective-permute-start.6) | collective-permute-done | bytes 458784 | tf_op jit(solution)/shard_map/ppermute | solution.py:245
  39.2 6.0 %collective-permute-done.1 = bf16[128,1792]{1,0:T(8,128)(2,1)S(1)} collective-permute-done((bf16[128,1792]{1,0:T(8,128)(2,1)S(1)}, bf16[128,1792]{1,0:T(8,128)(2,1)S(1)}, u32[]{:S(2)}, u32[]{:S(2)}) %collective-permute-start.1) | collective-permute-done | bytes 458784 | tf_op jit(solution)/shard_map/ppermute | solution.py:245
  45.9 9.2 %collective-permute-done = bf16[128,1792]{1,0:T(8,128)(2,1)S(1)} collective-permute-done((bf16[128,1792]{1,0:T(8,128)(2,1)S(1)}, bf16[128,1792]{1,0:T(8,128)(2,1)S(1)}, u32[]{:S(2)}, u32[]{:S(2)}) %collective-permute-start) | collective-permute-done | bytes 458784 | tf_op jit(solution)/shard_map/ppermute | solution.py:245
  57.8 2.1 collective-permute-done.8
  59.9 4.9 %collective-permute-done.2 = bf16[128,896]{1,0:T(8,128)(2,1)S(1)} collective-permute-done((bf16[128,896]{1,0:T(8,128)(2,1)S(1)}, bf16[128,896]{1,0:T(8,128)(2,1)S(1)}, u32[]{:S(2)}, u32[]{:S(2)}) %collective-permute-start.2) | collective-permute-done | bytes 229408 | tf_op jit(solution)/shard_map/ppermute | solution.py:245
  66.7 6.8 %all-to-all-start = ((f32[32,1,128]{2,1,0:T(1,128)}), f32[32,1,128]{2,1,0:T(1,128)S(1)}, u32[]{:S(2)}, u32[]{:S(2)}) async-start(f32[32,1,128]{2,1,0:T(1,128)} %broadcast_in_dim.190), calls=%async_computation | async-start | bytes 32768 | tf_op jit(solution)/shard_map/all_to_all | solution.py:275
  73.5 5.7 %all-to-all-done = f32[32,1,128]{2,1,0:T(1,128)S(1)} async-done(((f32[32,1,128]{2,1,0:T(1,128)}), f32[32,1,128]{2,1,0:T(1,128)S(1)}, u32[]{:S(2)}, u32[]{:S(2)}) %all-to-all-start) | async-done | bytes 16416 | tf_op jit(solution)/shard_map/all_to_all | solution.py:275
  79.4 61.2 %all-gather.3.cloned.1.call-done = bf16[4096,896]{1,0:T(8,128)(2,1)} async-done(((bf16[128,896]{1,0:T(8,128)(2,1)}), bf16[4096,896]{1,0:T(8,128)(2,1)}) %all-gather.3.cloned.1.call-update) | async-done | bytes 7340048 | tf_op jit(solution)/shard_map/all_gather | solution.py:280
  140.6 4.0 constant_dynamic-slice_fusion.12
  146.3 23.9 %exponential_reduce_fusion = (f32[512]{0:T(512)S(1)}, f32[512]{0:T(512)S(1)}, f32[512]{0:T(512)S(1)}, f32[512,2048]{1,0:T(8,128)}) fusion(f32[512]{0:T(512)S(1)} %bitcast.210, s32[2048]{0:T(1024)S(1)} %iota_add_fusion, s32[512]{0:T(512)S(1)} %bitcast.214, bf16[512,7168]{1,0:T(8,128)(2,1)S(1)} %constant_dynamic-update-slice_fusion.rows_ref, ...), kind=kOutput, calls=%fused_computation.10 | convolution fusion | flops 15040774144 | bytes 40912896 | tf_op jit(solution)/shard_map/dot_general | solution.py:61
  171.0 4.0 all-to-all-start.1
  175.0 7.5 %all-to-all-done.1 = f32[32,3,4,128]{3,2,1,0:T(4,128)S(1)} async-done(((f32[32,3,4,128]{3,2,1,0:T(4,128)}), f32[32,3,4,128]{3,2,1,0:T(4,128)S(1)}, u32[]{:S(2)}, u32[]{:S(2)}) %all-to-all-start.1) | async-done | bytes 196640 | tf_op jit(solution)/shard_map/all_to_all | solution.py:53
  182.7 3.2 fusion.3.grad_ref
  185.9 14.5 %convolution_convert_fusion = bf16[256,7168]{1,0:T(8,128)(2,1)} fusion(bf16[2048,7168]{1,0:T(8,128)(2,1)} %param.17, bf16[512,2048]{1,0:T(8,128)(2,1)S(1)} %fusion.3.grad_ref), kind=kOutput, calls=%fused_computation | convolution fusion | flops 7518027776 | bytes 34078720 | tf_op jit(solution)/shard_map/dot_general | solution.py:185
  201.2 13.3 %convolution_convert_fusion.1 = bf16[256,7168]{1,0:T(8,128)(2,1)S(1)} fusion(bf16[2048,7168]{1,0:T(8,128)(2,1)} %param.17, bf16[512,2048]{1,0:T(8,128)(2,1)S(1)} %fusion.3.grad_ref), kind=kOutput, calls=%fused_computation.1 | convolution fusion | flops 7518027776 | bytes 34078720 | tf_op jit(solution)/shard_map/dot_general | solution.py:185
  214.5 3.4 add_convert_fusion
  219.2 1.8 collective-permute-start.12
  221.0 17.9 %shard_map.169 = (bf16[2048,7168]{1,0:T(8,128)(2,1)}, f32[8,128]{1,0:T(8,128)S(1)}) custom-call(bf16[512,2048]{1,0:T(8,128)(2,1)S(1)} %fusion.3.grad_ref, bf16[512,7168]{1,0:T(8,128)(2,1)} %copy-done.8, bf16[64,7168]{1,0:T(8,128)(2,1)S(1)} %get-tuple-element.45.rest_0_, bf16[4,128,896]{2,1,0:T(8,128)(2,1)S(1)} %pad_maximum_fusion.4.rest_1_), custom_call_target="tpu_custom_call" | custom-call | flops 11274289152 | bytes 29360128 | tf_op jit(solution)/shard_map/pallas_call | solution.py:94
  238.9 2.7 collective-permute-done.12
  245.6 7.9 %collective-permute-done.13 = bf16[4,64,896]{2,1,0:T(8,128)(2,1)S(1)} collective-permute-done((bf16[4,64,896]{2,1,0:T(8,128)(2,1)S(1)}, bf16[4,64,896]{2,1,0:T(8,128)(2,1)S(1)}, u32[]{:S(2)}, u32[]{:S(2)}) %collective-permute-start.13) | collective-permute-done | bytes 458784 | tf_op jit(solution)/shard_map/ppermute | solution.py:28
  259.7 9.1 %collective-permute-done.14 = bf16[2,128,896]{2,1,0:T(8,128)(2,1)} collective-permute-done((bf16[2,128,896]{2,1,0:T(8,128)(2,1)}, bf16[2,128,896]{2,1,0:T(8,128)(2,1)}, u32[]{:S(2)}, u32[]{:S(2)}) %collective-permute-start.14) | collective-permute-done | bytes 458784 | tf_op jit(solution)/shard_map/ppermute | solution.py:28
  270.0 1.9 collective-permute-start.15
  272.3 8.4 %collective-permute-done.15 = bf16[128,896]{1,0:T(8,128)(2,1)S(1)} collective-permute-done((bf16[128,896]{1,0:T(8,128)(2,1)S(1)}, bf16[128,896]{1,0:T(8,128)(2,1)S(1)}, u32[]{:S(2)}, u32[]{:S(2)}) %collective-permute-start.15) | collective-permute-done | bytes 229408 | tf_op jit(solution)/shard_map/ppermute | solution.py:28
  284.4 4.4 %collective-permute-done.18 = bf16[128,896]{1,0:T(8,128)(2,1)S(1)} collective-permute-done((bf16[128,896]{1,0:T(8,128)(2,1)S(1)}, bf16[128,896]{1,0:T(8,128)(2,1)S(1)}, u32[]{:S(2)}, u32[]{:S(2)}) %collective-permute-start.18) | collective-permute-done | bytes 229408 | tf_op jit(solution)/shard_map/ppermute | solution.py:245
  288.8 3.1 collective-permute-done.16
  291.9 3.3 fusion.7
  297.8 2.2 fusion.17
  299.9 2.1 collective-permute-start.19
  304.7 4.1 fusion.20
  308.9 7.4 %shard_map.172 = (bf16[1792,896]{1,0:T(8,128)(2,1)}, f32[1792,128]{1,0:T(8,128)S(1)}) custom-call(bf16[512,1792]{1,0:T(8,128)(2,1)S(1)} %copy-done, bf16[512,896]{1,0:T(8,128)(2,1)S(1)} %get-tuple-element.37.grad_ref, bf16[1792,896]{1,0:T(8,128)(2,1)} %weight_ref.3), custom_call_target="tpu_custom_call" | custom-call | flops 1644167168 | bytes 9175040 | tf_op jit(solution)/shard_map/pallas_call | solution.py:162
  316.7 7.4 %shard_map.171 = (bf16[1792,896]{1,0:T(8,128)(2,1)}, f32[1792,128]{1,0:T(8,128)S(1)}) custom-call(bf16[512,1792]{1,0:T(8,128)(2,1)S(1)} %copy-done.1, bf16[512,896]{1,0:T(8,128)(2,1)S(1)} %get-tuple-element.37.grad_ref, bf16[1792,896]{1,0:T(8,128)(2,1)} %weight_ref.2), custom_call_target="tpu_custom_call" | custom-call | flops 1644167168 | bytes 9175040 | tf_op jit(solution)/shard_map/pallas_call | solution.py:162
  328.5 3.1 fusion.11
  331.6 9.4 %collective-permute-done.20 = bf16[2,128,896]{2,1,0:T(8,128)(2,1)} collective-permute-done((bf16[2,128,896]{2,1,0:T(8,128)(2,1)}, bf16[2,128,896]{2,1,0:T(8,128)(2,1)}, u32[]{:S(2)}, u32[]{:S(2)}) %collective-permute-start.20) | collective-permute-done | bytes 458784 | tf_op jit(solution)/shard_map/ppermute | solution.py:28
  344.8 1.8 collective-permute-start.24
  347.1 7.8 %collective-permute-done.21 = bf16[128,896]{1,0:T(8,128)(2,1)S(1)} collective-permute-done((bf16[128,896]{1,0:T(8,128)(2,1)S(1)}, bf16[128,896]{1,0:T(8,128)(2,1)S(1)}, u32[]{:S(2)}, u32[]{:S(2)}) %collective-permute-start.21) | collective-permute-done | bytes 229408 | tf_op jit(solution)/shard_map/ppermute | solution.py:28
  355.9 1.9 collective-permute-start.22
  357.8 4.2 %collective-permute-done.24 = bf16[2,128,896]{2,1,0:T(8,128)(2,1)S(1)} collective-permute-done((bf16[2,128,896]{2,1,0:T(8,128)(2,1)S(1)}, bf16[2,128,896]{2,1,0:T(8,128)(2,1)S(1)}, u32[]{:S(2)}, u32[]{:S(2)}) %collective-permute-start.24) | collective-permute-done | bytes 458784 | tf_op jit(solution)/shard_map/ppermute | solution.py:28
  364.0 11.8 %collective-permute-done.22.refs_1_ = bf16[128,896]{1,0:T(8,128)(2,1)S(1)} collective-permute-done((bf16[128,896]{1,0:T(8,128)(2,1)S(1)}, bf16[128,896]{1,0:T(8,128)(2,1)S(1)}, u32[]{:S(2)}, u32[]{:S(2)}) %collective-permute-start.22) | collective-permute-done | bytes 229408 | tf_op jit(solution)/shard_map/ppermute | solution.py:359
  377.2 4.4 %all-to-all-start.2 = ((f32[32,2,1024]{2,1,0:T(2,128)}), f32[32,2,1024]{2,1,0:T(2,128)}, u32[]{:S(2)}, u32[]{:S(2)}) async-start(f32[32,2,1024]{2,1,0:T(2,128)} %copy-done.2), calls=%async_computation.2 | async-start | bytes 524288 | tf_op jit(solution)/shard_map/all_to_all | solution.py:405
  381.6 9.3 %shard_map.175 = (bf16[2048,7168]{1,0:T(8,128)(2,1)}, f32[8,128]{1,0:T(8,128)}) custom-call(bf16[512,2048]{1,0:T(8,128)(2,1)S(1)} %fusion.3.grad_ref, bf16[512,7168]{1,0:T(8,128)(2,1)} %copy-done.8, bf16[2048,7168]{1,0:T(8,128)(2,1)} %get-tuple-element.21.rest_0_, bf16[4,64,896]{2,1,0:T(8,128)(2,1)S(1)} %pad_maximum_fusion.8.rest_1_), custom_call_target="tpu_custom_call", output_to_operand_aliasing={{0}: (2, {})} | custom-call | flops 3758096384 | bytes 14680064 | tf_op jit(solution)/shard_map/pallas_call | solution.py:94
  391.9 4.3 %collective-permute-start.26 = (bf16[128,896]{1,0:T(8,128)(2,1)S(1)}, bf16[128,896]{1,0:T(8,128)(2,1)S(1)}, u32[]{:S(2)}, u32[]{:S(2)}) collective-permute-start(bf16[128,896]{1,0:T(8,128)(2,1)S(1)} %fusion.28), channel_id=1, source_target_pairs={{0,0},{1,1},{2,8},{3,9},{4,16},{5,17},{6,24},{7,25},{8,2},{9,3},{1... | collective-permute-start | bytes 688136 | tf_op jit(solution)/shard_map/ppermute | solution.py:359
  398.7 1.9 subtract_convert_fusion.1
  400.6 7.8 %collective-permute-done.26 = bf16[128,896]{1,0:T(8,128)(2,1)S(1)} collective-permute-done((bf16[128,896]{1,0:T(8,128)(2,1)S(1)}, bf16[128,896]{1,0:T(8,128)(2,1)S(1)}, u32[]{:S(2)}, u32[]{:S(2)}) %collective-permute-start.26) | collective-permute-done | bytes 229408 | tf_op jit(solution)/shard_map/ppermute | solution.py:359
  408.4 1.8 subtract_convert_fusion
  (251 shorter events, 55.2 us)
Async XLA Ops:
  7.2 133.4 %all-gather.3.cloned.1.call-start = ((), (), s32[]{:S(2)}) async-start(), calls=%async_computation.3 | async-start | bytes 7569408 | tf_op jit(solution)/shard_map/all_gather | solution.py:280
  12.6 44.5 %copy-start.18 = (bf16[128,1792]{1,0:T(8,128)(2,1)}, bf16[128,1792]{1,0:T(8,128)(2,1)S(1)}, u32[]{:S(2)}) copy-start(bf16[128,1792]{1,0:T(8,128)(2,1)S(1)} %get-tuple-element.47) | copy-start | bytes 1376260
  12.6 12.9 %collective-permute-start.7 = (bf16[128,1792]{1,0:T(8,128)(2,1)S(1)}, bf16[128,1792]{1,0:T(8,128)(2,1)S(1)}, u32[]{:S(2)}, u32[]{:S(2)}) collective-permute-start(bf16[128,1792]{1,0:T(8,128)(2,1)S(1)} %get-tuple-element.49), channel_id=1, source_target_pairs={{0,24},{8,16},{16,8},{24,0},{1,25},{9,17},{17,9},{25,1},{2,26},{10... | collective-permute-start | bytes 1376264 | tf_op jit(solution)/shard_map/ppermute | solution.py:245
  14.3 11.9 %copy-start.16 = (bf16[128,1792]{1,0:T(8,128)(2,1)}, bf16[128,1792]{1,0:T(8,128)(2,1)S(1)}, u32[]{:S(2)}) copy-start(bf16[128,1792]{1,0:T(8,128)(2,1)S(1)} %get-tuple-element.51) | copy-start | bytes 1376260
  14.3 21.0 %collective-permute-start.6 = (bf16[128,1792]{1,0:T(8,128)(2,1)S(1)}, bf16[128,1792]{1,0:T(8,128)(2,1)S(1)}, u32[]{:S(2)}, u32[]{:S(2)}) collective-permute-start(bf16[128,1792]{1,0:T(8,128)(2,1)S(1)} %get-tuple-element.53), channel_id=1, source_target_pairs={{0,24},{8,16},{16,8},{24,0},{1,25},{9,17},{17,9},{25,1},{2,26},{10... | collective-permute-start | bytes 1376264 | tf_op jit(solution)/shard_map/ppermute | solution.py:245
  16.1 20.7 %collective-permute-start.4 = (bf16[128,1792]{1,0:T(8,128)(2,1)S(1)}, bf16[128,1792]{1,0:T(8,128)(2,1)S(1)}, u32[]{:S(2)}, u32[]{:S(2)}) collective-permute-start(bf16[128,1792]{1,0:T(8,128)(2,1)S(1)} %get-tuple-element.48), channel_id=1, source_target_pairs={{0,8},{8,0},{16,24},{24,16},{1,9},{9,1},{17,25},{25,17},{2,10},{10... | collective-permute-start | bytes 1376264 | tf_op jit(solution)/shard_map/ppermute | solution.py:245
  16.1 21.4 %collective-permute-start.3 = (bf16[128,1792]{1,0:T(8,128)(2,1)S(1)}, bf16[128,1792]{1,0:T(8,128)(2,1)S(1)}, u32[]{:S(2)}, u32[]{:S(2)}) collective-permute-start(bf16[128,1792]{1,0:T(8,128)(2,1)S(1)} %get-tuple-element.52), channel_id=1, source_target_pairs={{0,8},{8,0},{16,24},{24,16},{1,9},{9,1},{17,25},{25,17},{2,10},{10... | collective-permute-start | bytes 1376264 | tf_op jit(solution)/shard_map/ppermute | solution.py:245
  16.6 28.6 %collective-permute-start.1 = (bf16[128,1792]{1,0:T(8,128)(2,1)S(1)}, bf16[128,1792]{1,0:T(8,128)(2,1)S(1)}, u32[]{:S(2)}, u32[]{:S(2)}) collective-permute-start(bf16[128,1792]{1,0:T(8,128)(2,1)S(1)} %get-tuple-element.50), channel_id=1, source_target_pairs={{0,16},{8,24},{16,0},{24,8},{1,17},{9,25},{17,1},{25,9},{2,18},{10... | collective-permute-start | bytes 1376264 | tf_op jit(solution)/shard_map/ppermute | solution.py:245
  17.3 47.5 %copy-start.20 = (f32[128,896]{1,0:T(8,128)}, f32[128,896]{1,0:T(8,128)S(1)}, u32[]{:S(2)}) copy-start(f32[128,896]{1,0:T(8,128)S(1)} %fusion.66) | copy-start | bytes 1376260
  25.5 29.5 %collective-permute-start = (bf16[128,1792]{1,0:T(8,128)(2,1)S(1)}, bf16[128,1792]{1,0:T(8,128)(2,1)S(1)}, u32[]{:S(2)}, u32[]{:S(2)}) collective-permute-start(bf16[128,1792]{1,0:T(8,128)(2,1)S(1)} %get-tuple-element.54), channel_id=1, source_target_pairs={{0,16},{8,24},{16,0},{24,8},{1,17},{9,25},{17,1},{25,9},{2,18},{10... | collective-permute-start | bytes 1376264 | tf_op jit(solution)/shard_map/ppermute | solution.py:245
  36.8 23.1 %collective-permute-start.8 = (bf16[128,896]{1,0:T(8,128)(2,1)S(1)}, bf16[128,896]{1,0:T(8,128)(2,1)S(1)}, u32[]{:S(2)}, u32[]{:S(2)}) collective-permute-start(bf16[128,896]{1,0:T(8,128)(2,1)S(1)} %get-tuple-element.103), channel_id=1, source_target_pairs={{0,24},{8,16},{16,8},{24,0},{1,25},{9,17},{17,9},{25,1},{2,26},{10... | collective-permute-start | bytes 688136 | tf_op jit(solution)/shard_map/ppermute | solution.py:245
  39.0 20.9 %collective-permute-start.5 = (bf16[128,896]{1,0:T(8,128)(2,1)S(1)}, bf16[128,896]{1,0:T(8,128)(2,1)S(1)}, u32[]{:S(2)}, u32[]{:S(2)}) collective-permute-start(bf16[128,896]{1,0:T(8,128)(2,1)S(1)} %get-tuple-element.105), channel_id=1, source_target_pairs={{0,8},{8,0},{16,24},{24,16},{1,9},{9,1},{17,25},{25,17},{2,10},{10... | collective-permute-start | bytes 688136 | tf_op jit(solution)/shard_map/ppermute | solution.py:245
  45.2 11.3 %copy-start.41 = (bf16[128,1792]{1,0:T(8,128)(2,1)}, bf16[128,1792]{1,0:T(8,128)(2,1)S(1)}, u32[]{:S(2)}) copy-start(bf16[128,1792]{1,0:T(8,128)(2,1)S(1)} %collective-permute-done.1) | copy-start | bytes 1376260
  56.5 8.4 %collective-permute-start.2 = (bf16[128,896]{1,0:T(8,128)(2,1)S(1)}, bf16[128,896]{1,0:T(8,128)(2,1)S(1)}, u32[]{:S(2)}, u32[]{:S(2)}) collective-permute-start(bf16[128,896]{1,0:T(8,128)(2,1)S(1)} %get-tuple-element.107), channel_id=1, source_target_pairs={{0,16},{8,24},{16,0},{24,8},{1,17},{9,25},{17,1},{25,9},{2,18},{10... | collective-permute-start | bytes 688136 | tf_op jit(solution)/shard_map/ppermute | solution.py:245
  57.8 86.9 %copy-start.22 = (f32[128,896]{1,0:T(8,128)}, f32[128,896]{1,0:T(8,128)S(1)}, u32[]{:S(2)}) copy-start(f32[128,896]{1,0:T(8,128)S(1)} %fusion.67) | copy-start | bytes 1376260
  66.7 12.6 %all-to-all-start = ((f32[32,1,128]{2,1,0:T(1,128)}), f32[32,1,128]{2,1,0:T(1,128)S(1)}, u32[]{:S(2)}, u32[]{:S(2)}) async-start(f32[32,1,128]{2,1,0:T(1,128)} %broadcast_in_dim.190), calls=%async_computation | async-start | bytes 32768 | tf_op jit(solution)/shard_map/all_to_all | solution.py:275
  146.2 23.9 %copy-start.8 = (bf16[512,7168]{1,0:T(8,128)(2,1)}, bf16[512,7168]{1,0:T(8,128)(2,1)S(1)}, u32[]{:S(2)}) copy-start(bf16[512,7168]{1,0:T(8,128)(2,1)S(1)} %constant_dynamic-update-slice_fusion.rows_ref) | copy-start | bytes 22020100
  146.3 28.7 %copy-start.53 = (s32[512]{0:T(512)S(1)}, s32[512]{0:T(512)}, u32[]{:S(2)}) copy-start(s32[512]{0:T(512)} %param.19) | copy-start | bytes 6148
  171.0 11.5 %all-to-all-start.1 = ((f32[32,3,4,128]{3,2,1,0:T(4,128)}), f32[32,3,4,128]{3,2,1,0:T(4,128)S(1)}, u32[]{:S(2)}, u32[]{:S(2)}) async-start(f32[32,3,4,128]{3,2,1,0:T(4,128)} %broadcast_in_dim.200), calls=%async_computation.1 | async-start | bytes 393216 | tf_op jit(solution)/shard_map/all_to_all | solution.py:53
  200.5 14.1 %collective-permute-start.9 = (bf16[256,7168]{1,0:T(8,128)(2,1)}, bf16[256,7168]{1,0:T(8,128)(2,1)}, u32[]{:S(2)}, u32[]{:S(2)}) collective-permute-start(bf16[256,7168]{1,0:T(8,128)(2,1)} %convolution_convert_fusion), channel_id=1, source_target_pairs={{0,8},{8,0},{16,24},{24,16},{1,9},{9,1},{17,25},{25,17},{2,10},{10... | collective-permute-start | bytes 11010056 | tf_op jit(solution)/shard_map/ppermute | solution.py:28
  218.2 24.9 %collective-permute-start.10 = (bf16[64,7168]{1,0:T(8,128)(2,1)S(1)}, bf16[64,7168]{1,0:T(8,128)(2,1)S(1)}, u32[]{:S(2)}, u32[]{:S(2)}) collective-permute-start(bf16[64,7168]{1,0:T(8,128)(2,1)S(1)} %get-tuple-element.45.rest_0_), channel_id=1, source_target_pairs={{0,16},{8,24},{16,0},{24,8},{1,17},{9,25},{17,1},{25,9},{2,18},{10... | collective-permute-start | bytes 2752520 | tf_op jit(solution)/shard_map/ppermute | solution.py:28
  219.2 22.4 %collective-permute-start.12 = (bf16[4,128,896]{2,1,0:T(8,128)(2,1)S(1)}, bf16[4,128,896]{2,1,0:T(8,128)(2,1)S(1)}, u32[]{:S(2)}, u32[]{:S(2)}) collective-permute-start(bf16[4,128,896]{2,1,0:T(8,128)(2,1)S(1)} %pad_maximum_fusion.4.rest_1_), channel_id=1, source_target_pairs={{0,1},{1,0},{2,3},{3,2},{4,5},{5,4},{6,7},{7,6},{8,9},{9,8},{10,11... | collective-permute-start | bytes 2752520 | tf_op jit(solution)/shard_map/ppermute | solution.py:28
  241.9 11.7 %collective-permute-start.13 = (bf16[4,64,896]{2,1,0:T(8,128)(2,1)S(1)}, bf16[4,64,896]{2,1,0:T(8,128)(2,1)S(1)}, u32[]{:S(2)}, u32[]{:S(2)}) collective-permute-start(bf16[4,64,896]{2,1,0:T(8,128)(2,1)S(1)} %slice_bitcast_fusion.2), channel_id=1, source_target_pairs={{0,16},{8,24},{16,0},{24,8},{1,17},{9,25},{17,1},{25,9},{2,18},{10... | collective-permute-start | bytes 1376264 | tf_op jit(solution)/shard_map/ppermute | solution.py:28
  244.2 11.5 %collective-permute-start.11 = (bf16[4,64,896]{2,1,0:T(8,128)(2,1)S(1)}, bf16[4,64,896]{2,1,0:T(8,128)(2,1)}, u32[]{:S(2)}, u32[]{:S(2)}) collective-permute-start(bf16[4,64,896]{2,1,0:T(8,128)(2,1)S(1)} %pad_maximum_fusion.8.rest_1_), channel_id=1, source_target_pairs={{0,1},{1,0},{2,3},{3,2},{4,5},{5,4},{6,7},{7,6},{8,9},{9,8},{10,11... | collective-permute-start | bytes 1376264 | tf_op jit(solution)/shard_map/ppermute | solution.py:28
  257.9 11.0 %collective-permute-start.14 = (bf16[2,128,896]{2,1,0:T(8,128)(2,1)}, bf16[2,128,896]{2,1,0:T(8,128)(2,1)}, u32[]{:S(2)}, u32[]{:S(2)}) collective-permute-start(bf16[2,128,896]{2,1,0:T(8,128)(2,1)} %pad_maximum_fusion.9), channel_id=1, source_target_pairs={{0,2},{1,3},{2,0},{3,1},{4,6},{5,7},{6,4},{7,5},{8,10},{9,11},{10,... | collective-permute-start | bytes 1376264 | tf_op jit(solution)/shard_map/ppermute | solution.py:28
  259.7 12.2 %copy-start.21 = (f32[128,896]{1,0:T(8,128)S(1)}, f32[128,896]{1,0:T(8,128)}, u32[]{:S(2)}) copy-start(f32[128,896]{1,0:T(8,128)} %copy-done.20) | copy-start | bytes 1376260
  259.7 12.2 %copy-start.34 = (f32[128,896]{1,0:T(8,128)S(1)}, f32[128,896]{1,0:T(8,128)}, u32[]{:S(2)}) copy-start(f32[128,896]{1,0:T(8,128)} %get-tuple-element.104) | copy-start | bytes 1376260
  259.7 12.2 %copy-start.35 = (f32[128,896]{1,0:T(8,128)S(1)}, f32[128,896]{1,0:T(8,128)}, u32[]{:S(2)}) copy-start(f32[128,896]{1,0:T(8,128)} %get-tuple-element.106) | copy-start | bytes 1376260
  259.7 12.2 %copy-start.36 = (f32[128,896]{1,0:T(8,128)S(1)}, f32[128,896]{1,0:T(8,128)}, u32[]{:S(2)}) copy-start(f32[128,896]{1,0:T(8,128)} %get-tuple-element.108) | copy-start | bytes 1376260
  270.0 10.7 %collective-permute-start.15 = (bf16[128,896]{1,0:T(8,128)(2,1)S(1)}, bf16[128,896]{1,0:T(8,128)(2,1)S(1)}, u32[]{:S(2)}, u32[]{:S(2)}) collective-permute-start(bf16[128,896]{1,0:T(8,128)(2,1)S(1)} %fusion.38), channel_id=1, source_target_pairs={{0,4},{1,5},{2,6},{3,7},{4,0},{5,1},{6,2},{7,3},{8,12},{9,13},{10,... | collective-permute-start | bytes 688136 | tf_op jit(solution)/shard_map/ppermute | solution.py:28
  280.8 8.0 %collective-permute-start.18 = (bf16[128,896]{1,0:T(8,128)(2,1)S(1)}, bf16[128,896]{1,0:T(8,128)(2,1)S(1)}, u32[]{:S(2)}, u32[]{:S(2)}) collective-permute-start(bf16[128,896]{1,0:T(8,128)(2,1)S(1)} %fusion.37), channel_id=1, source_target_pairs={{0,24},{8,16},{16,8},{24,0},{1,25},{9,17},{17,9},{25,1},{2,26},{10... | collective-permute-start | bytes 688136 | tf_op jit(solution)/shard_map/ppermute | solution.py:245
  280.9 7.9 %collective-permute-start.17 = (bf16[128,896]{1,0:T(8,128)(2,1)S(1)}, bf16[128,896]{1,0:T(8,128)(2,1)S(1)}, u32[]{:S(2)}, u32[]{:S(2)}) collective-permute-start(bf16[128,896]{1,0:T(8,128)(2,1)S(1)} %fusion.37), channel_id=1, source_target_pairs={{0,8},{8,0},{16,24},{24,16},{1,9},{9,1},{17,25},{25,17},{2,10},{10... | collective-permute-start | bytes 688136 | tf_op jit(solution)/shard_map/ppermute | solution.py:245
  281.5 10.4 %collective-permute-start.16 = (bf16[128,896]{1,0:T(8,128)(2,1)S(1)}, bf16[128,896]{1,0:T(8,128)(2,1)S(1)}, u32[]{:S(2)}, u32[]{:S(2)}) collective-permute-start(bf16[128,896]{1,0:T(8,128)(2,1)S(1)} %fusion.37), channel_id=1, source_target_pairs={{0,16},{8,24},{16,0},{24,8},{1,17},{9,25},{17,1},{25,9},{2,18},{10... | collective-permute-start | bytes 688136 | tf_op jit(solution)/shard_map/ppermute | solution.py:245
  299.9 25.5 %collective-permute-start.19 = (bf16[4,128,896]{2,1,0:T(8,128)(2,1)}, bf16[4,128,896]{2,1,0:T(8,128)(2,1)}, u32[]{:S(2)}, u32[]{:S(2)}) collective-permute-start(bf16[4,128,896]{2,1,0:T(8,128)(2,1)} %bitcast.54), channel_id=1, source_target_pairs={{0,1},{1,0},{2,3},{3,2},{4,5},{5,4},{6,7},{7,6},{8,9},{9,8},{10,11... | collective-permute-start | bytes 2752520 | tf_op jit(solution)/shard_map/ppermute | solution.py:28
  308.9 34.5 %collective-permute-start.23 = (bf16[4,128,896]{2,1,0:T(8,128)(2,1)}, bf16[4,128,896]{2,1,0:T(8,128)(2,1)}, u32[]{:S(2)}, u32[]{:S(2)}) collective-permute-start(bf16[4,128,896]{2,1,0:T(8,128)(2,1)} %bitcast.74), channel_id=1, source_target_pairs={{0,1},{1,0},{2,3},{3,2},{4,5},{5,4},{6,7},{7,6},{8,9},{9,8},{10,11... | collective-permute-start | bytes 2752520 | tf_op jit(solution)/shard_map/ppermute | solution.py:28
  326.8 15.3 %copy-start.24 = (bf16[4,128,896]{2,1,0:T(8,128)(2,1)}, bf16[4,128,896]{2,1,0:T(8,128)(2,1)S(1)}, u32[]{:S(2)}) copy-start(bf16[4,128,896]{2,1,0:T(8,128)(2,1)S(1)} %add_convert_fusion.1) | copy-start | bytes 2752516
  327.8 13.2 %collective-permute-start.20 = (bf16[2,128,896]{2,1,0:T(8,128)(2,1)}, bf16[2,128,896]{2,1,0:T(8,128)(2,1)}, u32[]{:S(2)}, u32[]{:S(2)}) collective-permute-start(bf16[2,128,896]{2,1,0:T(8,128)(2,1)} %pad_maximum_fusion.10), channel_id=1, source_target_pairs={{0,2},{1,3},{2,0},{3,1},{4,6},{5,7},{6,4},{7,5},{8,10},{9,11},{10,... | collective-permute-start | bytes 1376264 | tf_op jit(solution)/shard_map/ppermute | solution.py:28
  342.1 12.7 %collective-permute-start.21 = (bf16[128,896]{1,0:T(8,128)(2,1)S(1)}, bf16[128,896]{1,0:T(8,128)(2,1)S(1)}, u32[]{:S(2)}, u32[]{:S(2)}) collective-permute-start(bf16[128,896]{1,0:T(8,128)(2,1)S(1)} %fusion.39.refs_2_), channel_id=1, source_target_pairs={{0,4},{1,5},{2,6},{3,7},{4,0},{5,1},{6,2},{7,3},{8,12},{9,13},{10,... | collective-permute-start | bytes 688136 | tf_op jit(solution)/shard_map/ppermute | solution.py:28
  344.8 17.2 %collective-permute-start.24 = (bf16[2,128,896]{2,1,0:T(8,128)(2,1)S(1)}, bf16[2,128,896]{2,1,0:T(8,128)(2,1)S(1)}, u32[]{:S(2)}, u32[]{:S(2)}) collective-permute-start(bf16[2,128,896]{2,1,0:T(8,128)(2,1)S(1)} %pad_maximum_fusion.11), channel_id=1, source_target_pairs={{0,2},{1,3},{2,0},{3,1},{4,6},{5,7},{6,4},{7,5},{8,10},{9,11},{10,... | collective-permute-start | bytes 1376264 | tf_op jit(solution)/shard_map/ppermute | solution.py:28
  355.9 19.9 %collective-permute-start.22 = (bf16[128,896]{1,0:T(8,128)(2,1)S(1)}, bf16[128,896]{1,0:T(8,128)(2,1)S(1)}, u32[]{:S(2)}, u32[]{:S(2)}) collective-permute-start(bf16[128,896]{1,0:T(8,128)(2,1)S(1)} %fusion.33), channel_id=1, source_target_pairs={{0,0},{1,1},{2,8},{3,9},{4,16},{5,17},{6,24},{7,25},{8,2},{9,3},{1... | collective-permute-start | bytes 688136 | tf_op jit(solution)/shard_map/ppermute | solution.py:359
  362.1 13.7 %copy-start.25 = (f32[2,128,896]{2,1,0:T(8,128)}, f32[2,128,896]{2,1,0:T(8,128)S(1)}, u32[]{:S(2)}) copy-start(f32[2,128,896]{2,1,0:T(8,128)S(1)} %convert_element_type.323) | copy-start | bytes 2752516
  362.9 28.0 %collective-permute-start.25 = (bf16[128,896]{1,0:T(8,128)(2,1)}, bf16[128,896]{1,0:T(8,128)(2,1)}, u32[]{:S(2)}, u32[]{:S(2)}) collective-permute-start(bf16[128,896]{1,0:T(8,128)(2,1)} %fusion.40.refs_2_), channel_id=1, source_target_pairs={{0,4},{1,5},{2,6},{3,7},{4,0},{5,1},{6,2},{7,3},{8,12},{9,13},{10,... | collective-permute-start | bytes 688136 | tf_op jit(solution)/shard_map/ppermute | solution.py:28
  377.2 19.0 %all-to-all-start.2 = ((f32[32,2,1024]{2,1,0:T(2,128)}), f32[32,2,1024]{2,1,0:T(2,128)}, u32[]{:S(2)}, u32[]{:S(2)}) async-start(f32[32,2,1024]{2,1,0:T(2,128)} %copy-done.2), calls=%async_computation.2 | async-start | bytes 524288 | tf_op jit(solution)/shard_map/all_to_all | solution.py:405
  381.6 17.1 %copy-start.58 = (f32[128]{0:T(128)S(1)}, f32[128]{0:T(128)}, u32[]{:S(2)}) copy-start(f32[128]{0:T(128)} %copy-done.57) | copy-start | bytes 1540
  381.6 17.1 %copy-start.60 = (f32[128]{0:T(128)S(1)}, f32[128]{0:T(128)}, u32[]{:S(2)}) copy-start(f32[128]{0:T(128)} %get-tuple-element.101) | copy-start | bytes 1540
  390.9 17.6 %copy-start.56 = (f32[128]{0:T(128)S(1)}, f32[128]{0:T(128)}, u32[]{:S(2)}) copy-start(f32[128]{0:T(128)} %copy-done.55) | copy-start | bytes 1540
  390.9 17.6 %copy-start.59 = (f32[128]{0:T(128)S(1)}, f32[128]{0:T(128)}, u32[]{:S(2)}) copy-start(f32[128]{0:T(128)} %get-tuple-element.99) | copy-start | bytes 1540
  391.9 16.5 %collective-permute-start.26 = (bf16[128,896]{1,0:T(8,128)(2,1)S(1)}, bf16[128,896]{1,0:T(8,128)(2,1)S(1)}, u32[]{:S(2)}, u32[]{:S(2)}) collective-permute-start(bf16[128,896]{1,0:T(8,128)(2,1)S(1)} %fusion.28), channel_id=1, source_target_pairs={{0,0},{1,1},{2,8},{3,9},{4,16},{5,17},{6,24},{7,25},{8,2},{9,3},{1... | collective-permute-start | bytes 688136 | tf_op jit(solution)/shard_map/ppermute | solution.py:359
  (44 other events, 233.3 us)
Sparse Core Ops, SparseCore 0:
  65.9 74.6 all-gather.2

commit v6 on v5

--- a/solution.py
+++ b/solution.py
@@ -77,12 +77,10 @@
     )
 
 
-def head_gradient(grad, rows_all, span, after, base=None):
+def head_gradient(grad, rows_all, after):
     tokens, entries = grad.shape
     width = rows_all.shape[1]
     chunk = 1024
-    begin, end = span
-    extra = ([] if base is None else [base]) + list(after)
 
     def body(grad_ref, rows_ref, *rest):
         out_ref, mark_ref = rest[-2:]
@@ -93,28 +91,27 @@
 
     return pl.pallas_call(
         body,
-        grid=(end - begin,),
+        grid=(entries // TILE,),
         in_specs=[
-            pl.BlockSpec((tokens, TILE), lambda step: (0, step + begin)),
+            pl.BlockSpec((tokens, TILE), lambda step: (0, step)),
             whole_block((tokens, width)),
         ]
-        + [pl.BlockSpec(memory_space=pl.ANY)] * len(extra),
+        + [pl.BlockSpec(memory_space=pl.ANY)] * len(after),
         out_specs=[
-            pl.BlockSpec((TILE, width), lambda step: (step + begin, 0)),
+            pl.BlockSpec((TILE, width), lambda step: (step, 0)),
             pl.BlockSpec((8, 128), lambda step: (0, 0)),
         ],
         out_shape=[
             jax.ShapeDtypeStruct((entries, width), BF16),
             jax.ShapeDtypeStruct((8, 128), F32),
         ],
-        input_output_aliases={} if base is None else {2: 0},
         compiler_params=pltpu.CompilerParams(vmem_limit_bytes=48 * 1024 * 1024),
         cost_estimate=pl.CostEstimate(
-            flops=2 * tokens * width * TILE * (end - begin),
-            bytes_accessed=2 * width * TILE * (end - begin) + 2 * tokens * width,
+            flops=2 * tokens * width * entries,
+            bytes_accessed=2 * width * entries + 2 * tokens * width,
             transcendentals=0,
         ),
-    )(grad, rows_all, *extra)
+    )(grad, rows_all, *after)
 
 
 def add_after(left, right, after):
@@ -148,12 +145,13 @@
     )(value, *after)
 
 
-def weight_gradient(normed, proj_grad, weight):
+def weight_gradient(normed, proj_grad, weight, after):
     tokens, feat = normed.shape
     cols = proj_grad.shape[1]
-    tile = 256 if feat % 256 == 0 else 128
-
-    def body(normed_ref, grad_ref, weight_ref, out_ref, sum_ref):
+    tile = feat // 2 if feat % 256 == 0 and feat // 2 % 128 == 0 else feat
+
+    def body(normed_ref, grad_ref, weight_ref, *rest):
+        out_ref, sum_ref = rest[-2:]
         grad = contract_first(normed_ref[...], grad_ref[...])
         out_ref[...] = grad.astype(BF16)
         total = jnp.sum(grad * weight_ref[...].astype(F32), axis=1, keepdims=True)
@@ -166,7 +164,8 @@
             pl.BlockSpec((tokens, tile), lambda step: (0, step)),
             whole_block((tokens, cols)),
             pl.BlockSpec((tile, cols), lambda step: (step, 0)),
-        ],
+        ]
+        + [pl.BlockSpec(memory_space=pl.ANY)] * len(after),
         [
             pl.BlockSpec((tile, cols), lambda step: (step, 0)),
             pl.BlockSpec((tile, 128), lambda step: (step, 0)),
@@ -177,7 +176,7 @@
         ],
         2 * tokens * feat * cols,
         4 * feat * cols + 2 * tokens * (feat + cols),
-    )(normed, proj_grad, weight)
+    )(normed, proj_grad, weight, *after)
     return out, sums[:, 0]
 
 
@@ -323,9 +322,7 @@
     last = column_chunk(last, b).astype(F32)
     for r, value in enumerate(last_sends, 1):
         last = last + dim_b.turn(value, r).astype(F32)
-    tiles = vocab_local // TILE
-    most = max(1, tiles * 3 // 4)
-    grad_head, mark = head_gradient(scaled_grad, gathered, (0, most), first_sends + last_sends)
+    grad_head, mark = head_gradient(scaled_grad, gathered, first_sends + last_sends)
     first = add_after(mine[0, :half], first_got[0], [mark])
     for value in first_got[1:]:
         first = (first.astype(F32) + value.astype(F32)).astype(BF16)
@@ -338,9 +335,6 @@
     kept = last[:, 0].astype(F32)
     for r in range(1, nx):
         kept = kept + dim_x.turn(last[:, r], -r).astype(F32)
-    grad_head, mark = head_gradient(
-        scaled_grad, gathered, (most, tiles), second_sends, base=grad_head
-    )
     summed = jnp.concatenate([first, kept.astype(BF16)], axis=1)
     summed = exchange_far(exchange_near(summed, dim_a), dim_a)
     scaled = jnp.concatenate([summed] + [send(summed, rc, rx) for rc, rx in places[1:]])
@@ -375,7 +369,8 @@
     kept_h = products(proj_hidden, b)
     for value in got_h:
         kept_h = kept_h + value.astype(F32)
-    pair_h = exchange_near(kept_h.astype(BF16), dim_a)
+    kept_h = kept_h.astype(BF16)
+    pair_h = exchange_near(kept_h, dim_a)
     kept_e = products(proj_embed, b)
     for value in got_e[1:]:
         kept_e = kept_e + value.astype(F32)
@@ -383,12 +378,17 @@
     hidden_moved = final_move(exchange_far(pair_h, dim_a))
     pair_e = exchange_near(kept_e, dim_a)
     hidden_back = hidden_moved.astype(F32)
-    embed_back = final_move(exchange_far(pair_e, dim_a)).astype(F32)
-
-    grad_proj_hidden, gain_h = weight_gradient(jnp.concatenate(blocks_h), proj_grad, proj_hidden)
-    grad_proj_embed, gain_e = weight_gradient(jnp.concatenate(blocks_e), proj_grad, proj_embed)
-
-    wide = proj_grad.astype(F32).reshape(nc, block, cols)
+    embed_summed = exchange_far(pair_e, dim_a)
+    embed_back = final_move(embed_summed).astype(F32)
+
+    grad_proj_hidden, gain_h = weight_gradient(
+        jnp.concatenate(blocks_h), proj_grad, proj_hidden, [kept_h]
+    )
+    grad_proj_embed, gain_e = weight_gradient(
+        jnp.concatenate(blocks_e), proj_grad, proj_embed, [pair_h[1]]
+    )
+
+    wide = lax.optimization_barrier(proj_grad).astype(F32).reshape(nc, block, cols)
     dots = jnp.stack(
         [jnp.sum(wide * jnp.stack(halves), axis=-1) for halves in (halves_h, halves_e)]
     )
@@ -401,7 +401,7 @@
     gains = jnp.where(holder, gains, F32(0.0)).reshape(nv, 2, cols)
     gains = jnp.broadcast_to(gains[None], (nc, nv, 2, cols))
     ends = jnp.concatenate([dots, gains], axis=-1).reshape(nc * nv, 2, block + cols)
-    ends = held_back(ends, [hidden_moved, pair_e[1]])
+    ends = held_back(ends, [embed_summed, hidden_moved])
     ends = jnp.sum(lax.all_to_all(ends, ("ctx", "vocab"), 0, 0, tiled=True), axis=0)
 
     def finish(kind, source, gain):

time: 426 us -> 424 us (level)
  waiting for transfers between devices: 192 us -> 209 us
  Pallas kernels: 43.6 us -> 33.4 us
  starting transfers between devices: 42.7 us -> 37.3 us
    ppermute x13, waiting for transfers between devices: 50.5 us -> 70.6 us  [move(): return lax.ppermute(value, self.axis, pairs)]
    ppermute x13, starting transfers between devices: 15.9 us -> 6.89 us  [move(): return lax.ppermute(value, self.axis, pairs)]
    pallas_call x2 -> x1, Pallas kernels: 27.2 us -> 22.3 us  [head_gradient(): pl.pallas_call(body, grid=(entries // TILE,), in_specs=[pl.BlockSpec((tok...]
    pallas_call x2, Pallas kernels: 14.8 us -> 10 us  [weight_gradient(): kernel_call(body, (feat // tile,), [pl.BlockSpec((tokens, tile), lambda s...]
  transfers between devices with their start and end apart: 31 -> 31, of which waited for: 21 -> 22; matrix products, arithmetic and copies ran while one was open for 12% -> 11% of each run, Pallas kernels for 10% -> 8%
where the time goes in v6:
time: 424 us; the launch traced here: 416 us
  waiting for transfers between devices  209 us (49%)
  matrix products  66.5 us (16%)
  starting transfers between devices  37.3 us (9%)
  other arithmetic  35.6 us (8%)
  Pallas kernels  33.4 us (8%)
  between operations  17.4 us (4%)
  local copies, waits for them, and re-layouts  16.7 us (4%)
    ppermute x13, waiting for transfers between devices, move(): return lax.ppermute(value, self.axis, pairs)  70.6 us
    all_gather x1, waiting for transfers between devices, local(): lax.all_gather(piece, ('ctx', 'vocab')).reshape(nc, nv, block, cols)  61.6 us
    ppermute x12, waiting for transfers between devices, send(): return lax.ppermute(value, 'ctx', pairs)  43.4 us
    dot_general x10, matrix products, dot(): return jnp.dot(left, right, preferred_element_type=F32)  35.4 us
    dot_general x5, matrix products, contract_last(): lax.dot_general(left, right, (((1,), (1,)), ((), ())), preferred_element_...  31.1 us
    pallas_call x1, Pallas kernels, head_gradient(): pl.pallas_call(body, grid=(entries // TILE,), in_specs=[pl.BlockSpec((tok...  22.3 us
    ppermute x2, waiting for transfers between devices, final_move(): return lax.ppermute(value, ('ctx', 'vocab'), pairs)  16.4 us
    pallas_call x2, Pallas kernels, weight_gradient(): kernel_call(body, (feat // tile,), [pl.BlockSpec((tokens, tile), lambda s...  10 us
  transfers between devices with their start and end apart: 31, of which 22 were waited for; matrix products, arithmetic and copies ran while one was open for 11% of the time, Pallas kernels for 8%

profile of v6, /device:TPU:2, one launch (start us, length us, event | category | flops | bytes accessed | tf_op | source)
XLA Modules:
  0.0 416.1 jit_solution(13441122185572116908)
XLA Ops:
  7.3 1.9 multiply_reduce_fusion.1
  10.7 2.0 multiply_convert_fusion.6
  14.4 2.1 collective-permute-start
  17.6 8.5 %collective-permute-done.1 = bf16[128,1792]{1,0:T(8,128)(2,1)S(1)} collective-permute-done((bf16[128,1792]{1,0:T(8,128)(2,1)S(1)}, bf16[128,1792]{1,0:T(8,128)(2,1)S(1)}, u32[]{:S(2)}, u32[]{:S(2)}) %collective-permute-start.1) | collective-permute-done | bytes 458784 | tf_op jit(solution)/shard_map/ppermute | solution.py:244
  26.8 9.2 %collective-permute-done = bf16[128,1792]{1,0:T(8,128)(2,1)S(1)} collective-permute-done((bf16[128,1792]{1,0:T(8,128)(2,1)S(1)}, bf16[128,1792]{1,0:T(8,128)(2,1)S(1)}, u32[]{:S(2)}, u32[]{:S(2)}) %collective-permute-start) | collective-permute-done | bytes 458784 | tf_op jit(solution)/shard_map/ppermute | solution.py:244
  35.9 1.4 add_convert_fusion.6
  39.5 13.8 %collective-permute-done.7 = bf16[128,1792]{1,0:T(8,128)(2,1)S(1)} collective-permute-done((bf16[128,1792]{1,0:T(8,128)(2,1)S(1)}, bf16[128,1792]{1,0:T(8,128)(2,1)S(1)}, u32[]{:S(2)}, u32[]{:S(2)}) %collective-permute-start.7) | collective-permute-done | bytes 458784 | tf_op jit(solution)/shard_map/ppermute | solution.py:244
  55.4 1.7 collective-permute-start.8
  57.8 2.5 collective-permute-done.2
  60.2 2.6 collective-permute-done.8
  64.8 7.2 %all-to-all-start = ((f32[32,1,128]{2,1,0:T(1,128)}), f32[32,1,128]{2,1,0:T(1,128)S(1)}, u32[]{:S(2)}, u32[]{:S(2)}) async-start(f32[32,1,128]{2,1,0:T(1,128)} %broadcast_in_dim.190), calls=%async_computation | async-start | bytes 32768 | tf_op jit(solution)/shard_map/all_to_all | solution.py:274
  72.1 5.7 %all-to-all-done = f32[32,1,128]{2,1,0:T(1,128)S(1)} async-done(((f32[32,1,128]{2,1,0:T(1,128)}), f32[32,1,128]{2,1,0:T(1,128)S(1)}, u32[]{:S(2)}, u32[]{:S(2)}) %all-to-all-start) | async-done | bytes 16416 | tf_op jit(solution)/shard_map/all_to_all | solution.py:274
  77.9 61.6 %all-gather.3.cloned.1.call-done = bf16[4096,896]{1,0:T(8,128)(2,1)} async-done(((bf16[128,896]{1,0:T(8,128)(2,1)}), bf16[4096,896]{1,0:T(8,128)(2,1)}) %all-gather.3.cloned.1.call-update) | async-done | bytes 7340048 | tf_op jit(solution)/shard_map/all_gather | solution.py:279
  139.5 4.0 constant_dynamic-slice_fusion.12
  145.2 23.9 %exponential_reduce_fusion = (f32[512]{0:T(512)S(1)}, f32[512]{0:T(512)S(1)}, f32[512]{0:T(512)S(1)}, f32[512,2048]{1,0:T(8,128)}) fusion(f32[512]{0:T(512)S(1)} %bitcast.210, s32[2048]{0:T(1024)S(1)} %iota_add_fusion, s32[512]{0:T(512)S(1)} %bitcast.214, bf16[512,7168]{1,0:T(8,128)(2,1)S(1)} %constant_dynamic-update-slice_fusion.rows_ref, ...), kind=kOutput, calls=%fused_computation.10 | convolution fusion | flops 15040774144 | bytes 40912896 | tf_op jit(solution)/shard_map/dot_general | solution.py:61
  169.9 4.0 all-to-all-start.1
  173.9 7.5 %all-to-all-done.1 = f32[32,3,4,128]{3,2,1,0:T(4,128)S(1)} async-done(((f32[32,3,4,128]{3,2,1,0:T(4,128)}), f32[32,3,4,128]{3,2,1,0:T(4,128)S(1)}, u32[]{:S(2)}, u32[]{:S(2)}) %all-to-all-start.1) | async-done | bytes 196640 | tf_op jit(solution)/shard_map/all_to_all | solution.py:53
  182.2 3.2 fusion.3.grad_ref
  185.4 14.5 %convolution_convert_fusion = bf16[256,7168]{1,0:T(8,128)(2,1)} fusion(bf16[2048,7168]{1,0:T(8,128)(2,1)} %param.17, bf16[512,2048]{1,0:T(8,128)(2,1)S(1)} %fusion.3.grad_ref), kind=kOutput, calls=%fused_computation | convolution fusion | flops 7518027776 | bytes 34078720 | tf_op jit(solution)/shard_map/dot_general | solution.py:184
  200.7 13.3 %convolution_convert_fusion.1 = bf16[256,7168]{1,0:T(8,128)(2,1)S(1)} fusion(bf16[2048,7168]{1,0:T(8,128)(2,1)} %param.17, bf16[512,2048]{1,0:T(8,128)(2,1)S(1)} %fusion.3.grad_ref), kind=kOutput, calls=%fused_computation.1 | convolution fusion | flops 7518027776 | bytes 34078720 | tf_op jit(solution)/shard_map/dot_general | solution.py:184
  214.1 3.4 add_convert_fusion
  219.0 1.5 collective-permute-start.10
  220.4 22.3 %shard_map.169 = (bf16[2048,7168]{1,0:T(8,128)(2,1)}, f32[8,128]{1,0:T(8,128)S(1)}) custom-call(bf16[512,2048]{1,0:T(8,128)(2,1)S(1)} %fusion.3.grad_ref, bf16[512,7168]{1,0:T(8,128)(2,1)} %copy-done.31, bf16[64,7168]{1,0:T(8,128)(2,1)S(1)} %get-tuple-element.43.rest_0_, bf16[4,128,896]{2,1,0:T(8,128)(2,1)S(1)} %pad_maximum_fusion.4.rest_1_), custom_call_target="tpu_custom_call" | custom-call | flops 15032385536 | bytes 36700160 | tf_op jit(solution)/shard_map/pallas_call | solution.py:92
  246.0 9.4 %collective-permute-done.13 = bf16[4,64,896]{2,1,0:T(8,128)(2,1)} collective-permute-done((bf16[4,64,896]{2,1,0:T(8,128)(2,1)S(1)}, bf16[4,64,896]{2,1,0:T(8,128)(2,1)}, u32[]{:S(2)}, u32[]{:S(2)}) %collective-permute-start.13) | collective-permute-done | bytes 458784 | tf_op jit(solution)/shard_map/ppermute | solution.py:28
  260.8 9.6 %collective-permute-done.14 = bf16[2,128,896]{2,1,0:T(8,128)(2,1)} collective-permute-done((bf16[2,128,896]{2,1,0:T(8,128)(2,1)}, bf16[2,128,896]{2,1,0:T(8,128)(2,1)}, u32[]{:S(2)}, u32[]{:S(2)}) %collective-permute-start.14) | collective-permute-done | bytes 458784 | tf_op jit(solution)/shard_map/ppermute | solution.py:28
  272.4 10.3 %collective-permute-done.15 = bf16[128,896]{1,0:T(8,128)(2,1)S(1)} collective-permute-done((bf16[128,896]{1,0:T(8,128)(2,1)S(1)}, bf16[128,896]{1,0:T(8,128)(2,1)S(1)}, u32[]{:S(2)}, u32[]{:S(2)}) %collective-permute-start.15) | collective-permute-done | bytes 229408 | tf_op jit(solution)/shard_map/ppermute | solution.py:28
  286.4 5.0 %collective-permute-done.16 = bf16[128,896]{1,0:T(8,128)(2,1)S(1)} collective-permute-done((bf16[128,896]{1,0:T(8,128)(2,1)S(1)}, bf16[128,896]{1,0:T(8,128)(2,1)S(1)}, u32[]{:S(2)}, u32[]{:S(2)}) %collective-permute-start.16) | collective-permute-done | bytes 229408 | tf_op jit(solution)/shard_map/ppermute | solution.py:244
  291.4 1.9 collective-permute-done.18
  293.3 2.3 fusion.6
  295.8 1.8 copy-done.5
  299.0 1.7 copy-done.7
  300.7 2.2 fusion.20
  305.1 16.8 %collective-permute-done.19 = bf16[4,128,896]{2,1,0:T(8,128)(2,1)S(1)} collective-permute-done((bf16[4,128,896]{2,1,0:T(8,128)(2,1)S(1)}, bf16[4,128,896]{2,1,0:T(8,128)(2,1)S(1)}, u32[]{:S(2)}, u32[]{:S(2)}) %collective-permute-start.19) | collective-permute-done | bytes 917536 | tf_op jit(solution)/shard_map/ppermute | solution.py:28
  323.0 2.5 fusion.11
  325.5 5.0 %shard_map.171 = (bf16[1792,896]{1,0:T(8,128)(2,1)}, f32[1792,128]{1,0:T(8,128)S(1)}) custom-call(bf16[512,1792]{1,0:T(8,128)(2,1)S(1)} %pad_maximum_fusion.2.normed_ref, bf16[512,896]{1,0:T(8,128)(2,1)S(1)} %get-tuple-element.38.grad_ref, bf16[1792,896]{1,0:T(8,128)(2,1)} %weight_ref.2, bf16[4,128,896]{2,1,0:T(8,128)(2,1)S(1)} %add_convert_fusion.1.rest_0_), custom_call_target="tpu_custom_call" | custom-call | flops 1644167168 | bytes 9175040 | tf_op jit(solution)/shard_map/pallas_call | solution.py:160
  330.8 5.3 %collective-permute-done.20 = bf16[2,128,896]{2,1,0:T(8,128)(2,1)S(1)} collective-permute-done((bf16[2,128,896]{2,1,0:T(8,128)(2,1)}, bf16[2,128,896]{2,1,0:T(8,128)(2,1)S(1)}, u32[]{:S(2)}, u32[]{:S(2)}) %collective-permute-start.20) | collective-permute-done | bytes 458784 | tf_op jit(solution)/shard_map/ppermute | solution.py:28
  336.6 4.9 %collective-permute-done.23.refs_1_ = bf16[4,128,896]{2,1,0:T(8,128)(2,1)S(1)} collective-permute-done((bf16[4,128,896]{2,1,0:T(8,128)(2,1)}, bf16[4,128,896]{2,1,0:T(8,128)(2,1)S(1)}, u32[]{:S(2)}, u32[]{:S(2)}) %collective-permute-start.23) | collective-permute-done | bytes 917536 | tf_op jit(solution)/shard_map/ppermute | solution.py:28
  345.4 5.0 %shard_map.172 = (bf16[1792,896]{1,0:T(8,128)(2,1)}, f32[1792,128]{1,0:T(8,128)S(1)}) custom-call(bf16[512,1792]{1,0:T(8,128)(2,1)S(1)} %copy-done, bf16[512,896]{1,0:T(8,128)(2,1)S(1)} %get-tuple-element.38.grad_ref, bf16[1792,896]{1,0:T(8,128)(2,1)} %weight_ref.3, bf16[128,896]{1,0:T(8,128)(2,1)S(1)} %fusion.39.rest_0_.refs_2_), custom_call_target="tpu_custom_call" | custom-call | flops 1644167168 | bytes 9175040 | tf_op jit(solution)/shard_map/pallas_call | solution.py:160
  351.0 8.2 %collective-permute-done.24 = bf16[2,128,896]{2,1,0:T(8,128)(2,1)} collective-permute-done((bf16[2,128,896]{2,1,0:T(8,128)(2,1)}, bf16[2,128,896]{2,1,0:T(8,128)(2,1)}, u32[]{:S(2)}, u32[]{:S(2)}) %collective-permute-start.24) | collective-permute-done | bytes 458784 | tf_op jit(solution)/shard_map/ppermute | solution.py:28
  361.6 5.3 %collective-permute-start.22 = (bf16[128,896]{1,0:T(8,128)(2,1)S(1)}, bf16[128,896]{1,0:T(8,128)(2,1)S(1)}, u32[]{:S(2)}, u32[]{:S(2)}) collective-permute-start(bf16[128,896]{1,0:T(8,128)(2,1)S(1)} %fusion.33), channel_id=1, source_target_pairs={{0,0},{1,1},{2,8},{3,9},{4,16},{5,17},{6,24},{7,25},{8,2},{9,3},{1... | collective-permute-start | bytes 688136 | tf_op jit(solution)/shard_map/ppermute | solution.py:353
  367.0 5.8 %collective-permute-done.25 = bf16[128,896]{1,0:T(8,128)(2,1)S(1)} collective-permute-done((bf16[128,896]{1,0:T(8,128)(2,1)S(1)}, bf16[128,896]{1,0:T(8,128)(2,1)S(1)}, u32[]{:S(2)}, u32[]{:S(2)}) %collective-permute-start.25) | collective-permute-done | bytes 229408 | tf_op jit(solution)/shard_map/ppermute | solution.py:28
  372.9 10.3 %collective-permute-done.22.refs_2_ = bf16[128,896]{1,0:T(8,128)(2,1)S(1)} collective-permute-done((bf16[128,896]{1,0:T(8,128)(2,1)S(1)}, bf16[128,896]{1,0:T(8,128)(2,1)S(1)}, u32[]{:S(2)}, u32[]{:S(2)}) %collective-permute-start.22) | collective-permute-done | bytes 229408 | tf_op jit(solution)/shard_map/ppermute | solution.py:353
  383.9 3.0 all-to-all-start.2
  388.2 4.3 %collective-permute-start.26 = (bf16[128,896]{1,0:T(8,128)(2,1)S(1)}, bf16[128,896]{1,0:T(8,128)(2,1)S(1)}, u32[]{:S(2)}, u32[]{:S(2)}) collective-permute-start(bf16[128,896]{1,0:T(8,128)(2,1)S(1)} %fusion.29.refs_1_), channel_id=1, source_target_pairs={{0,0},{1,1},{2,8},{3,9},{4,16},{5,17},{6,24},{7,25},{8,2},{9,3},{1... | collective-permute-start | bytes 688136 | tf_op jit(solution)/shard_map/ppermute | solution.py:353
  392.5 3.9 all-to-all-done.2
  398.0 1.8 subtract_convert_fusion.1
  399.8 6.1 %collective-permute-done.26 = bf16[128,896]{1,0:T(8,128)(2,1)S(1)} collective-permute-done((bf16[128,896]{1,0:T(8,128)(2,1)S(1)}, bf16[128,896]{1,0:T(8,128)(2,1)S(1)}, u32[]{:S(2)}, u32[]{:S(2)}) %collective-permute-start.26) | collective-permute-done | bytes 229408 | tf_op jit(solution)/shard_map/ppermute | solution.py:353
  405.9 1.8 subtract_convert_fusion
  (227 shorter events, 46.7 us)
Async XLA Ops:
  7.2 132.3 %all-gather.3.cloned.1.call-start = ((), (), s32[]{:S(2)}) async-start(), calls=%async_computation.3 | async-start | bytes 7569408 | tf_op jit(solution)/shard_map/all_gather | solution.py:279
  12.6 44.5 %copy-start.9 = (bf16[128,1792]{1,0:T(8,128)(2,1)}, bf16[128,1792]{1,0:T(8,128)(2,1)S(1)}, u32[]{:S(2)}) copy-start(bf16[128,1792]{1,0:T(8,128)(2,1)S(1)} %get-tuple-element.45) | copy-start | bytes 1376260
  12.6 13.5 %collective-permute-start.1 = (bf16[128,1792]{1,0:T(8,128)(2,1)S(1)}, bf16[128,1792]{1,0:T(8,128)(2,1)S(1)}, u32[]{:S(2)}, u32[]{:S(2)}) collective-permute-start(bf16[128,1792]{1,0:T(8,128)(2,1)S(1)} %get-tuple-element.48), channel_id=1, source_target_pairs={{0,16},{8,24},{16,0},{24,8},{1,17},{9,25},{17,1},{25,9},{2,18},{10... | collective-permute-start | bytes 1376264 | tf_op jit(solution)/shard_map/ppermute | solution.py:244
  14.4 12.4 %copy-start.11 = (bf16[128,1792]{1,0:T(8,128)(2,1)}, bf16[128,1792]{1,0:T(8,128)(2,1)S(1)}, u32[]{:S(2)}) copy-start(bf16[128,1792]{1,0:T(8,128)(2,1)S(1)} %get-tuple-element.49) | copy-start | bytes 1376260
  14.4 11.7 %copy-start.6 = (bf16[1792,896]{1,0:T(8,128)(2,1)S(1)}, bf16[1792,896]{1,0:T(8,128)(2,1)}, u32[]{:S(2)}) copy-start(bf16[1792,896]{1,0:T(8,128)(2,1)} %weight_ref.3) | copy-start | bytes 9633796
  14.4 21.5 %collective-permute-start = (bf16[128,1792]{1,0:T(8,128)(2,1)S(1)}, bf16[128,1792]{1,0:T(8,128)(2,1)S(1)}, u32[]{:S(2)}, u32[]{:S(2)}) collective-permute-start(bf16[128,1792]{1,0:T(8,128)(2,1)S(1)} %get-tuple-element.52), channel_id=1, source_target_pairs={{0,16},{8,24},{16,0},{24,8},{1,17},{9,25},{17,1},{25,9},{2,18},{10... | collective-permute-start | bytes 1376264 | tf_op jit(solution)/shard_map/ppermute | solution.py:244
  16.4 21.6 %collective-permute-start.3 = (bf16[128,1792]{1,0:T(8,128)(2,1)S(1)}, bf16[128,1792]{1,0:T(8,128)(2,1)S(1)}, u32[]{:S(2)}, u32[]{:S(2)}) collective-permute-start(bf16[128,1792]{1,0:T(8,128)(2,1)S(1)} %get-tuple-element.50), channel_id=1, source_target_pairs={{0,8},{8,0},{16,24},{24,16},{1,9},{9,1},{17,25},{25,17},{2,10},{10... | collective-permute-start | bytes 1376264 | tf_op jit(solution)/shard_map/ppermute | solution.py:244
  16.4 20.9 %collective-permute-start.4 = (bf16[128,1792]{1,0:T(8,128)(2,1)S(1)}, bf16[128,1792]{1,0:T(8,128)(2,1)S(1)}, u32[]{:S(2)}, u32[]{:S(2)}) collective-permute-start(bf16[128,1792]{1,0:T(8,128)(2,1)S(1)} %get-tuple-element.46), channel_id=1, source_target_pairs={{0,8},{8,0},{16,24},{24,16},{1,9},{9,1},{17,25},{25,17},{2,10},{10... | collective-permute-start | bytes 1376264 | tf_op jit(solution)/shard_map/ppermute | solution.py:244
  17.0 37.0 %collective-permute-start.6 = (bf16[128,1792]{1,0:T(8,128)(2,1)S(1)}, bf16[128,1792]{1,0:T(8,128)(2,1)S(1)}, u32[]{:S(2)}, u32[]{:S(2)}) collective-permute-start(bf16[128,1792]{1,0:T(8,128)(2,1)S(1)} %get-tuple-element.51), channel_id=1, source_target_pairs={{0,24},{8,16},{16,8},{24,0},{1,25},{9,17},{17,9},{25,1},{2,26},{10... | collective-permute-start | bytes 1376264 | tf_op jit(solution)/shard_map/ppermute | solution.py:244
  17.6 45.3 %copy-start.15 = (f32[128,896]{1,0:T(8,128)}, f32[128,896]{1,0:T(8,128)S(1)}, u32[]{:S(2)}) copy-start(f32[128,896]{1,0:T(8,128)S(1)} %fusion.65) | copy-start | bytes 1376260
  26.1 27.2 %collective-permute-start.7 = (bf16[128,1792]{1,0:T(8,128)(2,1)S(1)}, bf16[128,1792]{1,0:T(8,128)(2,1)S(1)}, u32[]{:S(2)}, u32[]{:S(2)}) collective-permute-start(bf16[128,1792]{1,0:T(8,128)(2,1)S(1)} %get-tuple-element.47), channel_id=1, source_target_pairs={{0,24},{8,16},{16,8},{24,0},{1,25},{9,17},{17,9},{25,1},{2,26},{10... | collective-permute-start | bytes 1376264 | tf_op jit(solution)/shard_map/ppermute | solution.py:244
  37.4 22.9 %collective-permute-start.2 = (bf16[128,896]{1,0:T(8,128)(2,1)S(1)}, bf16[128,896]{1,0:T(8,128)(2,1)S(1)}, u32[]{:S(2)}, u32[]{:S(2)}) collective-permute-start(bf16[128,896]{1,0:T(8,128)(2,1)S(1)} %get-tuple-element.105), channel_id=1, source_target_pairs={{0,16},{8,24},{16,0},{24,8},{1,17},{9,25},{17,1},{25,9},{2,18},{10... | collective-permute-start | bytes 688136 | tf_op jit(solution)/shard_map/ppermute | solution.py:244
  39.5 20.7 %collective-permute-start.5 = (bf16[128,896]{1,0:T(8,128)(2,1)S(1)}, bf16[128,896]{1,0:T(8,128)(2,1)S(1)}, u32[]{:S(2)}, u32[]{:S(2)}) collective-permute-start(bf16[128,896]{1,0:T(8,128)(2,1)S(1)} %get-tuple-element.103), channel_id=1, source_target_pairs={{0,8},{8,0},{16,24},{24,16},{1,9},{9,1},{17,25},{25,17},{2,10},{10... | collective-permute-start | bytes 688136 | tf_op jit(solution)/shard_map/ppermute | solution.py:244
  55.4 7.5 %collective-permute-start.8 = (bf16[128,896]{1,0:T(8,128)(2,1)S(1)}, bf16[128,896]{1,0:T(8,128)(2,1)S(1)}, u32[]{:S(2)}, u32[]{:S(2)}) collective-permute-start(bf16[128,896]{1,0:T(8,128)(2,1)S(1)} %get-tuple-element.101), channel_id=1, source_target_pairs={{0,24},{8,16},{16,8},{24,0},{1,25},{9,17},{17,9},{25,1},{2,26},{10... | collective-permute-start | bytes 688136 | tf_op jit(solution)/shard_map/ppermute | solution.py:244
  64.1 117.5 %copy-start.37 = (pred[4,4]{1,0:T(4,128)(4,1)}, pred[4,4]{1,0:T(4,128)(4,1)S(1)}, u32[]{:S(2)}) copy-start(pred[4,4]{1,0:T(4,128)(4,1)S(1)} %iota_compare_fusion) | copy-start | bytes 52
  64.8 13.0 %all-to-all-start = ((f32[32,1,128]{2,1,0:T(1,128)}), f32[32,1,128]{2,1,0:T(1,128)S(1)}, u32[]{:S(2)}, u32[]{:S(2)}) async-start(f32[32,1,128]{2,1,0:T(1,128)} %broadcast_in_dim.190), calls=%async_computation | async-start | bytes 32768 | tf_op jit(solution)/shard_map/all_to_all | solution.py:274
  145.1 24.0 %copy-start.31 = (bf16[512,7168]{1,0:T(8,128)(2,1)}, bf16[512,7168]{1,0:T(8,128)(2,1)S(1)}, u32[]{:S(2)}) copy-start(bf16[512,7168]{1,0:T(8,128)(2,1)S(1)} %constant_dynamic-update-slice_fusion.rows_ref) | copy-start | bytes 22020100
  145.2 28.8 %copy-start.39 = (s32[512]{0:T(512)S(1)}, s32[512]{0:T(512)}, u32[]{:S(2)}) copy-start(s32[512]{0:T(512)} %param.19) | copy-start | bytes 6148
  169.9 11.5 %all-to-all-start.1 = ((f32[32,3,4,128]{3,2,1,0:T(4,128)}), f32[32,3,4,128]{3,2,1,0:T(4,128)S(1)}, u32[]{:S(2)}, u32[]{:S(2)}) async-start(f32[32,3,4,128]{3,2,1,0:T(4,128)} %broadcast_in_dim.200), calls=%async_computation.1 | async-start | bytes 393216 | tf_op jit(solution)/shard_map/all_to_all | solution.py:53
  200.0 14.1 %collective-permute-start.9 = (bf16[256,7168]{1,0:T(8,128)(2,1)}, bf16[256,7168]{1,0:T(8,128)(2,1)}, u32[]{:S(2)}, u32[]{:S(2)}) collective-permute-start(bf16[256,7168]{1,0:T(8,128)(2,1)} %convolution_convert_fusion), channel_id=1, source_target_pairs={{0,8},{8,0},{16,24},{24,16},{1,9},{9,1},{17,25},{25,17},{2,10},{10... | collective-permute-start | bytes 11010056 | tf_op jit(solution)/shard_map/ppermute | solution.py:28
  218.1 24.6 %collective-permute-start.12 = (bf16[4,128,896]{2,1,0:T(8,128)(2,1)S(1)}, bf16[4,128,896]{2,1,0:T(8,128)(2,1)S(1)}, u32[]{:S(2)}, u32[]{:S(2)}) collective-permute-start(bf16[4,128,896]{2,1,0:T(8,128)(2,1)S(1)} %pad_maximum_fusion.4.rest_1_), channel_id=1, source_target_pairs={{0,1},{1,0},{2,3},{3,2},{4,5},{5,4},{6,7},{7,6},{8,9},{9,8},{10,11... | collective-permute-start | bytes 2752520 | tf_op jit(solution)/shard_map/ppermute | solution.py:28
  219.0 24.7 %collective-permute-start.10 = (bf16[64,7168]{1,0:T(8,128)(2,1)S(1)}, bf16[64,7168]{1,0:T(8,128)(2,1)S(1)}, u32[]{:S(2)}, u32[]{:S(2)}) collective-permute-start(bf16[64,7168]{1,0:T(8,128)(2,1)S(1)} %get-tuple-element.43.rest_0_), channel_id=1, source_target_pairs={{0,16},{8,24},{16,0},{24,8},{1,17},{9,25},{17,1},{25,9},{2,18},{10... | collective-permute-start | bytes 2752520 | tf_op jit(solution)/shard_map/ppermute | solution.py:28
  243.0 12.4 %collective-permute-start.13 = (bf16[4,64,896]{2,1,0:T(8,128)(2,1)S(1)}, bf16[4,64,896]{2,1,0:T(8,128)(2,1)}, u32[]{:S(2)}, u32[]{:S(2)}) collective-permute-start(bf16[4,64,896]{2,1,0:T(8,128)(2,1)S(1)} %slice_bitcast_fusion.2), channel_id=1, source_target_pairs={{0,16},{8,24},{16,0},{24,8},{1,17},{9,25},{17,1},{25,9},{2,18},{10... | collective-permute-start | bytes 1376264 | tf_op jit(solution)/shard_map/ppermute | solution.py:28
  244.7 12.2 %collective-permute-start.11 = (bf16[4,64,896]{2,1,0:T(8,128)(2,1)S(1)}, bf16[4,64,896]{2,1,0:T(8,128)(2,1)}, u32[]{:S(2)}, u32[]{:S(2)}) collective-permute-start(bf16[4,64,896]{2,1,0:T(8,128)(2,1)S(1)} %pad_maximum_fusion.8), channel_id=1, source_target_pairs={{0,1},{1,0},{2,3},{3,2},{4,5},{5,4},{6,7},{7,6},{8,9},{9,8},{10,11... | collective-permute-start | bytes 1376264 | tf_op jit(solution)/shard_map/ppermute | solution.py:28
  259.0 11.4 %collective-permute-start.14 = (bf16[2,128,896]{2,1,0:T(8,128)(2,1)}, bf16[2,128,896]{2,1,0:T(8,128)(2,1)}, u32[]{:S(2)}, u32[]{:S(2)}) collective-permute-start(bf16[2,128,896]{2,1,0:T(8,128)(2,1)} %pad_maximum_fusion.9), channel_id=1, source_target_pairs={{0,2},{1,3},{2,0},{3,1},{4,6},{5,7},{6,4},{7,5},{8,10},{9,11},{10,... | collective-permute-start | bytes 1376264 | tf_op jit(solution)/shard_map/ppermute | solution.py:28
  271.6 13.5 %copy-start.10 = (bf16[128,1792]{1,0:T(8,128)(2,1)S(1)}, bf16[128,1792]{1,0:T(8,128)(2,1)}, u32[]{:S(2)}) copy-start(bf16[128,1792]{1,0:T(8,128)(2,1)} %copy-done.9) | copy-start | bytes 1376260
  271.6 13.5 %copy-start.26 = (bf16[128,1792]{1,0:T(8,128)(2,1)S(1)}, bf16[128,1792]{1,0:T(8,128)(2,1)}, u32[]{:S(2)}) copy-start(bf16[128,1792]{1,0:T(8,128)(2,1)} %copy-done.25) | copy-start | bytes 1376260
  271.6 13.5 %copy-start.28 = (bf16[128,1792]{1,0:T(8,128)(2,1)S(1)}, bf16[128,1792]{1,0:T(8,128)(2,1)}, u32[]{:S(2)}) copy-start(bf16[128,1792]{1,0:T(8,128)(2,1)} %copy-done.27) | copy-start | bytes 1376260
  271.6 13.5 %copy-start.30 = (bf16[128,1792]{1,0:T(8,128)(2,1)S(1)}, bf16[128,1792]{1,0:T(8,128)(2,1)}, u32[]{:S(2)}) copy-start(bf16[128,1792]{1,0:T(8,128)(2,1)} %copy-done.29) | copy-start | bytes 1376260
  271.6 11.1 %collective-permute-start.15 = (bf16[128,896]{1,0:T(8,128)(2,1)S(1)}, bf16[128,896]{1,0:T(8,128)(2,1)S(1)}, u32[]{:S(2)}, u32[]{:S(2)}) collective-permute-start(bf16[128,896]{1,0:T(8,128)(2,1)S(1)} %fusion.38), channel_id=1, source_target_pairs={{0,4},{1,5},{2,6},{3,7},{4,0},{5,1},{6,2},{7,3},{8,12},{9,13},{10,... | collective-permute-start | bytes 688136 | tf_op jit(solution)/shard_map/ppermute | solution.py:28
  282.8 8.6 %collective-permute-start.16 = (bf16[128,896]{1,0:T(8,128)(2,1)S(1)}, bf16[128,896]{1,0:T(8,128)(2,1)S(1)}, u32[]{:S(2)}, u32[]{:S(2)}) collective-permute-start(bf16[128,896]{1,0:T(8,128)(2,1)S(1)} %fusion.37), channel_id=1, source_target_pairs={{0,16},{8,24},{16,0},{24,8},{1,17},{9,25},{17,1},{25,9},{2,18},{10... | collective-permute-start | bytes 688136 | tf_op jit(solution)/shard_map/ppermute | solution.py:244
  284.2 7.3 %collective-permute-start.17 = (bf16[128,896]{1,0:T(8,128)(2,1)S(1)}, bf16[128,896]{1,0:T(8,128)(2,1)S(1)}, u32[]{:S(2)}, u32[]{:S(2)}) collective-permute-start(bf16[128,896]{1,0:T(8,128)(2,1)S(1)} %fusion.37), channel_id=1, source_target_pairs={{0,8},{8,0},{16,24},{24,16},{1,9},{9,1},{17,25},{25,17},{2,10},{10... | collective-permute-start | bytes 688136 | tf_op jit(solution)/shard_map/ppermute | solution.py:244
  284.2 9.1 %collective-permute-start.18 = (bf16[128,896]{1,0:T(8,128)(2,1)S(1)}, bf16[128,896]{1,0:T(8,128)(2,1)S(1)}, u32[]{:S(2)}, u32[]{:S(2)}) collective-permute-start(bf16[128,896]{1,0:T(8,128)(2,1)S(1)} %fusion.37), channel_id=1, source_target_pairs={{0,24},{8,16},{16,8},{24,0},{1,25},{9,17},{17,9},{25,1},{2,26},{10... | collective-permute-start | bytes 688136 | tf_op jit(solution)/shard_map/ppermute | solution.py:244
  298.8 23.1 %collective-permute-start.19 = (bf16[4,128,896]{2,1,0:T(8,128)(2,1)S(1)}, bf16[4,128,896]{2,1,0:T(8,128)(2,1)S(1)}, u32[]{:S(2)}, u32[]{:S(2)}) collective-permute-start(bf16[4,128,896]{2,1,0:T(8,128)(2,1)S(1)} %bitcast.222), channel_id=1, source_target_pairs={{0,1},{1,0},{2,3},{3,2},{4,5},{5,4},{6,7},{7,6},{8,9},{9,8},{10,11... | collective-permute-start | bytes 2752520 | tf_op jit(solution)/shard_map/ppermute | solution.py:28
  302.9 38.7 %collective-permute-start.23 = (bf16[4,128,896]{2,1,0:T(8,128)(2,1)}, bf16[4,128,896]{2,1,0:T(8,128)(2,1)S(1)}, u32[]{:S(2)}, u32[]{:S(2)}) collective-permute-start(bf16[4,128,896]{2,1,0:T(8,128)(2,1)} %bitcast.74), channel_id=1, source_target_pairs={{0,1},{1,0},{2,3},{3,2},{4,5},{5,4},{6,7},{7,6},{8,9},{9,8},{10,11... | collective-permute-start | bytes 2752520 | tf_op jit(solution)/shard_map/ppermute | solution.py:28
  323.0 13.1 %collective-permute-start.20 = (bf16[2,128,896]{2,1,0:T(8,128)(2,1)}, bf16[2,128,896]{2,1,0:T(8,128)(2,1)S(1)}, u32[]{:S(2)}, u32[]{:S(2)}) collective-permute-start(bf16[2,128,896]{2,1,0:T(8,128)(2,1)} %pad_maximum_fusion.10), channel_id=1, source_target_pairs={{0,2},{1,3},{2,0},{3,1},{4,6},{5,7},{6,4},{7,5},{8,10},{9,11},{10,... | collective-permute-start | bytes 1376264 | tf_op jit(solution)/shard_map/ppermute | solution.py:28
  336.3 24.2 %collective-permute-start.21 = (bf16[128,896]{1,0:T(8,128)(2,1)S(1)}, bf16[128,896]{1,0:T(8,128)(2,1)S(1)}, u32[]{:S(2)}, u32[]{:S(2)}) collective-permute-start(bf16[128,896]{1,0:T(8,128)(2,1)S(1)} %fusion.39.rest_0_.refs_2_), channel_id=1, source_target_pairs={{0,4},{1,5},{2,6},{3,7},{4,0},{5,1},{6,2},{7,3},{8,12},{9,13},{10,... | collective-permute-start | bytes 688136 | tf_op jit(solution)/shard_map/ppermute | solution.py:28
  344.7 14.5 %collective-permute-start.24 = (bf16[2,128,896]{2,1,0:T(8,128)(2,1)}, bf16[2,128,896]{2,1,0:T(8,128)(2,1)}, u32[]{:S(2)}, u32[]{:S(2)}) collective-permute-start(bf16[2,128,896]{2,1,0:T(8,128)(2,1)} %pad_maximum_fusion.11), channel_id=1, source_target_pairs={{0,2},{1,3},{2,0},{3,1},{4,6},{5,7},{6,4},{7,5},{8,10},{9,11},{10,... | collective-permute-start | bytes 1376264 | tf_op jit(solution)/shard_map/ppermute | solution.py:28
  360.4 26.6 %copy-start.34 = (f32[3,4,128]{2,1,0:T(4,128)S(1)}, f32[3,4,128]{2,1,0:T(4,128)}, u32[]{:S(2)}) copy-start(f32[3,4,128]{2,1,0:T(4,128)} %copy-done.33) | copy-start | bytes 18436
  360.4 26.6 %copy-start.40 = (s32[512]{0:T(512)S(1)}, s32[512]{0:T(512)}, u32[]{:S(2)}) copy-start(s32[512]{0:T(512)} %param.19) | copy-start | bytes 6148
  360.4 37.6 %copy-start.46 = (f32[128]{0:T(128)S(1)}, f32[128]{0:T(128)}, u32[]{:S(2)}) copy-start(f32[128]{0:T(128)} %copy-done.45) | copy-start | bytes 1540
  360.4 37.6 %copy-start.48 = (f32[128]{0:T(128)S(1)}, f32[128]{0:T(128)}, u32[]{:S(2)}) copy-start(f32[128]{0:T(128)} %get-tuple-element.99) | copy-start | bytes 1540
  360.4 12.4 %collective-permute-start.25 = (bf16[128,896]{1,0:T(8,128)(2,1)S(1)}, bf16[128,896]{1,0:T(8,128)(2,1)S(1)}, u32[]{:S(2)}, u32[]{:S(2)}) collective-permute-start(bf16[128,896]{1,0:T(8,128)(2,1)S(1)} %fusion.40), channel_id=1, source_target_pairs={{0,4},{1,5},{2,6},{3,7},{4,0},{5,1},{6,2},{7,3},{8,12},{9,13},{10,... | collective-permute-start | bytes 688136 | tf_op jit(solution)/shard_map/ppermute | solution.py:28
  361.6 44.3 %copy-start.44 = (f32[128]{0:T(128)S(1)}, f32[128]{0:T(128)}, u32[]{:S(2)}) copy-start(f32[128]{0:T(128)} %copy-done.43) | copy-start | bytes 1540
  361.6 44.3 %copy-start.47 = (f32[128]{0:T(128)S(1)}, f32[128]{0:T(128)}, u32[]{:S(2)}) copy-start(f32[128]{0:T(128)} %get-tuple-element.97) | copy-start | bytes 1540
  361.6 21.6 %collective-permute-start.22 = (bf16[128,896]{1,0:T(8,128)(2,1)S(1)}, bf16[128,896]{1,0:T(8,128)(2,1)S(1)}, u32[]{:S(2)}, u32[]{:S(2)}) collective-permute-start(bf16[128,896]{1,0:T(8,128)(2,1)S(1)} %fusion.33), channel_id=1, source_target_pairs={{0,0},{1,1},{2,8},{3,9},{4,16},{5,17},{6,24},{7,25},{8,2},{9,3},{1... | collective-permute-start | bytes 688136 | tf_op jit(solution)/shard_map/ppermute | solution.py:353
  383.9 12.5 %all-to-all-start.2 = ((f32[32,2,1024]{2,1,0:T(2,128)}), f32[32,2,1024]{2,1,0:T(2,128)S(1)}, u32[]{:S(2)}, u32[]{:S(2)}) async-start(f32[32,2,1024]{2,1,0:T(2,128)} %shard_map.174), calls=%async_computation.2 | async-start | bytes 524288 | tf_op jit(solution)/shard_map/all_to_all | solution.py:405
  388.2 17.6 %collective-permute-start.26 = (bf16[128,896]{1,0:T(8,128)(2,1)S(1)}, bf16[128,896]{1,0:T(8,128)(2,1)S(1)}, u32[]{:S(2)}, u32[]{:S(2)}) collective-permute-start(bf16[128,896]{1,0:T(8,128)(2,1)S(1)} %fusion.29.refs_1_), channel_id=1, source_target_pairs={{0,0},{1,1},{2,8},{3,9},{4,16},{5,17},{6,24},{7,25},{8,2},{9,3},{1... | collective-permute-start | bytes 688136 | tf_op jit(solution)/shard_map/ppermute | solution.py:353
  (32 other events, 151.8 us)
Sparse Core Ops, SparseCore 0:
  64.0 75.4 all-gather.2

commit v7 on v6

--- a/solution.py
+++ b/solution.py
@@ -37,12 +37,13 @@
 def exchange_near(chunks, dim):
     here = dim.place()
     pick = [lax.dynamic_index_in_dim(chunks, here ^ bit, 0, keepdims=False) for bit in range(4)]
-    got = dim.swap(jnp.stack([pick[1], pick[3]]), 1).astype(F32)
-    return pick[0].astype(F32) + got[0], (pick[2].astype(F32) + got[1]).astype(BF16)
+    sent = jnp.stack([pick[1], pick[3]])
+    got = dim.swap(sent, 1).astype(F32)
+    return pick[0].astype(F32) + got[0], (pick[2].astype(F32) + got[1]).astype(BF16), sent
 
 
 def exchange_far(pair, dim):
-    near, far = pair
+    near, far = pair[:2]
     return (near + dim.swap(far, 2).astype(F32)).astype(BF16)
 
 
@@ -362,30 +363,67 @@
         weight_half = cut(weight, (place % 2) * cols, cols, 0)
         return contract_last(picked, weight_half).reshape(va, block, cols)
 
-    def exchanged(weight):
-        return [dim_b.swap(products(weight, b ^ r).astype(BF16), r) for r in range(1, vb)]
-
-    got_h, got_e = exchanged(proj_hidden), exchanged(proj_embed)
-    kept_h = products(proj_hidden, b)
-    for value in got_h:
-        kept_h = kept_h + value.astype(F32)
-    kept_h = kept_h.astype(BF16)
-    pair_h = exchange_near(kept_h, dim_a)
-    kept_e = products(proj_embed, b)
-    for value in got_e[1:]:
-        kept_e = kept_e + value.astype(F32)
-    kept_e = add_after(kept_e, got_e[0], [pair_h[1]])
-    hidden_moved = final_move(exchange_far(pair_h, dim_a))
-    pair_e = exchange_near(kept_e, dim_a)
-    hidden_back = hidden_moved.astype(F32)
-    embed_summed = exchange_far(pair_e, dim_a)
-    embed_back = final_move(embed_summed).astype(F32)
+    if vb == nv // nc:
+        def half_weight(weight, place):
+            return cut(weight, place * cols, cols, 0)
+
+        def along_b(weight):
+            return [
+                dim_b.swap(contract_last(proj_grad, half_weight(weight, b ^ r)).astype(BF16), r)
+                for r in range(1, vb)
+            ]
+
+        def to_owners(value):
+            value = value.reshape(nc, block, cols)
+            moved = [
+                send(value[index], rc, (nx - rx) % nx)
+                for index, (rc, rx) in enumerate(places[1:], 1)
+            ]
+            return [value[0]] + moved
+
+        def by_holder(pieces):
+            at = [(c ^ (i % 2)) * nx + (i // 2 - x) % nx for i in range(nc)]
+            stack = jnp.stack(pieces)
+            return jnp.stack(
+                [lax.dynamic_index_in_dim(stack, at[i], 0, keepdims=False) for i in range(nc)]
+            )
+
+        got_h, got_e = along_b(proj_hidden), along_b(proj_embed)
+        kept_h = contract_last(proj_grad, half_weight(proj_hidden, b))
+        for value in got_h:
+            kept_h = kept_h + value.astype(F32)
+        kept_h = kept_h.astype(BF16)
+        owned_h = to_owners(kept_h)
+        pair_h = exchange_near(by_holder(owned_h), dim_a)
+        kept_e = contract_last(proj_grad, half_weight(proj_embed, b))
+        for value in got_e[1:]:
+            kept_e = kept_e + value.astype(F32)
+        kept_e = add_after(kept_e, got_e[0], [pair_h[2]])
+        owned_e = to_owners(kept_e)
+        marks = [kept_h], [pair_h[2]], [owned_e[nx], pair_h[1]]
+        owned_e[nx] = held_back(owned_e[nx], [pair_h[1]])
+        hidden_back = exchange_far(pair_h, dim_a).astype(F32)
+        embed_back = exchange_far(exchange_near(by_holder(owned_e), dim_a), dim_a).astype(F32)
+    else:
+        got_h, got_e = [
+            [dim_b.swap(products(weight, b ^ r).astype(BF16), r) for r in range(1, vb)]
+            for weight in (proj_hidden, proj_embed)
+        ]
+        kept_h, kept_e = products(proj_hidden, b), products(proj_embed, b)
+        for value_h, value_e in zip(got_h, got_e):
+            kept_h = kept_h + value_h.astype(F32)
+            kept_e = kept_e + value_e.astype(F32)
+        pair_h = exchange_near(kept_h.astype(BF16), dim_a)
+        pair_e = exchange_near(kept_e.astype(BF16), dim_a)
+        hidden_back = final_move(exchange_far(pair_h, dim_a)).astype(F32)
+        embed_back = final_move(exchange_far(pair_e, dim_a)).astype(F32)
+        marks = [proj_grad], [proj_grad], [proj_grad]
 
     grad_proj_hidden, gain_h = weight_gradient(
-        jnp.concatenate(blocks_h), proj_grad, proj_hidden, [kept_h]
+        jnp.concatenate(blocks_h), proj_grad, proj_hidden, marks[0]
     )
     grad_proj_embed, gain_e = weight_gradient(
-        jnp.concatenate(blocks_e), proj_grad, proj_embed, [pair_h[1]]
+        jnp.concatenate(blocks_e), proj_grad, proj_embed, marks[1]
     )
 
     wide = lax.optimization_barrier(proj_grad).astype(F32).reshape(nc, block, cols)
@@ -401,7 +439,7 @@
     gains = jnp.where(holder, gains, F32(0.0)).reshape(nv, 2, cols)
     gains = jnp.broadcast_to(gains[None], (nc, nv, 2, cols))
     ends = jnp.concatenate([dots, gains], axis=-1).reshape(nc * nv, 2, block + cols)
-    ends = held_back(ends, [embed_summed, hidden_moved])
+    ends = held_back(ends, marks[2])
     ends = jnp.sum(lax.all_to_all(ends, ("ctx", "vocab"), 0, 0, tiled=True), axis=0)
 
     def finish(kind, source, gain):

time: 424 us -> 409 us (0.965)
  the two profiles are of different devices: /device:TPU:2 before, /device:TPU:0 now
where the time goes in v7:
time: 409 us; the launch traced here: 402 us
  waiting for transfers between devices  196 us (48%)
  matrix products  66.4 us (16%)
  starting transfers between devices  37.8 us (9%)
  other arithmetic  36.7 us (9%)
  Pallas kernels  34.8 us (9%)
  between operations  17.2 us (4%)
  local copies, waits for them, and re-layouts  13.6 us (3%)
    ppermute x13, waiting for transfers between devices, move(): return lax.ppermute(value, self.axis, pairs)  68.8 us
    all_gather x1, waiting for transfers between devices, local(): lax.all_gather(piece, ('ctx', 'vocab')).reshape(nc, nv, block, cols)  60.6 us
    ppermute x18, waiting for transfers between devices, send(): return lax.ppermute(value, 'ctx', pairs)  50.7 us
    dot_general x10, matrix products, dot(): return jnp.dot(left, right, preferred_element_type=F32)  35.4 us
    dot_general x5, matrix products, contract_last(): lax.dot_general(left, right, (((1,), (1,)), ((), ())), preferred_element_...  31 us
    pallas_call x1, Pallas kernels, head_gradient(): pl.pallas_call(body, grid=(entries // TILE,), in_specs=[pl.BlockSpec((tok...  22.2 us
    ppermute x18, starting transfers between devices, send(): return lax.ppermute(value, 'ctx', pairs)  15.4 us
    pallas_call x2, Pallas kernels, weight_gradient(): kernel_call(body, (feat // tile,), [pl.BlockSpec((tokens, tile), lambda s...  10.3 us
  transfers between devices with their start and end apart: 35, of which 21 were waited for; matrix products, arithmetic and copies ran while one was open for 12% of the time, Pallas kernels for 9%

profile of v7, /device:TPU:0, one launch (start us, length us, event | category | flops | bytes accessed | tf_op | source)
XLA Modules:
  0.0 402.1 jit_solution(8385313217810340354)
XLA Ops:
  7.3 2.0 multiply_reduce_fusion.1
  10.8 2.0 multiply_convert_fusion.6
  12.8 3.0 collective-permute-start.1
  18.1 1.6 collective-permute-start.6
  20.3 6.9 %collective-permute-done.1 = bf16[128,1792]{1,0:T(8,128)(2,1)S(1)} collective-permute-done((bf16[128,1792]{1,0:T(8,128)(2,1)S(1)}, bf16[128,1792]{1,0:T(8,128)(2,1)S(1)}, u32[]{:S(2)}, u32[]{:S(2)}) %collective-permute-start.1) | collective-permute-done | bytes 458784 | tf_op jit(solution)/shard_map/ppermute | solution.py:245
  27.8 9.2 %collective-permute-done = bf16[128,1792]{1,0:T(8,128)(2,1)S(1)} collective-permute-done((bf16[128,1792]{1,0:T(8,128)(2,1)S(1)}, bf16[128,1792]{1,0:T(8,128)(2,1)S(1)}, u32[]{:S(2)}, u32[]{:S(2)}) %collective-permute-start) | collective-permute-done | bytes 458784 | tf_op jit(solution)/shard_map/ppermute | solution.py:245
  37.0 1.4 add_convert_fusion.6
  38.4 2.1 collective-permute-start.2
  41.2 1.4 add_convert_fusion.5
  42.6 13.6 %collective-permute-done.7 = bf16[128,1792]{1,0:T(8,128)(2,1)S(1)} collective-permute-done((bf16[128,1792]{1,0:T(8,128)(2,1)S(1)}, bf16[128,1792]{1,0:T(8,128)(2,1)S(1)}, u32[]{:S(2)}, u32[]{:S(2)}) %collective-permute-start.7) | collective-permute-done | bytes 458784 | tf_op jit(solution)/shard_map/ppermute | solution.py:245
  56.9 1.4 add_convert_fusion.4
  58.4 1.9 collective-permute-start.8
  61.0 5.2 %collective-permute-done.8 = bf16[128,896]{1,0:T(8,128)(2,1)S(1)} collective-permute-done((bf16[128,896]{1,0:T(8,128)(2,1)S(1)}, bf16[128,896]{1,0:T(8,128)(2,1)S(1)}, u32[]{:S(2)}, u32[]{:S(2)}) %collective-permute-start.8) | collective-permute-done | bytes 229408 | tf_op jit(solution)/shard_map/ppermute | solution.py:245
  68.0 5.5 %all-to-all-start = ((f32[32,1,128]{2,1,0:T(1,128)}), f32[32,1,128]{2,1,0:T(1,128)S(1)}, u32[]{:S(2)}, u32[]{:S(2)}) async-start(f32[32,1,128]{2,1,0:T(1,128)} %broadcast_in_dim.190), calls=%async_computation | async-start | bytes 32768 | tf_op jit(solution)/shard_map/all_to_all | solution.py:275
  73.6 7.0 %all-to-all-done = f32[32,1,128]{2,1,0:T(1,128)S(1)} async-done(((f32[32,1,128]{2,1,0:T(1,128)}), f32[32,1,128]{2,1,0:T(1,128)S(1)}, u32[]{:S(2)}, u32[]{:S(2)}) %all-to-all-start) | async-done | bytes 16416 | tf_op jit(solution)/shard_map/all_to_all | solution.py:275
  80.8 60.6 %all-gather.3.cloned.1.call-done = bf16[4096,896]{1,0:T(8,128)(2,1)} async-done(((bf16[128,896]{1,0:T(8,128)(2,1)}), bf16[4096,896]{1,0:T(8,128)(2,1)}) %all-gather.3.cloned.1.call-update) | async-done | bytes 7340048 | tf_op jit(solution)/shard_map/all_gather | solution.py:280
  141.4 4.0 constant_dynamic-slice_fusion.12
  147.0 23.9 %exponential_reduce_fusion = (f32[512]{0:T(512)S(1)}, f32[512]{0:T(512)S(1)}, f32[512]{0:T(512)S(1)}, f32[512,2048]{1,0:T(8,128)}) fusion(f32[512]{0:T(512)S(1)} %bitcast.224, s32[2048]{0:T(1024)S(1)} %iota_add_fusion, s32[512]{0:T(512)S(1)} %bitcast.228, bf16[512,7168]{1,0:T(8,128)(2,1)S(1)} %constant_dynamic-update-slice_fusion.rows_ref, ...), kind=kOutput, calls=%fused_computation.10 | convolution fusion | flops 15040774144 | bytes 40912896 | tf_op jit(solution)/shard_map/dot_general | solution.py:62
  171.8 3.3 all-to-all-start.1
  175.1 8.5 %all-to-all-done.1 = f32[32,3,4,128]{3,2,1,0:T(4,128)S(1)} async-done(((f32[32,3,4,128]{3,2,1,0:T(4,128)}), f32[32,3,4,128]{3,2,1,0:T(4,128)S(1)}, u32[]{:S(2)}, u32[]{:S(2)}) %all-to-all-start.1) | async-done | bytes 196640 | tf_op jit(solution)/shard_map/all_to_all | solution.py:54
  183.8 3.2 fusion.3.grad_ref
  187.0 14.5 %convolution_convert_fusion = bf16[256,7168]{1,0:T(8,128)(2,1)} fusion(bf16[2048,7168]{1,0:T(8,128)(2,1)} %param.17, bf16[512,2048]{1,0:T(8,128)(2,1)S(1)} %fusion.3.grad_ref), kind=kOutput, calls=%fused_computation | convolution fusion | flops 7518027776 | bytes 34078720 | tf_op jit(solution)/shard_map/dot_general | solution.py:185
  201.7 13.3 %convolution_convert_fusion.1 = bf16[256,7168]{1,0:T(8,128)(2,1)S(1)} fusion(bf16[2048,7168]{1,0:T(8,128)(2,1)} %param.17, bf16[512,2048]{1,0:T(8,128)(2,1)S(1)} %fusion.3.grad_ref), kind=kOutput, calls=%fused_computation.1 | convolution fusion | flops 7518027776 | bytes 34078720 | tf_op jit(solution)/shard_map/dot_general | solution.py:185
  215.1 3.4 add_convert_fusion
  219.2 1.8 collective-permute-start.12
  221.5 22.2 %shard_map.169 = (bf16[2048,7168]{1,0:T(8,128)(2,1)}, f32[8,128]{1,0:T(8,128)S(1)}) custom-call(bf16[512,2048]{1,0:T(8,128)(2,1)S(1)} %fusion.3.grad_ref, bf16[512,7168]{1,0:T(8,128)(2,1)} %copy-done.28, bf16[64,7168]{1,0:T(8,128)(2,1)S(1)} %get-tuple-element.43.rest_0_, bf16[4,128,896]{2,1,0:T(8,128)(2,1)S(1)} %pad_maximum_fusion.4.rest_1_), custom_call_target="tpu_custom_call" | custom-call | flops 15032385536 | bytes 36700160 | tf_op jit(solution)/shard_map/pallas_call | solution.py:93
  244.0 1.6 collective-permute-start.13
  247.0 9.4 %collective-permute-done.13 = bf16[4,64,896]{2,1,0:T(8,128)(2,1)} collective-permute-done((bf16[4,64,896]{2,1,0:T(8,128)(2,1)S(1)}, bf16[4,64,896]{2,1,0:T(8,128)(2,1)}, u32[]{:S(2)}, u32[]{:S(2)}) %collective-permute-start.13) | collective-permute-done | bytes 458784 | tf_op jit(solution)/shard_map/ppermute | solution.py:28
  262.8 9.2 %collective-permute-done.14 = bf16[2,128,896]{2,1,0:T(8,128)(2,1)} collective-permute-done((bf16[2,128,896]{2,1,0:T(8,128)(2,1)}, bf16[2,128,896]{2,1,0:T(8,128)(2,1)}, u32[]{:S(2)}, u32[]{:S(2)}) %collective-permute-start.14) | collective-permute-done | bytes 458784 | tf_op jit(solution)/shard_map/ppermute | solution.py:28
  273.9 10.2 %collective-permute-done.15 = bf16[128,896]{1,0:T(8,128)(2,1)S(1)} collective-permute-done((bf16[128,896]{1,0:T(8,128)(2,1)S(1)}, bf16[128,896]{1,0:T(8,128)(2,1)S(1)}, u32[]{:S(2)}, u32[]{:S(2)}) %collective-permute-start.15) | collective-permute-done | bytes 229408 | tf_op jit(solution)/shard_map/ppermute | solution.py:28
  286.6 6.3 %collective-permute-done.16 = bf16[128,896]{1,0:T(8,128)(2,1)S(1)} collective-permute-done((bf16[128,896]{1,0:T(8,128)(2,1)S(1)}, bf16[128,896]{1,0:T(8,128)(2,1)S(1)}, u32[]{:S(2)}, u32[]{:S(2)}) %collective-permute-start.16) | collective-permute-done | bytes 229408 | tf_op jit(solution)/shard_map/ppermute | solution.py:245
  292.9 2.1 collective-permute-done.18
  295.0 2.3 fusion.6
  299.2 2.2 fusion.22
  303.4 2.5 fusion.11.refs_0_
  305.9 16.0 %collective-permute-done.19 = bf16[512,896]{1,0:T(8,128)(2,1)S(1)} collective-permute-done((bf16[512,896]{1,0:T(8,128)(2,1)S(1)}, bf16[512,896]{1,0:T(8,128)(2,1)S(1)}, u32[]{:S(2)}, u32[]{:S(2)}) %collective-permute-start.19) | collective-permute-done | bytes 917536 | tf_op jit(solution)/shard_map/ppermute | solution.py:28
  326.0 5.0 %shard_map.171 = (bf16[1792,896]{1,0:T(8,128)(2,1)}, f32[1792,128]{1,0:T(8,128)S(1)}) custom-call(bf16[512,1792]{1,0:T(8,128)(2,1)S(1)} %pad_maximum_fusion.2.normed_ref, bf16[512,896]{1,0:T(8,128)(2,1)S(1)} %get-tuple-element.38.grad_ref, bf16[1792,896]{1,0:T(8,128)(2,1)} %weight_ref.2, bf16[512,896]{1,0:T(8,128)(2,1)S(1)} %add_convert_fusion.1.rest_0_), custom_call_target="tpu_custom_call" | custom-call | flops 1644167168 | bytes 9175040 | tf_op jit(solution)/shard_map/pallas_call | solution.py:161
  332.6 3.0 collective-permute-done.22
  338.0 3.5 collective-permute-done.25.refs_1_
  345.6 5.3 %shard_map.172 = (bf16[1792,896]{1,0:T(8,128)(2,1)}, f32[1792,128]{1,0:T(8,128)S(1)}) custom-call(bf16[512,1792]{1,0:T(8,128)(2,1)S(1)} %pad_maximum_fusion.3.normed_ref, bf16[512,896]{1,0:T(8,128)(2,1)S(1)} %get-tuple-element.38.grad_ref, bf16[1792,896]{1,0:T(8,128)(2,1)} %weight_ref.3, bf16[2,128,896]{2,1,0:T(8,128)(2,1)S(1)} %pad_maximum_fusion.12.rest_0_.refs_2_), custom_call_target="tpu_custom_call" | custom-call | flops 1644167168 | bytes 9175040 | tf_op jit(solution)/shard_map/pallas_call | solution.py:161
  353.3 3.3 collective-permute-done.28
  359.3 3.7 all-to-all-start.2
  364.2 2.7 collective-permute-start.24
  367.0 9.7 %collective-permute-done.29 = bf16[2,128,896]{2,1,0:T(8,128)(2,1)} collective-permute-done((bf16[2,128,896]{2,1,0:T(8,128)(2,1)S(1)}, bf16[2,128,896]{2,1,0:T(8,128)(2,1)}, u32[]{:S(2)}, u32[]{:S(2)}) %collective-permute-start.29) | collective-permute-done | bytes 458784 | tf_op jit(solution)/shard_map/ppermute | solution.py:28
  380.0 7.6 %collective-permute-done.24 = bf16[128,896]{1,0:T(8,128)(2,1)} collective-permute-done((bf16[128,896]{1,0:T(8,128)(2,1)S(1)}, bf16[128,896]{1,0:T(8,128)(2,1)}, u32[]{:S(2)}, u32[]{:S(2)}) %collective-permute-start.24) | collective-permute-done | bytes 229408 | tf_op jit(solution)/shard_map/ppermute | solution.py:28
  387.7 2.1 subtract_convert_fusion.1
  389.7 2.3 collective-permute-done.30
  392.0 1.8 subtract_convert_fusion
  (214 shorter events, 50.3 us)
Async XLA Ops:
  7.2 134.2 %all-gather.3.cloned.1.call-start = ((), (), s32[]{:S(2)}) async-start(), calls=%async_computation.3 | async-start | bytes 7569408 | tf_op jit(solution)/shard_map/all_gather | solution.py:280
  12.8 47.5 %copy-start.6 = (bf16[128,1792]{1,0:T(8,128)(2,1)}, bf16[128,1792]{1,0:T(8,128)(2,1)S(1)}, u32[]{:S(2)}) copy-start(bf16[128,1792]{1,0:T(8,128)(2,1)S(1)} %get-tuple-element.45) | copy-start | bytes 1376260
  12.8 14.4 %collective-permute-start.1 = (bf16[128,1792]{1,0:T(8,128)(2,1)S(1)}, bf16[128,1792]{1,0:T(8,128)(2,1)S(1)}, u32[]{:S(2)}, u32[]{:S(2)}) collective-permute-start(bf16[128,1792]{1,0:T(8,128)(2,1)S(1)} %get-tuple-element.48), channel_id=1, source_target_pairs={{0,16},{8,24},{16,0},{24,8},{1,17},{9,25},{17,1},{25,9},{2,18},{10... | collective-permute-start | bytes 1376264 | tf_op jit(solution)/shard_map/ppermute | solution.py:245
  17.4 19.6 %collective-permute-start = (bf16[128,1792]{1,0:T(8,128)(2,1)S(1)}, bf16[128,1792]{1,0:T(8,128)(2,1)S(1)}, u32[]{:S(2)}, u32[]{:S(2)}) collective-permute-start(bf16[128,1792]{1,0:T(8,128)(2,1)S(1)} %get-tuple-element.52), channel_id=1, source_target_pairs={{0,16},{8,24},{16,0},{24,8},{1,17},{9,25},{17,1},{25,9},{2,18},{10... | collective-permute-start | bytes 1376264 | tf_op jit(solution)/shard_map/ppermute | solution.py:245
  17.5 23.6 %collective-permute-start.3 = (bf16[128,1792]{1,0:T(8,128)(2,1)S(1)}, bf16[128,1792]{1,0:T(8,128)(2,1)S(1)}, u32[]{:S(2)}, u32[]{:S(2)}) collective-permute-start(bf16[128,1792]{1,0:T(8,128)(2,1)S(1)} %get-tuple-element.50), channel_id=1, source_target_pairs={{0,8},{8,0},{16,24},{24,16},{1,9},{9,1},{17,25},{25,17},{2,10},{10... | collective-permute-start | bytes 1376264 | tf_op jit(solution)/shard_map/ppermute | solution.py:245
  17.6 22.9 %collective-permute-start.4 = (bf16[128,1792]{1,0:T(8,128)(2,1)S(1)}, bf16[128,1792]{1,0:T(8,128)(2,1)S(1)}, u32[]{:S(2)}, u32[]{:S(2)}) collective-permute-start(bf16[128,1792]{1,0:T(8,128)(2,1)S(1)} %get-tuple-element.46), channel_id=1, source_target_pairs={{0,8},{8,0},{16,24},{24,16},{1,9},{9,1},{17,25},{25,17},{2,10},{10... | collective-permute-start | bytes 1376264 | tf_op jit(solution)/shard_map/ppermute | solution.py:245
  18.1 38.8 %collective-permute-start.6 = (bf16[128,1792]{1,0:T(8,128)(2,1)S(1)}, bf16[128,1792]{1,0:T(8,128)(2,1)S(1)}, u32[]{:S(2)}, u32[]{:S(2)}) collective-permute-start(bf16[128,1792]{1,0:T(8,128)(2,1)S(1)} %get-tuple-element.51), channel_id=1, source_target_pairs={{0,24},{8,16},{16,8},{24,0},{1,25},{9,17},{17,9},{25,1},{2,26},{10... | collective-permute-start | bytes 1376264 | tf_op jit(solution)/shard_map/ppermute | solution.py:245
  20.3 45.9 %copy-start.10 = (f32[128,896]{1,0:T(8,128)}, f32[128,896]{1,0:T(8,128)S(1)}, u32[]{:S(2)}) copy-start(f32[128,896]{1,0:T(8,128)S(1)} %fusion.63) | copy-start | bytes 1376260
  27.2 11.3 %copy-start.22 = (bf16[128,1792]{1,0:T(8,128)(2,1)}, bf16[128,1792]{1,0:T(8,128)(2,1)S(1)}, u32[]{:S(2)}) copy-start(bf16[128,1792]{1,0:T(8,128)(2,1)S(1)} %collective-permute-done.1) | copy-start | bytes 1376260
  27.2 29.1 %collective-permute-start.7 = (bf16[128,1792]{1,0:T(8,128)(2,1)S(1)}, bf16[128,1792]{1,0:T(8,128)(2,1)S(1)}, u32[]{:S(2)}, u32[]{:S(2)}) collective-permute-start(bf16[128,1792]{1,0:T(8,128)(2,1)S(1)} %get-tuple-element.47), channel_id=1, source_target_pairs={{0,24},{8,16},{16,8},{24,0},{1,25},{9,17},{17,9},{25,1},{2,26},{10... | collective-permute-start | bytes 1376264 | tf_op jit(solution)/shard_map/ppermute | solution.py:245
  38.4 22.5 %collective-permute-start.2 = (bf16[128,896]{1,0:T(8,128)(2,1)S(1)}, bf16[128,896]{1,0:T(8,128)(2,1)S(1)}, u32[]{:S(2)}, u32[]{:S(2)}) collective-permute-start(bf16[128,896]{1,0:T(8,128)(2,1)S(1)} %get-tuple-element.113), channel_id=1, source_target_pairs={{0,16},{8,24},{16,0},{24,8},{1,17},{9,25},{17,1},{25,9},{2,18},{10... | collective-permute-start | bytes 688136 | tf_op jit(solution)/shard_map/ppermute | solution.py:245
  41.2 15.7 %copy-start.18 = (bf16[128,1792]{1,0:T(8,128)(2,1)}, bf16[128,1792]{1,0:T(8,128)(2,1)S(1)}, u32[]{:S(2)}) copy-start(bf16[128,1792]{1,0:T(8,128)(2,1)S(1)} %collective-permute-done.3) | copy-start | bytes 1376260
  42.6 18.3 %collective-permute-start.5 = (bf16[128,896]{1,0:T(8,128)(2,1)S(1)}, bf16[128,896]{1,0:T(8,128)(2,1)S(1)}, u32[]{:S(2)}, u32[]{:S(2)}) collective-permute-start(bf16[128,896]{1,0:T(8,128)(2,1)S(1)} %get-tuple-element.111), channel_id=1, source_target_pairs={{0,8},{8,0},{16,24},{24,16},{1,9},{9,1},{17,25},{25,17},{2,10},{10... | collective-permute-start | bytes 688136 | tf_op jit(solution)/shard_map/ppermute | solution.py:245
  58.4 7.8 %collective-permute-start.8 = (bf16[128,896]{1,0:T(8,128)(2,1)S(1)}, bf16[128,896]{1,0:T(8,128)(2,1)S(1)}, u32[]{:S(2)}, u32[]{:S(2)}) collective-permute-start(bf16[128,896]{1,0:T(8,128)(2,1)S(1)} %get-tuple-element.109), channel_id=1, source_target_pairs={{0,24},{8,16},{16,8},{24,0},{1,25},{9,17},{17,9},{25,1},{2,26},{10... | collective-permute-start | bytes 688136 | tf_op jit(solution)/shard_map/ppermute | solution.py:245
  68.0 12.6 %all-to-all-start = ((f32[32,1,128]{2,1,0:T(1,128)}), f32[32,1,128]{2,1,0:T(1,128)S(1)}, u32[]{:S(2)}, u32[]{:S(2)}) async-start(f32[32,1,128]{2,1,0:T(1,128)} %broadcast_in_dim.190), calls=%async_computation | async-start | bytes 32768 | tf_op jit(solution)/shard_map/all_to_all | solution.py:275
  147.0 24.0 %copy-start.28 = (bf16[512,7168]{1,0:T(8,128)(2,1)}, bf16[512,7168]{1,0:T(8,128)(2,1)S(1)}, u32[]{:S(2)}) copy-start(bf16[512,7168]{1,0:T(8,128)(2,1)S(1)} %constant_dynamic-update-slice_fusion.rows_ref) | copy-start | bytes 22020100
  147.0 28.1 %copy-start.32 = (s32[512]{0:T(512)S(1)}, s32[512]{0:T(512)}, u32[]{:S(2)}) copy-start(s32[512]{0:T(512)} %param.19) | copy-start | bytes 6148
  171.8 11.9 %all-to-all-start.1 = ((f32[32,3,4,128]{3,2,1,0:T(4,128)}), f32[32,3,4,128]{3,2,1,0:T(4,128)S(1)}, u32[]{:S(2)}, u32[]{:S(2)}) async-start(f32[32,3,4,128]{3,2,1,0:T(4,128)} %broadcast_in_dim.200), calls=%async_computation.1 | async-start | bytes 393216 | tf_op jit(solution)/shard_map/all_to_all | solution.py:54
  201.6 13.5 %collective-permute-start.9 = (bf16[256,7168]{1,0:T(8,128)(2,1)}, bf16[256,7168]{1,0:T(8,128)(2,1)}, u32[]{:S(2)}, u32[]{:S(2)}) collective-permute-start(bf16[256,7168]{1,0:T(8,128)(2,1)} %convolution_convert_fusion), channel_id=1, source_target_pairs={{0,8},{8,0},{16,24},{24,16},{1,9},{9,1},{17,25},{25,17},{2,10},{10... | collective-permute-start | bytes 11010056 | tf_op jit(solution)/shard_map/ppermute | solution.py:28
  219.2 24.5 %collective-permute-start.12 = (bf16[4,128,896]{2,1,0:T(8,128)(2,1)S(1)}, bf16[4,128,896]{2,1,0:T(8,128)(2,1)S(1)}, u32[]{:S(2)}, u32[]{:S(2)}) collective-permute-start(bf16[4,128,896]{2,1,0:T(8,128)(2,1)S(1)} %pad_maximum_fusion.4.rest_1_), channel_id=1, source_target_pairs={{0,1},{1,0},{2,3},{3,2},{4,5},{5,4},{6,7},{7,6},{8,9},{9,8},{10,11... | collective-permute-start | bytes 2752520 | tf_op jit(solution)/shard_map/ppermute | solution.py:28
  220.9 24.6 %collective-permute-start.10 = (bf16[64,7168]{1,0:T(8,128)(2,1)S(1)}, bf16[64,7168]{1,0:T(8,128)(2,1)S(1)}, u32[]{:S(2)}, u32[]{:S(2)}) collective-permute-start(bf16[64,7168]{1,0:T(8,128)(2,1)S(1)} %get-tuple-element.43.rest_0_), channel_id=1, source_target_pairs={{0,16},{8,24},{16,0},{24,8},{1,17},{9,25},{17,1},{25,9},{2,18},{10... | collective-permute-start | bytes 2752520 | tf_op jit(solution)/shard_map/ppermute | solution.py:28
  244.0 12.5 %collective-permute-start.13 = (bf16[4,64,896]{2,1,0:T(8,128)(2,1)S(1)}, bf16[4,64,896]{2,1,0:T(8,128)(2,1)}, u32[]{:S(2)}, u32[]{:S(2)}) collective-permute-start(bf16[4,64,896]{2,1,0:T(8,128)(2,1)S(1)} %slice_bitcast_fusion.2), channel_id=1, source_target_pairs={{0,16},{8,24},{16,0},{24,8},{1,17},{9,25},{17,1},{25,9},{2,18},{10... | collective-permute-start | bytes 1376264 | tf_op jit(solution)/shard_map/ppermute | solution.py:28
  246.6 14.6 %copy-start.11 = (f32[128,896]{1,0:T(8,128)S(1)}, f32[128,896]{1,0:T(8,128)}, u32[]{:S(2)}) copy-start(f32[128,896]{1,0:T(8,128)} %copy-done.10) | copy-start | bytes 1376260
  246.6 12.0 %collective-permute-start.11 = (bf16[4,64,896]{2,1,0:T(8,128)(2,1)S(1)}, bf16[4,64,896]{2,1,0:T(8,128)(2,1)S(1)}, u32[]{:S(2)}, u32[]{:S(2)}) collective-permute-start(bf16[4,64,896]{2,1,0:T(8,128)(2,1)S(1)} %pad_maximum_fusion.10), channel_id=1, source_target_pairs={{0,1},{1,0},{2,3},{3,2},{4,5},{5,4},{6,7},{7,6},{8,9},{9,8},{10,11... | collective-permute-start | bytes 1376264 | tf_op jit(solution)/shard_map/ppermute | solution.py:28
  260.6 11.3 %collective-permute-start.14 = (bf16[2,128,896]{2,1,0:T(8,128)(2,1)}, bf16[2,128,896]{2,1,0:T(8,128)(2,1)}, u32[]{:S(2)}, u32[]{:S(2)}) collective-permute-start(bf16[2,128,896]{2,1,0:T(8,128)(2,1)} %pad_maximum_fusion.11), channel_id=1, source_target_pairs={{0,2},{1,3},{2,0},{3,1},{4,6},{5,7},{6,4},{7,5},{8,10},{9,11},{10,... | collective-permute-start | bytes 1376264 | tf_op jit(solution)/shard_map/ppermute | solution.py:28
  273.0 13.4 %copy-start.7 = (bf16[128,1792]{1,0:T(8,128)(2,1)S(1)}, bf16[128,1792]{1,0:T(8,128)(2,1)}, u32[]{:S(2)}) copy-start(bf16[128,1792]{1,0:T(8,128)(2,1)} %copy-done.6) | copy-start | bytes 1376260
  273.0 13.4 %copy-start.23 = (bf16[128,1792]{1,0:T(8,128)(2,1)S(1)}, bf16[128,1792]{1,0:T(8,128)(2,1)}, u32[]{:S(2)}) copy-start(bf16[128,1792]{1,0:T(8,128)(2,1)} %copy-done.22) | copy-start | bytes 1376260
  273.1 13.4 %copy-start.25 = (bf16[128,1792]{1,0:T(8,128)(2,1)S(1)}, bf16[128,1792]{1,0:T(8,128)(2,1)}, u32[]{:S(2)}) copy-start(bf16[128,1792]{1,0:T(8,128)(2,1)} %copy-done.24) | copy-start | bytes 1376260
  273.1 13.4 %copy-start.27 = (bf16[128,1792]{1,0:T(8,128)(2,1)S(1)}, bf16[128,1792]{1,0:T(8,128)(2,1)}, u32[]{:S(2)}) copy-start(bf16[128,1792]{1,0:T(8,128)(2,1)} %copy-done.26) | copy-start | bytes 1376260
  273.1 11.0 %collective-permute-start.15 = (bf16[128,896]{1,0:T(8,128)(2,1)S(1)}, bf16[128,896]{1,0:T(8,128)(2,1)S(1)}, u32[]{:S(2)}, u32[]{:S(2)}) collective-permute-start(bf16[128,896]{1,0:T(8,128)(2,1)S(1)} %fusion.40), channel_id=1, source_target_pairs={{0,4},{1,5},{2,6},{3,7},{4,0},{5,1},{6,2},{7,3},{8,12},{9,13},{10,... | collective-permute-start | bytes 688136 | tf_op jit(solution)/shard_map/ppermute | solution.py:28
  284.2 13.0 %copy-start.2 = (bf16[1792,896]{1,0:T(8,128)(2,1)S(1)}, bf16[1792,896]{1,0:T(8,128)(2,1)}, u32[]{:S(2)}) copy-start(bf16[1792,896]{1,0:T(8,128)(2,1)} %weight_ref.2) | copy-start | bytes 9633796
  284.3 8.6 %collective-permute-start.16 = (bf16[128,896]{1,0:T(8,128)(2,1)S(1)}, bf16[128,896]{1,0:T(8,128)(2,1)S(1)}, u32[]{:S(2)}, u32[]{:S(2)}) collective-permute-start(bf16[128,896]{1,0:T(8,128)(2,1)S(1)} %fusion.39), channel_id=1, source_target_pairs={{0,16},{8,24},{16,0},{24,8},{1,17},{9,25},{17,1},{25,9},{2,18},{10... | collective-permute-start | bytes 688136 | tf_op jit(solution)/shard_map/ppermute | solution.py:245
  285.4 7.4 %collective-permute-start.17 = (bf16[128,896]{1,0:T(8,128)(2,1)S(1)}, bf16[128,896]{1,0:T(8,128)(2,1)S(1)}, u32[]{:S(2)}, u32[]{:S(2)}) collective-permute-start(bf16[128,896]{1,0:T(8,128)(2,1)S(1)} %fusion.39), channel_id=1, source_target_pairs={{0,8},{8,0},{16,24},{24,16},{1,9},{9,1},{17,25},{25,17},{2,10},{10... | collective-permute-start | bytes 688136 | tf_op jit(solution)/shard_map/ppermute | solution.py:245
  285.5 9.5 %collective-permute-start.18 = (bf16[128,896]{1,0:T(8,128)(2,1)S(1)}, bf16[128,896]{1,0:T(8,128)(2,1)S(1)}, u32[]{:S(2)}, u32[]{:S(2)}) collective-permute-start(bf16[128,896]{1,0:T(8,128)(2,1)S(1)} %fusion.39), channel_id=1, source_target_pairs={{0,24},{8,16},{16,8},{24,0},{1,25},{9,17},{17,9},{25,1},{2,26},{10... | collective-permute-start | bytes 688136 | tf_op jit(solution)/shard_map/ppermute | solution.py:245
  298.5 23.3 %collective-permute-start.19 = (bf16[512,896]{1,0:T(8,128)(2,1)S(1)}, bf16[512,896]{1,0:T(8,128)(2,1)S(1)}, u32[]{:S(2)}, u32[]{:S(2)}) collective-permute-start(bf16[512,896]{1,0:T(8,128)(2,1)S(1)} %fusion.19), channel_id=1, source_target_pairs={{0,1},{1,0},{2,3},{3,2},{4,5},{5,4},{6,7},{7,6},{8,9},{9,8},{10,11... | collective-permute-start | bytes 2752520 | tf_op jit(solution)/shard_map/ppermute | solution.py:28
  301.4 40.1 %collective-permute-start.25 = (bf16[512,896]{1,0:T(8,128)(2,1)}, bf16[512,896]{1,0:T(8,128)(2,1)}, u32[]{:S(2)}, u32[]{:S(2)}) collective-permute-start(bf16[512,896]{1,0:T(8,128)(2,1)} %fusion.22), channel_id=1, source_target_pairs={{0,1},{1,0},{2,3},{3,2},{4,5},{5,4},{6,7},{7,6},{8,9},{9,8},{10,11... | collective-permute-start | bytes 2752520 | tf_op jit(solution)/shard_map/ppermute | solution.py:28
  323.9 8.7 %collective-permute-start.20 = (bf16[128,896]{1,0:T(8,128)(2,1)}, bf16[128,896]{1,0:T(8,128)(2,1)S(1)}, u32[]{:S(2)}, u32[]{:S(2)}) collective-permute-start(bf16[128,896]{1,0:T(8,128)(2,1)} %get-tuple-element.80), channel_id=1, source_target_pairs={{0,16},{8,24},{16,0},{24,8},{1,17},{9,25},{17,1},{25,9},{2,18},{10... | collective-permute-start | bytes 688136 | tf_op jit(solution)/shard_map/ppermute | solution.py:245
  324.6 8.0 %collective-permute-start.21 = (bf16[128,896]{1,0:T(8,128)(2,1)}, bf16[128,896]{1,0:T(8,128)(2,1)}, u32[]{:S(2)}, u32[]{:S(2)}) collective-permute-start(bf16[128,896]{1,0:T(8,128)(2,1)} %get-tuple-element.79), channel_id=1, source_target_pairs={{0,8},{8,0},{16,24},{24,16},{1,9},{9,1},{17,25},{25,17},{2,10},{10... | collective-permute-start | bytes 688136 | tf_op jit(solution)/shard_map/ppermute | solution.py:245
  325.2 10.4 %collective-permute-start.22 = (bf16[128,896]{1,0:T(8,128)(2,1)S(1)}, bf16[128,896]{1,0:T(8,128)(2,1)}, u32[]{:S(2)}, u32[]{:S(2)}) collective-permute-start(bf16[128,896]{1,0:T(8,128)(2,1)S(1)} %get-tuple-element.78), channel_id=1, source_target_pairs={{0,24},{8,16},{16,8},{24,0},{1,25},{9,17},{17,9},{25,1},{2,26},{10... | collective-permute-start | bytes 688136 | tf_op jit(solution)/shard_map/ppermute | solution.py:245
  337.2 14.0 %collective-permute-start.23 = (bf16[2,128,896]{2,1,0:T(8,128)(2,1)S(1)}, bf16[2,128,896]{2,1,0:T(8,128)(2,1)}, u32[]{:S(2)}, u32[]{:S(2)}) collective-permute-start(bf16[2,128,896]{2,1,0:T(8,128)(2,1)S(1)} %pad_maximum_fusion.12.rest_0_.refs_2_), channel_id=1, source_target_pairs={{0,2},{1,3},{2,0},{3,1},{4,6},{5,7},{6,4},{7,5},{8,10},{9,11},{10,... | collective-permute-start | bytes 1376264 | tf_op jit(solution)/shard_map/ppermute | solution.py:28
  343.7 9.5 %collective-permute-start.26 = (bf16[128,896]{1,0:T(8,128)(2,1)}, bf16[128,896]{1,0:T(8,128)(2,1)S(1)}, u32[]{:S(2)}, u32[]{:S(2)}) collective-permute-start(bf16[128,896]{1,0:T(8,128)(2,1)} %get-tuple-element.70), channel_id=1, source_target_pairs={{0,8},{8,0},{16,24},{24,16},{1,9},{9,1},{17,25},{25,17},{2,10},{10... | collective-permute-start | bytes 688136 | tf_op jit(solution)/shard_map/ppermute | solution.py:245
  343.7 9.6 %collective-permute-start.27 = (bf16[128,896]{1,0:T(8,128)(2,1)}, bf16[128,896]{1,0:T(8,128)(2,1)}, u32[]{:S(2)}, u32[]{:S(2)}) collective-permute-start(bf16[128,896]{1,0:T(8,128)(2,1)} %get-tuple-element.69), channel_id=1, source_target_pairs={{0,16},{8,24},{16,0},{24,8},{1,17},{9,25},{17,1},{25,9},{2,18},{10... | collective-permute-start | bytes 688136 | tf_op jit(solution)/shard_map/ppermute | solution.py:245
  344.7 11.8 %collective-permute-start.28 = (bf16[128,896]{1,0:T(8,128)(2,1)}, bf16[128,896]{1,0:T(8,128)(2,1)}, u32[]{:S(2)}, u32[]{:S(2)}) collective-permute-start(bf16[128,896]{1,0:T(8,128)(2,1)} %get-tuple-element.68), channel_id=1, source_target_pairs={{0,24},{8,16},{16,8},{24,0},{1,25},{9,17},{17,9},{25,1},{2,26},{10... | collective-permute-start | bytes 688136 | tf_op jit(solution)/shard_map/ppermute | solution.py:245
  358.1 29.6 %copy-start.34 = (f32[128]{0:T(128)S(1)}, f32[128]{0:T(128)}, u32[]{:S(2)}) copy-start(f32[128]{0:T(128)} %copy-done.33) | copy-start | bytes 1540
  358.1 18.6 %collective-permute-start.29 = (bf16[2,128,896]{2,1,0:T(8,128)(2,1)S(1)}, bf16[2,128,896]{2,1,0:T(8,128)(2,1)}, u32[]{:S(2)}, u32[]{:S(2)}) collective-permute-start(bf16[2,128,896]{2,1,0:T(8,128)(2,1)S(1)} %pad_maximum_fusion.13), channel_id=1, source_target_pairs={{0,2},{1,3},{2,0},{3,1},{4,6},{5,7},{6,4},{7,5},{8,10},{9,11},{10,... | collective-permute-start | bytes 1376264 | tf_op jit(solution)/shard_map/ppermute | solution.py:28
  359.3 19.3 %all-to-all-start.2 = ((f32[32,2,1024]{2,1,0:T(2,128)}), f32[32,2,1024]{2,1,0:T(2,128)S(1)}, u32[]{:S(2)}, u32[]{:S(2)}) async-start(f32[32,2,1024]{2,1,0:T(2,128)} %shard_map.174), calls=%async_computation.2 | async-start | bytes 524288 | tf_op jit(solution)/shard_map/all_to_all | solution.py:443
  364.2 23.4 %collective-permute-start.24 = (bf16[128,896]{1,0:T(8,128)(2,1)S(1)}, bf16[128,896]{1,0:T(8,128)(2,1)}, u32[]{:S(2)}, u32[]{:S(2)}) collective-permute-start(bf16[128,896]{1,0:T(8,128)(2,1)S(1)} %fusion.41.refs_2_.refs_1_), channel_id=1, source_target_pairs={{0,4},{1,5},{2,6},{3,7},{4,0},{5,1},{6,2},{7,3},{8,12},{9,13},{10,... | collective-permute-start | bytes 688136 | tf_op jit(solution)/shard_map/ppermute | solution.py:28
  378.5 13.5 %collective-permute-start.30 = (bf16[128,896]{1,0:T(8,128)(2,1)}, bf16[128,896]{1,0:T(8,128)(2,1)S(1)}, u32[]{:S(2)}, u32[]{:S(2)}) collective-permute-start(bf16[128,896]{1,0:T(8,128)(2,1)} %fusion.42), channel_id=1, source_target_pairs={{0,4},{1,5},{2,6},{3,7},{4,0},{5,1},{6,2},{7,3},{8,12},{9,13},{10,... | collective-permute-start | bytes 688136 | tf_op jit(solution)/shard_map/ppermute | solution.py:28
  (23 other events, 144.8 us)
Sparse Core Ops, SparseCore 0:
  67.3 74.0 all-gather.2

commit v8 on v7

--- a/solution.py
+++ b/solution.py
@@ -248,20 +248,28 @@
         wide = wide.astype(F32)
         return lax.rsqrt(jnp.mean(wide * wide, axis=-1, keepdims=True) + EPSILON)
 
-    def normed_blocks(wide, scale, gain):
-        def piece(rc, rx):
-            start = (((x + rx) % nx) * 2 + (c ^ rc)) * feat
-            value = cut(wide, start, feat, 1).astype(F32)
-            return (value * scale * cut(gain, start, feat, 0)).astype(BF16)
-
-        far = {(rc, rx): send(piece(rc, rx), rc, rx) for rx in range(1, nx) for rc in range(2)}
-        far[1, 0] = send(piece(1, 0), 1, 0)
-        far[0, 0] = piece(0, 0)
-        return [far[place] for place in places]
+    def normed_piece(wide, scale, gain, rc, rx):
+        start = (((x + rx) % nx) * 2 + (c ^ rc)) * feat
+        value = cut(wide, start, feat, 1).astype(F32)
+        return (value * scale * cut(gain, start, feat, 0)).astype(BF16)
 
     hidden_scale, embed_scale = scale_of(hidden_state), scale_of(embedded_next)
-    blocks_h = normed_blocks(hidden_state, hidden_scale, gain_hidden)
-    blocks_e = normed_blocks(embedded_next, embed_scale, gain_embed)
+    even = b % 2 == 0
+    far_h, far_e = {}, {}
+    for rx in range(nx):
+        for rc in range(2):
+            piece_h = normed_piece(hidden_state, hidden_scale, gain_hidden, rc, rx)
+            piece_e = normed_piece(embedded_next, embed_scale, gain_embed, rc, rx)
+            if rx == 0:
+                far_h[rc, 0] = send(piece_h, rc, 0) if rc else piece_h
+                far_e[rc, 0] = send(piece_e, rc, 0) if rc else piece_e
+                continue
+            got = send(jnp.where(even, piece_h, piece_e), rc, rx)
+            twin = dim_b.swap(got, 1)
+            far_h[rc, rx] = jnp.where(even, got, twin)
+            far_e[rc, rx] = jnp.where(even, twin, got)
+    blocks_h = [far_h[place] for place in places]
+    blocks_e = [far_e[place] for place in places]
 
     halves_h = [dot(piece, proj_hidden) for piece in blocks_h]
     halves_e = [dot(piece, proj_embed) for piece in blocks_e]
@@ -400,9 +408,10 @@
             kept_e = kept_e + value.astype(F32)
         kept_e = add_after(kept_e, got_e[0], [pair_h[2]])
         owned_e = to_owners(kept_e)
-        marks = [kept_h], [pair_h[2]], [owned_e[nx], pair_h[1]]
         owned_e[nx] = held_back(owned_e[nx], [pair_h[1]])
-        hidden_back = exchange_far(pair_h, dim_a).astype(F32)
+        hidden_summed = exchange_far(pair_h, dim_a)
+        hidden_back = hidden_summed.astype(F32)
+        marks = [kept_h], [pair_h[2]], [owned_e[nx], hidden_summed]
         embed_back = exchange_far(exchange_near(by_holder(owned_e), dim_a), dim_a).astype(F32)
     else:
         got_h, got_e = [

time: 409 us -> 402 us (0.983)
  waiting for transfers between devices: 196 us -> 188 us
    ppermute x18 -> x16, waiting for transfers between devices: 50.7 us -> 36 us  [send(): return lax.ppermute(value, 'ctx', pairs)]
    ppermute x13 -> x15, waiting for transfers between devices: 68.8 us -> 74.4 us  [move(): return lax.ppermute(value, self.axis, pairs)]
    ppermute x18 -> x16, starting transfers between devices: 15.4 us -> 13 us  [send(): return lax.ppermute(value, 'ctx', pairs)]
    ppermute x13 -> x15, starting transfers between devices: 9.84 us -> 12.1 us  [move(): return lax.ppermute(value, self.axis, pairs)]
  transfers between devices with their start and end apart: 35 -> 35, of which waited for: 21 -> 23; matrix products, arithmetic and copies ran while one was open for 12% -> 12% of each run, Pallas kernels for 9% -> 9%
where the time goes in v8:
time: 402 us; the launch traced here: 395 us
  waiting for transfers between devices  188 us (47%)
  matrix products  66.5 us (17%)
  starting transfers between devices  37.8 us (9%)
  other arithmetic  37 us (9%)
  Pallas kernels  34.8 us (9%)
  between operations  17.3 us (4%)
  local copies, waits for them, and re-layouts  13.8 us (3%)
    ppermute x15, waiting for transfers between devices, move(): return lax.ppermute(value, self.axis, pairs)  74.4 us
    all_gather x1, waiting for transfers between devices, local(): lax.all_gather(piece, ('ctx', 'vocab')).reshape(nc, nv, block, cols)  60.6 us
    ppermute x16, waiting for transfers between devices, send(): return lax.ppermute(value, 'ctx', pairs)  36 us
    dot_general x10, matrix products, dot(): return jnp.dot(left, right, preferred_element_type=F32)  35.4 us
    dot_general x5, matrix products, contract_last(): lax.dot_general(left, right, (((1,), (1,)), ((), ())), preferred_element_...  31 us
    pallas_call x1, Pallas kernels, head_gradient(): pl.pallas_call(body, grid=(entries // TILE,), in_specs=[pl.BlockSpec((tok...  22.2 us
    ppermute x16, starting transfers between devices, send(): return lax.ppermute(value, 'ctx', pairs)  13 us
    ppermute x15, starting transfers between devices, move(): return lax.ppermute(value, self.axis, pairs)  12.1 us
  transfers between devices with their start and end apart: 35, of which 23 were waited for; matrix products, arithmetic and copies ran while one was open for 12% of the time, Pallas kernels for 9%

profile of v8, /device:TPU:0, one launch (start us, length us, event | category | flops | bytes accessed | tf_op | source)
XLA Modules:
  0.0 394.7 jit_solution(15656238104966353393)
XLA Ops:
  9.2 1.9 multiply_reduce_fusion.1
  11.2 1.9 multiply_reduce_fusion.2
  13.7 3.0 collective-permute-start
  18.7 9.4 %collective-permute-done = bf16[128,1792]{1,0:T(8,128)(2,1)S(1)} collective-permute-done((bf16[128,1792]{1,0:T(8,128)(2,1)S(1)}, bf16[128,1792]{1,0:T(8,128)(2,1)S(1)}, u32[]{:S(2)}, u32[]{:S(2)}) %collective-permute-start) | collective-permute-done | bytes 458784 | tf_op jit(solution)/shard_map/ppermute | solution.py:245
  28.1 2.1 collective-permute-start.1
  30.9 1.4 add_convert_fusion.5
  32.3 4.0 %collective-permute-done.6 = bf16[128,1792]{1,0:T(8,128)(2,1)S(1)} collective-permute-done((bf16[128,1792]{1,0:T(8,128)(2,1)S(1)}, bf16[128,1792]{1,0:T(8,128)(2,1)S(1)}, u32[]{:S(2)}, u32[]{:S(2)}) %collective-permute-start.6) | collective-permute-done | bytes 458784 | tf_op jit(solution)/shard_map/ppermute | solution.py:245
  36.4 1.5 collective-permute-start.7
  39.7 1.4 add_convert_fusion.6
  42.6 7.1 %collective-permute-done.7 = bf16[128,1792]{1,0:T(8,128)(2,1)S(1)} collective-permute-done((bf16[128,1792]{1,0:T(8,128)(2,1)S(1)}, bf16[128,1792]{1,0:T(8,128)(2,1)S(1)}, u32[]{:S(2)}, u32[]{:S(2)}) %collective-permute-start.7) | collective-permute-done | bytes 458784 | tf_op jit(solution)/shard_map/ppermute | solution.py:28
  50.4 1.4 add_convert_fusion.4
  53.4 6.2 %collective-permute-done.8 = bf16[128,896]{1,0:T(8,128)(2,1)S(1)} collective-permute-done((bf16[128,896]{1,0:T(8,128)(2,1)S(1)}, bf16[128,896]{1,0:T(8,128)(2,1)S(1)}, u32[]{:S(2)}, u32[]{:S(2)}) %collective-permute-start.8) | collective-permute-done | bytes 229408 | tf_op jit(solution)/shard_map/ppermute | solution.py:245
  61.5 5.9 %all-to-all-start = ((f32[32,1,128]{2,1,0:T(1,128)}), f32[32,1,128]{2,1,0:T(1,128)S(1)}, u32[]{:S(2)}, u32[]{:S(2)}) async-start(f32[32,1,128]{2,1,0:T(1,128)} %broadcast_in_dim.190), calls=%async_computation | async-start | bytes 32768 | tf_op jit(solution)/shard_map/all_to_all | solution.py:283
  67.4 7.0 %all-to-all-done = f32[32,1,128]{2,1,0:T(1,128)S(1)} async-done(((f32[32,1,128]{2,1,0:T(1,128)}), f32[32,1,128]{2,1,0:T(1,128)S(1)}, u32[]{:S(2)}, u32[]{:S(2)}) %all-to-all-start) | async-done | bytes 16416 | tf_op jit(solution)/shard_map/all_to_all | solution.py:283
  74.5 60.6 %all-gather.3.cloned.1.call-done = bf16[4096,896]{1,0:T(8,128)(2,1)} async-done(((bf16[128,896]{1,0:T(8,128)(2,1)}), bf16[4096,896]{1,0:T(8,128)(2,1)}) %all-gather.3.cloned.1.call-update) | async-done | bytes 7340048 | tf_op jit(solution)/shard_map/all_gather | solution.py:288
  135.1 4.0 %constant_dynamic-slice_fusion.12 = (bf16[1,8,128,896]{3,2,1,0:T(8,128)(2,1)S(1)}, bf16[1,8,128,896]{3,2,1,0:T(8,128)(2,1)S(1)}, bf16[1,8,128,896]{3,2,1,0:T(8,128)(2,1)S(1)}, bf16[1,8,128,896]{3,2,1,0:T(8,128)(2,1)S(1)}) fusion(bf16[4,8,128,896]{3,2,1,0:T(8,128)(2,1)} %bitcast.205, s32[]{:T(128)S(6)} %select_n.315, s32[]{:T(128)S(6)} %select_n.314, ...), kind=kLoop, calls=%fused_computation.154 | loop fusion | bytes 14680080 | tf_op jit(solution)/shard_map/jit(dynamic_index_in_dim)/dynamic_slice | solution.py:291
  140.8 23.9 %exponential_reduce_fusion = (f32[512]{0:T(512)S(1)}, f32[512]{0:T(512)S(1)}, f32[512]{0:T(512)S(1)}, f32[512,2048]{1,0:T(8,128)}) fusion(f32[512]{0:T(512)S(1)} %bitcast.222, s32[2048]{0:T(1024)S(1)} %iota_add_fusion, s32[512]{0:T(512)S(1)} %bitcast.226, bf16[512,7168]{1,0:T(8,128)(2,1)S(1)} %constant_dynamic-update-slice_fusion.rows_ref, ...), kind=kOutput, calls=%fused_computation.10 | convolution fusion | flops 15040774144 | bytes 40912896 | tf_op jit(solution)/shard_map/dot_general | solution.py:62
  165.5 3.3 all-to-all-start.1
  168.9 8.5 %all-to-all-done.1 = f32[32,3,4,128]{3,2,1,0:T(4,128)S(1)} async-done(((f32[32,3,4,128]{3,2,1,0:T(4,128)}), f32[32,3,4,128]{3,2,1,0:T(4,128)S(1)}, u32[]{:S(2)}, u32[]{:S(2)}) %all-to-all-start.1) | async-done | bytes 196640 | tf_op jit(solution)/shard_map/all_to_all | solution.py:54
  177.6 3.2 fusion.3.grad_ref
  180.8 14.5 %convolution_convert_fusion = bf16[256,7168]{1,0:T(8,128)(2,1)} fusion(bf16[2048,7168]{1,0:T(8,128)(2,1)} %param.17, bf16[512,2048]{1,0:T(8,128)(2,1)S(1)} %fusion.3.grad_ref), kind=kOutput, calls=%fused_computation | convolution fusion | flops 7518027776 | bytes 34078720 | tf_op jit(solution)/shard_map/dot_general | solution.py:185
  195.5 13.3 %convolution_convert_fusion.1 = bf16[256,7168]{1,0:T(8,128)(2,1)S(1)} fusion(bf16[2048,7168]{1,0:T(8,128)(2,1)} %param.17, bf16[512,2048]{1,0:T(8,128)(2,1)S(1)} %fusion.3.grad_ref), kind=kOutput, calls=%fused_computation.1 | convolution fusion | flops 7518027776 | bytes 34078720 | tf_op jit(solution)/shard_map/dot_general | solution.py:185
  208.8 3.4 add_convert_fusion
  212.9 1.8 collective-permute-start.12
  215.2 22.2 %shard_map.169 = (bf16[2048,7168]{1,0:T(8,128)(2,1)}, f32[8,128]{1,0:T(8,128)S(1)}) custom-call(bf16[512,2048]{1,0:T(8,128)(2,1)S(1)} %fusion.3.grad_ref, bf16[512,7168]{1,0:T(8,128)(2,1)} %copy-done.28, bf16[64,7168]{1,0:T(8,128)(2,1)S(1)} %get-tuple-element.45.rest_0_, bf16[4,128,896]{2,1,0:T(8,128)(2,1)S(1)} %pad_maximum_fusion.4.rest_1_), custom_call_target="tpu_custom_call" | custom-call | flops 15032385536 | bytes 36700160 | tf_op jit(solution)/shard_map/pallas_call | solution.py:93
  237.7 1.6 collective-permute-start.13
  240.8 9.4 %collective-permute-done.13 = bf16[4,64,896]{2,1,0:T(8,128)(2,1)} collective-permute-done((bf16[4,64,896]{2,1,0:T(8,128)(2,1)S(1)}, bf16[4,64,896]{2,1,0:T(8,128)(2,1)}, u32[]{:S(2)}, u32[]{:S(2)}) %collective-permute-start.13) | collective-permute-done | bytes 458784 | tf_op jit(solution)/shard_map/ppermute | solution.py:28
  255.4 1.6 pad_maximum_fusion
  257.2 9.0 %collective-permute-done.14 = bf16[2,128,896]{2,1,0:T(8,128)(2,1)} collective-permute-done((bf16[2,128,896]{2,1,0:T(8,128)(2,1)}, bf16[2,128,896]{2,1,0:T(8,128)(2,1)}, u32[]{:S(2)}, u32[]{:S(2)}) %collective-permute-start.14) | collective-permute-done | bytes 458784 | tf_op jit(solution)/shard_map/ppermute | solution.py:28
  268.1 10.2 %collective-permute-done.15 = bf16[128,896]{1,0:T(8,128)(2,1)S(1)} collective-permute-done((bf16[128,896]{1,0:T(8,128)(2,1)S(1)}, bf16[128,896]{1,0:T(8,128)(2,1)S(1)}, u32[]{:S(2)}, u32[]{:S(2)}) %collective-permute-start.15) | collective-permute-done | bytes 229408 | tf_op jit(solution)/shard_map/ppermute | solution.py:28
  279.1 1.6 collective-permute-start.18
  280.8 6.3 %collective-permute-done.16 = bf16[128,896]{1,0:T(8,128)(2,1)S(1)} collective-permute-done((bf16[128,896]{1,0:T(8,128)(2,1)S(1)}, bf16[128,896]{1,0:T(8,128)(2,1)S(1)}, u32[]{:S(2)}, u32[]{:S(2)}) %collective-permute-start.16) | collective-permute-done | bytes 229408 | tf_op jit(solution)/shard_map/ppermute | solution.py:245
  288.3 2.3 fusion.6
  292.6 2.2 fusion.22
  296.8 2.5 fusion.11.refs_0_
  299.2 15.3 %collective-permute-done.19 = bf16[512,896]{1,0:T(8,128)(2,1)S(1)} collective-permute-done((bf16[512,896]{1,0:T(8,128)(2,1)S(1)}, bf16[512,896]{1,0:T(8,128)(2,1)S(1)}, u32[]{:S(2)}, u32[]{:S(2)}) %collective-permute-start.19) | collective-permute-done | bytes 917536 | tf_op jit(solution)/shard_map/ppermute | solution.py:28
  316.6 2.0 collective-permute-start.20
  319.5 5.0 %shard_map.171 = (bf16[1792,896]{1,0:T(8,128)(2,1)}, f32[1792,128]{1,0:T(8,128)S(1)}) custom-call(bf16[512,1792]{1,0:T(8,128)(2,1)S(1)} %pad_maximum_fusion.2.normed_ref, bf16[512,896]{1,0:T(8,128)(2,1)S(1)} %get-tuple-element.38.grad_ref, bf16[1792,896]{1,0:T(8,128)(2,1)} %weight_ref.2, bf16[512,896]{1,0:T(8,128)(2,1)S(1)} %add_convert_fusion.1.rest_0_), custom_call_target="tpu_custom_call" | custom-call | flops 1644167168 | bytes 9175040 | tf_op jit(solution)/shard_map/pallas_call | solution.py:161
  325.0 5.4 %collective-permute-done.22 = bf16[128,896]{1,0:T(8,128)(2,1)} collective-permute-done((bf16[128,896]{1,0:T(8,128)(2,1)S(1)}, bf16[128,896]{1,0:T(8,128)(2,1)}, u32[]{:S(2)}, u32[]{:S(2)}) %collective-permute-start.22) | collective-permute-done | bytes 229408 | tf_op jit(solution)/shard_map/ppermute | solution.py:245
  332.7 1.6 collective-permute-done.25.refs_1_
  338.6 5.3 %shard_map.172 = (bf16[1792,896]{1,0:T(8,128)(2,1)}, f32[1792,128]{1,0:T(8,128)S(1)}) custom-call(bf16[512,1792]{1,0:T(8,128)(2,1)S(1)} %pad_maximum_fusion.3.normed_ref, bf16[512,896]{1,0:T(8,128)(2,1)S(1)} %get-tuple-element.38.grad_ref, bf16[1792,896]{1,0:T(8,128)(2,1)} %weight_ref.3, bf16[2,128,896]{2,1,0:T(8,128)(2,1)S(1)} %pad_maximum_fusion.12.rest_0_.refs_2_), custom_call_target="tpu_custom_call" | custom-call | flops 1644167168 | bytes 9175040 | tf_op jit(solution)/shard_map/pallas_call | solution.py:161
  345.9 3.4 collective-permute-done.28
  351.5 7.2 %collective-permute-done.24 = bf16[128,896]{1,0:T(8,128)(2,1)S(1)} collective-permute-done((bf16[128,896]{1,0:T(8,128)(2,1)S(1)}, bf16[128,896]{1,0:T(8,128)(2,1)S(1)}, u32[]{:S(2)}, u32[]{:S(2)}) %collective-permute-start.24) | collective-permute-done | bytes 229408 | tf_op jit(solution)/shard_map/ppermute | solution.py:28
  359.6 3.4 all-to-all-start.2
  364.2 5.9 %collective-permute-done.29 = bf16[2,128,896]{2,1,0:T(8,128)(2,1)} collective-permute-done((bf16[2,128,896]{2,1,0:T(8,128)(2,1)}, bf16[2,128,896]{2,1,0:T(8,128)(2,1)}, u32[]{:S(2)}, u32[]{:S(2)}) %collective-permute-start.29) | collective-permute-done | bytes 458784 | tf_op jit(solution)/shard_map/ppermute | solution.py:28
  375.2 1.8 subtract_convert_fusion.1
  378.4 6.2 %collective-permute-done.30 = bf16[128,896]{1,0:T(8,128)(2,1)S(1)} collective-permute-done((bf16[128,896]{1,0:T(8,128)(2,1)S(1)}, bf16[128,896]{1,0:T(8,128)(2,1)S(1)}, u32[]{:S(2)}, u32[]{:S(2)}) %collective-permute-start.30) | collective-permute-done | bytes 229408 | tf_op jit(solution)/shard_map/ppermute | solution.py:28
  384.6 1.8 subtract_convert_fusion
  (212 shorter events, 53.4 us)
Async XLA Ops:
  7.2 127.9 %all-gather.3.cloned.1.call-start = ((), (), s32[]{:S(2)}) async-start(), calls=%async_computation.3 | async-start | bytes 7569408 | tf_op jit(solution)/shard_map/all_gather | solution.py:288
  13.7 14.4 %collective-permute-start = (bf16[128,1792]{1,0:T(8,128)(2,1)S(1)}, bf16[128,1792]{1,0:T(8,128)(2,1)S(1)}, u32[]{:S(2)}, u32[]{:S(2)}) collective-permute-start(bf16[128,1792]{1,0:T(8,128)(2,1)S(1)} %get-tuple-element.43), channel_id=1, source_target_pairs={{0,16},{8,24},{16,0},{24,8},{1,17},{9,25},{17,1},{25,9},{2,18},{10... | collective-permute-start | bytes 1376264 | tf_op jit(solution)/shard_map/ppermute | solution.py:245
  17.0 35.7 %copy-start.14 = (bf16[128,1792]{1,0:T(8,128)(2,1)}, bf16[128,1792]{1,0:T(8,128)(2,1)S(1)}, u32[]{:S(2)}) copy-start(bf16[128,1792]{1,0:T(8,128)(2,1)S(1)} %get-tuple-element.47) | copy-start | bytes 1376260
  17.0 13.1 %copy-start.3 = (bf16[1792,896]{1,0:T(8,128)(2,1)S(1)}, bf16[1792,896]{1,0:T(8,128)(2,1)}, u32[]{:S(2)}) copy-start(bf16[1792,896]{1,0:T(8,128)(2,1)} %weight_ref.3) | copy-start | bytes 9633796
  17.1 13.1 %collective-permute-start.4 = (bf16[128,1792]{1,0:T(8,128)(2,1)S(1)}, bf16[128,1792]{1,0:T(8,128)(2,1)S(1)}, u32[]{:S(2)}, u32[]{:S(2)}) collective-permute-start(bf16[128,1792]{1,0:T(8,128)(2,1)S(1)} %get-tuple-element.48), channel_id=1, source_target_pairs={{0,8},{8,0},{16,24},{24,16},{1,9},{9,1},{17,25},{25,17},{2,10},{10... | collective-permute-start | bytes 1376264 | tf_op jit(solution)/shard_map/ppermute | solution.py:245
  17.4 13.4 %copy-start.16 = (bf16[128,1792]{1,0:T(8,128)(2,1)}, bf16[128,1792]{1,0:T(8,128)(2,1)S(1)}, u32[]{:S(2)}) copy-start(bf16[128,1792]{1,0:T(8,128)(2,1)S(1)} %get-tuple-element.49) | copy-start | bytes 1376260
  17.4 13.4 %collective-permute-start.3 = (bf16[128,1792]{1,0:T(8,128)(2,1)S(1)}, bf16[128,1792]{1,0:T(8,128)(2,1)S(1)}, u32[]{:S(2)}, u32[]{:S(2)}) collective-permute-start(bf16[128,1792]{1,0:T(8,128)(2,1)S(1)} %get-tuple-element.50), channel_id=1, source_target_pairs={{0,8},{8,0},{16,24},{24,16},{1,9},{9,1},{17,25},{25,17},{2,10},{10... | collective-permute-start | bytes 1376264 | tf_op jit(solution)/shard_map/ppermute | solution.py:245
  18.0 18.4 %collective-permute-start.6 = (bf16[128,1792]{1,0:T(8,128)(2,1)S(1)}, bf16[128,1792]{1,0:T(8,128)(2,1)S(1)}, u32[]{:S(2)}, u32[]{:S(2)}) collective-permute-start(bf16[128,1792]{1,0:T(8,128)(2,1)S(1)} %get-tuple-element.44), channel_id=1, source_target_pairs={{0,24},{8,16},{16,8},{24,0},{1,25},{9,17},{17,9},{25,1},{2,26},{10... | collective-permute-start | bytes 1376264 | tf_op jit(solution)/shard_map/ppermute | solution.py:245
  18.7 40.9 %copy-start.11 = (f32[128,896]{1,0:T(8,128)}, f32[128,896]{1,0:T(8,128)S(1)}, u32[]{:S(2)}) copy-start(f32[128,896]{1,0:T(8,128)S(1)} %fusion.65) | copy-start | bytes 1376260
  28.1 10.9 %collective-permute-start.1 = (bf16[128,1792]{1,0:T(8,128)(2,1)S(1)}, bf16[128,1792]{1,0:T(8,128)(2,1)S(1)}, u32[]{:S(2)}, u32[]{:S(2)}) collective-permute-start(bf16[128,1792]{1,0:T(8,128)(2,1)S(1)} %collective-permute-done), channel_id=1, source_target_pairs={{0,1},{1,0},{2,3},{3,2},{4,5},{5,4},{6,7},{7,6},{8,9},{9,8},{10,11... | collective-permute-start | bytes 1376264 | tf_op jit(solution)/shard_map/ppermute | solution.py:28
  32.3 21.1 %collective-permute-start.5 = (bf16[128,896]{1,0:T(8,128)(2,1)S(1)}, bf16[128,896]{1,0:T(8,128)(2,1)S(1)}, u32[]{:S(2)}, u32[]{:S(2)}) collective-permute-start(bf16[128,896]{1,0:T(8,128)(2,1)S(1)} %get-tuple-element.113), channel_id=1, source_target_pairs={{0,8},{8,0},{16,24},{24,16},{1,9},{9,1},{17,25},{25,17},{2,10},{10... | collective-permute-start | bytes 688136 | tf_op jit(solution)/shard_map/ppermute | solution.py:245
  36.4 13.3 %collective-permute-start.7 = (bf16[128,1792]{1,0:T(8,128)(2,1)S(1)}, bf16[128,1792]{1,0:T(8,128)(2,1)S(1)}, u32[]{:S(2)}, u32[]{:S(2)}) collective-permute-start(bf16[128,1792]{1,0:T(8,128)(2,1)S(1)} %collective-permute-done.6), channel_id=1, source_target_pairs={{0,1},{1,0},{2,3},{3,2},{4,5},{5,4},{6,7},{7,6},{8,9},{9,8},{10,11... | collective-permute-start | bytes 1376264 | tf_op jit(solution)/shard_map/ppermute | solution.py:28
  41.2 12.2 %collective-permute-start.2 = (bf16[128,896]{1,0:T(8,128)(2,1)S(1)}, bf16[128,896]{1,0:T(8,128)(2,1)S(1)}, u32[]{:S(2)}, u32[]{:S(2)}) collective-permute-start(bf16[128,896]{1,0:T(8,128)(2,1)S(1)} %get-tuple-element.115), channel_id=1, source_target_pairs={{0,16},{8,24},{16,0},{24,8},{1,17},{9,25},{17,1},{25,9},{2,18},{10... | collective-permute-start | bytes 688136 | tf_op jit(solution)/shard_map/ppermute | solution.py:245
  51.9 7.7 %collective-permute-start.8 = (bf16[128,896]{1,0:T(8,128)(2,1)S(1)}, bf16[128,896]{1,0:T(8,128)(2,1)S(1)}, u32[]{:S(2)}, u32[]{:S(2)}) collective-permute-start(bf16[128,896]{1,0:T(8,128)(2,1)S(1)} %get-tuple-element.111), channel_id=1, source_target_pairs={{0,24},{8,16},{16,8},{24,0},{1,25},{9,17},{17,9},{25,1},{2,26},{10... | collective-permute-start | bytes 688136 | tf_op jit(solution)/shard_map/ppermute | solution.py:245
  61.5 13.0 %all-to-all-start = ((f32[32,1,128]{2,1,0:T(1,128)}), f32[32,1,128]{2,1,0:T(1,128)S(1)}, u32[]{:S(2)}, u32[]{:S(2)}) async-start(f32[32,1,128]{2,1,0:T(1,128)} %broadcast_in_dim.190), calls=%async_computation | async-start | bytes 32768 | tf_op jit(solution)/shard_map/all_to_all | solution.py:283
  140.8 24.0 %copy-start.28 = (bf16[512,7168]{1,0:T(8,128)(2,1)}, bf16[512,7168]{1,0:T(8,128)(2,1)S(1)}, u32[]{:S(2)}) copy-start(bf16[512,7168]{1,0:T(8,128)(2,1)S(1)} %constant_dynamic-update-slice_fusion.rows_ref) | copy-start | bytes 22020100
  140.8 28.1 %copy-start.31 = (s32[512]{0:T(512)S(1)}, s32[512]{0:T(512)}, u32[]{:S(2)}) copy-start(s32[512]{0:T(512)} %param.19) | copy-start | bytes 6148
  165.5 11.8 %all-to-all-start.1 = ((f32[32,3,4,128]{3,2,1,0:T(4,128)}), f32[32,3,4,128]{3,2,1,0:T(4,128)S(1)}, u32[]{:S(2)}, u32[]{:S(2)}) async-start(f32[32,3,4,128]{3,2,1,0:T(4,128)} %broadcast_in_dim.200), calls=%async_computation.1 | async-start | bytes 393216 | tf_op jit(solution)/shard_map/all_to_all | solution.py:54
  195.3 13.5 %collective-permute-start.9 = (bf16[256,7168]{1,0:T(8,128)(2,1)}, bf16[256,7168]{1,0:T(8,128)(2,1)}, u32[]{:S(2)}, u32[]{:S(2)}) collective-permute-start(bf16[256,7168]{1,0:T(8,128)(2,1)} %convolution_convert_fusion), channel_id=1, source_target_pairs={{0,8},{8,0},{16,24},{24,16},{1,9},{9,1},{17,25},{25,17},{2,10},{10... | collective-permute-start | bytes 11010056 | tf_op jit(solution)/shard_map/ppermute | solution.py:28
  212.9 24.5 %collective-permute-start.12 = (bf16[4,128,896]{2,1,0:T(8,128)(2,1)S(1)}, bf16[4,128,896]{2,1,0:T(8,128)(2,1)S(1)}, u32[]{:S(2)}, u32[]{:S(2)}) collective-permute-start(bf16[4,128,896]{2,1,0:T(8,128)(2,1)S(1)} %pad_maximum_fusion.4.rest_1_), channel_id=1, source_target_pairs={{0,1},{1,0},{2,3},{3,2},{4,5},{5,4},{6,7},{7,6},{8,9},{9,8},{10,11... | collective-permute-start | bytes 2752520 | tf_op jit(solution)/shard_map/ppermute | solution.py:28
  214.7 24.6 %collective-permute-start.10 = (bf16[64,7168]{1,0:T(8,128)(2,1)S(1)}, bf16[64,7168]{1,0:T(8,128)(2,1)S(1)}, u32[]{:S(2)}, u32[]{:S(2)}) collective-permute-start(bf16[64,7168]{1,0:T(8,128)(2,1)S(1)} %get-tuple-element.45.rest_0_), channel_id=1, source_target_pairs={{0,16},{8,24},{16,0},{24,8},{1,17},{9,25},{17,1},{25,9},{2,18},{10... | collective-permute-start | bytes 2752520 | tf_op jit(solution)/shard_map/ppermute | solution.py:28
  237.7 12.5 %collective-permute-start.13 = (bf16[4,64,896]{2,1,0:T(8,128)(2,1)S(1)}, bf16[4,64,896]{2,1,0:T(8,128)(2,1)}, u32[]{:S(2)}, u32[]{:S(2)}) collective-permute-start(bf16[4,64,896]{2,1,0:T(8,128)(2,1)S(1)} %slice_bitcast_fusion.2), channel_id=1, source_target_pairs={{0,16},{8,24},{16,0},{24,8},{1,17},{9,25},{17,1},{25,9},{2,18},{10... | collective-permute-start | bytes 1376264 | tf_op jit(solution)/shard_map/ppermute | solution.py:28
  240.5 12.3 %collective-permute-start.11 = (bf16[4,64,896]{2,1,0:T(8,128)(2,1)}, bf16[4,64,896]{2,1,0:T(8,128)(2,1)}, u32[]{:S(2)}, u32[]{:S(2)}) collective-permute-start(bf16[4,64,896]{2,1,0:T(8,128)(2,1)} %pad_maximum_fusion.10), channel_id=1, source_target_pairs={{0,1},{1,0},{2,3},{3,2},{4,5},{5,4},{6,7},{7,6},{8,9},{9,8},{10,11... | collective-permute-start | bytes 1376264 | tf_op jit(solution)/shard_map/ppermute | solution.py:28
  254.8 11.3 %collective-permute-start.14 = (bf16[2,128,896]{2,1,0:T(8,128)(2,1)}, bf16[2,128,896]{2,1,0:T(8,128)(2,1)}, u32[]{:S(2)}, u32[]{:S(2)}) collective-permute-start(bf16[2,128,896]{2,1,0:T(8,128)(2,1)} %pad_maximum_fusion.11), channel_id=1, source_target_pairs={{0,2},{1,3},{2,0},{3,1},{4,6},{5,7},{6,4},{7,5},{8,10},{9,11},{10,... | collective-permute-start | bytes 1376264 | tf_op jit(solution)/shard_map/ppermute | solution.py:28
  257.0 11.0 %copy-start.17 = (bf16[128,1792]{1,0:T(8,128)(2,1)S(1)}, bf16[128,1792]{1,0:T(8,128)(2,1)}, u32[]{:S(2)}) copy-start(bf16[128,1792]{1,0:T(8,128)(2,1)} %copy-done.16) | copy-start | bytes 1376260
  257.0 11.0 %copy-start.25 = (bf16[128,1792]{1,0:T(8,128)(2,1)S(1)}, bf16[128,1792]{1,0:T(8,128)(2,1)}, u32[]{:S(2)}) copy-start(bf16[128,1792]{1,0:T(8,128)(2,1)} %copy-done.24) | copy-start | bytes 1376260
  267.2 13.4 %copy-start.15 = (bf16[128,1792]{1,0:T(8,128)(2,1)S(1)}, bf16[128,1792]{1,0:T(8,128)(2,1)}, u32[]{:S(2)}) copy-start(bf16[128,1792]{1,0:T(8,128)(2,1)} %copy-done.14) | copy-start | bytes 1376260
  267.3 13.4 %copy-start.19 = (bf16[128,1792]{1,0:T(8,128)(2,1)S(1)}, bf16[128,1792]{1,0:T(8,128)(2,1)}, u32[]{:S(2)}) copy-start(bf16[128,1792]{1,0:T(8,128)(2,1)} %copy-done.18) | copy-start | bytes 1376260
  267.3 13.4 %copy-start.21 = (bf16[128,1792]{1,0:T(8,128)(2,1)S(1)}, bf16[128,1792]{1,0:T(8,128)(2,1)}, u32[]{:S(2)}) copy-start(bf16[128,1792]{1,0:T(8,128)(2,1)} %copy-done.20) | copy-start | bytes 1376260
  267.3 13.4 %copy-start.27 = (bf16[128,1792]{1,0:T(8,128)(2,1)S(1)}, bf16[128,1792]{1,0:T(8,128)(2,1)}, u32[]{:S(2)}) copy-start(bf16[128,1792]{1,0:T(8,128)(2,1)} %copy-done.26) | copy-start | bytes 1376260
  267.3 11.0 %collective-permute-start.15 = (bf16[128,896]{1,0:T(8,128)(2,1)S(1)}, bf16[128,896]{1,0:T(8,128)(2,1)S(1)}, u32[]{:S(2)}, u32[]{:S(2)}) collective-permute-start(bf16[128,896]{1,0:T(8,128)(2,1)S(1)} %fusion.42), channel_id=1, source_target_pairs={{0,4},{1,5},{2,6},{3,7},{4,0},{5,1},{6,2},{7,3},{8,12},{9,13},{10,... | collective-permute-start | bytes 688136 | tf_op jit(solution)/shard_map/ppermute | solution.py:28
  278.5 12.2 %copy-start.2 = (bf16[1792,896]{1,0:T(8,128)(2,1)S(1)}, bf16[1792,896]{1,0:T(8,128)(2,1)}, u32[]{:S(2)}) copy-start(bf16[1792,896]{1,0:T(8,128)(2,1)} %weight_ref.2) | copy-start | bytes 9633796
  278.5 8.6 %collective-permute-start.16 = (bf16[128,896]{1,0:T(8,128)(2,1)S(1)}, bf16[128,896]{1,0:T(8,128)(2,1)S(1)}, u32[]{:S(2)}, u32[]{:S(2)}) collective-permute-start(bf16[128,896]{1,0:T(8,128)(2,1)S(1)} %fusion.41), channel_id=1, source_target_pairs={{0,16},{8,24},{16,0},{24,8},{1,17},{9,25},{17,1},{25,9},{2,18},{10... | collective-permute-start | bytes 688136 | tf_op jit(solution)/shard_map/ppermute | solution.py:245
  279.1 8.0 %collective-permute-start.17 = (bf16[128,896]{1,0:T(8,128)(2,1)S(1)}, bf16[128,896]{1,0:T(8,128)(2,1)S(1)}, u32[]{:S(2)}, u32[]{:S(2)}) collective-permute-start(bf16[128,896]{1,0:T(8,128)(2,1)S(1)} %fusion.41), channel_id=1, source_target_pairs={{0,8},{8,0},{16,24},{24,16},{1,9},{9,1},{17,25},{25,17},{2,10},{10... | collective-permute-start | bytes 688136 | tf_op jit(solution)/shard_map/ppermute | solution.py:245
  279.1 9.2 %collective-permute-start.18 = (bf16[128,896]{1,0:T(8,128)(2,1)S(1)}, bf16[128,896]{1,0:T(8,128)(2,1)S(1)}, u32[]{:S(2)}, u32[]{:S(2)}) collective-permute-start(bf16[128,896]{1,0:T(8,128)(2,1)S(1)} %fusion.41), channel_id=1, source_target_pairs={{0,24},{8,16},{16,8},{24,0},{1,25},{9,17},{17,9},{25,1},{2,26},{10... | collective-permute-start | bytes 688136 | tf_op jit(solution)/shard_map/ppermute | solution.py:245
  291.9 22.6 %collective-permute-start.19 = (bf16[512,896]{1,0:T(8,128)(2,1)S(1)}, bf16[512,896]{1,0:T(8,128)(2,1)S(1)}, u32[]{:S(2)}, u32[]{:S(2)}) collective-permute-start(bf16[512,896]{1,0:T(8,128)(2,1)S(1)} %fusion.19), channel_id=1, source_target_pairs={{0,1},{1,0},{2,3},{3,2},{4,5},{5,4},{6,7},{7,6},{8,9},{9,8},{10,11... | collective-permute-start | bytes 2752520 | tf_op jit(solution)/shard_map/ppermute | solution.py:28
  294.7 39.6 %collective-permute-start.25 = (bf16[512,896]{1,0:T(8,128)(2,1)}, bf16[512,896]{1,0:T(8,128)(2,1)}, u32[]{:S(2)}, u32[]{:S(2)}) collective-permute-start(bf16[512,896]{1,0:T(8,128)(2,1)} %fusion.22), channel_id=1, source_target_pairs={{0,1},{1,0},{2,3},{3,2},{4,5},{5,4},{6,7},{7,6},{8,9},{9,8},{10,11... | collective-permute-start | bytes 2752520 | tf_op jit(solution)/shard_map/ppermute | solution.py:28
  316.6 8.3 %collective-permute-start.20 = (bf16[128,896]{1,0:T(8,128)(2,1)}, bf16[128,896]{1,0:T(8,128)(2,1)S(1)}, u32[]{:S(2)}, u32[]{:S(2)}) collective-permute-start(bf16[128,896]{1,0:T(8,128)(2,1)} %get-tuple-element.78), channel_id=1, source_target_pairs={{0,16},{8,24},{16,0},{24,8},{1,17},{9,25},{17,1},{25,9},{2,18},{10... | collective-permute-start | bytes 688136 | tf_op jit(solution)/shard_map/ppermute | solution.py:245
  318.6 6.3 %collective-permute-start.21 = (bf16[128,896]{1,0:T(8,128)(2,1)}, bf16[128,896]{1,0:T(8,128)(2,1)}, u32[]{:S(2)}, u32[]{:S(2)}) collective-permute-start(bf16[128,896]{1,0:T(8,128)(2,1)} %get-tuple-element.77), channel_id=1, source_target_pairs={{0,8},{8,0},{16,24},{24,16},{1,9},{9,1},{17,25},{25,17},{2,10},{10... | collective-permute-start | bytes 688136 | tf_op jit(solution)/shard_map/ppermute | solution.py:245
  318.6 11.7 %collective-permute-start.22 = (bf16[128,896]{1,0:T(8,128)(2,1)S(1)}, bf16[128,896]{1,0:T(8,128)(2,1)}, u32[]{:S(2)}, u32[]{:S(2)}) collective-permute-start(bf16[128,896]{1,0:T(8,128)(2,1)S(1)} %get-tuple-element.76), channel_id=1, source_target_pairs={{0,24},{8,16},{16,8},{24,0},{1,25},{9,17},{17,9},{25,1},{2,26},{10... | collective-permute-start | bytes 688136 | tf_op jit(solution)/shard_map/ppermute | solution.py:245
  331.9 12.7 %collective-permute-start.23 = (bf16[2,128,896]{2,1,0:T(8,128)(2,1)S(1)}, bf16[2,128,896]{2,1,0:T(8,128)(2,1)}, u32[]{:S(2)}, u32[]{:S(2)}) collective-permute-start(bf16[2,128,896]{2,1,0:T(8,128)(2,1)S(1)} %pad_maximum_fusion.12.rest_0_.refs_2_), channel_id=1, source_target_pairs={{0,2},{1,3},{2,0},{3,1},{4,6},{5,7},{6,4},{7,5},{8,10},{9,11},{10,... | collective-permute-start | bytes 1376264 | tf_op jit(solution)/shard_map/ppermute | solution.py:28
  336.6 9.3 %collective-permute-start.26 = (bf16[128,896]{1,0:T(8,128)(2,1)}, bf16[128,896]{1,0:T(8,128)(2,1)S(1)}, u32[]{:S(2)}, u32[]{:S(2)}) collective-permute-start(bf16[128,896]{1,0:T(8,128)(2,1)} %get-tuple-element.68), channel_id=1, source_target_pairs={{0,8},{8,0},{16,24},{24,16},{1,9},{9,1},{17,25},{25,17},{2,10},{10... | collective-permute-start | bytes 688136 | tf_op jit(solution)/shard_map/ppermute | solution.py:245
  337.0 8.8 %collective-permute-start.27 = (bf16[128,896]{1,0:T(8,128)(2,1)}, bf16[128,896]{1,0:T(8,128)(2,1)}, u32[]{:S(2)}, u32[]{:S(2)}) collective-permute-start(bf16[128,896]{1,0:T(8,128)(2,1)} %get-tuple-element.67), channel_id=1, source_target_pairs={{0,16},{8,24},{16,0},{24,8},{1,17},{9,25},{17,1},{25,9},{2,18},{10... | collective-permute-start | bytes 688136 | tf_op jit(solution)/shard_map/ppermute | solution.py:245
  338.5 10.8 %collective-permute-start.28 = (bf16[128,896]{1,0:T(8,128)(2,1)}, bf16[128,896]{1,0:T(8,128)(2,1)}, u32[]{:S(2)}, u32[]{:S(2)}) collective-permute-start(bf16[128,896]{1,0:T(8,128)(2,1)} %get-tuple-element.66), channel_id=1, source_target_pairs={{0,24},{8,16},{16,8},{24,0},{1,25},{9,17},{17,9},{25,1},{2,26},{10... | collective-permute-start | bytes 688136 | tf_op jit(solution)/shard_map/ppermute | solution.py:245
  345.7 13.1 %collective-permute-start.24 = (bf16[128,896]{1,0:T(8,128)(2,1)S(1)}, bf16[128,896]{1,0:T(8,128)(2,1)S(1)}, u32[]{:S(2)}, u32[]{:S(2)}) collective-permute-start(bf16[128,896]{1,0:T(8,128)(2,1)S(1)} %fusion.43.refs_1_), channel_id=1, source_target_pairs={{0,4},{1,5},{2,6},{3,7},{4,0},{5,1},{6,2},{7,3},{8,12},{9,13},{10,... | collective-permute-start | bytes 688136 | tf_op jit(solution)/shard_map/ppermute | solution.py:28
  351.5 18.6 %collective-permute-start.29 = (bf16[2,128,896]{2,1,0:T(8,128)(2,1)}, bf16[2,128,896]{2,1,0:T(8,128)(2,1)}, u32[]{:S(2)}, u32[]{:S(2)}) collective-permute-start(bf16[2,128,896]{2,1,0:T(8,128)(2,1)} %pad_maximum_fusion.13), channel_id=1, source_target_pairs={{0,2},{1,3},{2,0},{3,1},{4,6},{5,7},{6,4},{7,5},{8,10},{9,11},{10,... | collective-permute-start | bytes 1376264 | tf_op jit(solution)/shard_map/ppermute | solution.py:28
  359.6 14.1 %all-to-all-start.2 = ((f32[32,2,1024]{2,1,0:T(2,128)}), f32[32,2,1024]{2,1,0:T(2,128)S(1)}, u32[]{:S(2)}, u32[]{:S(2)}) async-start(f32[32,2,1024]{2,1,0:T(2,128)} %shard_map.175), calls=%async_computation.2 | async-start | bytes 524288 | tf_op jit(solution)/shard_map/all_to_all | solution.py:452
  371.2 13.4 %collective-permute-start.30 = (bf16[128,896]{1,0:T(8,128)(2,1)S(1)}, bf16[128,896]{1,0:T(8,128)(2,1)S(1)}, u32[]{:S(2)}, u32[]{:S(2)}) collective-permute-start(bf16[128,896]{1,0:T(8,128)(2,1)S(1)} %fusion.44), channel_id=1, source_target_pairs={{0,4},{1,5},{2,6},{3,7},{4,0},{5,1},{6,2},{7,3},{8,12},{9,13},{10,... | collective-permute-start | bytes 688136 | tf_op jit(solution)/shard_map/ppermute | solution.py:28
  (20 other events, 87.1 us)
Sparse Core Ops, SparseCore 0:
  60.7 74.3 all-gather.2
